TPU v7x, 32 devices: a whole 2x2x4 slice. The times are simulated.
32 devices in a mesh: groups: 2 (over y), seq: 4 (over z), head: 4 (over x, core).
Axes of the slice: x: 2, y: 2, z: 4, core: 2. Of those that a mesh axis runs over, the one named last changes fastest.
Arguments:
- source_cache: bfloat16 [4, 8, 2048, 256], P('groups', 'head', 'seq'), parts along dimension 0, may hold values from -160 to 160
- kept_blocks: int32 [4, 8, 4], P('groups'), parts along dimension 0, may hold values from 0 to 15, as said below
- new_hidden: bfloat16 [4, 4, 8192], P('groups', None, 'seq'), parts along dimension 0, may hold values from -6 to 6
- norm_gain: bfloat16 [8192], P('seq'), may hold values from 0.099609375 to 1.8984375
- w_query: bfloat16 [8192, 8192], P('seq', 'head'), may hold values from -1 to 1
- w_keyval: bfloat16 [8192, 8, 256], P('seq', 'head'), may hold values from -4 to 4
- w_out: bfloat16 [8192, 8192], P('head', 'seq'), may hold values from -0.0625 to 0.0625
Outputs:
- kept_cache: bfloat16 [4, 8, 512, 256], P('head', ('groups', 'seq')), parts along dimension 1
- decoded: bfloat16 [4, 4, 8192], P('groups', None, 'seq'), parts along dimension 0
There are 2 independent parts, one for each index of `groups`. A program takes and returns all parts, laid end to end along the dimension named above; an argument that names none is the same for every part. Nothing has to cross between parts.
Inputs may be any that keep to these rules, and one draw needn't show every extreme that they name: `kept_blocks`: each row is increasing; block b lies on index b // 4 of seq. At most 2 kept blocks of one request and head lie on one index of seq. The number of indices that hold exactly 2 of them differs between request-head pairs, from 1 to 2; in every request some pair reaches that largest number.
All inputs are finite; a program needn't handle non-finite values.
Results may differ from a plain program's by a relative error of at most 0.0065.
Values may be sent and summed in bfloat16 or wider, within the bound.
No kernel may reach another device: no remote copies, remote signals or barrier semaphores. Data moves between devices by JAX's collectives and lax.ppermute only.
A program may use at most 128 MiB of HBM per device.

v0:
```python
import math

import jax
import jax.numpy as jnp
from jax import lax
from jax.sharding import PartitionSpec as P

D = 8192
HD = 128
QPK = 8
BLK = 128
MOST = 2


rope_base = 500000.0


def rotate(tensor, angles):
    half_dim = tensor.shape[-1] // 2
    lower_half = tensor[..., :half_dim]
    upper_half = tensor[..., half_dim:]
    cosine = jnp.cos(angles)
    sine_part = jnp.sin(angles)
    return jnp.concatenate(
        [
            lower_half * cosine - upper_half * sine_part,
            upper_half * cosine + lower_half * sine_part,
        ],
        axis=-1,
    )


def pick_rows(source_table, row_index):
    return source_table[row_index]


def shards(source_cache, kept_blocks, new_hidden, norm_gain, w_query, w_keyval, w_out):
    seq_count = lax.axis_size("seq")
    seq_index = lax.axis_index("seq")
    head_index = lax.axis_index("head")
    requests, heads_local, source_tokens, row_width = source_cache.shape
    source_blocks = source_tokens // BLK
    kept_count = kept_blocks.shape[2]
    step_count = new_hidden.shape[1]
    width_local = new_hidden.shape[2]
    pair_count = requests * heads_local
    score_scale = 1.0 / math.sqrt(HD)
    hidden = new_hidden.astype(jnp.float32)
    scaled = (
        (hidden * norm_gain.astype(jnp.float32))
        .astype(jnp.bfloat16)
        .reshape(requests * step_count, width_local)
    )
    part_query = jnp.dot(scaled, w_query, preferred_element_type=jnp.float32)
    part_keyval = jnp.dot(
        scaled,
        w_keyval.reshape(width_local, heads_local * 2 * HD),
        preferred_element_type=jnp.float32,
    )
    part_square = jnp.sum(hidden * hidden, axis=-1)
    sum_query, sum_keyval, sum_square = lax.psum((part_query, part_keyval, part_square), "seq")
    inverse_norm = lax.rsqrt(sum_square / D + 1e-05)
    norm_five = inverse_norm[:, :, None, None, None]
    prompt_length = source_blocks * BLK * seq_count
    positions = prompt_length + jnp.arange(step_count, dtype=jnp.float32)
    frequency = rope_base ** (-jnp.arange(HD // 2, dtype=jnp.float32) * 2.0 / HD)
    angles = positions[:, None] * frequency[None, :]
    queries = rotate(
        sum_query.reshape(requests, step_count, heads_local, QPK, HD) * norm_five,
        angles[:, None, None, :],
    ).astype(jnp.bfloat16)
    keyval = sum_keyval.reshape(requests, step_count, heads_local, 2, HD) * norm_five
    new_key = rotate(keyval[:, :, :, 0], angles[:, None, :]).astype(jnp.bfloat16)
    new_value = keyval[:, :, :, 1].astype(jnp.bfloat16)
    pair_queries = queries.transpose(0, 2, 1, 3, 4).reshape(pair_count, step_count * QPK, HD)
    pair_keys = new_key.transpose(0, 2, 1, 3).reshape(pair_count, step_count, HD)
    pair_values = new_value.transpose(0, 2, 1, 3).reshape(pair_count, step_count, HD)
    row_step = jnp.arange(step_count * QPK) // QPK
    allowed = jnp.arange(step_count)[None, :] <= row_step[:, None]
    pair_kept = lax.dynamic_slice_in_dim(
        kept_blocks, head_index * heads_local, heads_local, 1
    ).reshape(pair_count, kept_count)
    source_index = pair_kept // source_blocks
    kept_here = jnp.sum((source_index == seq_index).astype(jnp.int32), axis=1)
    run_start = jnp.sum((source_index < seq_index).astype(jnp.int32), axis=1)
    slot_number = jnp.arange(MOST)
    slot_rank = jnp.minimum(run_start[:, None] + slot_number[None, :], kept_count - 1)
    filled = slot_number[None, :] < kept_here[:, None]
    picked = jnp.take_along_axis(pair_kept, slot_rank, axis=1) - seq_index * source_blocks
    picked = jnp.clip(picked, 0, source_blocks - 1)
    cache_blocks = source_cache.reshape(pair_count, source_blocks, BLK * row_width)
    outgoing = jax.vmap(pick_rows)(cache_blocks, picked)
    outgoing = jnp.where(filled[:, :, None], outgoing, jnp.zeros((), jnp.bfloat16))
    received = lax.all_to_all(outgoing, "seq", split_axis=0, concat_axis=0, tiled=True)
    own_kept = lax.dynamic_index_in_dim(pair_kept, seq_index, 0, keepdims=False)
    own_source = own_kept // source_blocks
    own_start = jnp.sum((own_source[None, :] < own_source[:, None]).astype(jnp.int32), axis=1)
    own_slot = jnp.arange(kept_count) - own_start
    arrived = received.reshape(seq_count * MOST, BLK * row_width)
    kept_rows = jnp.take(arrived, own_source * MOST + own_slot, axis=0)
    kept_local = kept_rows.reshape(kept_count * BLK, row_width)
    kept_cache = kept_local.reshape(1, 1, kept_count * BLK, row_width)
    own_query = lax.dynamic_index_in_dim(pair_queries, seq_index, 0, keepdims=False)
    own_key = lax.dynamic_index_in_dim(pair_keys, seq_index, 0, keepdims=False)
    own_value = lax.dynamic_index_in_dim(pair_values, seq_index, 0, keepdims=False)
    contract_last = (((1,), (1,)), ((), ()))
    cached_keys = kept_local[:, :HD]
    cached_values = kept_local[:, HD:]
    score_kept = (
        lax.dot_general(own_query, cached_keys, contract_last, preferred_element_type=jnp.float32)
        * score_scale
    )
    score_new = (
        lax.dot_general(own_query, own_key, contract_last, preferred_element_type=jnp.float32)
        * score_scale
    )
    score_new = jnp.where(allowed, score_new, -jnp.inf)
    row_max = jnp.maximum(jnp.max(score_kept, axis=1), jnp.max(score_new, axis=1))[:, None]
    weight_kept = jnp.exp(score_kept - row_max)
    weight_new = jnp.exp(score_new - row_max)
    denominator = jnp.sum(weight_kept, axis=1) + jnp.sum(weight_new, axis=1)
    numerator = jnp.dot(
        weight_kept.astype(jnp.bfloat16), cached_values, preferred_element_type=jnp.float32
    )
    numerator = numerator + jnp.dot(
        weight_new.astype(jnp.bfloat16), own_value, preferred_element_type=jnp.float32
    )
    attended = (numerator / denominator[:, None]).astype(jnp.bfloat16).reshape(step_count, QPK * HD)
    gathered = lax.all_gather(attended[None], "seq", axis=0, tiled=True)
    grouped = gathered.reshape(requests, heads_local, step_count, QPK * HD)
    projected = jnp.einsum(
        "rltc,lcd->rtd",
        grouped,
        w_out.reshape(heads_local, QPK * HD, width_local),
        preferred_element_type=jnp.float32,
    )
    summed = lax.psum(projected, "head")
    decoded = (hidden + summed).astype(jnp.bfloat16)
    return (kept_cache, decoded)


def solution(mesh):
    in_specs = (
        P("groups", "head", "seq", None),
        P("groups", None, None),
        P("groups", None, "seq"),
        P("seq"),
        P("seq", "head"),
        P("seq", "head", None),
        P("head", "seq"),
    )
    out_specs = (P("head", ("groups", "seq"), None, None), P("groups", None, "seq"))
    return jax.shard_map(shards, mesh=mesh, in_specs=in_specs, out_specs=out_specs, check_vma=False)
```

profile of v0, /device:TPU:0, one launch (start us, length us, event | category | flops | bytes accessed | tf_op | source)
XLA Modules:
  0.0 123.8 jit_solution(7607649276905900024)
XLA Ops:
  7.2 0.8 add_select_fusion
  8.3 0.7 gather_fusion.1
  9.3 1.9 %reshape.490 = bf16[4,4,32768]{2,1,0:T(4,128)(2,1)S(1)} reshape(bf16[2,2,512,256]{3,2,1,0:T(8,128)(2,1)} %param.7) | data formatting | bytes 2097152 | tf_op jit(solution)/shard_map/reshape | solution.py:91
  11.1 2.1 %gather_fusion.2 = bf16[8,32768]{1,0:T(8,128)(2,1)S(1)} fusion(bf16[4,4,32768]{2,1,0:T(4,128)(2,1)S(1)} %reshape.490, s32[8]{0:T(128)S(1)} %reshape.515), kind=kCustom, calls=%fused_computation.2 | custom fusion | bytes 1048640 | tf_op jit(solution)/shard_map/vmap()/gather | solution.py:34
  13.2 0.3 reshape.518
  13.7 1.3 %broadcast_select_fusion = bf16[4,2,32768]{2,1,0:T(2,128)(2,1)} fusion(bf16[4,2,32768]{2,1,0:T(2,128)(2,1)S(1)} %reshape.518, pred[4,2]{1,0:T(4,128)(4,1)S(1)} %iota_compare_fusion.1), kind=kLoop, calls=%fused_computation.11 | loop fusion | flops 262144 | bytes 1048584 | tf_op jit(solution)/shard_map/jit(_where)/select_n | solution.py:93
  15.0 6.3 %all-to-all-start = ((bf16[4,2,32768]{2,1,0:T(2,128)(2,1)}), bf16[4,2,32768]{2,1,0:T(2,128)(2,1)S(1)}, u32[]{:S(2)}, u32[]{:S(2)}) async-start(bf16[4,2,32768]{2,1,0:T(2,128)(2,1)} %broadcast_select_fusion), calls=%async_computation | async-start | bytes 1048576 | tf_op jit(solution)/shard_map/all_to_all | solution.py:94
  21.4 4.7 %convolution_bitcast_fusion.1 = f32[1,8,16,128]{3,1,2,0:T(8,128)S(1)} fusion(bf16[8,2048]{1,0:T(8,128)(2,1)S(1)} %reshape.492, bf16[2048,2048]{1,0:T(8,128)(2,1)} %param.11), kind=kOutput, calls=%fused_computation.5 | convolution fusion | flops 67108864 | bytes 8486912 | tf_op jit(solution)/shard_map/dot_general | solution.py:54
  26.2 0.6 copy.21
  27.2 0.5 copy.27
  27.7 0.4 fusion.38
  28.1 19.5 %all-reduce = (f32[2,4]{1,0:T(2,128)S(1)}, f32[2,4,2,2,128]{4,2,1,0,3:T(2,128)S(1)}) all-reduce(f32[2,4]{1,0:T(2,128)S(1)} %get-tuple-element.10, f32[2,4,2,2,128]{4,2,1,0,3:T(2,128)S(1)} %copy.22), channel_id=1, replica_groups=mesh['groups'=2,'seq'=4,'head'=4] {'seq'}, use_global_device_ids=true, to_apply=%region_5.6 | all-reduce | flops 4104 | bytes 32832 | tf_op jit(solution)/shard_map/psum | solution.py:61
  48.1 14.3 %all-reduce.4.cloned.1.call-done = f32[2,4,2,8,128]{4,3,1,2,0:T(8,128)} async-done(((f32[2,4,2,8,128]{4,3,1,2,0:T(8,128)}), f32[2,4,2,8,128]{4,3,1,2,0:T(8,128)}) %all-reduce.4.cloned.1.call-update) | async-done | bytes 65552 | tf_op jit(solution)/shard_map/psum | solution.py:61
  62.5 0.9 broadcast_multiply_fusion
  63.7 0.2 reshape.491
  63.9 0.8 gather_fusion
  65.1 0.3 fusion.36
  65.3 0.2 fusion.9
  65.5 0.2 fusion.3
  66.2 13.1 %all_gather.3 = bf16[4,4,1024]{2,1,0:T(4,128)(2,1)S(1)} all-gather(bf16[1,4,1024]{2,1,0:T(4,128)(2,1)S(1)} %broadcast_in_dim_reshape.3), channel_id=1, replica_groups=mesh['groups'=2,'seq'=4,'head'=4] {'seq'}, dimensions={0}, use_global_device_ids=true | all-gather | bytes 40960 | tf_op jit(solution)/shard_map/all_gather | solution.py:129
  79.3 5.3 %convolution_bitcast_fusion = f32[2,4,2048]{2,1,0:T(4,128)} fusion(bf16[2,2,4,1024]{3,2,1,0:T(4,128)(2,1)S(1)} %bitcast.97, bf16[2,1024,2048,1]{2,1,0,3:T(8,128)(2,1)} %bitcast.93), kind=kOutput, calls=%fused_computation.3 | convolution fusion | flops 67108864 | bytes 8486912 | tf_op jit(solution)/shard_map/rltc,lcd->rtd/dot_general | solution.py:131
  84.6 0.8 broadcast_select_fusion.2
  85.4 30.1 %all-reduce.6.cloned.1.call-done = f32[2,4,2048]{2,1,0:T(4,128)} async-done(((f32[2,4,2048]{2,1,0:T(4,128)}), f32[2,4,2048]{2,1,0:T(4,128)}) %all-reduce.6.cloned.1.call-update) | async-done | bytes 65552 | tf_op jit(solution)/shard_map/psum | solution.py:137
  115.5 1.5 %fusion.8 = bf16[2,4,2048]{2,1,0:T(4,128)(2,1)} fusion(f32[2,4,2048]{2,1,0:T(4,128)} %all-reduce.6.cloned.1.call-done, bf16[2,4,2048]{2,1,0:T(4,128)(2,1)S(1)} %copy-done.1), kind=kLoop, calls=%fused_computation.22 | loop fusion | flops 49152 | bytes 131072 | tf_op jit(solution)/shard_map/convert_element_type | solution.py:138
  (57 shorter events, 2.8 us)
Async XLA Ops:
  7.2 14.1 %copy-start.2 = (bf16[2048]{0:T(1024)(128)(2,1)S(1)}, bf16[2048]{0:T(1024)(128)(2,1)}, u32[]{:S(2)}) copy-start(bf16[2048]{0:T(1024)(128)(2,1)} %param.10) | copy-start | bytes 12292
  7.2 14.1 %copy-start.1 = (bf16[2,4,2048]{2,1,0:T(4,128)(2,1)S(1)}, bf16[2,4,2048]{2,1,0:T(4,128)(2,1)}, u32[]{:S(2)}) copy-start(bf16[2,4,2048]{2,1,0:T(4,128)(2,1)} %param.9) | copy-start | bytes 98308
  15.0 48.7 %all-to-all-start = ((bf16[4,2,32768]{2,1,0:T(2,128)(2,1)}), bf16[4,2,32768]{2,1,0:T(2,128)(2,1)S(1)}, u32[]{:S(2)}, u32[]{:S(2)}) async-start(bf16[4,2,32768]{2,1,0:T(2,128)(2,1)} %broadcast_select_fusion), calls=%async_computation | async-start | bytes 1048576 | tf_op jit(solution)/shard_map/all_to_all | solution.py:94
  21.3 5.9 %copy-start = (bf16[2048,2,256]{2,1,0:T(2,128)(2,1)S(1)}, bf16[2048,2,256]{2,1,0:T(2,128)(2,1)}, u32[]{:S(2)}) copy-start(bf16[2048,2,256]{2,1,0:T(2,128)(2,1)} %param.12) | copy-start | bytes 6291460
  21.3 41.2 %all-reduce.4.cloned.1.call-start = ((), (), s32[]{:S(2)}) async-start(), calls=%async_computation.1 | async-start | bytes 131072 | tf_op jit(solution)/shard_map/psum | solution.py:61
  26.8 88.7 %all-reduce.6.cloned.1.call-start = ((), (), s32[]{:S(2)}) async-start(), calls=%async_computation.2 | async-start | bytes 131072 | tf_op jit(solution)/shard_map/psum | solution.py:137
Sparse Core Ops, SparseCore 0:
  26.9 35.4 all-reduce.3
  84.7 30.7 all-reduce.5
where the time goes:
time: 124 us
  waiting for transfers between devices  44.5 us (36%)
  blocking collectives  32.6 us (26%)
  between operations  14.3 us (12%)
  matrix products  11.1 us (9%)
  local copies, waits for them, and re-layouts  8.13 us (7%)
  other arithmetic  6.85 us (6%)
  starting transfers between devices  6.36 us (5%)
    psum x1, waiting for transfers between devices, shards(): summed = lax.psum(projected, 'head')  30.1 us
    psum x1, blocking collectives, shards(): lax.psum((part_query, part_keyval, part_square), 'seq')  19.5 us
    psum x1, waiting for transfers between devices, shards(): lax.psum((part_query, part_keyval, part_square), 'seq')  14.3 us
    all_gather x1, blocking collectives, shards(): gathered = lax.all_gather(attended[None], 'seq', axis=0, tiled=True)  13.1 us
    all_to_all x1, starting transfers between devices, shards(): lax.all_to_all(outgoing, 'seq', split_axis=0, concat_axis=0, tiled=True)  6.32 us
    dot_general x1, matrix products, shards(): jnp.einsum('rltc,lcd->rtd', grouped, w_out.reshape(heads_local, QPK * HD,...  5.27 us
    dot_general x1, matrix products, shards(): part_query = jnp.dot(scaled, w_query, preferred_element_type=jnp.float32)  4.69 us
    gather x3, local copies, waits for them, and re-layouts, pick_rows(): return source_table[row_index]  2.48 us
  transfers between devices with their start and end apart: 3, of which 2 were waited for; matrix products, arithmetic and copies ran while one was open for 7% of the time, Pallas kernels for 0%

commit v1 on v0

v1 whole, which is shorter than its diff:
```python
import functools
import math

import jax
import jax.numpy as jnp
import numpy as np
from jax import lax
from jax.experimental import pallas as pl
from jax.experimental.pallas import tpu as pltpu
from jax.sharding import PartitionSpec as P

D = 8192
HD = 128
QPK = 8
BLK = 128
MOST = 2
ROPE_BASE = 500000.0
EPS = 1e-05

CONTRACT_LAST = (((1,), (1,)), ((), ()))


def rope_tables(prompt_length, step_count):
    positions = prompt_length + np.arange(2 * step_count) % step_count
    frequency = ROPE_BASE ** (-np.arange(HD // 2, dtype=np.float64) * 2.0 / HD)
    angles = positions[:, None] * frequency[None, :]
    cosine = np.concatenate([np.cos(angles)] * 2, axis=1)
    sine = np.concatenate([-np.sin(angles), np.sin(angles)], axis=1)
    return cosine.astype(np.float32), sine.astype(np.float32)


def rotate(v, cosine, sine):
    swapped = jnp.concatenate([v[..., HD // 2 :], v[..., : HD // 2]], axis=-1)
    return v * cosine + swapped * sine


def pick_kernel(kept_ref, cache_ref, out_ref, sem):
    requests, heads_local, source_tokens, _ = cache_ref.shape
    source_blocks = source_tokens // BLK
    kept_count = kept_ref.shape[2]
    me = lax.axis_index("seq")
    first_head = lax.axis_index("head") * heads_local

    def pair_body(pair, carry):
        request = lax.div(pair, heads_local)
        local = lax.rem(pair, heads_local)
        head = first_head + local

        def count(k, total):
            block = kept_ref[request, head, k]
            return total + (block < me * source_blocks).astype(jnp.int32)

        start = lax.fori_loop(0, kept_count, count, jnp.int32(0), unroll=kept_count <= 8)
        for slot in range(MOST):
            rank = jnp.minimum(start + slot, kept_count - 1)
            block = kept_ref[request, head, rank] - me * source_blocks
            block = jnp.clip(block, 0, source_blocks - 1)
            rows = pl.ds(pl.multiple_of(block * BLK, BLK), BLK)
            pltpu.make_async_copy(
                cache_ref.at[request, local, rows], out_ref.at[pair, slot], sem
            ).start()
        return carry

    pair_count = requests * heads_local
    lax.fori_loop(0, pair_count, pair_body, 0, unroll=pair_count <= 8)
    pltpu.make_async_copy(out_ref, out_ref, sem).wait()


def pick(kept_blocks, source_cache):
    requests, heads_local, _, row_width = source_cache.shape
    pair_count = requests * heads_local
    return pl.pallas_call(
        pick_kernel,
        out_shape=jax.ShapeDtypeStruct((pair_count, MOST, BLK, row_width), jnp.bfloat16),
        in_specs=[
            pl.BlockSpec(memory_space=pltpu.SMEM),
            pl.BlockSpec(memory_space=pl.ANY),
        ],
        out_specs=pl.BlockSpec(memory_space=pl.ANY),
        scratch_shapes=[pltpu.SemaphoreType.DMA],
        name="pick_blocks",
    )(kept_blocks, source_cache)


def chunk_copies(w_ref, buffer, sems, rows):
    return [
        pltpu.make_async_copy(
            w_ref.at[pl.ds(i * rows, rows)], buffer.at[pl.ds(i * rows, rows)], sems.at[i]
        )
        for i in range(w_ref.shape[0] // rows)
    ]


def project_kernel(rows, hidden_ref, gain_ref, wq_ref, wkv_ref, out_ref, wq, wkv, sem_q, sem_kv):
    requests, step_count, width = hidden_ref.shape
    copies_q = chunk_copies(wq_ref, wq, sem_q, rows)
    copies_kv = chunk_copies(wkv_ref, wkv, sem_kv, rows)
    for copy_q, copy_kv in zip(copies_q, copies_kv):
        copy_q.start()
        copy_kv.start()
    hidden = jnp.concatenate(
        [hidden_ref[r].astype(jnp.float32) for r in range(requests)], axis=0
    )
    square = jnp.sum(hidden * hidden, axis=1, keepdims=True)
    scaled = (hidden * gain_ref[...].astype(jnp.float32)).astype(jnp.bfloat16)
    query = jnp.zeros((requests * step_count, wq.shape[1]), jnp.float32)
    keyval = jnp.zeros((requests * step_count, wkv.shape[1]), jnp.float32)
    for i, (copy_q, copy_kv) in enumerate(zip(copies_q, copies_kv)):
        piece = scaled[:, i * rows : (i + 1) * rows]
        here = pl.ds(i * rows, rows)
        copy_q.wait()
        query += jnp.dot(piece, wq[here], preferred_element_type=jnp.float32)
        copy_kv.wait()
        keyval += jnp.dot(piece, wkv[here], preferred_element_type=jnp.float32)
    heads_local = out_ref.shape[0] // requests
    for r in range(requests):
        steps = slice(r * step_count, (r + 1) * step_count)
        square_rows = jnp.broadcast_to(square[steps], (step_count, HD))
        for l in range(heads_local):
            pair = r * heads_local + l
            pieces = [
                query[steps, (l * QPK + h) * HD : (l * QPK + h + 1) * HD] for h in range(QPK)
            ]
            pieces += [
                keyval[steps, (l * 2 + h) * HD : (l * 2 + h + 1) * HD] for h in range(2)
            ]
            pieces += [square_rows, square_rows]
            for j, piece in enumerate(pieces):
                out_ref[pair, j * step_count : (j + 1) * step_count, :] = piece


def project(new_hidden, norm_gain, w_query, w_keyval, pair_count):
    requests, step_count, width = new_hidden.shape
    rows = min(256, width)
    chunks = width // rows
    return pl.pallas_call(
        functools.partial(project_kernel, rows),
        out_shape=jax.ShapeDtypeStruct((pair_count, (QPK + 4) * step_count, HD), jnp.float32),
        in_specs=[
            pl.BlockSpec(memory_space=pltpu.VMEM),
            pl.BlockSpec(memory_space=pltpu.VMEM),
            pl.BlockSpec(memory_space=pl.ANY),
            pl.BlockSpec(memory_space=pl.ANY),
        ],
        out_specs=pl.BlockSpec(memory_space=pltpu.VMEM),
        scratch_shapes=[
            pltpu.VMEM(w_query.shape, jnp.bfloat16),
            pltpu.VMEM(w_keyval.shape, jnp.bfloat16),
            pltpu.SemaphoreType.DMA((chunks,)),
            pltpu.SemaphoreType.DMA((chunks,)),
        ],
        compiler_params=pltpu.CompilerParams(vmem_limit_bytes=24 * 1024 * 1024),
        cost_estimate=pl.CostEstimate(
            flops=2 * requests * step_count * width * (w_query.shape[1] + w_keyval.shape[1]),
            bytes_accessed=2 * width * (w_query.shape[1] + w_keyval.shape[1]),
            transcendentals=0,
        ),
        name="project",
    )(new_hidden, norm_gain, w_query, w_keyval)


def attend_kernel(
    source_blocks, heads_local, kept_ref, blocks_ref, parts_ref, cos_ref, sin_ref,
    cache_ref, attended_ref, kept, sem_in, sem_out,
):
    kept_count = kept_ref.shape[2]
    step_count = cos_ref.shape[0] // 2
    me = lax.axis_index("seq")
    request = lax.div(me, heads_local)
    head = lax.axis_index("head") * heads_local + lax.rem(me, heads_local)

    def start_copy(k, carry):
        previous, slot = carry
        source = lax.div(kept_ref[request, head, k], source_blocks)
        slot = jnp.where(source == previous, jnp.minimum(slot + 1, MOST - 1), 0)
        rows = pl.ds(pl.multiple_of(k * BLK, BLK), BLK)
        pltpu.make_async_copy(blocks_ref.at[source, slot], kept.at[rows], sem_in).start()
        return source, slot

    lax.fori_loop(
        0, kept_count, start_copy, (jnp.int32(-1), jnp.int32(0)), unroll=kept_count <= 8
    )
    total = jnp.sum(parts_ref[...], axis=0)
    query_rows = QPK * step_count
    inverse = lax.rsqrt(total[query_rows + 2 * step_count :] * (1.0 / D) + EPS)
    cosine, sine = cos_ref[...], sin_ref[...]
    query = total[:query_rows].reshape(QPK // 2, 2 * step_count, HD) * inverse[None]
    query = rotate(query, cosine[None], sine[None]).reshape(query_rows, HD).astype(jnp.bfloat16)
    keyval = total[query_rows : query_rows + 2 * step_count] * inverse
    new_key = rotate(keyval, cosine, sine).astype(jnp.bfloat16)
    new_value = jnp.concatenate([keyval[step_count:], keyval[:step_count]], axis=0)
    new_value = new_value.astype(jnp.bfloat16)
    scale = 1.0 / math.sqrt(HD)
    score_new = (
        lax.dot_general(query, new_key, CONTRACT_LAST, preferred_element_type=jnp.float32) * scale
    )
    row = lax.broadcasted_iota(jnp.int32, score_new.shape, 0)
    column = lax.broadcasted_iota(jnp.int32, score_new.shape, 1)
    score_new = jnp.where(column <= lax.rem(row, step_count), score_new, -jnp.inf)

    pltpu.make_async_copy(kept, kept, sem_in).wait()
    out_copy = pltpu.make_async_copy(kept, cache_ref.at[0, 0], sem_out)
    out_copy.start()
    score_kept = (
        lax.dot_general(query, kept[:, :HD], CONTRACT_LAST, preferred_element_type=jnp.float32)
        * scale
    )
    row_max = jnp.maximum(
        jnp.max(score_kept, axis=1, keepdims=True), jnp.max(score_new, axis=1, keepdims=True)
    )
    weight_kept = jnp.exp(score_kept - row_max)
    weight_new = jnp.exp(score_new - row_max)
    denominator = jnp.sum(weight_kept, axis=1, keepdims=True) + jnp.sum(
        weight_new, axis=1, keepdims=True
    )
    numerator = jnp.dot(
        weight_kept.astype(jnp.bfloat16), kept[:, HD:], preferred_element_type=jnp.float32
    )
    numerator += jnp.dot(
        weight_new.astype(jnp.bfloat16), new_value, preferred_element_type=jnp.float32
    )
    attended = (numerator / denominator).astype(jnp.bfloat16)
    for i in range(attended_ref.shape[0]):
        attended_ref[i] = attended
    out_copy.wait()


def attend(kept_blocks, blocks, parts, source_blocks, heads_local, step_count, seq_count):
    kept_count = kept_blocks.shape[2]
    row_width = blocks.shape[-1]
    cosine, sine = rope_tables(source_blocks * BLK * seq_count, step_count)
    return pl.pallas_call(
        functools.partial(attend_kernel, source_blocks, heads_local),
        out_shape=(
            jax.ShapeDtypeStruct((1, 1, kept_count * BLK, row_width), jnp.bfloat16),
            jax.ShapeDtypeStruct((seq_count, QPK * step_count, HD), jnp.bfloat16),
        ),
        in_specs=[
            pl.BlockSpec(memory_space=pltpu.SMEM),
            pl.BlockSpec(memory_space=pl.ANY),
            pl.BlockSpec(memory_space=pltpu.VMEM),
            pl.BlockSpec(memory_space=pltpu.VMEM),
            pl.BlockSpec(memory_space=pltpu.VMEM),
        ],
        out_specs=(
            pl.BlockSpec(memory_space=pl.ANY),
            pl.BlockSpec(memory_space=pltpu.VMEM),
        ),
        scratch_shapes=[
            pltpu.VMEM((kept_count * BLK, row_width), jnp.bfloat16),
            pltpu.SemaphoreType.DMA,
            pltpu.SemaphoreType.DMA,
        ],
        compiler_params=pltpu.CompilerParams(vmem_limit_bytes=24 * 1024 * 1024),
        name="attend",
    )(kept_blocks, blocks, parts, jnp.asarray(cosine), jnp.asarray(sine))


def output_kernel(rows, heads_local, gathered_ref, w_ref, out_ref, w, sems):
    copies = chunk_copies(w_ref, w, sems, rows)
    for copy in copies:
        copy.start()
    pair_count, query_rows, _ = gathered_ref.shape
    step_count = query_rows // QPK
    requests = pair_count // heads_local
    total = jnp.zeros((requests * step_count, w.shape[1]), jnp.float32)
    pairs = [gathered_ref[p].astype(jnp.float32) for p in range(pair_count)]
    for i, copy in enumerate(copies):
        pieces = []
        for column in range(i * rows // HD, (i + 1) * rows // HD):
            l, h = divmod(column, QPK)
            pieces.append(
                jnp.concatenate(
                    [
                        pairs[r * heads_local + l][h * step_count : (h + 1) * step_count]
                        for r in range(requests)
                    ],
                    axis=0,
                )
            )
        merged = jnp.concatenate(pieces, axis=1).astype(jnp.bfloat16)
        copy.wait()
        total += jnp.dot(
            merged, w[pl.ds(i * rows, rows)], preferred_element_type=jnp.float32
        )
    for i in range(out_ref.shape[0]):
        out_ref[i] = total


def output(gathered, w_out, heads_local, head_count):
    pair_count, query_rows, _ = gathered.shape
    total_rows = pair_count // heads_local * (query_rows // QPK)
    rows = 256
    return pl.pallas_call(
        functools.partial(output_kernel, rows, heads_local),
        out_shape=jax.ShapeDtypeStruct((head_count, total_rows, w_out.shape[1]), jnp.float32),
        in_specs=[
            pl.BlockSpec(memory_space=pltpu.VMEM),
            pl.BlockSpec(memory_space=pl.ANY),
        ],
        out_specs=pl.BlockSpec(memory_space=pltpu.VMEM),
        scratch_shapes=[
            pltpu.VMEM(w_out.shape, jnp.bfloat16),
            pltpu.SemaphoreType.DMA((w_out.shape[0] // rows,)),
        ],
        compiler_params=pltpu.CompilerParams(vmem_limit_bytes=24 * 1024 * 1024),
        name="output_projection",
    )(gathered, w_out)


def shards(source_cache, kept_blocks, new_hidden, norm_gain, w_query, w_keyval, w_out):
    seq_count = lax.axis_size("seq")
    head_count = lax.axis_size("head")
    requests, heads_local, source_tokens, _ = source_cache.shape
    _, step_count, width = new_hidden.shape
    pair_count = requests * heads_local

    outgoing = pick(kept_blocks, source_cache)
    blocks = lax.all_to_all(outgoing, "seq", split_axis=0, concat_axis=0, tiled=True)
    parts = project(
        new_hidden, norm_gain.reshape(1, width), w_query, w_keyval.reshape(width, -1), pair_count
    )
    parts = lax.all_to_all(parts, "seq", split_axis=0, concat_axis=0, tiled=True)
    kept_cache, attended = attend(
        kept_blocks, blocks, parts, source_tokens // BLK, heads_local, step_count, seq_count
    )
    gathered = lax.all_to_all(attended, "seq", split_axis=0, concat_axis=0, tiled=True)
    terms = output(gathered, w_out, heads_local, head_count)
    terms = lax.all_to_all(terms, "head", split_axis=0, concat_axis=0, tiled=True)
    summed = jnp.sum(terms, axis=0).reshape(requests, step_count, width)
    decoded = (new_hidden.astype(jnp.float32) + summed).astype(jnp.bfloat16)
    return (kept_cache, decoded)


def solution(mesh):
    in_specs = (
        P("groups", "head", "seq", None),
        P("groups", None, None),
        P("groups", None, "seq"),
        P("seq"),
        P("seq", "head"),
        P("seq", "head", None),
        P("head", "seq"),
    )
    out_specs = (P("head", ("groups", "seq"), None, None), P("groups", None, "seq"))
    return jax.shard_map(shards, mesh=mesh, in_specs=in_specs, out_specs=out_specs, check_vma=False)
```

time: 124 us -> 80.9 us (0.65)
  waiting for transfers between devices: 44.5 us -> 0.01 us
  Pallas kernels: 0 us -> 25 us
  between operations: 14.3 us -> 0.73 us
  matrix products: 11.1 us -> 0 us
  other arithmetic: 6.85 us -> 0.65 us
  local copies, waits for them, and re-layouts: 8.13 us -> 11.7 us
  blocking collectives: 32.6 us -> 35.8 us
    psum x2 -> x0, waiting for transfers between devices: 44.4 us -> none  [the longest x1 30.1 us: shards(): summed = lax.psum(projected, 'head')]
    all_to_all x0 -> x3, blocking collectives: none -> 35.8 us  [the longest x1 19 us: shards(): lax.all_to_all(outgoing, 'seq', split_axis=0, concat_axis=0, tiled=True)]
    pallas_call x0 -> x4, Pallas kernels: none -> 25 us  [the longest x1 17.8 us: pick(): pl.pallas_call(pick_kernel, out_shape=jax.ShapeDtypeStruct((pair_count, M...]
    psum x1 -> x0, blocking collectives: 19.5 us -> none  [shards(): lax.psum((part_query, part_keyval, part_square), 'seq')]
    all_gather x1 -> x0, blocking collectives: 13.1 us -> none  [shards(): gathered = lax.all_gather(attended[None], 'seq', axis=0, tiled=True)]
    dot_general x7 -> x0, matrix products: 11.1 us -> none  [the longest x1 5.27 us: shards(): jnp.einsum('rltc,lcd->rtd', grouped, w_out.reshape(heads_local, QPK * HD,...]
    unnamed x8 -> x18, local copies, waits for them, and re-layouts: 0.53 us -> 11 us
    gather x9 -> x0, local copies, waits for them, and re-layouts: 4.45 us -> none  [the longest x3 2.48 us: pick_rows(): return source_table[row_index]]
  transfers between devices with their start and end apart: 3 -> 1, of which waited for: 2 -> 0; matrix products, arithmetic and copies ran while one was open for 7% -> 1% of each run, Pallas kernels for 0% -> 22%
where the time goes in v1:
time: 80.9 us; the launch traced here: 80.2 us
  blocking collectives  35.8 us (44%)
  Pallas kernels  25 us (31%)
  local copies, waits for them, and re-layouts  11.7 us (14%)
  starting transfers between devices  6.33 us (8%)
    all_to_all x1, blocking collectives, shards(): lax.all_to_all(outgoing, 'seq', split_axis=0, concat_axis=0, tiled=True)  19 us
    pallas_call x1, Pallas kernels, pick(): pl.pallas_call(pick_kernel, out_shape=jax.ShapeDtypeStruct((pair_count, M...  17.8 us
    unnamed x18, local copies, waits for them, and re-layouts  11 us
    all_to_all x1, blocking collectives, shards(): lax.all_to_all(terms, 'head', split_axis=0, concat_axis=0, tiled=True)  8.6 us
    all_to_all x1, blocking collectives, shards(): lax.all_to_all(attended, 'seq', split_axis=0, concat_axis=0, tiled=True)  8.19 us
    all_to_all x1, starting transfers between devices, shards(): lax.all_to_all(parts, 'seq', split_axis=0, concat_axis=0, tiled=True)  6.33 us
    pallas_call x1, Pallas kernels, project(): pl.pallas_call(functools.partial(project_kernel, rows), out_shape=jax.Sha...  3.29 us
    pallas_call x1, Pallas kernels, attend(): pl.pallas_call(functools.partial(attend_kernel, source_blocks, heads_loca...  1.98 us
  transfers between devices with their start and end apart: 1, of which 0 were waited for; matrix products, arithmetic and copies ran while one was open for 1% of the time, Pallas kernels for 22%

profile of v1, /device:TPU:0, one launch (start us, length us, event | category | flops | bytes accessed | tf_op | source)
XLA Modules:
  0.0 80.2 jit_solution(4517435095635151357)
XLA Ops:
  0.6 0.0 copy-start.7
  0.6 0.7 reshape.13.gain_ref
  1.3 2.1 %copy.13 = bf16[256,8,2,256]{3,1,2,0:T(8,128)(2,1)S(1)} copy(bf16[256,8,2,256]{3,2,1,0:T(2,128)(2,1)} %bitcast.3) | data formatting | bytes 4194304
  3.4 0.0 copy-start
  3.4 3.4 %copy-done = bf16[2048,2048]{1,0:T(8,128)(2,1)S(1)} copy-done((bf16[2048,2048]{1,0:T(8,128)(2,1)S(1)}, bf16[2048,2048]{1,0:T(8,128)(2,1)}, u32[]{:S(2)}) %copy-start) | copy-done | bytes 8388632
  6.8 0.8 copy-done.2
  7.6 3.3 %project.1 = f32[4,48,128]{2,1,0:T(8,128)} custom-call(bf16[2,4,2048]{2,1,0:T(4,128)(2,1)S(1)} %copy-done.2, bf16[1,2048]{1,0:T(2,128)(2,1)S(1)} %reshape.13.gain_ref, bf16[2048,2048]{1,0:T(8,128)(2,1)S(1)} %copy-done, bf16[2048,512]{1,0:T(8,128)(2,1)S(1)} %bitcast.2), custom_call_target="tpu_custom_call" | custom-call | flops 83886080 | bytes 10485760 | tf_op jit(solution)/shard_map/project/pallas_call | solution.py:136
  10.9 0.0 copy-start.3
  10.9 6.3 %all-to-all-start.1 = ((f32[4,48,128]{2,1,0:T(8,128)}), f32[4,48,128]{2,1,0:T(8,128)S(1)}, u32[]{:S(2)}, u32[]{:S(2)}) async-start(f32[4,48,128]{2,1,0:T(8,128)} %project.1), calls=%async_computation.1 | async-start | bytes 196608 | tf_op jit(solution)/shard_map/all_to_all | solution.py:323
  17.2 0.0 copy-done.7
  17.2 0.7 copy.12.kept_ref
  17.9 17.8 %pick_blocks.1 = bf16[4,2,128,256]{3,2,1,0:T(8,128)(2,1)} custom-call(s32[2,8,4]{2,1,0:T(8,128)} %copy.12.kept_ref, bf16[2,2,512,256]{3,2,1,0:T(8,128)(2,1)} %cache_ref.1), custom_call_target="tpu_custom_call" | custom-call | tf_op jit(solution)/shard_map/pick_blocks/pallas_call | solution.py:72
  35.7 0.0 all-to-all-done.1.parts_ref
  35.7 19.0 %all_to_all.20.blocks_ref = bf16[4,2,128,256]{3,2,1,0:T(8,128)(2,1)S(1)} all-to-all(bf16[4,2,128,256]{3,2,1,0:T(8,128)(2,1)} %pick_blocks.1), channel_id=1, replica_groups=mesh['groups'=2,'seq'=4,'head'=4] {'seq'}, dimensions={0} | all-to-all | bytes 1048576 | tf_op jit(solution)/shard_map/all_to_all | solution.py:319
  54.7 0.0 copy-done.5
  54.7 0.0 copy-done.6
  54.7 0.7 copy-done.4
  55.4 2.0 %attend.1 = (bf16[1,1,512,256]{3,2,1,0:T(8,128)(2,1)}, bf16[4,32,128]{2,1,0:T(8,128)(2,1)S(1)}) custom-call(s32[2,8,4]{2,1,0:T(8,128)S(1)} %copy-done.4, bf16[4,2,128,256]{3,2,1,0:T(8,128)(2,1)S(1)} %all_to_all.20.blocks_ref, f32[4,48,128]{2,1,0:T(8,128)S(1)} %all-to-all-done.1.parts_ref, f32[8,128]{1,0:T(8,128)S(1)} %copy-done.6, f32[8,128]{1,0:T(8,128)S(1)} %copy-done.5), custom_call_target="tpu_custom_call" | custom-call | tf_op jit(solution)/shard_map/attend/pallas_call | solution.py:232
  57.4 8.2 %all_to_all.21.gathered_ref = bf16[4,32,128]{2,1,0:T(8,128)(2,1)S(1)} all-to-all(bf16[4,32,128]{2,1,0:T(8,128)(2,1)S(1)} %get-tuple-element.5), channel_id=1, replica_groups=mesh['groups'=2,'seq'=4,'head'=4] {'seq'}, dimensions={0} | all-to-all | bytes 65536 | tf_op jit(solution)/shard_map/all_to_all | solution.py:327
  65.6 3.4 %copy-done.1 = bf16[2048,2048]{1,0:T(8,128)(2,1)S(1)} copy-done((bf16[2048,2048]{1,0:T(8,128)(2,1)S(1)}, bf16[2048,2048]{1,0:T(8,128)(2,1)}, u32[]{:S(2)}) %copy-start.1) | copy-done | bytes 8388632
  69.0 1.9 %output_projection.1 = f32[4,8,2048]{2,1,0:T(8,128)S(1)} custom-call(bf16[4,32,128]{2,1,0:T(8,128)(2,1)S(1)} %all_to_all.21.gathered_ref, bf16[2048,2048]{1,0:T(8,128)(2,1)S(1)} %copy-done.1), custom_call_target="tpu_custom_call" | custom-call | tf_op jit(solution)/shard_map/output_projection/pallas_call | solution.py:294
  70.9 8.6 %all_to_all.22 = f32[4,8,2048]{2,1,0:T(8,128)S(1)} all-to-all(f32[4,8,2048]{2,1,0:T(8,128)S(1)} %output_projection.1), channel_id=1, replica_groups=mesh['groups'=2,'seq'=4,'head'=4] {'head'}, dimensions={0} | all-to-all | bytes 524288 | tf_op jit(solution)/shard_map/all_to_all | solution.py:329
  79.6 0.0 copy-done.3
  79.6 0.6 add_convert_fusion
  (7 shorter events, 0.0 us)
Async XLA Ops:
  0.6 16.6 %copy-start.7 = (s32[2,8,4]{1,2,0:T(4,128)S(1)}, s32[2,8,4]{1,2,0:T(4,128)}, u32[]{:S(2)}) copy-start(s32[2,8,4]{1,2,0:T(4,128)} %param.10) | copy-start | bytes 772
  1.3 53.4 %copy-start.5 = (f32[8,128]{1,0:T(8,128)S(1)}, f32[8,128]{1,0:T(8,128)}, u32[]{:S(2)}) copy-start(f32[8,128]{1,0:T(8,128)} %constant.7.clone.sin_ref) | copy-start | bytes 12292
  1.3 53.4 %copy-start.6 = (f32[8,128]{1,0:T(8,128)S(1)}, f32[8,128]{1,0:T(8,128)}, u32[]{:S(2)}) copy-start(f32[8,128]{1,0:T(8,128)} %constant.6.clone.cos_ref) | copy-start | bytes 12292
  3.4 3.4 %copy-start = (bf16[2048,2048]{1,0:T(8,128)(2,1)S(1)}, bf16[2048,2048]{1,0:T(8,128)(2,1)}, u32[]{:S(2)}) copy-start(bf16[2048,2048]{1,0:T(8,128)(2,1)} %wq_ref.1) | copy-start | bytes 25165828
  6.8 0.8 copy-start.2
  10.9 68.7 %copy-start.3 = (bf16[2,4,2048]{2,1,0:T(4,128)(2,1)S(1)}, bf16[2,4,2048]{2,1,0:T(4,128)(2,1)}, u32[]{:S(2)}) copy-start(bf16[2,4,2048]{2,1,0:T(4,128)(2,1)} %hidden_ref.1) | copy-start | bytes 98308
  10.9 24.8 %all-to-all-start.1 = ((f32[4,48,128]{2,1,0:T(8,128)}), f32[4,48,128]{2,1,0:T(8,128)S(1)}, u32[]{:S(2)}, u32[]{:S(2)}) async-start(f32[4,48,128]{2,1,0:T(8,128)} %project.1), calls=%async_computation.1 | async-start | bytes 196608 | tf_op jit(solution)/shard_map/all_to_all | solution.py:323
  54.7 0.7 copy-start.4
  65.6 3.4 %copy-start.1 = (bf16[2048,2048]{1,0:T(8,128)(2,1)S(1)}, bf16[2048,2048]{1,0:T(8,128)(2,1)}, u32[]{:S(2)}) copy-start(bf16[2048,2048]{1,0:T(8,128)(2,1)} %w_ref.1) | copy-start | bytes 25165828

commit v2 on v1

v2 whole, which is shorter than its diff:
```python
import functools
import math

import jax
import jax.numpy as jnp
import numpy as np
from jax import lax
from jax.experimental import pallas as pl
from jax.experimental.pallas import tpu as pltpu
from jax.sharding import PartitionSpec as P

D = 8192
HD = 128
QPK = 8
BLK = 128
MOST = 2
ROPE_BASE = 500000.0
EPS = 1e-05

CONTRACT_LAST = (((1,), (1,)), ((), ()))


def rope_tables(prompt_length, step_count):
    positions = prompt_length + np.arange(2 * step_count) % step_count
    frequency = ROPE_BASE ** (-np.arange(HD // 2, dtype=np.float64) * 2.0 / HD)
    angles = positions[:, None] * frequency[None, :]
    cosine = np.concatenate([np.cos(angles)] * 2, axis=1)
    sine = np.concatenate([-np.sin(angles), np.sin(angles)], axis=1)
    return cosine.astype(np.float32), sine.astype(np.float32)


def rotate(v, cosine, sine):
    swapped = jnp.concatenate([v[..., HD // 2 :], v[..., : HD // 2]], axis=-1)
    return v * cosine + swapped * sine


def is_direct(count):
    return count <= 8 and count & (count - 1) == 0


def exchange(outgoing, axis):
    if len(outgoing) == 1:
        return [lax.all_to_all(outgoing[0], axis, split_axis=0, concat_axis=0, tiled=True)]
    count = len(outgoing)
    return [outgoing[0]] + [
        lax.ppermute(outgoing[k], axis, [(i, i ^ k) for i in range(count)])
        for k in range(1, count)
    ]


def pick_kernel(kept_ref, cache_ref, *refs):
    outs, sem = refs[:-1], refs[-1]
    requests, heads_local, source_tokens, _ = cache_ref.shape
    source_blocks = source_tokens // BLK
    kept_count = kept_ref.shape[2]
    me = lax.axis_index("seq")
    first_head = lax.axis_index("head") * heads_local

    def copy_pair(pair, out_ref):
        request = lax.div(pair, heads_local)
        local = lax.rem(pair, heads_local)
        head = first_head + local

        def count(k, total):
            block = kept_ref[request, head, k]
            return total + (block < me * source_blocks).astype(jnp.int32)

        start = lax.fori_loop(0, kept_count, count, jnp.int32(0), unroll=kept_count <= 8)
        for slot in range(MOST):
            rank = jnp.minimum(start + slot, kept_count - 1)
            block = kept_ref[request, head, rank] - me * source_blocks
            block = jnp.clip(block, 0, source_blocks - 1)
            rows = pl.ds(pl.multiple_of(block * BLK, BLK), BLK)
            pltpu.make_async_copy(
                cache_ref.at[request, local, rows], out_ref.at[slot], sem
            ).start()

    pair_count = requests * heads_local
    if len(outs) == 1:

        def pair_body(pair, carry):
            copy_pair(pair, outs[0].at[pair])
            return carry

        lax.fori_loop(0, pair_count, pair_body, 0)
    else:
        for offset, out_ref in enumerate(outs):
            copy_pair(jnp.bitwise_xor(me, offset), out_ref)
    for out_ref in outs:
        pltpu.make_async_copy(out_ref, out_ref, sem).wait()


def pick(kept_blocks, source_cache):
    requests, heads_local, _, row_width = source_cache.shape
    pair_count = requests * heads_local
    block = (MOST, BLK, row_width)
    if is_direct(pair_count):
        shapes = [jax.ShapeDtypeStruct(block, jnp.bfloat16)] * pair_count
    else:
        shapes = [jax.ShapeDtypeStruct((pair_count,) + block, jnp.bfloat16)]
    return pl.pallas_call(
        pick_kernel,
        out_shape=shapes,
        in_specs=[
            pl.BlockSpec(memory_space=pltpu.SMEM),
            pl.BlockSpec(memory_space=pl.ANY),
        ],
        out_specs=[pl.BlockSpec(memory_space=pltpu.VMEM)] * len(shapes),
        scratch_shapes=[pltpu.SemaphoreType.DMA],
        compiler_params=pltpu.CompilerParams(vmem_limit_bytes=12 * 1024 * 1024),
        name="pick_blocks",
    )(kept_blocks, source_cache)


def project_kernel(hidden_ref, gain_ref, wq_ref, wkv_ref, *outs):
    requests, step_count, width = hidden_ref.shape
    hidden = jnp.concatenate(
        [hidden_ref[r].astype(jnp.float32) for r in range(requests)], axis=0
    )
    square = jnp.sum(hidden * hidden, axis=1, keepdims=True)
    scaled = (hidden * gain_ref[...].astype(jnp.float32)).astype(jnp.bfloat16)
    query = jnp.dot(scaled, wq_ref[...], preferred_element_type=jnp.float32)
    keyval = jnp.dot(scaled, wkv_ref[...], preferred_element_type=jnp.float32)
    heads_local = wkv_ref.shape[1] // (2 * HD)
    me = lax.axis_index("seq")

    def write_pair(out_ref, pieces):
        for j, piece in enumerate(pieces):
            out_ref[j * step_count : (j + 1) * step_count, :] = piece

    for r in range(requests):
        steps = slice(r * step_count, (r + 1) * step_count)
        square_rows = jnp.broadcast_to(square[steps], (step_count, HD))
        for l in range(heads_local):
            pair = r * heads_local + l
            pieces = [
                query[steps, (l * QPK + h) * HD : (l * QPK + h + 1) * HD] for h in range(QPK)
            ]
            pieces += [
                keyval[steps, (l * 2 + h) * HD : (l * 2 + h + 1) * HD] for h in range(2)
            ]
            pieces += [square_rows, square_rows]
            if len(outs) == 1:
                write_pair(outs[0].at[pair], pieces)
            else:
                for offset, out_ref in enumerate(outs):
                    pl.when(jnp.bitwise_xor(me, offset) == pair)(
                        functools.partial(write_pair, out_ref, pieces)
                    )


def project(new_hidden, norm_gain, w_query, w_keyval, pair_count):
    requests, step_count, width = new_hidden.shape
    block = ((QPK + 4) * step_count, HD)
    if is_direct(pair_count):
        shapes = [jax.ShapeDtypeStruct(block, jnp.float32)] * pair_count
    else:
        shapes = [jax.ShapeDtypeStruct((pair_count,) + block, jnp.float32)]
    return pl.pallas_call(
        project_kernel,
        out_shape=shapes,
        in_specs=[pl.BlockSpec(memory_space=pltpu.VMEM)] * 4,
        out_specs=[pl.BlockSpec(memory_space=pltpu.VMEM)] * len(shapes),
        compiler_params=pltpu.CompilerParams(vmem_limit_bytes=24 * 1024 * 1024),
        cost_estimate=pl.CostEstimate(
            flops=2 * requests * step_count * width * (w_query.shape[1] + w_keyval.shape[1]),
            bytes_accessed=2 * width * (w_query.shape[1] + w_keyval.shape[1]),
            transcendentals=0,
        ),
        name="project",
    )(
        new_hidden,
        norm_gain,
        pltpu.with_memory_space_constraint(w_query, pltpu.VMEM),
        pltpu.with_memory_space_constraint(w_keyval, pltpu.VMEM),
    )


def attend_kernel(source_blocks, heads_local, seq_count, kept_ref, cos_ref, sin_ref, *refs):
    arrivals = (len(refs) - 5) // 2
    blocks_refs, parts_refs = refs[:arrivals], refs[arrivals : 2 * arrivals]
    cache_ref, attended_ref, kept, sem_in, sem_out = refs[2 * arrivals :]
    kept_count = kept_ref.shape[2]
    step_count = cos_ref.shape[0] // 2
    me = lax.axis_index("seq")
    request = lax.div(me, heads_local)
    head = lax.axis_index("head") * heads_local + lax.rem(me, heads_local)

    def start_copy(k, carry):
        previous, slot = carry
        source = lax.div(kept_ref[request, head, k], source_blocks)
        slot = jnp.where(source == previous, jnp.minimum(slot + 1, MOST - 1), 0)
        rows = pl.ds(pl.multiple_of(k * BLK, BLK), BLK)
        if arrivals == 1:
            pltpu.make_async_copy(
                blocks_refs[0].at[source, slot], kept.at[rows], sem_in
            ).start()
        else:
            for offset, blocks_ref in enumerate(blocks_refs):
                pl.when(jnp.bitwise_xor(me, offset) == source)(
                    pltpu.make_async_copy(blocks_ref.at[slot], kept.at[rows], sem_in).start
                )
        return source, slot

    lax.fori_loop(
        0, kept_count, start_copy, (jnp.int32(-1), jnp.int32(0)), unroll=kept_count <= 8
    )
    if arrivals == 1:
        total = jnp.sum(parts_refs[0][...], axis=0)
    else:
        total = sum(ref[...] for ref in parts_refs)
    query_rows = QPK * step_count
    inverse = lax.rsqrt(total[query_rows + 2 * step_count :] * (1.0 / D) + EPS)
    cosine, sine = cos_ref[...], sin_ref[...]
    query = total[:query_rows].reshape(QPK // 2, 2 * step_count, HD) * inverse[None]
    query = rotate(query, cosine[None], sine[None]).reshape(query_rows, HD).astype(jnp.bfloat16)
    keyval = total[query_rows : query_rows + 2 * step_count] * inverse
    new_key = rotate(keyval, cosine, sine).astype(jnp.bfloat16)
    new_value = jnp.concatenate([keyval[step_count:], keyval[:step_count]], axis=0)
    new_value = new_value.astype(jnp.bfloat16)
    scale = 1.0 / math.sqrt(HD)
    score_new = (
        lax.dot_general(query, new_key, CONTRACT_LAST, preferred_element_type=jnp.float32) * scale
    )
    row = lax.broadcasted_iota(jnp.int32, score_new.shape, 0)
    column = lax.broadcasted_iota(jnp.int32, score_new.shape, 1)
    score_new = jnp.where(column <= lax.rem(row, step_count), score_new, -jnp.inf)

    pltpu.make_async_copy(kept, kept, sem_in).wait()
    out_copy = pltpu.make_async_copy(kept, cache_ref.at[0, 0], sem_out)
    out_copy.start()
    score_kept = (
        lax.dot_general(query, kept[:, :HD], CONTRACT_LAST, preferred_element_type=jnp.float32)
        * scale
    )
    row_max = jnp.maximum(
        jnp.max(score_kept, axis=1, keepdims=True), jnp.max(score_new, axis=1, keepdims=True)
    )
    weight_kept = jnp.exp(score_kept - row_max)
    weight_new = jnp.exp(score_new - row_max)
    denominator = jnp.sum(weight_kept, axis=1, keepdims=True) + jnp.sum(
        weight_new, axis=1, keepdims=True
    )
    numerator = jnp.dot(
        weight_kept.astype(jnp.bfloat16), kept[:, HD:], preferred_element_type=jnp.float32
    )
    numerator += jnp.dot(
        weight_new.astype(jnp.bfloat16), new_value, preferred_element_type=jnp.float32
    )
    attended = (numerator / denominator).astype(jnp.bfloat16)
    if arrivals == 1:
        for i in range(attended_ref.shape[0]):
            attended_ref[i] = attended
    else:
        attended_ref[...] = attended
    out_copy.wait()


def attend(kept_blocks, blocks, parts, source_blocks, heads_local, step_count, seq_count):
    kept_count = kept_blocks.shape[2]
    row_width = blocks[0].shape[-1]
    cosine, sine = rope_tables(source_blocks * BLK * seq_count, step_count)
    shape = (QPK * step_count, HD)
    if len(blocks) == 1:
        shape = (seq_count,) + shape
    vmem = pl.BlockSpec(memory_space=pltpu.VMEM)
    anywhere = pl.BlockSpec(memory_space=pl.ANY)
    kept_cache, attended = pl.pallas_call(
        functools.partial(attend_kernel, source_blocks, heads_local, seq_count),
        out_shape=(
            jax.ShapeDtypeStruct((1, 1, kept_count * BLK, row_width), jnp.bfloat16),
            jax.ShapeDtypeStruct(shape, jnp.bfloat16),
        ),
        in_specs=[pl.BlockSpec(memory_space=pltpu.SMEM), vmem, vmem]
        + [anywhere] * len(blocks)
        + [vmem] * len(parts),
        out_specs=(anywhere, vmem),
        scratch_shapes=[
            pltpu.VMEM((kept_count * BLK, row_width), jnp.bfloat16),
            pltpu.SemaphoreType.DMA,
            pltpu.SemaphoreType.DMA,
        ],
        compiler_params=pltpu.CompilerParams(vmem_limit_bytes=24 * 1024 * 1024),
        name="attend",
    )(kept_blocks, jnp.asarray(cosine), jnp.asarray(sine), *blocks, *parts)
    return kept_cache, [attended] * len(blocks) if len(blocks) == 1 else [attended] * seq_count


def output_kernel(heads_local, w_ref, *refs):
    gathered_refs, out_ref = refs[:-1], refs[-1]
    query_rows = gathered_refs[0].shape[-2]
    step_count = query_rows // QPK
    if len(gathered_refs) == 1:
        pair_count = gathered_refs[0].shape[0]
        pairs = [gathered_refs[0][p].astype(jnp.float32) for p in range(pair_count)]
    else:
        pair_count = len(gathered_refs)
        me = lax.axis_index("seq")
        arrived = [ref[...].astype(jnp.float32) for ref in gathered_refs]
        pairs = arrived
        bit = 1
        while bit < pair_count:
            swap = jnp.bitwise_and(me, bit) != 0
            pairs = [jnp.where(swap, pairs[p ^ bit], pairs[p]) for p in range(pair_count)]
            bit *= 2
    requests = pair_count // heads_local
    pieces = []
    for l in range(heads_local):
        for h in range(QPK):
            rows = slice(h * step_count, (h + 1) * step_count)
            pieces.append(
                jnp.concatenate(
                    [pairs[r * heads_local + l][rows] for r in range(requests)], axis=0
                )
            )
    merged = jnp.concatenate(pieces, axis=1).astype(jnp.bfloat16)
    total = jnp.dot(merged, w_ref[...], preferred_element_type=jnp.float32)
    if len(out_ref.shape) == 2:
        out_ref[...] = total
    else:
        for i in range(out_ref.shape[0]):
            out_ref[i] = total


def output(gathered, w_out, heads_local, pair_count, head_count):
    query_rows = gathered[0].shape[-2]
    total_rows = pair_count // heads_local * (query_rows // QPK)
    shape = (total_rows, w_out.shape[1])
    if not is_direct(head_count):
        shape = (head_count,) + shape
    vmem = pl.BlockSpec(memory_space=pltpu.VMEM)
    terms = pl.pallas_call(
        functools.partial(output_kernel, heads_local),
        out_shape=jax.ShapeDtypeStruct(shape, jnp.float32),
        in_specs=[vmem] * (1 + len(gathered)),
        out_specs=vmem,
        compiler_params=pltpu.CompilerParams(vmem_limit_bytes=24 * 1024 * 1024),
        name="output_projection",
    )(pltpu.with_memory_space_constraint(w_out, pltpu.VMEM), *gathered)
    return [terms] * (head_count if is_direct(head_count) else 1)


def shards(source_cache, kept_blocks, new_hidden, norm_gain, w_query, w_keyval, w_out):
    seq_count = lax.axis_size("seq")
    head_count = lax.axis_size("head")
    requests, heads_local, source_tokens, _ = source_cache.shape
    _, step_count, width = new_hidden.shape
    pair_count = requests * heads_local

    blocks = exchange(pick(kept_blocks, source_cache), "seq")
    parts = project(
        new_hidden, norm_gain.reshape(1, width), w_query, w_keyval.reshape(width, -1), pair_count
    )
    parts = exchange(parts, "seq")
    kept_cache, attended = attend(
        kept_blocks, blocks, parts, source_tokens // BLK, heads_local, step_count, seq_count
    )
    gathered = exchange(attended, "seq")
    terms = exchange(output(gathered, w_out, heads_local, pair_count, head_count), "head")
    if len(terms) == 1:
        summed = jnp.sum(terms[0], axis=0)
    else:
        while len(terms) > 1:
            terms = [terms[i] + terms[i + 1] for i in range(0, len(terms), 2)]
        summed = terms[0]
    summed = summed.reshape(requests, step_count, width)
    decoded = (new_hidden.astype(jnp.float32) + summed).astype(jnp.bfloat16)
    return (kept_cache, decoded)


def solution(mesh):
    in_specs = (
        P("groups", "head", "seq", None),
        P("groups", None, None),
        P("groups", None, "seq"),
        P("seq"),
        P("seq", "head"),
        P("seq", "head", None),
        P("head", "seq"),
    )
    out_specs = (P("head", ("groups", "seq"), None, None), P("groups", None, "seq"))
    return jax.shard_map(shards, mesh=mesh, in_specs=in_specs, out_specs=out_specs, check_vma=False)
```

time: 80.9 us -> 46.4 us (0.57)
  blocking collectives: 35.8 us -> 0 us
  Pallas kernels: 25 us -> 6.24 us
  starting transfers between devices: 6.33 us -> 19.7 us
  waiting for transfers between devices: 0.01 us -> 9.76 us
  local copies, waits for them, and re-layouts: 11.7 us -> 8.91 us
    all_to_all x3 -> x0, blocking collectives: 35.8 us -> none  [the longest x1 19 us: shards(): lax.all_to_all(outgoing, 'seq', split_axis=0, concat_axis=0, tiled=True)]
    ppermute x0 -> x12, starting transfers between devices: none -> 19.7 us  [exchange(): lax.ppermute(outgoing[k], axis, [(i, i ^ k) for i in range(count)])]
    pallas_call x3, Pallas kernels: 23 us -> 4.18 us  [the longest x1 1.52 us: pick(): pl.pallas_call(pick_kernel, out_shape=shapes, in_specs=[pl.BlockSpec(memo...]
    ppermute x0 -> x12, waiting for transfers between devices: none -> 9.76 us  [exchange(): lax.ppermute(outgoing[k], axis, [(i, i ^ k) for i in range(count)])]
    all_to_all x1 -> x0, starting transfers between devices: 6.33 us -> none  [shards(): lax.all_to_all(parts, 'seq', split_axis=0, concat_axis=0, tiled=True)]
    unnamed x18 -> x16, local copies, waits for them, and re-layouts: 11 us -> 8.19 us
  transfers between devices with their start and end apart: 1 -> 12, of which waited for: 0 -> 5; matrix products, arithmetic and copies ran while one was open for 1% -> 6% of each run, Pallas kernels for 22% -> 3%
where the time goes in v2:
time: 46.4 us; the launch traced here: 46 us
  starting transfers between devices  19.7 us (42%)
  waiting for transfers between devices  9.76 us (21%)
  local copies, waits for them, and re-layouts  8.91 us (19%)
  Pallas kernels  6.24 us (13%)
  between operations  0.74 us (2%)
  other arithmetic  0.65 us (1%)
    ppermute x12, starting transfers between devices, exchange(): lax.ppermute(outgoing[k], axis, [(i, i ^ k) for i in range(count)])  19.7 us
    ppermute x12, waiting for transfers between devices, exchange(): lax.ppermute(outgoing[k], axis, [(i, i ^ k) for i in range(count)])  9.76 us
    unnamed x16, local copies, waits for them, and re-layouts  8.19 us
    pallas_call x1, Pallas kernels, attend(): pl.pallas_call(functools.partial(attend_kernel, source_blocks, heads_loca...  2.06 us
    pallas_call x1, Pallas kernels, pick(): pl.pallas_call(pick_kernel, out_shape=shapes, in_specs=[pl.BlockSpec(memo...  1.52 us
    pallas_call x1, Pallas kernels, project(): pl.pallas_call(project_kernel, out_shape=shapes, in_specs=[pl.BlockSpec(m...  1.48 us
    pallas_call x1, Pallas kernels, output(): pl.pallas_call(functools.partial(output_kernel, heads_local), out_shape=j...  1.19 us
  transfers between devices with their start and end apart: 12, of which 5 were waited for; matrix products, arithmetic and copies ran while one was open for 6% of the time, Pallas kernels for 3%

profile of v2, /device:TPU:0, one launch (start us, length us, event | category | flops | bytes accessed | tf_op | source)
XLA Modules:
  0.0 46.0 jit_solution(7459880631259007255)
XLA Ops:
  0.7 0.8 %copy.12.kept_ref = s32[2,8,4]{2,1,0:T(8,128)S(1)} copy(s32[2,8,4]{1,2,0:T(4,128)} %param.10) | data formatting | bytes 512 | tf_op args[1]
  1.4 1.2 %copy-done.2 = bf16[2,2,512,256]{3,2,1,0:T(8,128)(2,1)S(1)} copy-done((bf16[2,2,512,256]{3,2,1,0:T(8,128)(2,1)S(1)}, bf16[2,2,512,256]{3,2,1,0:T(8,128)(2,1)}, u32[]{:S(2)}) %copy-start.2) | copy-done | bytes 1048600
  2.7 1.5 %pick_blocks.1 = (bf16[2,128,256]{2,1,0:T(8,128)(2,1)S(1)}, bf16[2,128,256]{2,1,0:T(8,128)(2,1)S(1)}, bf16[2,128,256]{2,1,0:T(8,128)(2,1)S(1)}, bf16[2,128,256]{2,1,0:T(8,128)(2,1)S(1)}) custom-call(s32[2,8,4]{2,1,0:T(8,128)S(1)} %copy.12.kept_ref, bf16[2,2,512,256]{3,2,1,0:T(8,128)(2,1)S(1)} %copy-done.2), custom_call_target="tpu_custom_call" | custom-call | tf_op jit(solution)/shard_map/pick_blocks/pallas_call | solution.py:101
  4.2 3.1 %collective-permute-start = (bf16[2,128,256]{2,1,0:T(8,128)(2,1)S(1)}, bf16[2,128,256]{2,1,0:T(8,128)(2,1)S(1)}, u32[]{:S(2)}, u32[]{:S(2)}) collective-permute-start(bf16[2,128,256]{2,1,0:T(8,128)(2,1)S(1)} %get-tuple-element.13), channel_id=1, source_target_pairs={{0,4},{4,0},{8,12},{12,8},{1,5},{5,1},{9,13},{13,9},{2,6},{6,2},{1... | collective-permute-start | bytes 393224 | tf_op jit(solution)/shard_map/ppermute | solution.py:46
  7.3 2.6 %collective-permute-start.1 = (bf16[2,128,256]{2,1,0:T(8,128)(2,1)S(1)}, bf16[2,128,256]{2,1,0:T(8,128)(2,1)S(1)}, u32[]{:S(2)}, u32[]{:S(2)}) collective-permute-start(bf16[2,128,256]{2,1,0:T(8,128)(2,1)S(1)} %get-tuple-element.14), channel_id=1, source_target_pairs={{0,8},{4,12},{8,0},{12,4},{1,9},{5,13},{9,1},{13,5},{2,10},{6,14},... | collective-permute-start | bytes 393224 | tf_op jit(solution)/shard_map/ppermute | solution.py:46
  9.9 0.7 %reshape.13.gain_ref = bf16[1,2048]{1,0:T(2,128)(2,1)S(1)} reshape(bf16[2048]{0:T(1024)(128)(2,1)} %param.12) | data formatting | bytes 8192 | tf_op jit(solution)/shard_map/reshape | solution.py:352
  10.6 2.0 %copy.13 = bf16[256,8,2,256]{3,1,2,0:T(8,128)(2,1)S(1)} copy(bf16[256,8,2,256]{3,2,1,0:T(2,128)(2,1)} %bitcast.3) | data formatting | bytes 4194304
  12.6 3.4 %copy-done = bf16[2048,2048]{1,0:T(8,128)(2,1)S(1)} copy-done((bf16[2048,2048]{1,0:T(8,128)(2,1)S(1)}, bf16[2048,2048]{1,0:T(8,128)(2,1)}, u32[]{:S(2)}) %copy-start) | copy-done | bytes 8388632
  16.0 0.8 %copy-done.3 = bf16[2,4,2048]{2,1,0:T(4,128)(2,1)S(1)} copy-done((bf16[2,4,2048]{2,1,0:T(4,128)(2,1)S(1)}, bf16[2,4,2048]{2,1,0:T(4,128)(2,1)}, u32[]{:S(2)}) %copy-start.3) | copy-done | bytes 32792
  16.7 1.5 %project.1 = (f32[48,128]{1,0:T(8,128)S(1)}, f32[48,128]{1,0:T(8,128)S(1)}, f32[48,128]{1,0:T(8,128)S(1)}, f32[48,128]{1,0:T(8,128)S(1)}) custom-call(bf16[2,4,2048]{2,1,0:T(4,128)(2,1)S(1)} %copy-done.3, bf16[1,2048]{1,0:T(2,128)(2,1)S(1)} %reshape.13.gain_ref, bf16[2048,2048]{1,0:T(8,128)(2,1)S(1)} %copy-done, bf16[2048,512]{1,0:T(8,128)(2,1)S(1)} %bitcast.2), custom_call_target="tpu_custom_call" | custom-call | flops 83886080 | bytes 10485760 | tf_op jit(solution)/shard_map/project/pallas_call | solution.py:159
  18.2 1.0 %collective-permute-start.3 = (f32[48,128]{1,0:T(8,128)S(1)}, f32[48,128]{1,0:T(8,128)S(1)}, u32[]{:S(2)}, u32[]{:S(2)}) collective-permute-start(f32[48,128]{1,0:T(8,128)S(1)} %get-tuple-element.17), channel_id=1, source_target_pairs={{0,4},{4,0},{8,12},{12,8},{1,5},{5,1},{9,13},{13,9},{2,6},{6,2},{1... | collective-permute-start | bytes 73736 | tf_op jit(solution)/shard_map/ppermute | solution.py:46
  19.2 3.5 %collective-permute-start.4 = (f32[48,128]{1,0:T(8,128)S(1)}, f32[48,128]{1,0:T(8,128)S(1)}, u32[]{:S(2)}, u32[]{:S(2)}) collective-permute-start(f32[48,128]{1,0:T(8,128)S(1)} %get-tuple-element.18), channel_id=1, source_target_pairs={{0,8},{4,12},{8,0},{12,4},{1,9},{5,13},{9,1},{13,5},{2,10},{6,14},... | collective-permute-start | bytes 73736 | tf_op jit(solution)/shard_map/ppermute | solution.py:46
  22.7 3.3 %collective-permute-start.5 = (f32[48,128]{1,0:T(8,128)S(1)}, f32[48,128]{1,0:T(8,128)S(1)}, u32[]{:S(2)}, u32[]{:S(2)}) collective-permute-start(f32[48,128]{1,0:T(8,128)S(1)} %get-tuple-element.19), channel_id=1, source_target_pairs={{0,12},{4,8},{8,4},{12,0},{1,13},{5,9},{9,5},{13,1},{2,14},{6,10},... | collective-permute-start | bytes 73736 | tf_op jit(solution)/shard_map/ppermute | solution.py:46
  26.0 2.4 %collective-permute-done.5.refs_7_ = f32[48,128]{1,0:T(8,128)S(1)} collective-permute-done((f32[48,128]{1,0:T(8,128)S(1)}, f32[48,128]{1,0:T(8,128)S(1)}, u32[]{:S(2)}, u32[]{:S(2)}) %collective-permute-start.5) | collective-permute-done | bytes 24608 | tf_op jit(solution)/shard_map/ppermute | solution.py:46
  28.4 2.1 %attend.1 = (bf16[1,1,512,256]{3,2,1,0:T(8,128)(2,1)}, bf16[32,128]{1,0:T(8,128)(2,1)S(1)}) custom-call(s32[2,8,4]{2,1,0:T(8,128)S(1)} %copy.12.kept_ref, f32[8,128]{1,0:T(8,128)S(1)} %copy-done.6, f32[8,128]{1,0:T(8,128)S(1)} %copy-done.5, bf16[2,128,256]{2,1,0:T(8,128)(2,1)S(1)} %get-tuple-element.12.refs_0_, ...), custom_call_target="tpu_custom_call" | custom-call | tf_op jit(solution)/shard_map/attend/pallas_call | solution.py:268
  30.4 3.3 %collective-permute-start.8 = (bf16[32,128]{1,0:T(8,128)(2,1)S(1)}, bf16[32,128]{1,0:T(8,128)(2,1)S(1)}, u32[]{:S(2)}, u32[]{:S(2)}) collective-permute-start(bf16[32,128]{1,0:T(8,128)(2,1)S(1)} %get-tuple-element.21.refs_0_), channel_id=1, source_target_pairs={{0,12},{4,8},{8,4},{12,0},{1,13},{5,9},{9,5},{13,1},{2,14},{6,10},... | collective-permute-start | bytes 24584 | tf_op jit(solution)/shard_map/ppermute | solution.py:46
  33.8 1.1 %collective-permute-start.6 = (bf16[32,128]{1,0:T(8,128)(2,1)S(1)}, bf16[32,128]{1,0:T(8,128)(2,1)S(1)}, u32[]{:S(2)}, u32[]{:S(2)}) collective-permute-start(bf16[32,128]{1,0:T(8,128)(2,1)S(1)} %get-tuple-element.21.refs_0_), channel_id=1, source_target_pairs={{0,4},{4,0},{8,12},{12,8},{1,5},{5,1},{9,13},{13,9},{2,6},{6,2},{1... | collective-permute-start | bytes 24584 | tf_op jit(solution)/shard_map/ppermute | solution.py:46
  34.9 1.1 %collective-permute-done.8.refs_3_ = bf16[32,128]{1,0:T(8,128)(2,1)S(1)} collective-permute-done((bf16[32,128]{1,0:T(8,128)(2,1)S(1)}, bf16[32,128]{1,0:T(8,128)(2,1)S(1)}, u32[]{:S(2)}, u32[]{:S(2)}) %collective-permute-start.8) | collective-permute-done | bytes 8224 | tf_op jit(solution)/shard_map/ppermute | solution.py:46
  35.9 2.4 %collective-permute-done.7.refs_2_ = bf16[32,128]{1,0:T(8,128)(2,1)S(1)} collective-permute-done((bf16[32,128]{1,0:T(8,128)(2,1)S(1)}, bf16[32,128]{1,0:T(8,128)(2,1)S(1)}, u32[]{:S(2)}, u32[]{:S(2)}) %collective-permute-start.7) | collective-permute-done | bytes 8224 | tf_op jit(solution)/shard_map/ppermute | solution.py:46
  38.3 1.2 %output_projection.1 = f32[8,2048]{1,0:T(8,128)S(1)} custom-call(bf16[2048,2048]{1,0:T(8,128)(2,1)S(1)} %copy-done.1, bf16[32,128]{1,0:T(8,128)(2,1)S(1)} %get-tuple-element.21.refs_0_, bf16[32,128]{1,0:T(8,128)(2,1)S(1)} %collective-permute-done.6.refs_1_, bf16[32,128]{1,0:T(8,128)(2,1)S(1)} %collective-permute-done.7.refs_2_, ...), custom_call_target="tpu_custom_call" | custom-call | tf_op jit(solution)/shard_map/output_projection/pallas_call | solution.py:332
  39.5 1.5 %collective-permute-start.10 = (f32[8,2048]{1,0:T(8,128)S(1)}, f32[8,2048]{1,0:T(8,128)S(1)}, u32[]{:S(2)}, u32[]{:S(2)}) collective-permute-start(f32[8,2048]{1,0:T(8,128)S(1)} %output_projection.1), channel_id=1, source_target_pairs={{0,2},{1,3},{2,0},{3,1},{4,6},{5,7},{6,4},{7,5},{8,10},{9,11},{10,... | collective-permute-start | bytes 196616 | tf_op jit(solution)/shard_map/ppermute | solution.py:46
  41.4 2.5 %collective-permute-done.11 = f32[8,2048]{1,0:T(8,128)S(1)} collective-permute-done((f32[8,2048]{1,0:T(8,128)S(1)}, f32[8,2048]{1,0:T(8,128)S(1)}, u32[]{:S(2)}, u32[]{:S(2)}) %collective-permute-start.11) | collective-permute-done | bytes 65568 | tf_op jit(solution)/shard_map/ppermute | solution.py:46
  43.9 1.5 %collective-permute-done.10 = f32[8,2048]{1,0:T(8,128)S(1)} collective-permute-done((f32[8,2048]{1,0:T(8,128)S(1)}, f32[8,2048]{1,0:T(8,128)S(1)}, u32[]{:S(2)}, u32[]{:S(2)}) %collective-permute-start.10) | collective-permute-done | bytes 65568 | tf_op jit(solution)/shard_map/ppermute | solution.py:46
  45.4 0.6 %add_convert_fusion = bf16[2,4,2048]{2,1,0:T(4,128)(2,1)} fusion(f32[2,4,2048]{2,1,0:T(4,128)S(1)} %reshape.15, bf16[2,4,2048]{2,1,0:T(4,128)(2,1)S(1)} %copy-done.4), kind=kLoop, calls=%fused_computation | loop fusion | flops 49152 | bytes 131072 | tf_op jit(solution)/shard_map/convert_element_type | solution.py:367
  (24 shorter events, 0.4 us)
Async XLA Ops:
  0.6 27.7 %copy-start.5 = (f32[8,128]{1,0:T(8,128)S(1)}, f32[8,128]{1,0:T(8,128)}, u32[]{:S(2)}) copy-start(f32[8,128]{1,0:T(8,128)} %constant.5.clone.sin_ref) | copy-start | bytes 12292
  0.6 27.7 %copy-start.6 = (f32[8,128]{1,0:T(8,128)S(1)}, f32[8,128]{1,0:T(8,128)}, u32[]{:S(2)}) copy-start(f32[8,128]{1,0:T(8,128)} %constant.4.clone.cos_ref) | copy-start | bytes 12292
  1.4 1.2 %copy-start.2 = (bf16[2,2,512,256]{3,2,1,0:T(8,128)(2,1)S(1)}, bf16[2,2,512,256]{3,2,1,0:T(8,128)(2,1)}, u32[]{:S(2)}) copy-start(bf16[2,2,512,256]{3,2,1,0:T(8,128)(2,1)} %cache_ref.1) | copy-start | bytes 3145732
  4.2 24.2 %collective-permute-start = (bf16[2,128,256]{2,1,0:T(8,128)(2,1)S(1)}, bf16[2,128,256]{2,1,0:T(8,128)(2,1)S(1)}, u32[]{:S(2)}, u32[]{:S(2)}) collective-permute-start(bf16[2,128,256]{2,1,0:T(8,128)(2,1)S(1)} %get-tuple-element.13), channel_id=1, source_target_pairs={{0,4},{4,0},{8,12},{12,8},{1,5},{5,1},{9,13},{13,9},{2,6},{6,2},{1... | collective-permute-start | bytes 393224 | tf_op jit(solution)/shard_map/ppermute | solution.py:46
  7.3 21.1 %collective-permute-start.1 = (bf16[2,128,256]{2,1,0:T(8,128)(2,1)S(1)}, bf16[2,128,256]{2,1,0:T(8,128)(2,1)S(1)}, u32[]{:S(2)}, u32[]{:S(2)}) collective-permute-start(bf16[2,128,256]{2,1,0:T(8,128)(2,1)S(1)} %get-tuple-element.14), channel_id=1, source_target_pairs={{0,8},{4,12},{8,0},{12,4},{1,9},{5,13},{9,1},{13,5},{2,10},{6,14},... | collective-permute-start | bytes 393224 | tf_op jit(solution)/shard_map/ppermute | solution.py:46
  9.9 18.5 %collective-permute-start.2 = (bf16[2,128,256]{2,1,0:T(8,128)(2,1)S(1)}, bf16[2,128,256]{2,1,0:T(8,128)(2,1)S(1)}, u32[]{:S(2)}, u32[]{:S(2)}) collective-permute-start(bf16[2,128,256]{2,1,0:T(8,128)(2,1)S(1)} %get-tuple-element.15), channel_id=1, source_target_pairs={{0,12},{4,8},{8,4},{12,0},{1,13},{5,9},{9,5},{13,1},{2,14},{6,10},... | collective-permute-start | bytes 393224 | tf_op jit(solution)/shard_map/ppermute | solution.py:46
  12.6 3.4 %copy-start = (bf16[2048,2048]{1,0:T(8,128)(2,1)S(1)}, bf16[2048,2048]{1,0:T(8,128)(2,1)}, u32[]{:S(2)}) copy-start(bf16[2048,2048]{1,0:T(8,128)(2,1)} %wq_ref.1) | copy-start | bytes 25165828
  16.0 0.8 %copy-start.3 = (bf16[2,4,2048]{2,1,0:T(4,128)(2,1)S(1)}, bf16[2,4,2048]{2,1,0:T(4,128)(2,1)}, u32[]{:S(2)}) copy-start(bf16[2,4,2048]{2,1,0:T(4,128)(2,1)} %hidden_ref.1) | copy-start | bytes 98308
  16.7 21.6 %copy-start.1 = (bf16[2048,2048]{1,0:T(8,128)(2,1)S(1)}, bf16[2048,2048]{1,0:T(8,128)(2,1)}, u32[]{:S(2)}) copy-start(bf16[2048,2048]{1,0:T(8,128)(2,1)} %w_ref.1) | copy-start | bytes 25165828
  16.7 28.6 %copy-start.4 = (bf16[2,4,2048]{2,1,0:T(4,128)(2,1)S(1)}, bf16[2,4,2048]{2,1,0:T(4,128)(2,1)}, u32[]{:S(2)}) copy-start(bf16[2,4,2048]{2,1,0:T(4,128)(2,1)} %hidden_ref.1) | copy-start | bytes 98308
  18.2 4.5 %collective-permute-start.3 = (f32[48,128]{1,0:T(8,128)S(1)}, f32[48,128]{1,0:T(8,128)S(1)}, u32[]{:S(2)}, u32[]{:S(2)}) collective-permute-start(f32[48,128]{1,0:T(8,128)S(1)} %get-tuple-element.17), channel_id=1, source_target_pairs={{0,4},{4,0},{8,12},{12,8},{1,5},{5,1},{9,13},{13,9},{2,6},{6,2},{1... | collective-permute-start | bytes 73736 | tf_op jit(solution)/shard_map/ppermute | solution.py:46
  19.2 6.8 %collective-permute-start.4 = (f32[48,128]{1,0:T(8,128)S(1)}, f32[48,128]{1,0:T(8,128)S(1)}, u32[]{:S(2)}, u32[]{:S(2)}) collective-permute-start(f32[48,128]{1,0:T(8,128)S(1)} %get-tuple-element.18), channel_id=1, source_target_pairs={{0,8},{4,12},{8,0},{12,4},{1,9},{5,13},{9,1},{13,5},{2,10},{6,14},... | collective-permute-start | bytes 73736 | tf_op jit(solution)/shard_map/ppermute | solution.py:46
  22.7 5.6 %collective-permute-start.5 = (f32[48,128]{1,0:T(8,128)S(1)}, f32[48,128]{1,0:T(8,128)S(1)}, u32[]{:S(2)}, u32[]{:S(2)}) collective-permute-start(f32[48,128]{1,0:T(8,128)S(1)} %get-tuple-element.19), channel_id=1, source_target_pairs={{0,12},{4,8},{8,4},{12,0},{1,13},{5,9},{9,5},{13,1},{2,14},{6,10},... | collective-permute-start | bytes 73736 | tf_op jit(solution)/shard_map/ppermute | solution.py:46
  30.4 5.5 %collective-permute-start.8 = (bf16[32,128]{1,0:T(8,128)(2,1)S(1)}, bf16[32,128]{1,0:T(8,128)(2,1)S(1)}, u32[]{:S(2)}, u32[]{:S(2)}) collective-permute-start(bf16[32,128]{1,0:T(8,128)(2,1)S(1)} %get-tuple-element.21.refs_0_), channel_id=1, source_target_pairs={{0,12},{4,8},{8,4},{12,0},{1,13},{5,9},{9,5},{13,1},{2,14},{6,10},... | collective-permute-start | bytes 24584 | tf_op jit(solution)/shard_map/ppermute | solution.py:46
  33.8 4.5 %collective-permute-start.7 = (bf16[32,128]{1,0:T(8,128)(2,1)S(1)}, bf16[32,128]{1,0:T(8,128)(2,1)S(1)}, u32[]{:S(2)}, u32[]{:S(2)}) collective-permute-start(bf16[32,128]{1,0:T(8,128)(2,1)S(1)} %get-tuple-element.21.refs_0_), channel_id=1, source_target_pairs={{0,8},{4,12},{8,0},{12,4},{1,9},{5,13},{9,1},{13,5},{2,10},{6,14},... | collective-permute-start | bytes 24584 | tf_op jit(solution)/shard_map/ppermute | solution.py:46
  33.8 4.5 %collective-permute-start.6 = (bf16[32,128]{1,0:T(8,128)(2,1)S(1)}, bf16[32,128]{1,0:T(8,128)(2,1)S(1)}, u32[]{:S(2)}, u32[]{:S(2)}) collective-permute-start(bf16[32,128]{1,0:T(8,128)(2,1)S(1)} %get-tuple-element.21.refs_0_), channel_id=1, source_target_pairs={{0,4},{4,0},{8,12},{12,8},{1,5},{5,1},{9,13},{13,9},{2,6},{6,2},{1... | collective-permute-start | bytes 24584 | tf_op jit(solution)/shard_map/ppermute | solution.py:46
  39.5 4.4 %collective-permute-start.11 = (f32[8,2048]{1,0:T(8,128)S(1)}, f32[8,2048]{1,0:T(8,128)S(1)}, u32[]{:S(2)}, u32[]{:S(2)}) collective-permute-start(f32[8,2048]{1,0:T(8,128)S(1)} %output_projection.1), channel_id=1, source_target_pairs={{0,3},{1,2},{2,1},{3,0},{4,7},{5,6},{6,5},{7,4},{8,11},{9,10},{10,... | collective-permute-start | bytes 196616 | tf_op jit(solution)/shard_map/ppermute | solution.py:46
  39.5 5.8 %collective-permute-start.10 = (f32[8,2048]{1,0:T(8,128)S(1)}, f32[8,2048]{1,0:T(8,128)S(1)}, u32[]{:S(2)}, u32[]{:S(2)}) collective-permute-start(f32[8,2048]{1,0:T(8,128)S(1)} %output_projection.1), channel_id=1, source_target_pairs={{0,2},{1,3},{2,0},{3,1},{4,6},{5,7},{6,4},{7,5},{8,10},{9,11},{10,... | collective-permute-start | bytes 196616 | tf_op jit(solution)/shard_map/ppermute | solution.py:46
  41.1 4.3 %collective-permute-start.9 = (f32[8,2048]{1,0:T(8,128)S(1)}, f32[8,2048]{1,0:T(8,128)S(1)}, u32[]{:S(2)}, u32[]{:S(2)}) collective-permute-start(f32[8,2048]{1,0:T(8,128)S(1)} %output_projection.1), channel_id=1, source_target_pairs={{0,1},{1,0},{2,3},{3,2},{4,5},{5,4},{6,7},{7,6},{8,9},{9,8},{10,11... | collective-permute-start | bytes 196616 | tf_op jit(solution)/shard_map/ppermute | solution.py:46

commit v3 on v2

--- a/solution.py
+++ b/solution.py
@@ -52,7 +52,7 @@
     outs, sem = refs[:-1], refs[-1]
     requests, heads_local, source_tokens, _ = cache_ref.shape
     source_blocks = source_tokens // BLK
-    kept_count = kept_ref.shape[2]
+    kept_count = kept_ref.shape[1]
     me = lax.axis_index("seq")
     first_head = lax.axis_index("head") * heads_local
 
@@ -62,13 +62,13 @@
         head = first_head + local
 
         def count(k, total):
-            block = kept_ref[request, head, k]
+            block = kept_ref[request, k, head]
             return total + (block < me * source_blocks).astype(jnp.int32)
 
         start = lax.fori_loop(0, kept_count, count, jnp.int32(0), unroll=kept_count <= 8)
         for slot in range(MOST):
             rank = jnp.minimum(start + slot, kept_count - 1)
-            block = kept_ref[request, head, rank] - me * source_blocks
+            block = kept_ref[request, rank, head] - me * source_blocks
             block = jnp.clip(block, 0, source_blocks - 1)
             rows = pl.ds(pl.multiple_of(block * BLK, BLK), BLK)
             pltpu.make_async_copy(
@@ -109,19 +109,75 @@
         scratch_shapes=[pltpu.SemaphoreType.DMA],
         compiler_params=pltpu.CompilerParams(vmem_limit_bytes=12 * 1024 * 1024),
         name="pick_blocks",
-    )(kept_blocks, source_cache)
-
-
-def project_kernel(hidden_ref, gain_ref, wq_ref, wkv_ref, *outs):
+    )(kept_blocks, pltpu.with_memory_space_constraint(source_cache, pltpu.HBM))
+
+
+def interleave(rows):
+    count, width = rows.shape
+    chunks = width // HD
+    stacked = jnp.concatenate(
+        [rows[:, c * HD : (c + 1) * HD] for c in range(chunks)], axis=0
+    ).astype(jnp.bfloat16)
+    source = lax.broadcasted_iota(jnp.int32, (HD, 4 * HD), 0)
+    target = lax.broadcasted_iota(jnp.int32, (HD, 4 * HD), 1)
+    place = jnp.where(target < 2 * HD, 2 * source, 2 * source + 1 + 2 * HD)
+    spread = (place == target).astype(jnp.bfloat16)
+    wide = jnp.dot(stacked, spread, preferred_element_type=jnp.float32)
+    return [
+        jnp.concatenate(
+            [
+                wide[c * count : (c + 1) * count, : 2 * HD],
+                wide[c * count : (c + 1) * count, 2 * HD :],
+            ],
+            axis=0,
+        ).astype(jnp.bfloat16)
+        for c in range(chunks)
+    ]
+
+
+def chunk_copies(w_ref, buffer, sems, rows):
+    return [
+        pltpu.make_async_copy(
+            w_ref.at[pl.ds(i * rows, rows)], buffer.at[pl.ds(i * rows, rows)], sems.at[i]
+        )
+        for i in range(w_ref.shape[0] // rows)
+    ]
+
+
+def project_kernel(rows, hidden_ref, gain_ref, wq_ref, wkv_ref, *refs):
+    outs = refs[:-4]
+    wq, wkv, sem_q, sem_kv = refs[-4:]
+    copies_q = chunk_copies(wq_ref, wq, sem_q, rows)
+    copies_kv = chunk_copies(wkv_ref, wkv, sem_kv, rows)
+    for copy_q, copy_kv in zip(copies_q, copies_kv):
+        copy_kv.start()
+        copy_q.start()
     requests, step_count, width = hidden_ref.shape
+    heads_local = wkv_ref.shape[1]
+    row_count = requests * step_count
     hidden = jnp.concatenate(
         [hidden_ref[r].astype(jnp.float32) for r in range(requests)], axis=0
     )
     square = jnp.sum(hidden * hidden, axis=1, keepdims=True)
     scaled = (hidden * gain_ref[...].astype(jnp.float32)).astype(jnp.bfloat16)
-    query = jnp.dot(scaled, wq_ref[...], preferred_element_type=jnp.float32)
-    keyval = jnp.dot(scaled, wkv_ref[...], preferred_element_type=jnp.float32)
-    heads_local = wkv_ref.shape[1] // (2 * HD)
+    spread = interleave(scaled.astype(jnp.float32))
+    query = jnp.zeros((row_count, wq.shape[1]), jnp.float32)
+    keyval = jnp.zeros((heads_local * row_count, wkv.shape[2]), jnp.float32)
+    per_chunk = rows // HD
+    for i, (copy_q, copy_kv) in enumerate(zip(copies_q, copies_kv)):
+        copy_kv.wait()
+        for c in range(i * per_chunk, (i + 1) * per_chunk):
+            keyval += jnp.dot(
+                spread[c],
+                wkv[c * HD : (c + 1) * HD].reshape(heads_local * HD, wkv.shape[2]),
+                preferred_element_type=jnp.float32,
+            )
+        copy_q.wait()
+        query += jnp.dot(
+            scaled[:, i * rows : (i + 1) * rows],
+            wq[i * rows : (i + 1) * rows, :],
+            preferred_element_type=jnp.float32,
+        )
     me = lax.axis_index("seq")
 
     def write_pair(out_ref, pieces):
@@ -136,10 +192,8 @@
             pieces = [
                 query[steps, (l * QPK + h) * HD : (l * QPK + h + 1) * HD] for h in range(QPK)
             ]
-            pieces += [
-                keyval[steps, (l * 2 + h) * HD : (l * 2 + h + 1) * HD] for h in range(2)
-            ]
-            pieces += [square_rows, square_rows]
+            own = keyval[l * row_count + r * step_count : l * row_count + (r + 1) * step_count]
+            pieces += [own[:, :HD], own[:, HD:], square_rows, square_rows]
             if len(outs) == 1:
                 write_pair(outs[0].at[pair], pieces)
             else:
@@ -151,36 +205,49 @@
 
 def project(new_hidden, norm_gain, w_query, w_keyval, pair_count):
     requests, step_count, width = new_hidden.shape
+    rows = min(256, width)
+    chunks = width // rows
     block = ((QPK + 4) * step_count, HD)
     if is_direct(pair_count):
         shapes = [jax.ShapeDtypeStruct(block, jnp.float32)] * pair_count
     else:
         shapes = [jax.ShapeDtypeStruct((pair_count,) + block, jnp.float32)]
+    vmem = pl.BlockSpec(memory_space=pltpu.VMEM)
+    anywhere = pl.BlockSpec(memory_space=pl.ANY)
+    weights = w_query.size + w_keyval.size
     return pl.pallas_call(
-        project_kernel,
+        functools.partial(project_kernel, rows),
         out_shape=shapes,
-        in_specs=[pl.BlockSpec(memory_space=pltpu.VMEM)] * 4,
-        out_specs=[pl.BlockSpec(memory_space=pltpu.VMEM)] * len(shapes),
+        in_specs=[vmem, vmem, anywhere, anywhere],
+        out_specs=[vmem] * len(shapes),
+        scratch_shapes=[
+            pltpu.VMEM(w_query.shape, jnp.bfloat16),
+            pltpu.VMEM(w_keyval.shape, jnp.bfloat16),
+            pltpu.SemaphoreType.DMA((chunks,)),
+            pltpu.SemaphoreType.DMA((chunks,)),
+        ],
         compiler_params=pltpu.CompilerParams(vmem_limit_bytes=24 * 1024 * 1024),
         cost_estimate=pl.CostEstimate(
-            flops=2 * requests * step_count * width * (w_query.shape[1] + w_keyval.shape[1]),
-            bytes_accessed=2 * width * (w_query.shape[1] + w_keyval.shape[1]),
+            flops=2 * requests * step_count * weights,
+            bytes_accessed=2 * weights,
             transcendentals=0,
         ),
         name="project",
     )(
         new_hidden,
         norm_gain,
-        pltpu.with_memory_space_constraint(w_query, pltpu.VMEM),
-        pltpu.with_memory_space_constraint(w_keyval, pltpu.VMEM),
+        pltpu.with_memory_space_constraint(w_query, pltpu.HBM),
+        pltpu.with_memory_space_constraint(w_keyval, pltpu.HBM),
     )
 
 
 def attend_kernel(source_blocks, heads_local, seq_count, kept_ref, cos_ref, sin_ref, *refs):
-    arrivals = (len(refs) - 5) // 2
+    direct = is_direct(seq_count)
+    arrivals = seq_count if direct else 1
     blocks_refs, parts_refs = refs[:arrivals], refs[arrivals : 2 * arrivals]
-    cache_ref, attended_ref, kept, sem_in, sem_out = refs[2 * arrivals :]
-    kept_count = kept_ref.shape[2]
+    cache_ref, attended_ref, sem = refs[2 * arrivals : 2 * arrivals + 3]
+    kept = cache_ref.at[0, 0] if direct else refs[-1]
+    kept_count = kept_ref.shape[1]
     step_count = cos_ref.shape[0] // 2
     me = lax.axis_index("seq")
     request = lax.div(me, heads_local)
@@ -188,27 +255,27 @@
 
     def start_copy(k, carry):
         previous, slot = carry
-        source = lax.div(kept_ref[request, head, k], source_blocks)
+        source = lax.div(kept_ref[request, k, head], source_blocks)
         slot = jnp.where(source == previous, jnp.minimum(slot + 1, MOST - 1), 0)
-        rows = pl.ds(pl.multiple_of(k * BLK, BLK), BLK)
-        if arrivals == 1:
-            pltpu.make_async_copy(
-                blocks_refs[0].at[source, slot], kept.at[rows], sem_in
-            ).start()
+        target = kept.at[pl.ds(pl.multiple_of(k * BLK, BLK), BLK)]
+        if not direct:
+            pltpu.make_async_copy(blocks_refs[0].at[source, slot], target, sem).start()
         else:
             for offset, blocks_ref in enumerate(blocks_refs):
                 pl.when(jnp.bitwise_xor(me, offset) == source)(
-                    pltpu.make_async_copy(blocks_ref.at[slot], kept.at[rows], sem_in).start
+                    pltpu.make_async_copy(blocks_ref.at[slot], target, sem).start
                 )
         return source, slot
 
     lax.fori_loop(
         0, kept_count, start_copy, (jnp.int32(-1), jnp.int32(0)), unroll=kept_count <= 8
     )
-    if arrivals == 1:
+    if direct:
+        total = sum(ref[...] for ref in parts_refs)
+    else:
         total = jnp.sum(parts_refs[0][...], axis=0)
-    else:
-        total = sum(ref[...] for ref in parts_refs)
+        pltpu.make_async_copy(kept, kept, sem).wait()
+        pltpu.make_async_copy(kept, cache_ref.at[0, 0], sem).start()
     query_rows = QPK * step_count
     inverse = lax.rsqrt(total[query_rows + 2 * step_count :] * (1.0 / D) + EPS)
     cosine, sine = cos_ref[...], sin_ref[...]
@@ -219,71 +286,72 @@
     new_value = jnp.concatenate([keyval[step_count:], keyval[:step_count]], axis=0)
     new_value = new_value.astype(jnp.bfloat16)
     scale = 1.0 / math.sqrt(HD)
-    score_new = (
-        lax.dot_general(query, new_key, CONTRACT_LAST, preferred_element_type=jnp.float32) * scale
-    )
-    row = lax.broadcasted_iota(jnp.int32, score_new.shape, 0)
-    column = lax.broadcasted_iota(jnp.int32, score_new.shape, 1)
-    score_new = jnp.where(column <= lax.rem(row, step_count), score_new, -jnp.inf)
-
-    pltpu.make_async_copy(kept, kept, sem_in).wait()
-    out_copy = pltpu.make_async_copy(kept, cache_ref.at[0, 0], sem_out)
-    out_copy.start()
-    score_kept = (
-        lax.dot_general(query, kept[:, :HD], CONTRACT_LAST, preferred_element_type=jnp.float32)
-        * scale
-    )
-    row_max = jnp.maximum(
-        jnp.max(score_kept, axis=1, keepdims=True), jnp.max(score_new, axis=1, keepdims=True)
-    )
-    weight_kept = jnp.exp(score_kept - row_max)
-    weight_new = jnp.exp(score_new - row_max)
-    denominator = jnp.sum(weight_kept, axis=1, keepdims=True) + jnp.sum(
-        weight_new, axis=1, keepdims=True
-    )
-    numerator = jnp.dot(
-        weight_kept.astype(jnp.bfloat16), kept[:, HD:], preferred_element_type=jnp.float32
-    )
-    numerator += jnp.dot(
-        weight_new.astype(jnp.bfloat16), new_value, preferred_element_type=jnp.float32
-    )
+    score = lax.dot_general(query, new_key, CONTRACT_LAST, preferred_element_type=jnp.float32)
+    row = lax.broadcasted_iota(jnp.int32, score.shape, 0)
+    column = lax.broadcasted_iota(jnp.int32, score.shape, 1)
+    scores = [jnp.where(column <= lax.rem(row, step_count), score * scale, -jnp.inf)]
+    values = [new_value]
+    def add_block(block, filled):
+        score = lax.dot_general(
+            query, block[:, :HD], CONTRACT_LAST, preferred_element_type=jnp.float32
+        )
+        column = lax.broadcasted_iota(jnp.int32, score.shape, 1)
+        scores.append(jnp.where(column < filled * BLK, score * scale, -jnp.inf))
+        values.append(block[:, HD:])
+
+    if direct:
+        for offset, ref in enumerate(blocks_refs):
+            source = jnp.bitwise_xor(me, offset)
+            filled = jnp.int32(0)
+            for k in range(kept_count):
+                here = lax.div(kept_ref[request, k, head], source_blocks) == source
+                filled += here.astype(jnp.int32)
+            add_block(ref[...].reshape(MOST * BLK, 2 * HD), filled)
+    else:
+        add_block(kept[...], kept_count)
+    row_max = functools.reduce(
+        jnp.maximum, [jnp.max(score, axis=1, keepdims=True) for score in scores]
+    )
+    denominator = jnp.zeros((query_rows, 1), jnp.float32)
+    numerator = jnp.zeros((query_rows, HD), jnp.float32)
+    for score, value in zip(scores, values):
+        weight = jnp.exp(score - row_max)
+        denominator += jnp.sum(weight, axis=1, keepdims=True)
+        numerator += jnp.dot(
+            weight.astype(jnp.bfloat16), value, preferred_element_type=jnp.float32
+        )
     attended = (numerator / denominator).astype(jnp.bfloat16)
-    if arrivals == 1:
-        for i in range(attended_ref.shape[0]):
+    if direct:
+        attended_ref[...] = attended
+    else:
+        for i in range(seq_count):
             attended_ref[i] = attended
-    else:
-        attended_ref[...] = attended
-    out_copy.wait()
+    pltpu.make_async_copy(cache_ref, cache_ref, sem).wait()
 
 
 def attend(kept_blocks, blocks, parts, source_blocks, heads_local, step_count, seq_count):
-    kept_count = kept_blocks.shape[2]
+    kept_count = kept_blocks.shape[1]
     row_width = blocks[0].shape[-1]
     cosine, sine = rope_tables(source_blocks * BLK * seq_count, step_count)
     shape = (QPK * step_count, HD)
     if len(blocks) == 1:
         shape = (seq_count,) + shape
     vmem = pl.BlockSpec(memory_space=pltpu.VMEM)
-    anywhere = pl.BlockSpec(memory_space=pl.ANY)
     kept_cache, attended = pl.pallas_call(
         functools.partial(attend_kernel, source_blocks, heads_local, seq_count),
         out_shape=(
             jax.ShapeDtypeStruct((1, 1, kept_count * BLK, row_width), jnp.bfloat16),
             jax.ShapeDtypeStruct(shape, jnp.bfloat16),
         ),
-        in_specs=[pl.BlockSpec(memory_space=pltpu.SMEM), vmem, vmem]
-        + [anywhere] * len(blocks)
-        + [vmem] * len(parts),
-        out_specs=(anywhere, vmem),
-        scratch_shapes=[
-            pltpu.VMEM((kept_count * BLK, row_width), jnp.bfloat16),
-            pltpu.SemaphoreType.DMA,
-            pltpu.SemaphoreType.DMA,
-        ],
+        in_specs=[pl.BlockSpec(memory_space=pltpu.SMEM)]
+        + [vmem] * (2 + len(blocks) + len(parts)),
+        out_specs=(pl.BlockSpec(memory_space=pl.ANY), vmem),
+        scratch_shapes=[pltpu.SemaphoreType.DMA]
+        + ([pltpu.VMEM((kept_count * BLK, row_width), jnp.bfloat16)] if len(blocks) == 1 else []),
         compiler_params=pltpu.CompilerParams(vmem_limit_bytes=24 * 1024 * 1024),
         name="attend",
     )(kept_blocks, jnp.asarray(cosine), jnp.asarray(sine), *blocks, *parts)
-    return kept_cache, [attended] * len(blocks) if len(blocks) == 1 else [attended] * seq_count
+    return kept_cache, [attended] * (1 if len(blocks) == 1 else seq_count)
 
 
 def output_kernel(heads_local, w_ref, *refs):
@@ -347,10 +415,9 @@
     _, step_count, width = new_hidden.shape
     pair_count = requests * heads_local
 
+    kept_blocks = kept_blocks.transpose(0, 2, 1)
     blocks = exchange(pick(kept_blocks, source_cache), "seq")
-    parts = project(
-        new_hidden, norm_gain.reshape(1, width), w_query, w_keyval.reshape(width, -1), pair_count
-    )
+    parts = project(new_hidden, norm_gain.reshape(1, width), w_query, w_keyval, pair_count)
     parts = exchange(parts, "seq")
     kept_cache, attended = attend(
         kept_blocks, blocks, parts, source_tokens // BLK, heads_local, step_count, seq_count

time: 46.4 us -> 42.8 us (0.922)
  local copies, waits for them, and re-layouts: 8.91 us -> 2.33 us
  Pallas kernels: 6.24 us -> 9.44 us
    unnamed x16 -> x14, local copies, waits for them, and re-layouts: 8.19 us -> 1.61 us
    pallas_call x1, Pallas kernels: 1.48 us -> 4.54 us  [project(): pl.pallas_call(functools.partial(project_kernel, rows), out_shape=shapes,...]
    pallas_call x1, Pallas kernels: 1.52 us -> 2.09 us  [pick(): pl.pallas_call(pick_kernel, out_shape=shapes, in_specs=[pl.BlockSpec(memo...]
  transfers between devices with their start and end apart: 12 -> 12, of which waited for: 5 -> 5; matrix products, arithmetic and copies ran while one was open for 6% -> 2% of each run, Pallas kernels for 3% -> 11%
where the time goes in v3:
time: 42.8 us; the launch traced here: 42.5 us
  starting transfers between devices  19.8 us (46%)
  waiting for transfers between devices  9.58 us (22%)
  Pallas kernels  9.44 us (22%)
  local copies, waits for them, and re-layouts  2.33 us (5%)
  between operations  0.73 us (2%)
  other arithmetic  0.65 us (2%)
    ppermute x12, starting transfers between devices, exchange(): lax.ppermute(outgoing[k], axis, [(i, i ^ k) for i in range(count)])  19.8 us
    ppermute x12, waiting for transfers between devices, exchange(): lax.ppermute(outgoing[k], axis, [(i, i ^ k) for i in range(count)])  9.58 us
    pallas_call x1, Pallas kernels, project(): pl.pallas_call(functools.partial(project_kernel, rows), out_shape=shapes,...  4.54 us
    pallas_call x1, Pallas kernels, pick(): pl.pallas_call(pick_kernel, out_shape=shapes, in_specs=[pl.BlockSpec(memo...  2.09 us
    pallas_call x1, Pallas kernels, attend(): pl.pallas_call(functools.partial(attend_kernel, source_blocks, heads_loca...  1.62 us
    unnamed x14, local copies, waits for them, and re-layouts  1.61 us
    pallas_call x1, Pallas kernels, output(): pl.pallas_call(functools.partial(output_kernel, heads_local), out_shape=j...  1.19 us
  transfers between devices with their start and end apart: 12, of which 5 were waited for; matrix products, arithmetic and copies ran while one was open for 2% of the time, Pallas kernels for 11%

profile of v3, /device:TPU:0, one launch (start us, length us, event | category | flops | bytes accessed | tf_op | source)
XLA Modules:
  0.0 42.5 jit_solution(5485095921150274639)
XLA Ops:
  0.6 0.0 copy-start.3
  0.7 0.8 %copy-done.3 = s32[2,8,4]{1,2,0:T(4,128)S(1)} copy-done((s32[2,8,4]{1,2,0:T(4,128)S(1)}, s32[2,8,4]{1,2,0:T(4,128)}, u32[]{:S(2)}) %copy-start.3) | copy-done | bytes 280
  1.5 2.1 %pick_blocks.1 = (bf16[2,128,256]{2,1,0:T(8,128)(2,1)S(1)}, bf16[2,128,256]{2,1,0:T(8,128)(2,1)S(1)}, bf16[2,128,256]{2,1,0:T(8,128)(2,1)S(1)}, bf16[2,128,256]{2,1,0:T(8,128)(2,1)S(1)}) custom-call(s32[2,4,8]{2,1,0:T(4,128)S(1)} %bitcast.1, bf16[2,2,512,256]{3,2,1,0:T(8,128)(2,1)} %cache_ref.1), custom_call_target="tpu_custom_call" | custom-call | tf_op jit(solution)/shard_map/pick_blocks/pallas_call | solution.py:101
  3.6 3.1 %collective-permute-start = (bf16[2,128,256]{2,1,0:T(8,128)(2,1)S(1)}, bf16[2,128,256]{2,1,0:T(8,128)(2,1)S(1)}, u32[]{:S(2)}, u32[]{:S(2)}) collective-permute-start(bf16[2,128,256]{2,1,0:T(8,128)(2,1)S(1)} %get-tuple-element.13), channel_id=1, source_target_pairs={{0,4},{4,0},{8,12},{12,8},{1,5},{5,1},{9,13},{13,9},{2,6},{6,2},{1... | collective-permute-start | bytes 393224 | tf_op jit(solution)/shard_map/ppermute | solution.py:46
  6.7 2.6 %collective-permute-start.1 = (bf16[2,128,256]{2,1,0:T(8,128)(2,1)S(1)}, bf16[2,128,256]{2,1,0:T(8,128)(2,1)S(1)}, u32[]{:S(2)}, u32[]{:S(2)}) collective-permute-start(bf16[2,128,256]{2,1,0:T(8,128)(2,1)S(1)} %get-tuple-element.14), channel_id=1, source_target_pairs={{0,8},{4,12},{8,0},{12,4},{1,9},{5,13},{9,1},{13,5},{2,10},{6,14},... | collective-permute-start | bytes 393224 | tf_op jit(solution)/shard_map/ppermute | solution.py:46
  9.3 0.7 %reshape.10.gain_ref = bf16[1,2048]{1,0:T(2,128)(2,1)S(1)} reshape(bf16[2048]{0:T(1024)(128)(2,1)} %param.12) | data formatting | bytes 8192 | tf_op jit(solution)/shard_map/reshape | solution.py:420
  10.0 0.8 %copy-done.1 = bf16[2,4,2048]{2,1,0:T(4,128)(2,1)S(1)} copy-done((bf16[2,4,2048]{2,1,0:T(4,128)(2,1)S(1)}, bf16[2,4,2048]{2,1,0:T(4,128)(2,1)}, u32[]{:S(2)}) %copy-start.1) | copy-done | bytes 32792
  10.7 4.5 %project.1 = (f32[48,128]{1,0:T(8,128)S(1)}, f32[48,128]{1,0:T(8,128)S(1)}, f32[48,128]{1,0:T(8,128)S(1)}, f32[48,128]{1,0:T(8,128)S(1)}) custom-call(bf16[2,4,2048]{2,1,0:T(4,128)(2,1)S(1)} %copy-done.1, bf16[1,2048]{1,0:T(2,128)(2,1)S(1)} %reshape.10.gain_ref, bf16[2048,2048]{1,0:T(8,128)(2,1)} %wq_ref.1, bf16[2048,2,256]{2,1,0:T(2,128)(2,1)} %wkv_ref.1), custom_call_target="tpu_custom_call" | custom-call | flops 83886080 | bytes 10485760 | tf_op jit(solution)/shard_map/project/pallas_call | solution.py:218
  15.3 1.0 %collective-permute-start.3 = (f32[48,128]{1,0:T(8,128)S(1)}, f32[48,128]{1,0:T(8,128)S(1)}, u32[]{:S(2)}, u32[]{:S(2)}) collective-permute-start(f32[48,128]{1,0:T(8,128)S(1)} %get-tuple-element.17), channel_id=1, source_target_pairs={{0,4},{4,0},{8,12},{12,8},{1,5},{5,1},{9,13},{13,9},{2,6},{6,2},{1... | collective-permute-start | bytes 73736 | tf_op jit(solution)/shard_map/ppermute | solution.py:46
  16.2 3.5 %collective-permute-start.4 = (f32[48,128]{1,0:T(8,128)S(1)}, f32[48,128]{1,0:T(8,128)S(1)}, u32[]{:S(2)}, u32[]{:S(2)}) collective-permute-start(f32[48,128]{1,0:T(8,128)S(1)} %get-tuple-element.18), channel_id=1, source_target_pairs={{0,8},{4,12},{8,0},{12,4},{1,9},{5,13},{9,1},{13,5},{2,10},{6,14},... | collective-permute-start | bytes 73736 | tf_op jit(solution)/shard_map/ppermute | solution.py:46
  19.7 3.3 %collective-permute-start.5 = (f32[48,128]{1,0:T(8,128)S(1)}, f32[48,128]{1,0:T(8,128)S(1)}, u32[]{:S(2)}, u32[]{:S(2)}) collective-permute-start(f32[48,128]{1,0:T(8,128)S(1)} %get-tuple-element.19), channel_id=1, source_target_pairs={{0,12},{4,8},{8,4},{12,0},{1,13},{5,9},{9,5},{13,1},{2,14},{6,10},... | collective-permute-start | bytes 73736 | tf_op jit(solution)/shard_map/ppermute | solution.py:46
  23.0 0.0 collective-permute-done.4.refs_6_
  23.0 2.4 %collective-permute-done.5.refs_7_ = f32[48,128]{1,0:T(8,128)S(1)} collective-permute-done((f32[48,128]{1,0:T(8,128)S(1)}, f32[48,128]{1,0:T(8,128)S(1)}, u32[]{:S(2)}, u32[]{:S(2)}) %collective-permute-start.5) | collective-permute-done | bytes 24608 | tf_op jit(solution)/shard_map/ppermute | solution.py:46
  25.4 1.6 %attend.1 = (bf16[1,1,512,256]{3,2,1,0:T(8,128)(2,1)}, bf16[32,128]{1,0:T(8,128)(2,1)S(1)}) custom-call(s32[2,4,8]{2,1,0:T(4,128)S(1)} %bitcast.2, f32[8,128]{1,0:T(8,128)S(1)} %copy-done.6, f32[8,128]{1,0:T(8,128)S(1)} %copy-done.5, bf16[2,128,256]{2,1,0:T(8,128)(2,1)S(1)} %get-tuple-element.12.refs_0_, ...), custom_call_target="tpu_custom_call" | custom-call | tf_op jit(solution)/shard_map/attend/pallas_call | solution.py:340
  27.0 3.2 %collective-permute-start.8 = (bf16[32,128]{1,0:T(8,128)(2,1)S(1)}, bf16[32,128]{1,0:T(8,128)(2,1)S(1)}, u32[]{:S(2)}, u32[]{:S(2)}) collective-permute-start(bf16[32,128]{1,0:T(8,128)(2,1)S(1)} %get-tuple-element.21.refs_0_), channel_id=1, source_target_pairs={{0,12},{4,8},{8,4},{12,0},{1,13},{5,9},{9,5},{13,1},{2,14},{6,10},... | collective-permute-start | bytes 24584 | tf_op jit(solution)/shard_map/ppermute | solution.py:46
  30.2 1.3 %collective-permute-start.6 = (bf16[32,128]{1,0:T(8,128)(2,1)S(1)}, bf16[32,128]{1,0:T(8,128)(2,1)S(1)}, u32[]{:S(2)}, u32[]{:S(2)}) collective-permute-start(bf16[32,128]{1,0:T(8,128)(2,1)S(1)} %get-tuple-element.21.refs_0_), channel_id=1, source_target_pairs={{0,4},{4,0},{8,12},{12,8},{1,5},{5,1},{9,13},{13,9},{2,6},{6,2},{1... | collective-permute-start | bytes 24584 | tf_op jit(solution)/shard_map/ppermute | solution.py:46
  31.5 1.1 %collective-permute-done.8.refs_3_ = bf16[32,128]{1,0:T(8,128)(2,1)S(1)} collective-permute-done((bf16[32,128]{1,0:T(8,128)(2,1)S(1)}, bf16[32,128]{1,0:T(8,128)(2,1)S(1)}, u32[]{:S(2)}, u32[]{:S(2)}) %collective-permute-start.8) | collective-permute-done | bytes 8224 | tf_op jit(solution)/shard_map/ppermute | solution.py:46
  32.6 2.2 %collective-permute-done.7.refs_2_ = bf16[32,128]{1,0:T(8,128)(2,1)S(1)} collective-permute-done((bf16[32,128]{1,0:T(8,128)(2,1)S(1)}, bf16[32,128]{1,0:T(8,128)(2,1)S(1)}, u32[]{:S(2)}, u32[]{:S(2)}) %collective-permute-start.7) | collective-permute-done | bytes 8224 | tf_op jit(solution)/shard_map/ppermute | solution.py:46
  34.8 1.2 %output_projection.1 = f32[8,2048]{1,0:T(8,128)S(1)} custom-call(bf16[2048,2048]{1,0:T(8,128)(2,1)S(1)} %copy-done, bf16[32,128]{1,0:T(8,128)(2,1)S(1)} %get-tuple-element.21.refs_0_, bf16[32,128]{1,0:T(8,128)(2,1)S(1)} %collective-permute-done.6.refs_1_, bf16[32,128]{1,0:T(8,128)(2,1)S(1)} %collective-permute-done.7.refs_2_, ...), custom_call_target="tpu_custom_call" | custom-call | tf_op jit(solution)/shard_map/output_projection/pallas_call | solution.py:400
  36.0 1.5 %collective-permute-start.10 = (f32[8,2048]{1,0:T(8,128)S(1)}, f32[8,2048]{1,0:T(8,128)S(1)}, u32[]{:S(2)}, u32[]{:S(2)}) collective-permute-start(f32[8,2048]{1,0:T(8,128)S(1)} %output_projection.1), channel_id=1, source_target_pairs={{0,2},{1,3},{2,0},{3,1},{4,6},{5,7},{6,4},{7,5},{8,10},{9,11},{10,... | collective-permute-start | bytes 196616 | tf_op jit(solution)/shard_map/ppermute | solution.py:46
  37.5 0.3 collective-permute-start.9
  37.8 2.5 %collective-permute-done.11 = f32[8,2048]{1,0:T(8,128)S(1)} collective-permute-done((f32[8,2048]{1,0:T(8,128)S(1)}, f32[8,2048]{1,0:T(8,128)S(1)}, u32[]{:S(2)}, u32[]{:S(2)}) %collective-permute-start.11) | collective-permute-done | bytes 65568 | tf_op jit(solution)/shard_map/ppermute | solution.py:46
  40.3 1.4 %collective-permute-done.10 = f32[8,2048]{1,0:T(8,128)S(1)} collective-permute-done((f32[8,2048]{1,0:T(8,128)S(1)}, f32[8,2048]{1,0:T(8,128)S(1)}, u32[]{:S(2)}, u32[]{:S(2)}) %collective-permute-start.10) | collective-permute-done | bytes 65568 | tf_op jit(solution)/shard_map/ppermute | solution.py:46
  41.8 0.6 %add_convert_fusion = bf16[2,4,2048]{2,1,0:T(4,128)(2,1)} fusion(f32[2,4,2048]{2,1,0:T(4,128)S(1)} %reshape.11, bf16[2,4,2048]{2,1,0:T(4,128)(2,1)S(1)} %copy-done.2), kind=kLoop, calls=%fused_computation | loop fusion | flops 49152 | bytes 131072 | tf_op jit(solution)/shard_map/convert_element_type | solution.py:434
  (22 shorter events, 0.1 us)
Async XLA Ops:
  0.6 34.1 %copy-start = (bf16[2048,2048]{1,0:T(8,128)(2,1)S(1)}, bf16[2048,2048]{1,0:T(8,128)(2,1)}, u32[]{:S(2)}) copy-start(bf16[2048,2048]{1,0:T(8,128)(2,1)} %w_ref.1) | copy-start | bytes 25165828
  0.6 0.8 %copy-start.3 = (s32[2,8,4]{1,2,0:T(4,128)S(1)}, s32[2,8,4]{1,2,0:T(4,128)}, u32[]{:S(2)}) copy-start(s32[2,8,4]{1,2,0:T(4,128)} %param.10) | copy-start | bytes 772
  3.6 21.8 %collective-permute-start = (bf16[2,128,256]{2,1,0:T(8,128)(2,1)S(1)}, bf16[2,128,256]{2,1,0:T(8,128)(2,1)S(1)}, u32[]{:S(2)}, u32[]{:S(2)}) collective-permute-start(bf16[2,128,256]{2,1,0:T(8,128)(2,1)S(1)} %get-tuple-element.13), channel_id=1, source_target_pairs={{0,4},{4,0},{8,12},{12,8},{1,5},{5,1},{9,13},{13,9},{2,6},{6,2},{1... | collective-permute-start | bytes 393224 | tf_op jit(solution)/shard_map/ppermute | solution.py:46
  6.7 18.7 %collective-permute-start.1 = (bf16[2,128,256]{2,1,0:T(8,128)(2,1)S(1)}, bf16[2,128,256]{2,1,0:T(8,128)(2,1)S(1)}, u32[]{:S(2)}, u32[]{:S(2)}) collective-permute-start(bf16[2,128,256]{2,1,0:T(8,128)(2,1)S(1)} %get-tuple-element.14), channel_id=1, source_target_pairs={{0,8},{4,12},{8,0},{12,4},{1,9},{5,13},{9,1},{13,5},{2,10},{6,14},... | collective-permute-start | bytes 393224 | tf_op jit(solution)/shard_map/ppermute | solution.py:46
  9.3 16.1 %collective-permute-start.2 = (bf16[2,128,256]{2,1,0:T(8,128)(2,1)S(1)}, bf16[2,128,256]{2,1,0:T(8,128)(2,1)S(1)}, u32[]{:S(2)}, u32[]{:S(2)}) collective-permute-start(bf16[2,128,256]{2,1,0:T(8,128)(2,1)S(1)} %get-tuple-element.15), channel_id=1, source_target_pairs={{0,12},{4,8},{8,4},{12,0},{1,13},{5,9},{9,5},{13,1},{2,14},{6,10},... | collective-permute-start | bytes 393224 | tf_op jit(solution)/shard_map/ppermute | solution.py:46
  10.0 0.8 %copy-start.1 = (bf16[2,4,2048]{2,1,0:T(4,128)(2,1)S(1)}, bf16[2,4,2048]{2,1,0:T(4,128)(2,1)}, u32[]{:S(2)}) copy-start(bf16[2,4,2048]{2,1,0:T(4,128)(2,1)} %hidden_ref.1) | copy-start | bytes 98308
  10.7 14.7 %copy-start.4 = (s32[2,8,4]{1,2,0:T(4,128)S(1)}, s32[2,8,4]{1,2,0:T(4,128)}, u32[]{:S(2)}) copy-start(s32[2,8,4]{1,2,0:T(4,128)} %param.10) | copy-start | bytes 772
  10.7 14.7 %copy-start.5 = (f32[8,128]{1,0:T(8,128)S(1)}, f32[8,128]{1,0:T(8,128)}, u32[]{:S(2)}) copy-start(f32[8,128]{1,0:T(8,128)} %constant.5.clone.sin_ref) | copy-start | bytes 12292
  10.7 14.7 %copy-start.6 = (f32[8,128]{1,0:T(8,128)S(1)}, f32[8,128]{1,0:T(8,128)}, u32[]{:S(2)}) copy-start(f32[8,128]{1,0:T(8,128)} %constant.4.clone.cos_ref) | copy-start | bytes 12292
  10.7 31.1 %copy-start.2 = (bf16[2,4,2048]{2,1,0:T(4,128)(2,1)S(1)}, bf16[2,4,2048]{2,1,0:T(4,128)(2,1)}, u32[]{:S(2)}) copy-start(bf16[2,4,2048]{2,1,0:T(4,128)(2,1)} %hidden_ref.1) | copy-start | bytes 98308
  15.3 4.5 %collective-permute-start.3 = (f32[48,128]{1,0:T(8,128)S(1)}, f32[48,128]{1,0:T(8,128)S(1)}, u32[]{:S(2)}, u32[]{:S(2)}) collective-permute-start(f32[48,128]{1,0:T(8,128)S(1)} %get-tuple-element.17), channel_id=1, source_target_pairs={{0,4},{4,0},{8,12},{12,8},{1,5},{5,1},{9,13},{13,9},{2,6},{6,2},{1... | collective-permute-start | bytes 73736 | tf_op jit(solution)/shard_map/ppermute | solution.py:46
  16.2 6.8 %collective-permute-start.4 = (f32[48,128]{1,0:T(8,128)S(1)}, f32[48,128]{1,0:T(8,128)S(1)}, u32[]{:S(2)}, u32[]{:S(2)}) collective-permute-start(f32[48,128]{1,0:T(8,128)S(1)} %get-tuple-element.18), channel_id=1, source_target_pairs={{0,8},{4,12},{8,0},{12,4},{1,9},{5,13},{9,1},{13,5},{2,10},{6,14},... | collective-permute-start | bytes 73736 | tf_op jit(solution)/shard_map/ppermute | solution.py:46
  19.7 5.6 %collective-permute-start.5 = (f32[48,128]{1,0:T(8,128)S(1)}, f32[48,128]{1,0:T(8,128)S(1)}, u32[]{:S(2)}, u32[]{:S(2)}) collective-permute-start(f32[48,128]{1,0:T(8,128)S(1)} %get-tuple-element.19), channel_id=1, source_target_pairs={{0,12},{4,8},{8,4},{12,0},{1,13},{5,9},{9,5},{13,1},{2,14},{6,10},... | collective-permute-start | bytes 73736 | tf_op jit(solution)/shard_map/ppermute | solution.py:46
  27.0 5.5 %collective-permute-start.8 = (bf16[32,128]{1,0:T(8,128)(2,1)S(1)}, bf16[32,128]{1,0:T(8,128)(2,1)S(1)}, u32[]{:S(2)}, u32[]{:S(2)}) collective-permute-start(bf16[32,128]{1,0:T(8,128)(2,1)S(1)} %get-tuple-element.21.refs_0_), channel_id=1, source_target_pairs={{0,12},{4,8},{8,4},{12,0},{1,13},{5,9},{9,5},{13,1},{2,14},{6,10},... | collective-permute-start | bytes 24584 | tf_op jit(solution)/shard_map/ppermute | solution.py:46
  30.2 4.5 %collective-permute-start.7 = (bf16[32,128]{1,0:T(8,128)(2,1)S(1)}, bf16[32,128]{1,0:T(8,128)(2,1)S(1)}, u32[]{:S(2)}, u32[]{:S(2)}) collective-permute-start(bf16[32,128]{1,0:T(8,128)(2,1)S(1)} %get-tuple-element.21.refs_0_), channel_id=1, source_target_pairs={{0,8},{4,12},{8,0},{12,4},{1,9},{5,13},{9,1},{13,5},{2,10},{6,14},... | collective-permute-start | bytes 24584 | tf_op jit(solution)/shard_map/ppermute | solution.py:46
  30.2 4.5 %collective-permute-start.6 = (bf16[32,128]{1,0:T(8,128)(2,1)S(1)}, bf16[32,128]{1,0:T(8,128)(2,1)S(1)}, u32[]{:S(2)}, u32[]{:S(2)}) collective-permute-start(bf16[32,128]{1,0:T(8,128)(2,1)S(1)} %get-tuple-element.21.refs_0_), channel_id=1, source_target_pairs={{0,4},{4,0},{8,12},{12,8},{1,5},{5,1},{9,13},{13,9},{2,6},{6,2},{1... | collective-permute-start | bytes 24584 | tf_op jit(solution)/shard_map/ppermute | solution.py:46
  36.0 4.4 %collective-permute-start.11 = (f32[8,2048]{1,0:T(8,128)S(1)}, f32[8,2048]{1,0:T(8,128)S(1)}, u32[]{:S(2)}, u32[]{:S(2)}) collective-permute-start(f32[8,2048]{1,0:T(8,128)S(1)} %output_projection.1), channel_id=1, source_target_pairs={{0,3},{1,2},{2,1},{3,0},{4,7},{5,6},{6,5},{7,4},{8,11},{9,10},{10,... | collective-permute-start | bytes 196616 | tf_op jit(solution)/shard_map/ppermute | solution.py:46
  36.0 5.8 %collective-permute-start.10 = (f32[8,2048]{1,0:T(8,128)S(1)}, f32[8,2048]{1,0:T(8,128)S(1)}, u32[]{:S(2)}, u32[]{:S(2)}) collective-permute-start(f32[8,2048]{1,0:T(8,128)S(1)} %output_projection.1), channel_id=1, source_target_pairs={{0,2},{1,3},{2,0},{3,1},{4,6},{5,7},{6,4},{7,5},{8,10},{9,11},{10,... | collective-permute-start | bytes 196616 | tf_op jit(solution)/shard_map/ppermute | solution.py:46
  37.5 4.3 %collective-permute-start.9 = (f32[8,2048]{1,0:T(8,128)S(1)}, f32[8,2048]{1,0:T(8,128)S(1)}, u32[]{:S(2)}, u32[]{:S(2)}) collective-permute-start(f32[8,2048]{1,0:T(8,128)S(1)} %output_projection.1), channel_id=1, source_target_pairs={{0,1},{1,0},{2,3},{3,2},{4,5},{5,4},{6,7},{7,6},{8,9},{9,8},{10,11... | collective-permute-start | bytes 196616 | tf_op jit(solution)/shard_map/ppermute | solution.py:46

commit v4 on v3

v4 whole, which is shorter than its diff:
```python
import functools
import math

import jax
import jax.numpy as jnp
import numpy as np
from jax import lax
from jax.experimental import pallas as pl
from jax.experimental.pallas import tpu as pltpu
from jax.sharding import PartitionSpec as P

D = 8192
HD = 128
QPK = 8
BLK = 128
MOST = 2
ROPE_BASE = 500000.0
EPS = 1e-05

CONTRACT_LAST = (((1,), (1,)), ((), ()))


def rope_tables(prompt_length, step_count):
    positions = prompt_length + np.arange(2 * step_count) % step_count
    frequency = ROPE_BASE ** (-np.arange(HD // 2, dtype=np.float64) * 2.0 / HD)
    angles = positions[:, None] * frequency[None, :]
    cosine = np.concatenate([np.cos(angles)] * 2, axis=1)
    sine = np.concatenate([-np.sin(angles), np.sin(angles)], axis=1)
    return cosine.astype(np.float32), sine.astype(np.float32)


def rotate(v, cosine, sine):
    swapped = jnp.concatenate([v[..., HD // 2 :], v[..., : HD // 2]], axis=-1)
    return v * cosine + swapped * sine


def is_direct(count):
    return count <= 4 and count & (count - 1) == 0


def swap(outgoing, axis, offset):
    count = lax.axis_size(axis)
    return lax.ppermute(outgoing, axis, [(i, i ^ offset) for i in range(count)])


def all_to_all(outgoing, axis):
    return lax.all_to_all(outgoing, axis, split_axis=0, concat_axis=0, tiled=True)


def start_picks(kept_ref, cache_ref, pair, out_ref, sem):
    _, heads_local, source_tokens, _ = cache_ref.shape
    source_blocks = source_tokens // BLK
    kept_count = kept_ref.shape[1]
    me = lax.axis_index("seq")
    request = lax.div(pair, heads_local)
    local = lax.rem(pair, heads_local)
    head = lax.axis_index("head") * heads_local + local

    def count(k, total):
        block = kept_ref[request, k, head]
        return total + (block < me * source_blocks).astype(jnp.int32)

    start = lax.fori_loop(0, kept_count, count, jnp.int32(0), unroll=kept_count <= 8)
    for slot in range(MOST):
        rank = jnp.minimum(start + slot, kept_count - 1)
        block = kept_ref[request, rank, head] - me * source_blocks
        block = jnp.clip(block, 0, source_blocks - 1)
        rows = pl.ds(pl.multiple_of(block * BLK, BLK), BLK)
        pltpu.make_async_copy(
            cache_ref.at[request, local, rows], out_ref.at[pl.ds(slot * BLK, BLK)], sem
        ).start()


def pick_kernel(offsets, kept_ref, cache_ref, *refs):
    outs, sem = refs[:-1], refs[-1]
    if offsets:
        me = lax.axis_index("seq")
        for offset, out_ref in zip(offsets, outs):
            start_picks(kept_ref, cache_ref, jnp.bitwise_xor(me, offset), out_ref, sem)
    else:

        def pair_body(pair, carry):
            start_picks(kept_ref, cache_ref, pair, outs[0].at[pair], sem)
            return carry

        lax.fori_loop(0, outs[0].shape[0], pair_body, 0)
    for out_ref in outs:
        pltpu.make_async_copy(out_ref, out_ref, sem).wait()


def pick(kept_blocks, source_cache, offsets):
    requests, heads_local, _, row_width = source_cache.shape
    block = (MOST * BLK, row_width)
    if offsets:
        shapes = [jax.ShapeDtypeStruct(block, jnp.bfloat16)] * len(offsets)
    else:
        shapes = [jax.ShapeDtypeStruct((requests * heads_local,) + block, jnp.bfloat16)]
    return pl.pallas_call(
        functools.partial(pick_kernel, offsets),
        out_shape=shapes,
        in_specs=[
            pl.BlockSpec(memory_space=pltpu.SMEM),
            pl.BlockSpec(memory_space=pl.ANY),
        ],
        out_specs=[pl.BlockSpec(memory_space=pltpu.VMEM)] * len(shapes),
        scratch_shapes=[pltpu.SemaphoreType.DMA],
        compiler_params=pltpu.CompilerParams(vmem_limit_bytes=8 * 1024 * 1024),
        cost_estimate=pl.CostEstimate(flops=10**10, bytes_accessed=0, transcendentals=0),
        name="pick_blocks",
    )(kept_blocks, pltpu.with_memory_space_constraint(source_cache, pltpu.HBM))


def interleave(rows):
    count, width = rows.shape
    chunks = width // HD
    stacked = jnp.concatenate(
        [rows[:, c * HD : (c + 1) * HD] for c in range(chunks)], axis=0
    ).astype(jnp.bfloat16)
    source = lax.broadcasted_iota(jnp.int32, (HD, 4 * HD), 0)
    target = lax.broadcasted_iota(jnp.int32, (HD, 4 * HD), 1)
    place = jnp.where(target < 2 * HD, 2 * source, 2 * source + 1 + 2 * HD)
    spread = (place == target).astype(jnp.bfloat16)
    wide = jnp.dot(stacked, spread, preferred_element_type=jnp.float32)
    return [
        jnp.concatenate(
            [
                wide[c * count : (c + 1) * count, : 2 * HD],
                wide[c * count : (c + 1) * count, 2 * HD :],
            ],
            axis=0,
        ).astype(jnp.bfloat16)
        for c in range(chunks)
    ]


def project_kernel(direct, after_ref, hidden_ref, gain_ref, wq_ref, wkv_ref, *outs):
    del after_ref
    requests, step_count, width = hidden_ref.shape
    heads_local = wkv_ref.shape[1]
    row_count = requests * step_count
    me = lax.axis_index("seq")
    hidden = jnp.concatenate(
        [hidden_ref[r].astype(jnp.float32) for r in range(requests)], axis=0
    )
    square = jnp.sum(hidden * hidden, axis=1, keepdims=True)
    gain = gain_ref[...].astype(jnp.float32)
    scaled = jnp.concatenate(
        [hidden[:, c * HD : (c + 1) * HD] * gain[c : c + 1] for c in range(width // HD)], axis=1
    ).astype(jnp.bfloat16)
    query = jnp.dot(scaled, wq_ref[...], preferred_element_type=jnp.float32)
    keyval = jnp.zeros((heads_local * row_count, wkv_ref.shape[2]), jnp.float32)
    for c, spread in enumerate(interleave(scaled.astype(jnp.float32))):
        alternate = wkv_ref[c * HD : (c + 1) * HD].reshape(heads_local * HD, wkv_ref.shape[2])
        keyval += jnp.dot(spread, alternate, preferred_element_type=jnp.float32)

    def pieces_of(r, l):
        steps = slice(r * step_count, (r + 1) * step_count)
        square_rows = jnp.broadcast_to(square[steps], (step_count, HD))
        own = keyval[l * row_count + r * step_count : l * row_count + (r + 1) * step_count]
        heads = [query[steps, (l * QPK + h) * HD : (l * QPK + h + 1) * HD] for h in range(QPK)]
        return heads + [own[:, :HD], own[:, HD:], square_rows, square_rows]

    def write_pair(out_ref, pieces):
        for j, piece in enumerate(pieces):
            out_ref[j * step_count : (j + 1) * step_count, :] = piece

    for r in range(requests):
        for l in range(heads_local):
            pair = r * heads_local + l
            pieces = pieces_of(r, l)
            if not direct:
                write_pair(outs[0].at[pair], pieces)
                continue
            for offset, out_ref in enumerate(outs):
                pl.when(jnp.bitwise_xor(me, offset) == pair)(
                    functools.partial(write_pair, out_ref, pieces)
                )


def project(after, new_hidden, norm_gain, w_query, w_keyval, pair_count, direct):
    requests, step_count, width = new_hidden.shape
    terms = ((QPK + 4) * step_count, HD)
    if direct:
        shapes = [jax.ShapeDtypeStruct(terms, jnp.float32)] * pair_count
    else:
        shapes = [jax.ShapeDtypeStruct((pair_count,) + terms, jnp.float32)]
    vmem = pl.BlockSpec(memory_space=pltpu.VMEM)
    weights = w_query.size + w_keyval.size
    return pl.pallas_call(
        functools.partial(project_kernel, direct),
        out_shape=shapes,
        in_specs=[pl.BlockSpec(memory_space=pl.ANY), vmem, vmem, vmem, vmem],
        out_specs=[vmem] * len(shapes),
        compiler_params=pltpu.CompilerParams(vmem_limit_bytes=8 * 1024 * 1024),
        cost_estimate=pl.CostEstimate(
            flops=2 * requests * step_count * weights,
            bytes_accessed=2 * weights,
            transcendentals=0,
        ),
        name="project",
    )(
        after,
        new_hidden,
        norm_gain.reshape(width // HD, HD),
        pltpu.with_memory_space_constraint(w_query, pltpu.VMEM),
        pltpu.with_memory_space_constraint(w_keyval, pltpu.VMEM),
    )


def attend_kernel(direct, source_blocks, heads_local, kept_ref, cos_ref, sin_ref, *refs):
    kept_count = kept_ref.shape[1]
    step_count = cos_ref.shape[0] // 2
    me = lax.axis_index("seq")
    request = lax.div(me, heads_local)
    head = lax.axis_index("head") * heads_local + lax.rem(me, heads_local)
    if direct:
        cache_ref, attended_ref, sem = refs[-3:]
        half = len(refs[:-3]) // 2
        by_offset, parts_refs = refs[:half][::-1], refs[half : 2 * half][::-1]
        kept = cache_ref.at[0, 0]
    else:
        parts_ref, blocks_ref, cache_ref, attended_ref, sem, kept = refs

    def start_copy(k, carry):
        previous, slot = carry
        source = lax.div(kept_ref[request, k, head], source_blocks)
        slot = jnp.where(source == previous, jnp.minimum(slot + 1, MOST - 1), 0)
        target = kept.at[pl.ds(pl.multiple_of(k * BLK, BLK), BLK)]
        rows = pl.ds(pl.multiple_of(slot * BLK, BLK), BLK)
        if direct:
            for offset, ref in enumerate(by_offset):
                pl.when(jnp.bitwise_xor(me, offset) == source)(
                    pltpu.make_async_copy(ref.at[rows], target, sem).start
                )
        else:
            pltpu.make_async_copy(blocks_ref.at[source, rows], target, sem).start()
        return source, slot

    lax.fori_loop(
        0, kept_count, start_copy, (jnp.int32(-1), jnp.int32(0)), unroll=kept_count <= 8
    )
    if direct:
        total = sum(ref[...] for ref in parts_refs)
    else:
        total = jnp.sum(parts_ref[...], axis=0)
        pltpu.make_async_copy(kept, kept, sem).wait()
        pltpu.make_async_copy(kept, cache_ref.at[0, 0], sem).start()
    query_rows = QPK * step_count
    inverse = lax.rsqrt(total[query_rows + 2 * step_count :] * (1.0 / D) + EPS)
    cosine, sine = cos_ref[...], sin_ref[...]
    query = total[:query_rows].reshape(QPK // 2, 2 * step_count, HD) * inverse[None]
    query = rotate(query, cosine[None], sine[None]).reshape(query_rows, HD).astype(jnp.bfloat16)
    keyval = total[query_rows : query_rows + 2 * step_count] * inverse
    new_key = rotate(keyval, cosine, sine).astype(jnp.bfloat16)
    new_value = jnp.concatenate([keyval[step_count:], keyval[:step_count]], axis=0)
    new_value = new_value.astype(jnp.bfloat16)
    scale = 1.0 / math.sqrt(HD)
    score = lax.dot_general(query, new_key, CONTRACT_LAST, preferred_element_type=jnp.float32)
    row = lax.broadcasted_iota(jnp.int32, score.shape, 0)
    column = lax.broadcasted_iota(jnp.int32, score.shape, 1)
    scores = [jnp.where(column <= lax.rem(row, step_count), score * scale, -jnp.inf)]
    values = [new_value]
    def add_block(block, filled):
        score = lax.dot_general(
            query, block[:, :HD], CONTRACT_LAST, preferred_element_type=jnp.float32
        )
        column = lax.broadcasted_iota(jnp.int32, score.shape, 1)
        scores.append(jnp.where(column < filled * BLK, score * scale, -jnp.inf))
        values.append(block[:, HD:])

    if direct:
        for offset, ref in enumerate(by_offset):
            source = jnp.bitwise_xor(me, offset)
            filled = jnp.int32(0)
            for k in range(kept_count):
                here = lax.div(kept_ref[request, k, head], source_blocks) == source
                filled += here.astype(jnp.int32)
            add_block(ref[: MOST * BLK, :], filled)
    else:
        add_block(kept[...], kept_count)
    row_max = functools.reduce(
        jnp.maximum, [jnp.max(score, axis=1, keepdims=True) for score in scores]
    )
    denominator = jnp.zeros((query_rows, 1), jnp.float32)
    numerator = jnp.zeros((query_rows, HD), jnp.float32)
    for score, value in zip(scores, values):
        weight = jnp.exp(score - row_max)
        denominator += jnp.sum(weight, axis=1, keepdims=True)
        numerator += jnp.dot(
            weight.astype(jnp.bfloat16), value, preferred_element_type=jnp.float32
        )
    attended = (numerator / denominator).astype(jnp.bfloat16)
    if direct:
        attended_ref[...] = attended
    else:
        for i in range(attended_ref.shape[0]):
            attended_ref[i] = attended
    pltpu.make_async_copy(cache_ref, cache_ref, sem).wait()


def attend(kept_blocks, arrivals, source_blocks, heads_local, step_count, seq_count, direct):
    kept_count = kept_blocks.shape[1]
    row_width = 2 * HD
    cosine, sine = rope_tables(source_blocks * BLK * seq_count, step_count)
    shape = (QPK * step_count, HD)
    scratch = [pltpu.SemaphoreType.DMA]
    if not direct:
        shape = (seq_count,) + shape
        scratch.append(pltpu.VMEM((kept_count * BLK, row_width), jnp.bfloat16))
    vmem = pl.BlockSpec(memory_space=pltpu.VMEM)
    return pl.pallas_call(
        functools.partial(attend_kernel, direct, source_blocks, heads_local),
        out_shape=(
            jax.ShapeDtypeStruct((1, 1, kept_count * BLK, row_width), jnp.bfloat16),
            jax.ShapeDtypeStruct(shape, jnp.bfloat16),
        ),
        in_specs=[pl.BlockSpec(memory_space=pltpu.SMEM)] + [vmem] * (2 + len(arrivals)),
        out_specs=(pl.BlockSpec(memory_space=pl.ANY), vmem),
        scratch_shapes=scratch,
        compiler_params=pltpu.CompilerParams(vmem_limit_bytes=16 * 1024 * 1024),
        name="attend",
    )(kept_blocks, jnp.asarray(cosine), jnp.asarray(sine), *arrivals)


def output_kernel(heads_local, w_ref, *refs):
    gathered_refs, out_ref = refs[:-1], refs[-1]
    query_rows = gathered_refs[0].shape[-2]
    step_count = query_rows // QPK
    if len(gathered_refs) == 1:
        pair_count = gathered_refs[0].shape[0]
        pairs = [gathered_refs[0][p].astype(jnp.float32) for p in range(pair_count)]
    else:
        pair_count = len(gathered_refs)
        me = lax.axis_index("seq")
        arrived = [ref[...].astype(jnp.float32) for ref in gathered_refs]
        pairs = arrived
        bit = 1
        while bit < pair_count:
            swap = jnp.bitwise_and(me, bit) != 0
            pairs = [jnp.where(swap, pairs[p ^ bit], pairs[p]) for p in range(pair_count)]
            bit *= 2
    requests = pair_count // heads_local
    pieces = []
    for l in range(heads_local):
        for h in range(QPK):
            rows = slice(h * step_count, (h + 1) * step_count)
            pieces.append(
                jnp.concatenate(
                    [pairs[r * heads_local + l][rows] for r in range(requests)], axis=0
                )
            )
    merged = jnp.concatenate(pieces, axis=1).astype(jnp.bfloat16)
    total = jnp.dot(merged, w_ref[...], preferred_element_type=jnp.float32)
    if len(out_ref.shape) == 2:
        out_ref[...] = total
    else:
        for i in range(out_ref.shape[0]):
            out_ref[i] = total


def output(gathered, w_out, heads_local, pair_count, head_count):
    query_rows = gathered[0].shape[-2]
    total_rows = pair_count // heads_local * (query_rows // QPK)
    shape = (total_rows, w_out.shape[1])
    if not is_direct(head_count):
        shape = (head_count,) + shape
    vmem = pl.BlockSpec(memory_space=pltpu.VMEM)
    terms = pl.pallas_call(
        functools.partial(output_kernel, heads_local),
        out_shape=jax.ShapeDtypeStruct(shape, jnp.float32),
        in_specs=[vmem] * (1 + len(gathered)),
        out_specs=vmem,
        compiler_params=pltpu.CompilerParams(vmem_limit_bytes=8 * 1024 * 1024),
        name="output_projection",
    )(pltpu.with_memory_space_constraint(w_out, pltpu.VMEM), *gathered)
    return terms


def shards(source_cache, kept_blocks, new_hidden, norm_gain, w_query, w_keyval, w_out):
    seq_count = lax.axis_size("seq")
    head_count = lax.axis_size("head")
    requests, heads_local, source_tokens, _ = source_cache.shape
    _, step_count, width = new_hidden.shape
    pair_count = requests * heads_local

    kept_blocks = kept_blocks.transpose(0, 2, 1)
    direct = is_direct(seq_count)
    weights = (new_hidden, norm_gain, w_query, w_keyval)
    if direct:
        partners = range(1, seq_count)
        own, *blocks = pick(kept_blocks, source_cache, range(seq_count))
        blocks = [own] + [swap(blocks[k - 1], "seq", k) for k in partners]
        own, *parts = project(blocks[1], *weights, pair_count, direct)
        parts = [own] + [swap(parts[k - 1], "seq", k) for k in partners]
        arrivals = blocks[::-1] + parts[::-1]
    else:
        (blocks,) = pick(kept_blocks, source_cache, ())
        (parts,) = project(blocks, *weights, pair_count, direct)
        arrivals = [all_to_all(parts, "seq"), all_to_all(blocks, "seq")]
    kept_cache, attended = attend(
        kept_blocks, arrivals, source_tokens // BLK, heads_local, step_count, seq_count, direct
    )
    if direct:
        gathered = [attended] + [swap(attended, "seq", k) for k in range(1, seq_count)]
    else:
        gathered = [all_to_all(attended, "seq")]
    terms = output(gathered, w_out, heads_local, pair_count, head_count)
    if is_direct(head_count):
        terms = [terms] + [swap(terms, "head", k) for k in range(1, head_count)]
        while len(terms) > 1:
            terms = [terms[i] + terms[i + 1] for i in range(0, len(terms), 2)]
        summed = terms[0]
    else:
        summed = jnp.sum(all_to_all(terms, "head"), axis=0)
    summed = summed.reshape(requests, step_count, width)
    decoded = (new_hidden.astype(jnp.float32) + summed).astype(jnp.bfloat16)
    return (kept_cache, decoded)


def solution(mesh):
    in_specs = (
        P("groups", "head", "seq", None),
        P("groups", None, None),
        P("groups", None, "seq"),
        P("seq"),
        P("seq", "head"),
        P("seq", "head", None),
        P("head", "seq"),
    )
    out_specs = (P("head", ("groups", "seq"), None, None), P("groups", None, "seq"))
    return jax.shard_map(shards, mesh=mesh, in_specs=in_specs, out_specs=out_specs, check_vma=False)
```

time: 42.8 us -> 39.9 us (0.932)
  Pallas kernels: 9.44 us -> 7.33 us
  waiting for transfers between devices: 9.58 us -> 11.5 us
  local copies, waits for them, and re-layouts: 2.33 us -> 0.9 us
  starting transfers between devices: 19.8 us -> 18.6 us
    pallas_call x3, Pallas kernels: 8.25 us -> 6.14 us  [the longest x1 2.39 us: pick(): pl.pallas_call(functools.partial(pick_kernel, offsets), out_shape=shapes,...]
    ppermute x12, waiting for transfers between devices: 9.58 us -> 11.5 us  [swap(): return lax.ppermute(outgoing, axis, [(i, i ^ offset) for i in range(count)])]
    ppermute x12, starting transfers between devices: 19.8 us -> 18.6 us  [swap(): return lax.ppermute(outgoing, axis, [(i, i ^ offset) for i in range(count)])]
    unnamed x14 -> x20, local copies, waits for them, and re-layouts: 1.61 us -> 0.88 us
    reshape x1 -> x0, local copies, waits for them, and re-layouts: 0.69 us -> none  [shards(): norm_gain.reshape(1, width)]
  transfers between devices with their start and end apart: 12 -> 12, of which waited for: 5 -> 7; matrix products, arithmetic and copies ran while one was open for 2% -> 0% of each run, Pallas kernels for 11% -> 5%
where the time goes in v4:
time: 39.9 us; the launch traced here: 39.8 us
  starting transfers between devices  18.6 us (47%)
  waiting for transfers between devices  11.5 us (29%)
  Pallas kernels  7.33 us (18%)
  local copies, waits for them, and re-layouts  0.9 us (2%)
  between operations  0.76 us (2%)
  other arithmetic  0.65 us (2%)
    ppermute x12, starting transfers between devices, swap(): return lax.ppermute(outgoing, axis, [(i, i ^ offset) for i in range(count)])  18.6 us
    ppermute x12, waiting for transfers between devices, swap(): return lax.ppermute(outgoing, axis, [(i, i ^ offset) for i in range(count)])  11.5 us
    pallas_call x1, Pallas kernels, pick(): pl.pallas_call(functools.partial(pick_kernel, offsets), out_shape=shapes,...  2.39 us
    pallas_call x1, Pallas kernels, project(): pl.pallas_call(functools.partial(project_kernel, direct), out_shape=shape...  2.13 us
    pallas_call x1, Pallas kernels, attend(): pl.pallas_call(functools.partial(attend_kernel, direct, source_blocks, he...  1.62 us
    pallas_call x1, Pallas kernels, output(): pl.pallas_call(functools.partial(output_kernel, heads_local), out_shape=j...  1.19 us
    unnamed x20, local copies, waits for them, and re-layouts  0.88 us
  transfers between devices with their start and end apart: 12, of which 7 were waited for; matrix products, arithmetic and copies ran while one was open for 0% of the time, Pallas kernels for 5%

profile of v4, /device:TPU:0, one launch (start us, length us, event | category | flops | bytes accessed | tf_op | source)
XLA Modules:
  0.0 39.8 jit_solution(12574651688984695970)
XLA Ops:
  0.7 0.8 %copy-done.4 = s32[2,8,4]{1,2,0:T(4,128)S(1)} copy-done((s32[2,8,4]{1,2,0:T(4,128)S(1)}, s32[2,8,4]{1,2,0:T(4,128)}, u32[]{:S(2)}) %copy-start.4) | copy-done | bytes 280
  1.5 2.4 %pick_blocks.1 = (bf16[256,256]{1,0:T(8,128)(2,1)S(1)}, bf16[256,256]{1,0:T(8,128)(2,1)S(1)}, bf16[256,256]{1,0:T(8,128)(2,1)S(1)}, bf16[256,256]{1,0:T(8,128)(2,1)S(1)}) custom-call(s32[2,4,8]{2,1,0:T(4,128)S(1)} %bitcast.5, bf16[2,2,512,256]{3,2,1,0:T(8,128)(2,1)} %cache_ref.1), custom_call_target="tpu_custom_call" | custom-call | flops 10000000000 | tf_op jit(solution)/shard_map/pick_blocks/pallas_call | solution.py:98
  3.9 0.0 copy-start.6
  3.9 0.0 copy-start.7
  3.9 3.1 %collective-permute-start.2 = (bf16[256,256]{1,0:T(8,128)(2,1)S(1)}, bf16[256,256]{1,0:T(8,128)(2,1)S(1)}, u32[]{:S(2)}, u32[]{:S(2)}) collective-permute-start(bf16[256,256]{1,0:T(8,128)(2,1)S(1)} %get-tuple-element.14), channel_id=1, source_target_pairs={{0,4},{4,0},{8,12},{12,8},{1,5},{5,1},{9,13},{13,9},{2,6},{6,2},{1... | collective-permute-start | bytes 393224 | tf_op jit(solution)/shard_map/ppermute | solution.py:43
  7.0 2.5 %collective-permute-start = (bf16[256,256]{1,0:T(8,128)(2,1)S(1)}, bf16[256,256]{1,0:T(8,128)(2,1)S(1)}, u32[]{:S(2)}, u32[]{:S(2)}) collective-permute-start(bf16[256,256]{1,0:T(8,128)(2,1)S(1)} %get-tuple-element.12), channel_id=1, source_target_pairs={{0,12},{4,8},{8,4},{12,0},{1,13},{5,9},{9,5},{13,1},{2,14},{6,10},... | collective-permute-start | bytes 393224 | tf_op jit(solution)/shard_map/ppermute | solution.py:43
  9.5 0.1 collective-permute-start.1
  9.6 0.9 %collective-permute-done.2.after_ref.refs_2_ = bf16[256,256]{1,0:T(8,128)(2,1)S(1)} collective-permute-done((bf16[256,256]{1,0:T(8,128)(2,1)S(1)}, bf16[256,256]{1,0:T(8,128)(2,1)S(1)}, u32[]{:S(2)}, u32[]{:S(2)}) %collective-permute-start.2) | collective-permute-done | bytes 131104 | tf_op jit(solution)/shard_map/ppermute | solution.py:43
  10.5 2.1 %project.1 = (f32[48,128]{1,0:T(8,128)S(1)}, f32[48,128]{1,0:T(8,128)S(1)}, f32[48,128]{1,0:T(8,128)S(1)}, f32[48,128]{1,0:T(8,128)S(1)}) custom-call(bf16[256,256]{1,0:T(8,128)(2,1)S(1)} %collective-permute-done.2.after_ref.refs_2_, bf16[2,4,2048]{2,1,0:T(4,128)(2,1)S(1)} %copy-done.2, bf16[16,128]{1,0:T(8,128)(2,1)S(1)} %bitcast.4, ...), custom_call_target="tpu_custom_call" | custom-call | flops 83886080 | bytes 10485760 | tf_op jit(solution)/shard_map/project/pallas_call | solution.py:189
  12.7 5.9 %collective-permute-start.3 = (f32[48,128]{1,0:T(8,128)S(1)}, f32[48,128]{1,0:T(8,128)S(1)}, u32[]{:S(2)}, u32[]{:S(2)}) collective-permute-start(f32[48,128]{1,0:T(8,128)S(1)} %get-tuple-element.16), channel_id=1, source_target_pairs={{0,12},{4,8},{8,4},{12,0},{1,13},{5,9},{9,5},{13,1},{2,14},{6,10},... | collective-permute-start | bytes 73736 | tf_op jit(solution)/shard_map/ppermute | solution.py:43
  18.6 0.6 %collective-permute-start.5 = (f32[48,128]{1,0:T(8,128)S(1)}, f32[48,128]{1,0:T(8,128)S(1)}, u32[]{:S(2)}, u32[]{:S(2)}) collective-permute-start(f32[48,128]{1,0:T(8,128)S(1)} %get-tuple-element.18), channel_id=1, source_target_pairs={{0,4},{4,0},{8,12},{12,8},{1,5},{5,1},{9,13},{13,9},{2,6},{6,2},{1... | collective-permute-start | bytes 73736 | tf_op jit(solution)/shard_map/ppermute | solution.py:43
  19.3 3.7 %collective-permute-done.1.refs_1_ = bf16[256,256]{1,0:T(8,128)(2,1)S(1)} collective-permute-done((bf16[256,256]{1,0:T(8,128)(2,1)S(1)}, bf16[256,256]{1,0:T(8,128)(2,1)S(1)}, u32[]{:S(2)}, u32[]{:S(2)}) %collective-permute-start.1) | collective-permute-done | bytes 131104 | tf_op jit(solution)/shard_map/ppermute | solution.py:43
  22.9 0.5 %collective-permute-done.4.refs_5_ = f32[48,128]{1,0:T(8,128)S(1)} collective-permute-done((f32[48,128]{1,0:T(8,128)S(1)}, f32[48,128]{1,0:T(8,128)S(1)}, u32[]{:S(2)}, u32[]{:S(2)}) %collective-permute-start.4) | collective-permute-done | bytes 24608 | tf_op jit(solution)/shard_map/ppermute | solution.py:43
  23.4 1.6 %attend.1 = (bf16[1,1,512,256]{3,2,1,0:T(8,128)(2,1)}, bf16[32,128]{1,0:T(8,128)(2,1)S(1)}) custom-call(s32[2,4,8]{2,1,0:T(4,128)S(1)} %bitcast.6, f32[8,128]{1,0:T(8,128)S(1)} %copy-done.7, f32[8,128]{1,0:T(8,128)S(1)} %copy-done.6, bf16[256,256]{1,0:T(8,128)(2,1)S(1)} %collective-permute-done.refs_0_, bf16[256,256]{1,0:T(8,128)(2,1)S(1)} %collective-permute-done.1.refs_1_, ...), custom_call_target="tpu_custom_call" | custom-call | tf_op jit(solution)/shard_map/attend/pallas_call | solution.py:311
  25.0 2.7 %collective-permute-start.8 = (bf16[32,128]{1,0:T(8,128)(2,1)S(1)}, bf16[32,128]{1,0:T(8,128)(2,1)S(1)}, u32[]{:S(2)}, u32[]{:S(2)}) collective-permute-start(bf16[32,128]{1,0:T(8,128)(2,1)S(1)} %get-tuple-element.21.refs_0_), channel_id=1, source_target_pairs={{0,12},{4,8},{8,4},{12,0},{1,13},{5,9},{9,5},{13,1},{2,14},{6,10},... | collective-permute-start | bytes 24584 | tf_op jit(solution)/shard_map/ppermute | solution.py:43
  27.7 1.7 %collective-permute-start.6 = (bf16[32,128]{1,0:T(8,128)(2,1)S(1)}, bf16[32,128]{1,0:T(8,128)(2,1)S(1)}, u32[]{:S(2)}, u32[]{:S(2)}) collective-permute-start(bf16[32,128]{1,0:T(8,128)(2,1)S(1)} %get-tuple-element.21.refs_0_), channel_id=1, source_target_pairs={{0,4},{4,0},{8,12},{12,8},{1,5},{5,1},{9,13},{13,9},{2,6},{6,2},{1... | collective-permute-start | bytes 24584 | tf_op jit(solution)/shard_map/ppermute | solution.py:43
  29.5 1.1 %collective-permute-done.8.refs_3_ = bf16[32,128]{1,0:T(8,128)(2,1)S(1)} collective-permute-done((bf16[32,128]{1,0:T(8,128)(2,1)S(1)}, bf16[32,128]{1,0:T(8,128)(2,1)S(1)}, u32[]{:S(2)}, u32[]{:S(2)}) %collective-permute-start.8) | collective-permute-done | bytes 8224 | tf_op jit(solution)/shard_map/ppermute | solution.py:43
  30.5 1.7 %collective-permute-done.7.refs_2_ = bf16[32,128]{1,0:T(8,128)(2,1)S(1)} collective-permute-done((bf16[32,128]{1,0:T(8,128)(2,1)S(1)}, bf16[32,128]{1,0:T(8,128)(2,1)S(1)}, u32[]{:S(2)}, u32[]{:S(2)}) %collective-permute-start.7) | collective-permute-done | bytes 8224 | tf_op jit(solution)/shard_map/ppermute | solution.py:43
  32.3 1.2 %output_projection.1 = f32[8,2048]{1,0:T(8,128)S(1)} custom-call(bf16[2048,2048]{1,0:T(8,128)(2,1)S(1)} %bitcast.3, bf16[32,128]{1,0:T(8,128)(2,1)S(1)} %get-tuple-element.21.refs_0_, bf16[32,128]{1,0:T(8,128)(2,1)S(1)} %collective-permute-done.6.refs_1_, bf16[32,128]{1,0:T(8,128)(2,1)S(1)} %collective-permute-done.7.refs_2_, ...), custom_call_target="tpu_custom_call" | custom-call | tf_op jit(solution)/shard_map/output_projection/pallas_call | solution.py:368
  33.5 1.4 %collective-permute-start.10 = (f32[8,2048]{1,0:T(8,128)S(1)}, f32[8,2048]{1,0:T(8,128)S(1)}, u32[]{:S(2)}, u32[]{:S(2)}) collective-permute-start(f32[8,2048]{1,0:T(8,128)S(1)} %output_projection.1), channel_id=1, source_target_pairs={{0,2},{1,3},{2,0},{3,1},{4,6},{5,7},{6,4},{7,5},{8,10},{9,11},{10,... | collective-permute-start | bytes 196616 | tf_op jit(solution)/shard_map/ppermute | solution.py:43
  34.9 0.5 %collective-permute-start.9 = (f32[8,2048]{1,0:T(8,128)S(1)}, f32[8,2048]{1,0:T(8,128)S(1)}, u32[]{:S(2)}, u32[]{:S(2)}) collective-permute-start(f32[8,2048]{1,0:T(8,128)S(1)} %output_projection.1), channel_id=1, source_target_pairs={{0,1},{1,0},{2,3},{3,2},{4,5},{5,4},{6,7},{7,6},{8,9},{9,8},{10,11... | collective-permute-start | bytes 196616 | tf_op jit(solution)/shard_map/ppermute | solution.py:43
  35.4 2.5 %collective-permute-done.11 = f32[8,2048]{1,0:T(8,128)S(1)} collective-permute-done((f32[8,2048]{1,0:T(8,128)S(1)}, f32[8,2048]{1,0:T(8,128)S(1)}, u32[]{:S(2)}, u32[]{:S(2)}) %collective-permute-start.11) | collective-permute-done | bytes 65568 | tf_op jit(solution)/shard_map/ppermute | solution.py:43
  37.9 1.2 %collective-permute-done.10 = f32[8,2048]{1,0:T(8,128)S(1)} collective-permute-done((f32[8,2048]{1,0:T(8,128)S(1)}, f32[8,2048]{1,0:T(8,128)S(1)}, u32[]{:S(2)}, u32[]{:S(2)}) %collective-permute-start.10) | collective-permute-done | bytes 65568 | tf_op jit(solution)/shard_map/ppermute | solution.py:43
  39.1 0.6 %add_convert_fusion = bf16[2,4,2048]{2,1,0:T(4,128)(2,1)} fusion(f32[2,4,2048]{2,1,0:T(4,128)S(1)} %reshape.11, bf16[2,4,2048]{2,1,0:T(4,128)(2,1)S(1)} %copy-done.2), kind=kLoop, calls=%fused_computation | loop fusion | flops 49152 | bytes 131072 | tf_op jit(solution)/shard_map/convert_element_type | solution.py:416
  (28 shorter events, 0.1 us)
Async XLA Ops:
  0.6 31.6 %slice-start = ((s8[8388608]{0:T(1024)(128)(4,1)}), s8[4194304]{0:T(1024)(128)(4,1)S(1)}, s32[]{:S(2)}) async-start(s8[8388608]{0:T(1024)(128)(4,1)} %bitcast.2), calls=%async_computation | async-start | bytes 8388608
  0.6 0.8 %copy-start.4 = (s32[2,8,4]{1,2,0:T(4,128)S(1)}, s32[2,8,4]{1,2,0:T(4,128)}, u32[]{:S(2)}) copy-start(s32[2,8,4]{1,2,0:T(4,128)} %param.10) | copy-start | bytes 772
  1.5 9.0 %copy-start = (bf16[2048,2048]{1,0:T(8,128)(2,1)S(1)}, bf16[2048,2048]{1,0:T(8,128)(2,1)}, u32[]{:S(2)}) copy-start(bf16[2048,2048]{1,0:T(8,128)(2,1)} %wq_ref.1) | copy-start | bytes 25165828
  1.5 9.0 %copy-start.1 = (bf16[2048,2,256]{2,1,0:T(2,128)(2,1)S(1)}, bf16[2048,2,256]{2,1,0:T(2,128)(2,1)}, u32[]{:S(2)}) copy-start(bf16[2048,2,256]{2,1,0:T(2,128)(2,1)} %wkv_ref.1) | copy-start | bytes 6291460
  1.5 9.0 %copy-start.2 = (bf16[2,4,2048]{2,1,0:T(4,128)(2,1)S(1)}, bf16[2,4,2048]{2,1,0:T(4,128)(2,1)}, u32[]{:S(2)}) copy-start(bf16[2,4,2048]{2,1,0:T(4,128)(2,1)} %hidden_ref.1) | copy-start | bytes 98308
  1.5 9.0 %copy-start.3 = (bf16[2048]{0:T(1024)(128)(2,1)S(1)}, bf16[2048]{0:T(1024)(128)(2,1)}, u32[]{:S(2)}) copy-start(bf16[2048]{0:T(1024)(128)(2,1)} %param.12) | copy-start | bytes 12292
  1.5 30.8 %slice-start.1 = ((s8[8388608]{0:T(1024)(128)(4,1)}), s8[4194304]{0:T(1024)(128)(4,1)S(1)}, s32[]{:S(2)}) async-start(s8[8388608]{0:T(1024)(128)(4,1)} %bitcast.2), calls=%async_computation.1 | async-start | bytes 8388608
  3.9 19.5 %copy-start.5 = (s32[2,8,4]{1,2,0:T(4,128)S(1)}, s32[2,8,4]{1,2,0:T(4,128)}, u32[]{:S(2)}) copy-start(s32[2,8,4]{1,2,0:T(4,128)} %param.10) | copy-start | bytes 772
  3.9 19.5 %copy-start.6 = (f32[8,128]{1,0:T(8,128)S(1)}, f32[8,128]{1,0:T(8,128)}, u32[]{:S(2)}) copy-start(f32[8,128]{1,0:T(8,128)} %constant.5.clone.sin_ref) | copy-start | bytes 12292
  3.9 19.5 %copy-start.7 = (f32[8,128]{1,0:T(8,128)S(1)}, f32[8,128]{1,0:T(8,128)}, u32[]{:S(2)}) copy-start(f32[8,128]{1,0:T(8,128)} %constant.4.clone.cos_ref) | copy-start | bytes 12292
  3.9 6.6 %collective-permute-start.2 = (bf16[256,256]{1,0:T(8,128)(2,1)S(1)}, bf16[256,256]{1,0:T(8,128)(2,1)S(1)}, u32[]{:S(2)}, u32[]{:S(2)}) collective-permute-start(bf16[256,256]{1,0:T(8,128)(2,1)S(1)} %get-tuple-element.14), channel_id=1, source_target_pairs={{0,4},{4,0},{8,12},{12,8},{1,5},{5,1},{9,13},{13,9},{2,6},{6,2},{1... | collective-permute-start | bytes 393224 | tf_op jit(solution)/shard_map/ppermute | solution.py:43
  7.0 12.2 %collective-permute-start = (bf16[256,256]{1,0:T(8,128)(2,1)S(1)}, bf16[256,256]{1,0:T(8,128)(2,1)S(1)}, u32[]{:S(2)}, u32[]{:S(2)}) collective-permute-start(bf16[256,256]{1,0:T(8,128)(2,1)S(1)} %get-tuple-element.12), channel_id=1, source_target_pairs={{0,12},{4,8},{8,4},{12,0},{1,13},{5,9},{9,5},{13,1},{2,14},{6,10},... | collective-permute-start | bytes 393224 | tf_op jit(solution)/shard_map/ppermute | solution.py:43
  9.5 13.4 %collective-permute-start.1 = (bf16[256,256]{1,0:T(8,128)(2,1)S(1)}, bf16[256,256]{1,0:T(8,128)(2,1)S(1)}, u32[]{:S(2)}, u32[]{:S(2)}) collective-permute-start(bf16[256,256]{1,0:T(8,128)(2,1)S(1)} %get-tuple-element.13), channel_id=1, source_target_pairs={{0,8},{4,12},{8,0},{12,4},{1,9},{5,13},{9,1},{13,5},{2,10},{6,14},... | collective-permute-start | bytes 393224 | tf_op jit(solution)/shard_map/ppermute | solution.py:43
  12.7 10.2 %collective-permute-start.3 = (f32[48,128]{1,0:T(8,128)S(1)}, f32[48,128]{1,0:T(8,128)S(1)}, u32[]{:S(2)}, u32[]{:S(2)}) collective-permute-start(f32[48,128]{1,0:T(8,128)S(1)} %get-tuple-element.16), channel_id=1, source_target_pairs={{0,12},{4,8},{8,4},{12,0},{1,13},{5,9},{9,5},{13,1},{2,14},{6,10},... | collective-permute-start | bytes 73736 | tf_op jit(solution)/shard_map/ppermute | solution.py:43
  18.6 4.8 %collective-permute-start.4 = (f32[48,128]{1,0:T(8,128)S(1)}, f32[48,128]{1,0:T(8,128)S(1)}, u32[]{:S(2)}, u32[]{:S(2)}) collective-permute-start(f32[48,128]{1,0:T(8,128)S(1)} %get-tuple-element.17), channel_id=1, source_target_pairs={{0,8},{4,12},{8,0},{12,4},{1,9},{5,13},{9,1},{13,5},{2,10},{6,14},... | collective-permute-start | bytes 73736 | tf_op jit(solution)/shard_map/ppermute | solution.py:43
  18.6 4.8 %collective-permute-start.5 = (f32[48,128]{1,0:T(8,128)S(1)}, f32[48,128]{1,0:T(8,128)S(1)}, u32[]{:S(2)}, u32[]{:S(2)}) collective-permute-start(f32[48,128]{1,0:T(8,128)S(1)} %get-tuple-element.18), channel_id=1, source_target_pairs={{0,4},{4,0},{8,12},{12,8},{1,5},{5,1},{9,13},{13,9},{2,6},{6,2},{1... | collective-permute-start | bytes 73736 | tf_op jit(solution)/shard_map/ppermute | solution.py:43
  25.0 5.5 %collective-permute-start.8 = (bf16[32,128]{1,0:T(8,128)(2,1)S(1)}, bf16[32,128]{1,0:T(8,128)(2,1)S(1)}, u32[]{:S(2)}, u32[]{:S(2)}) collective-permute-start(bf16[32,128]{1,0:T(8,128)(2,1)S(1)} %get-tuple-element.21.refs_0_), channel_id=1, source_target_pairs={{0,12},{4,8},{8,4},{12,0},{1,13},{5,9},{9,5},{13,1},{2,14},{6,10},... | collective-permute-start | bytes 24584 | tf_op jit(solution)/shard_map/ppermute | solution.py:43
  27.7 4.5 %collective-permute-start.7 = (bf16[32,128]{1,0:T(8,128)(2,1)S(1)}, bf16[32,128]{1,0:T(8,128)(2,1)S(1)}, u32[]{:S(2)}, u32[]{:S(2)}) collective-permute-start(bf16[32,128]{1,0:T(8,128)(2,1)S(1)} %get-tuple-element.21.refs_0_), channel_id=1, source_target_pairs={{0,8},{4,12},{8,0},{12,4},{1,9},{5,13},{9,1},{13,5},{2,10},{6,14},... | collective-permute-start | bytes 24584 | tf_op jit(solution)/shard_map/ppermute | solution.py:43
  27.7 4.5 %collective-permute-start.6 = (bf16[32,128]{1,0:T(8,128)(2,1)S(1)}, bf16[32,128]{1,0:T(8,128)(2,1)S(1)}, u32[]{:S(2)}, u32[]{:S(2)}) collective-permute-start(bf16[32,128]{1,0:T(8,128)(2,1)S(1)} %get-tuple-element.21.refs_0_), channel_id=1, source_target_pairs={{0,4},{4,0},{8,12},{12,8},{1,5},{5,1},{9,13},{13,9},{2,6},{6,2},{1... | collective-permute-start | bytes 24584 | tf_op jit(solution)/shard_map/ppermute | solution.py:43
  33.5 4.4 %collective-permute-start.11 = (f32[8,2048]{1,0:T(8,128)S(1)}, f32[8,2048]{1,0:T(8,128)S(1)}, u32[]{:S(2)}, u32[]{:S(2)}) collective-permute-start(f32[8,2048]{1,0:T(8,128)S(1)} %output_projection.1), channel_id=1, source_target_pairs={{0,3},{1,2},{2,1},{3,0},{4,7},{5,6},{6,5},{7,4},{8,11},{9,10},{10,... | collective-permute-start | bytes 196616 | tf_op jit(solution)/shard_map/ppermute | solution.py:43
  33.5 5.6 %collective-permute-start.10 = (f32[8,2048]{1,0:T(8,128)S(1)}, f32[8,2048]{1,0:T(8,128)S(1)}, u32[]{:S(2)}, u32[]{:S(2)}) collective-permute-start(f32[8,2048]{1,0:T(8,128)S(1)} %output_projection.1), channel_id=1, source_target_pairs={{0,2},{1,3},{2,0},{3,1},{4,6},{5,7},{6,4},{7,5},{8,10},{9,11},{10,... | collective-permute-start | bytes 196616 | tf_op jit(solution)/shard_map/ppermute | solution.py:43
  34.9 4.2 %collective-permute-start.9 = (f32[8,2048]{1,0:T(8,128)S(1)}, f32[8,2048]{1,0:T(8,128)S(1)}, u32[]{:S(2)}, u32[]{:S(2)}) collective-permute-start(f32[8,2048]{1,0:T(8,128)S(1)} %output_projection.1), channel_id=1, source_target_pairs={{0,1},{1,0},{2,3},{3,2},{4,5},{5,4},{6,7},{7,6},{8,9},{9,8},{10,11... | collective-permute-start | bytes 196616 | tf_op jit(solution)/shard_map/ppermute | solution.py:43

commit v5 on v4

--- a/solution.py
+++ b/solution.py
@@ -35,7 +35,7 @@
 
 
 def is_direct(count):
-    return count <= 4 and count & (count - 1) == 0
+    return count == 4
 
 
 def swap(outgoing, axis, offset):
@@ -71,8 +71,9 @@
         ).start()
 
 
-def pick_kernel(offsets, kept_ref, cache_ref, *refs):
-    outs, sem = refs[:-1], refs[-1]
+def pick_kernel(offsets, kept_hbm_ref, cache_ref, *refs):
+    outs, kept_ref, sem = refs[:-2], refs[-2], refs[-1]
+    pltpu.sync_copy(kept_hbm_ref, kept_ref)
     if offsets:
         me = lax.axis_index("seq")
         for offset, out_ref in zip(offsets, outs):
@@ -98,16 +99,19 @@
     return pl.pallas_call(
         functools.partial(pick_kernel, offsets),
         out_shape=shapes,
-        in_specs=[
-            pl.BlockSpec(memory_space=pltpu.SMEM),
-            pl.BlockSpec(memory_space=pl.ANY),
+        in_specs=[pl.BlockSpec(memory_space=pl.ANY)] * 2,
+        out_specs=[pl.BlockSpec(memory_space=pltpu.VMEM)] * len(shapes),
+        scratch_shapes=[
+            pltpu.SMEM(kept_blocks.shape, jnp.int32),
+            pltpu.SemaphoreType.DMA,
         ],
-        out_specs=[pl.BlockSpec(memory_space=pltpu.VMEM)] * len(shapes),
-        scratch_shapes=[pltpu.SemaphoreType.DMA],
         compiler_params=pltpu.CompilerParams(vmem_limit_bytes=8 * 1024 * 1024),
         cost_estimate=pl.CostEstimate(flops=10**10, bytes_accessed=0, transcendentals=0),
         name="pick_blocks",
-    )(kept_blocks, pltpu.with_memory_space_constraint(source_cache, pltpu.HBM))
+    )(
+        pltpu.with_memory_space_constraint(kept_blocks, pltpu.HBM),
+        pltpu.with_memory_space_constraint(source_cache, pltpu.HBM),
+    )
 
 
 def interleave(rows):
@@ -189,7 +193,7 @@
     return pl.pallas_call(
         functools.partial(project_kernel, direct),
         out_shape=shapes,
-        in_specs=[pl.BlockSpec(memory_space=pl.ANY), vmem, vmem, vmem, vmem],
+        in_specs=[pl.BlockSpec(memory_space=pl.ANY)] + [vmem] * 4,
         out_specs=[vmem] * len(shapes),
         compiler_params=pltpu.CompilerParams(vmem_limit_bytes=8 * 1024 * 1024),
         cost_estimate=pl.CostEstimate(
@@ -215,8 +219,7 @@
     head = lax.axis_index("head") * heads_local + lax.rem(me, heads_local)
     if direct:
         cache_ref, attended_ref, sem = refs[-3:]
-        half = len(refs[:-3]) // 2
-        by_offset, parts_refs = refs[:half][::-1], refs[half : 2 * half][::-1]
+        by_offset, parts_refs = refs[:4][::-1], refs[4:8][::-1]
         kept = cache_ref.at[0, 0]
     else:
         parts_ref, blocks_ref, cache_ref, attended_ref, sem, kept = refs
@@ -388,10 +391,10 @@
     weights = (new_hidden, norm_gain, w_query, w_keyval)
     if direct:
         partners = range(1, seq_count)
-        own, *blocks = pick(kept_blocks, source_cache, range(seq_count))
-        blocks = [own] + [swap(blocks[k - 1], "seq", k) for k in partners]
-        own, *parts = project(blocks[1], *weights, pair_count, direct)
-        parts = [own] + [swap(parts[k - 1], "seq", k) for k in partners]
+        blocks = pick(kept_blocks, source_cache, range(seq_count))
+        parts = project(blocks[0], *weights, pair_count, direct)
+        blocks = [blocks[0]] + [swap(blocks[k], "seq", k) for k in partners]
+        parts = [parts[0]] + [swap(parts[k], "seq", k) for k in partners]
         arrivals = blocks[::-1] + parts[::-1]
     else:
         (blocks,) = pick(kept_blocks, source_cache, ())
@@ -406,10 +409,8 @@
         gathered = [all_to_all(attended, "seq")]
     terms = output(gathered, w_out, heads_local, pair_count, head_count)
     if is_direct(head_count):
-        terms = [terms] + [swap(terms, "head", k) for k in range(1, head_count)]
-        while len(terms) > 1:
-            terms = [terms[i] + terms[i + 1] for i in range(0, len(terms), 2)]
-        summed = terms[0]
+        terms = terms + swap(terms, "head", 2)
+        summed = terms + swap(terms, "head", 1)
     else:
         summed = jnp.sum(all_to_all(terms, "head"), axis=0)
     summed = summed.reshape(requests, step_count, width)

time: 39.9 us -> 40 us (level)
  local copies, waits for them, and re-layouts: 0.9 us -> 0.07 us
  waiting for transfers between devices: 11.5 us -> 12 us
    unnamed x20 -> x18, local copies, waits for them, and re-layouts: 0.88 us -> 0.05 us
    ppermute x12 -> x11, starting transfers between devices: 18.6 us -> 19 us  [swap(): return lax.ppermute(outgoing, axis, [(i, i ^ offset) for i in range(count)])]
    ppermute x12 -> x11, waiting for transfers between devices: 11.5 us -> 12 us  [swap(): return lax.ppermute(outgoing, axis, [(i, i ^ offset) for i in range(count)])]
  transfers between devices with their start and end apart: 12 -> 11, of which waited for: 7 -> 7; matrix products, arithmetic and copies ran while one was open for 0% -> 0% of each run, Pallas kernels for 5% -> 5%
where the time goes in v5:
time: 40 us; the launch traced here: 39.8 us
  starting transfers between devices  19 us (48%)
  waiting for transfers between devices  12 us (30%)
  Pallas kernels  7.28 us (18%)
  between operations  0.79 us (2%)
  other arithmetic  0.65 us (2%)
    ppermute x11, starting transfers between devices, swap(): return lax.ppermute(outgoing, axis, [(i, i ^ offset) for i in range(count)])  19 us
    ppermute x11, waiting for transfers between devices, swap(): return lax.ppermute(outgoing, axis, [(i, i ^ offset) for i in range(count)])  12 us
    pallas_call x1, Pallas kernels, pick(): pl.pallas_call(functools.partial(pick_kernel, offsets), out_shape=shapes,...  2.36 us
    pallas_call x1, Pallas kernels, project(): pl.pallas_call(functools.partial(project_kernel, direct), out_shape=shape...  2.12 us
    pallas_call x1, Pallas kernels, attend(): pl.pallas_call(functools.partial(attend_kernel, direct, source_blocks, he...  1.62 us
    pallas_call x1, Pallas kernels, output(): pl.pallas_call(functools.partial(output_kernel, heads_local), out_shape=j...  1.19 us
  transfers between devices with their start and end apart: 11, of which 7 were waited for; matrix products, arithmetic and copies ran while one was open for 0% of the time, Pallas kernels for 5%

profile of v5, /device:TPU:0, one launch (start us, length us, event | category | flops | bytes accessed | tf_op | source)
XLA Modules:
  0.0 39.8 jit_solution(4447670927953854050)
XLA Ops:
  0.7 2.4 %pick_blocks.1 = (bf16[256,256]{1,0:T(8,128)(2,1)S(1)}, bf16[256,256]{1,0:T(8,128)(2,1)S(1)}, bf16[256,256]{1,0:T(8,128)(2,1)S(1)}, bf16[256,256]{1,0:T(8,128)(2,1)S(1)}) custom-call(s32[2,4,8]{2,1,0:T(4,128)} %bitcast.5, bf16[2,2,512,256]{3,2,1,0:T(8,128)(2,1)} %cache_ref.1), custom_call_target="tpu_custom_call" | custom-call | flops 10000000000 | tf_op jit(solution)/shard_map/pick_blocks/pallas_call | solution.py:99
  3.1 0.0 copy-start.4
  3.1 0.0 copy-start.5
  3.1 0.0 copy-start.6
  3.1 5.1 %collective-permute-start = (bf16[256,256]{1,0:T(8,128)(2,1)S(1)}, bf16[256,256]{1,0:T(8,128)(2,1)S(1)}, u32[]{:S(2)}, u32[]{:S(2)}) collective-permute-start(bf16[256,256]{1,0:T(8,128)(2,1)S(1)} %get-tuple-element.12), channel_id=1, source_target_pairs={{0,12},{4,8},{8,4},{12,0},{1,13},{5,9},{9,5},{13,1},{2,14},{6,10},... | collective-permute-start | bytes 393224 | tf_op jit(solution)/shard_map/ppermute | solution.py:43
  8.2 0.6 %collective-permute-start.2 = (bf16[256,256]{1,0:T(8,128)(2,1)S(1)}, bf16[256,256]{1,0:T(8,128)(2,1)S(1)}, u32[]{:S(2)}, u32[]{:S(2)}) collective-permute-start(bf16[256,256]{1,0:T(8,128)(2,1)S(1)} %get-tuple-element.14), channel_id=1, source_target_pairs={{0,4},{4,0},{8,12},{12,8},{1,5},{5,1},{9,13},{13,9},{2,6},{6,2},{1... | collective-permute-start | bytes 393224 | tf_op jit(solution)/shard_map/ppermute | solution.py:43
  8.9 2.1 %project.1 = (f32[48,128]{1,0:T(8,128)S(1)}, f32[48,128]{1,0:T(8,128)S(1)}, f32[48,128]{1,0:T(8,128)S(1)}, f32[48,128]{1,0:T(8,128)S(1)}) custom-call(bf16[256,256]{1,0:T(8,128)(2,1)S(1)} %get-tuple-element.15.after_ref.refs_3_, bf16[2,4,2048]{2,1,0:T(4,128)(2,1)S(1)} %copy-done.2, bf16[16,128]{1,0:T(8,128)(2,1)S(1)} %bitcast.4, ...), custom_call_target="tpu_custom_call" | custom-call | flops 83886080 | bytes 10485760 | tf_op jit(solution)/shard_map/project/pallas_call | solution.py:193
  11.0 3.8 %collective-permute-start.3 = (f32[48,128]{1,0:T(8,128)S(1)}, f32[48,128]{1,0:T(8,128)S(1)}, u32[]{:S(2)}, u32[]{:S(2)}) collective-permute-start(f32[48,128]{1,0:T(8,128)S(1)} %get-tuple-element.16), channel_id=1, source_target_pairs={{0,12},{4,8},{8,4},{12,0},{1,13},{5,9},{9,5},{13,1},{2,14},{6,10},... | collective-permute-start | bytes 73736 | tf_op jit(solution)/shard_map/ppermute | solution.py:43
  14.8 3.4 %collective-permute-done.3.refs_4_ = f32[48,128]{1,0:T(8,128)S(1)} collective-permute-done((f32[48,128]{1,0:T(8,128)S(1)}, f32[48,128]{1,0:T(8,128)S(1)}, u32[]{:S(2)}, u32[]{:S(2)}) %collective-permute-start.3) | collective-permute-done | bytes 24608 | tf_op jit(solution)/shard_map/ppermute | solution.py:43
  18.3 3.4 %collective-permute-start.5 = (f32[48,128]{1,0:T(8,128)S(1)}, f32[48,128]{1,0:T(8,128)S(1)}, u32[]{:S(2)}, u32[]{:S(2)}) collective-permute-start(f32[48,128]{1,0:T(8,128)S(1)} %get-tuple-element.18), channel_id=1, source_target_pairs={{0,4},{4,0},{8,12},{12,8},{1,5},{5,1},{9,13},{13,9},{2,6},{6,2},{1... | collective-permute-start | bytes 73736 | tf_op jit(solution)/shard_map/ppermute | solution.py:43
  21.7 1.8 %collective-permute-done.5.refs_6_ = f32[48,128]{1,0:T(8,128)S(1)} collective-permute-done((f32[48,128]{1,0:T(8,128)S(1)}, f32[48,128]{1,0:T(8,128)S(1)}, u32[]{:S(2)}, u32[]{:S(2)}) %collective-permute-start.5) | collective-permute-done | bytes 24608 | tf_op jit(solution)/shard_map/ppermute | solution.py:43
  23.5 1.6 %attend.1 = (bf16[1,1,512,256]{3,2,1,0:T(8,128)(2,1)}, bf16[32,128]{1,0:T(8,128)(2,1)S(1)}) custom-call(s32[2,4,8]{2,1,0:T(4,128)S(1)} %bitcast.6, f32[8,128]{1,0:T(8,128)S(1)} %copy-done.6, f32[8,128]{1,0:T(8,128)S(1)} %copy-done.5, bf16[256,256]{1,0:T(8,128)(2,1)S(1)} %collective-permute-done.refs_0_, bf16[256,256]{1,0:T(8,128)(2,1)S(1)} %collective-permute-done.1.refs_1_, ...), custom_call_target="tpu_custom_call" | custom-call | tf_op jit(solution)/shard_map/attend/pallas_call | solution.py:314
  25.2 2.4 %collective-permute-start.8 = (bf16[32,128]{1,0:T(8,128)(2,1)S(1)}, bf16[32,128]{1,0:T(8,128)(2,1)S(1)}, u32[]{:S(2)}, u32[]{:S(2)}) collective-permute-start(bf16[32,128]{1,0:T(8,128)(2,1)S(1)} %get-tuple-element.21.refs_0_), channel_id=1, source_target_pairs={{0,12},{4,8},{8,4},{12,0},{1,13},{5,9},{9,5},{13,1},{2,14},{6,10},... | collective-permute-start | bytes 24584 | tf_op jit(solution)/shard_map/ppermute | solution.py:43
  27.6 1.2 %collective-permute-start.7 = (bf16[32,128]{1,0:T(8,128)(2,1)S(1)}, bf16[32,128]{1,0:T(8,128)(2,1)S(1)}, u32[]{:S(2)}, u32[]{:S(2)}) collective-permute-start(bf16[32,128]{1,0:T(8,128)(2,1)S(1)} %get-tuple-element.21.refs_0_), channel_id=1, source_target_pairs={{0,8},{4,12},{8,0},{12,4},{1,9},{5,13},{9,1},{13,5},{2,10},{6,14},... | collective-permute-start | bytes 24584 | tf_op jit(solution)/shard_map/ppermute | solution.py:43
  28.7 0.9 %collective-permute-start.6 = (bf16[32,128]{1,0:T(8,128)(2,1)S(1)}, bf16[32,128]{1,0:T(8,128)(2,1)S(1)}, u32[]{:S(2)}, u32[]{:S(2)}) collective-permute-start(bf16[32,128]{1,0:T(8,128)(2,1)S(1)} %get-tuple-element.21.refs_0_), channel_id=1, source_target_pairs={{0,4},{4,0},{8,12},{12,8},{1,5},{5,1},{9,13},{13,9},{2,6},{6,2},{1... | collective-permute-start | bytes 24584 | tf_op jit(solution)/shard_map/ppermute | solution.py:43
  29.6 1.1 %collective-permute-done.8.refs_3_ = bf16[32,128]{1,0:T(8,128)(2,1)S(1)} collective-permute-done((bf16[32,128]{1,0:T(8,128)(2,1)S(1)}, bf16[32,128]{1,0:T(8,128)(2,1)S(1)}, u32[]{:S(2)}, u32[]{:S(2)}) %collective-permute-start.8) | collective-permute-done | bytes 8224 | tf_op jit(solution)/shard_map/ppermute | solution.py:43
  30.7 1.4 %collective-permute-done.7.refs_2_ = bf16[32,128]{1,0:T(8,128)(2,1)S(1)} collective-permute-done((bf16[32,128]{1,0:T(8,128)(2,1)S(1)}, bf16[32,128]{1,0:T(8,128)(2,1)S(1)}, u32[]{:S(2)}, u32[]{:S(2)}) %collective-permute-start.7) | collective-permute-done | bytes 8224 | tf_op jit(solution)/shard_map/ppermute | solution.py:43
  32.1 0.3 collective-permute-done.6.refs_1_
  32.4 1.2 %output_projection.1 = f32[8,2048]{1,0:T(8,128)S(1)} custom-call(bf16[2048,2048]{1,0:T(8,128)(2,1)S(1)} %bitcast.3, bf16[32,128]{1,0:T(8,128)(2,1)S(1)} %get-tuple-element.21.refs_0_, bf16[32,128]{1,0:T(8,128)(2,1)S(1)} %collective-permute-done.6.refs_1_, bf16[32,128]{1,0:T(8,128)(2,1)S(1)} %collective-permute-done.7.refs_2_, ...), custom_call_target="tpu_custom_call" | custom-call | tf_op jit(solution)/shard_map/output_projection/pallas_call | solution.py:371
  33.6 1.5 %collective-permute-start.9 = (f32[8,2048]{1,0:T(8,128)S(1)}, f32[8,2048]{1,0:T(8,128)S(1)}, u32[]{:S(2)}, u32[]{:S(2)}) collective-permute-start(f32[8,2048]{1,0:T(8,128)S(1)} %output_projection.1), channel_id=1, source_target_pairs={{0,2},{1,3},{2,0},{3,1},{4,6},{5,7},{6,4},{7,5},{8,10},{9,11},{10,... | collective-permute-start | bytes 196616 | tf_op jit(solution)/shard_map/ppermute | solution.py:43
  35.1 2.8 %collective-permute-done.9 = f32[8,2048]{1,0:T(8,128)S(1)} collective-permute-done((f32[8,2048]{1,0:T(8,128)S(1)}, f32[8,2048]{1,0:T(8,128)S(1)}, u32[]{:S(2)}, u32[]{:S(2)}) %collective-permute-start.9) | collective-permute-done | bytes 65568 | tf_op jit(solution)/shard_map/ppermute | solution.py:43
  37.9 0.1 collective-permute-start.10
  37.9 1.2 %collective-permute-done.10 = f32[8,2048]{1,0:T(8,128)S(1)} collective-permute-done((f32[8,2048]{1,0:T(8,128)S(1)}, f32[8,2048]{1,0:T(8,128)S(1)}, u32[]{:S(2)}, u32[]{:S(2)}) %collective-permute-start.10) | collective-permute-done | bytes 65568 | tf_op jit(solution)/shard_map/ppermute | solution.py:43
  39.2 0.6 %add_convert_fusion = bf16[2,4,2048]{2,1,0:T(4,128)(2,1)} fusion(f32[2,4,2048]{2,1,0:T(4,128)S(1)} %reshape.11, bf16[2,4,2048]{2,1,0:T(4,128)(2,1)S(1)} %copy-done.2), kind=kLoop, calls=%fused_computation | loop fusion | flops 49152 | bytes 131072 | tf_op jit(solution)/shard_map/convert_element_type | solution.py:417
  (25 shorter events, 0.1 us)
Async XLA Ops:
  0.6 31.7 %slice-start = ((s8[8388608]{0:T(1024)(128)(4,1)}), s8[4194304]{0:T(1024)(128)(4,1)S(1)}, s32[]{:S(2)}) async-start(s8[8388608]{0:T(1024)(128)(4,1)} %bitcast.2), calls=%async_computation | async-start | bytes 8388608
  0.6 8.2 %copy-start = (bf16[2048,2048]{1,0:T(8,128)(2,1)S(1)}, bf16[2048,2048]{1,0:T(8,128)(2,1)}, u32[]{:S(2)}) copy-start(bf16[2048,2048]{1,0:T(8,128)(2,1)} %wq_ref.1) | copy-start | bytes 25165828
  0.7 8.2 %copy-start.1 = (bf16[2048,2,256]{2,1,0:T(2,128)(2,1)S(1)}, bf16[2048,2,256]{2,1,0:T(2,128)(2,1)}, u32[]{:S(2)}) copy-start(bf16[2048,2,256]{2,1,0:T(2,128)(2,1)} %wkv_ref.1) | copy-start | bytes 6291460
  0.7 8.2 %copy-start.2 = (bf16[2,4,2048]{2,1,0:T(4,128)(2,1)S(1)}, bf16[2,4,2048]{2,1,0:T(4,128)(2,1)}, u32[]{:S(2)}) copy-start(bf16[2,4,2048]{2,1,0:T(4,128)(2,1)} %hidden_ref.1) | copy-start | bytes 98308
  0.7 8.2 %copy-start.3 = (bf16[2048]{0:T(1024)(128)(2,1)S(1)}, bf16[2048]{0:T(1024)(128)(2,1)}, u32[]{:S(2)}) copy-start(bf16[2048]{0:T(1024)(128)(2,1)} %param.12) | copy-start | bytes 12292
  0.7 31.7 %slice-start.1 = ((s8[8388608]{0:T(1024)(128)(4,1)}), s8[4194304]{0:T(1024)(128)(4,1)S(1)}, s32[]{:S(2)}) async-start(s8[8388608]{0:T(1024)(128)(4,1)} %bitcast.2), calls=%async_computation.1 | async-start | bytes 8388608
  3.1 20.5 %copy-start.4 = (s32[2,8,4]{1,2,0:T(4,128)S(1)}, s32[2,8,4]{1,2,0:T(4,128)}, u32[]{:S(2)}) copy-start(s32[2,8,4]{1,2,0:T(4,128)} %param.10) | copy-start | bytes 772
  3.1 20.5 %copy-start.5 = (f32[8,128]{1,0:T(8,128)S(1)}, f32[8,128]{1,0:T(8,128)}, u32[]{:S(2)}) copy-start(f32[8,128]{1,0:T(8,128)} %constant.5.clone.sin_ref) | copy-start | bytes 12292
  3.1 20.4 %copy-start.6 = (f32[8,128]{1,0:T(8,128)S(1)}, f32[8,128]{1,0:T(8,128)}, u32[]{:S(2)}) copy-start(f32[8,128]{1,0:T(8,128)} %constant.4.clone.cos_ref) | copy-start | bytes 12292
  3.1 20.4 %collective-permute-start = (bf16[256,256]{1,0:T(8,128)(2,1)S(1)}, bf16[256,256]{1,0:T(8,128)(2,1)S(1)}, u32[]{:S(2)}, u32[]{:S(2)}) collective-permute-start(bf16[256,256]{1,0:T(8,128)(2,1)S(1)} %get-tuple-element.12), channel_id=1, source_target_pairs={{0,12},{4,8},{8,4},{12,0},{1,13},{5,9},{9,5},{13,1},{2,14},{6,10},... | collective-permute-start | bytes 393224 | tf_op jit(solution)/shard_map/ppermute | solution.py:43
  8.2 15.3 %collective-permute-start.1 = (bf16[256,256]{1,0:T(8,128)(2,1)S(1)}, bf16[256,256]{1,0:T(8,128)(2,1)S(1)}, u32[]{:S(2)}, u32[]{:S(2)}) collective-permute-start(bf16[256,256]{1,0:T(8,128)(2,1)S(1)} %get-tuple-element.13), channel_id=1, source_target_pairs={{0,8},{4,12},{8,0},{12,4},{1,9},{5,13},{9,1},{13,5},{2,10},{6,14},... | collective-permute-start | bytes 393224 | tf_op jit(solution)/shard_map/ppermute | solution.py:43
  8.2 15.3 %collective-permute-start.2 = (bf16[256,256]{1,0:T(8,128)(2,1)S(1)}, bf16[256,256]{1,0:T(8,128)(2,1)S(1)}, u32[]{:S(2)}, u32[]{:S(2)}) collective-permute-start(bf16[256,256]{1,0:T(8,128)(2,1)S(1)} %get-tuple-element.14), channel_id=1, source_target_pairs={{0,4},{4,0},{8,12},{12,8},{1,5},{5,1},{9,13},{13,9},{2,6},{6,2},{1... | collective-permute-start | bytes 393224 | tf_op jit(solution)/shard_map/ppermute | solution.py:43
  11.0 7.3 %collective-permute-start.3 = (f32[48,128]{1,0:T(8,128)S(1)}, f32[48,128]{1,0:T(8,128)S(1)}, u32[]{:S(2)}, u32[]{:S(2)}) collective-permute-start(f32[48,128]{1,0:T(8,128)S(1)} %get-tuple-element.16), channel_id=1, source_target_pairs={{0,12},{4,8},{8,4},{12,0},{1,13},{5,9},{9,5},{13,1},{2,14},{6,10},... | collective-permute-start | bytes 73736 | tf_op jit(solution)/shard_map/ppermute | solution.py:43
  14.8 6.9 %collective-permute-start.4 = (f32[48,128]{1,0:T(8,128)S(1)}, f32[48,128]{1,0:T(8,128)S(1)}, u32[]{:S(2)}, u32[]{:S(2)}) collective-permute-start(f32[48,128]{1,0:T(8,128)S(1)} %get-tuple-element.17), channel_id=1, source_target_pairs={{0,8},{4,12},{8,0},{12,4},{1,9},{5,13},{9,1},{13,5},{2,10},{6,14},... | collective-permute-start | bytes 73736 | tf_op jit(solution)/shard_map/ppermute | solution.py:43
  18.3 5.2 %collective-permute-start.5 = (f32[48,128]{1,0:T(8,128)S(1)}, f32[48,128]{1,0:T(8,128)S(1)}, u32[]{:S(2)}, u32[]{:S(2)}) collective-permute-start(f32[48,128]{1,0:T(8,128)S(1)} %get-tuple-element.18), channel_id=1, source_target_pairs={{0,4},{4,0},{8,12},{12,8},{1,5},{5,1},{9,13},{13,9},{2,6},{6,2},{1... | collective-permute-start | bytes 73736 | tf_op jit(solution)/shard_map/ppermute | solution.py:43
  25.2 5.5 %collective-permute-start.8 = (bf16[32,128]{1,0:T(8,128)(2,1)S(1)}, bf16[32,128]{1,0:T(8,128)(2,1)S(1)}, u32[]{:S(2)}, u32[]{:S(2)}) collective-permute-start(bf16[32,128]{1,0:T(8,128)(2,1)S(1)} %get-tuple-element.21.refs_0_), channel_id=1, source_target_pairs={{0,12},{4,8},{8,4},{12,0},{1,13},{5,9},{9,5},{13,1},{2,14},{6,10},... | collective-permute-start | bytes 24584 | tf_op jit(solution)/shard_map/ppermute | solution.py:43
  27.6 4.5 %collective-permute-start.7 = (bf16[32,128]{1,0:T(8,128)(2,1)S(1)}, bf16[32,128]{1,0:T(8,128)(2,1)S(1)}, u32[]{:S(2)}, u32[]{:S(2)}) collective-permute-start(bf16[32,128]{1,0:T(8,128)(2,1)S(1)} %get-tuple-element.21.refs_0_), channel_id=1, source_target_pairs={{0,8},{4,12},{8,0},{12,4},{1,9},{5,13},{9,1},{13,5},{2,10},{6,14},... | collective-permute-start | bytes 24584 | tf_op jit(solution)/shard_map/ppermute | solution.py:43
  28.7 3.7 %collective-permute-start.6 = (bf16[32,128]{1,0:T(8,128)(2,1)S(1)}, bf16[32,128]{1,0:T(8,128)(2,1)S(1)}, u32[]{:S(2)}, u32[]{:S(2)}) collective-permute-start(bf16[32,128]{1,0:T(8,128)(2,1)S(1)} %get-tuple-element.21.refs_0_), channel_id=1, source_target_pairs={{0,4},{4,0},{8,12},{12,8},{1,5},{5,1},{9,13},{13,9},{2,6},{6,2},{1... | collective-permute-start | bytes 24584 | tf_op jit(solution)/shard_map/ppermute | solution.py:43
  33.6 4.3 %collective-permute-start.9 = (f32[8,2048]{1,0:T(8,128)S(1)}, f32[8,2048]{1,0:T(8,128)S(1)}, u32[]{:S(2)}, u32[]{:S(2)}) collective-permute-start(f32[8,2048]{1,0:T(8,128)S(1)} %output_projection.1), channel_id=1, source_target_pairs={{0,2},{1,3},{2,0},{3,1},{4,6},{5,7},{6,4},{7,5},{8,10},{9,11},{10,... | collective-permute-start | bytes 196616 | tf_op jit(solution)/shard_map/ppermute | solution.py:43
  37.9 1.3 %collective-permute-start.10 = (f32[8,2048]{1,0:T(8,128)S(1)}, f32[8,2048]{1,0:T(8,128)S(1)}, u32[]{:S(2)}, u32[]{:S(2)}) collective-permute-start(f32[8,2048]{1,0:T(8,128)S(1)} %add.9), channel_id=1, source_target_pairs={{0,1},{1,0},{2,3},{3,2},{4,5},{5,4},{6,7},{7,6},{8,9},{9,8},{10,11... | collective-permute-start | bytes 196616 | tf_op jit(solution)/shard_map/ppermute | solution.py:43

commit v6 on v5

--- a/solution.py
+++ b/solution.py
@@ -392,8 +392,9 @@
     if direct:
         partners = range(1, seq_count)
         blocks = pick(kept_blocks, source_cache, range(seq_count))
-        parts = project(blocks[0], *weights, pair_count, direct)
+        parts = list(project(blocks[0], *weights, pair_count, direct))
         blocks = [blocks[0]] + [swap(blocks[k], "seq", k) for k in partners]
+        parts[1], blocks[1] = lax.optimization_barrier((parts[1], blocks[1]))
         parts = [parts[0]] + [swap(parts[k], "seq", k) for k in partners]
         arrivals = blocks[::-1] + parts[::-1]
     else:

time: 40 us -> 39 us (0.975)
  starting transfers between devices: 19 us -> 16.2 us
  waiting for transfers between devices: 12 us -> 13.8 us
    ppermute x11, starting transfers between devices: 19 us -> 16.2 us  [swap(): return lax.ppermute(outgoing, axis, [(i, i ^ offset) for i in range(count)])]
    ppermute x11, waiting for transfers between devices: 12 us -> 13.8 us  [swap(): return lax.ppermute(outgoing, axis, [(i, i ^ offset) for i in range(count)])]
  transfers between devices with their start and end apart: 11 -> 11, of which waited for: 7 -> 6; matrix products, arithmetic and copies ran while one was open for 0% -> 0% of each run, Pallas kernels for 5% -> 5%
where the time goes in v6:
time: 39 us; the launch traced here: 38.8 us
  starting transfers between devices  16.2 us (42%)
  waiting for transfers between devices  13.8 us (35%)
  Pallas kernels  7.28 us (19%)
  between operations  0.8 us (2%)
  other arithmetic  0.65 us (2%)
    ppermute x11, starting transfers between devices, swap(): return lax.ppermute(outgoing, axis, [(i, i ^ offset) for i in range(count)])  16.2 us
    ppermute x11, waiting for transfers between devices, swap(): return lax.ppermute(outgoing, axis, [(i, i ^ offset) for i in range(count)])  13.8 us
    pallas_call x1, Pallas kernels, pick(): pl.pallas_call(functools.partial(pick_kernel, offsets), out_shape=shapes,...  2.36 us
    pallas_call x1, Pallas kernels, project(): pl.pallas_call(functools.partial(project_kernel, direct), out_shape=shape...  2.12 us
    pallas_call x1, Pallas kernels, attend(): pl.pallas_call(functools.partial(attend_kernel, direct, source_blocks, he...  1.62 us
    pallas_call x1, Pallas kernels, output(): pl.pallas_call(functools.partial(output_kernel, heads_local), out_shape=j...  1.19 us
  transfers between devices with their start and end apart: 11, of which 6 were waited for; matrix products, arithmetic and copies ran while one was open for 0% of the time, Pallas kernels for 5%

profile of v6, /device:TPU:0, one launch (start us, length us, event | category | flops | bytes accessed | tf_op | source)
XLA Modules:
  0.0 38.8 jit_solution(6014857254890368207)
XLA Ops:
  0.7 2.4 %pick_blocks.1 = (bf16[256,256]{1,0:T(8,128)(2,1)S(1)}, bf16[256,256]{1,0:T(8,128)(2,1)S(1)}, bf16[256,256]{1,0:T(8,128)(2,1)S(1)}, bf16[256,256]{1,0:T(8,128)(2,1)S(1)}) custom-call(s32[2,4,8]{2,1,0:T(4,128)} %bitcast.5, bf16[2,2,512,256]{3,2,1,0:T(8,128)(2,1)} %cache_ref.1), custom_call_target="tpu_custom_call" | custom-call | flops 10000000000 | tf_op jit(solution)/shard_map/pick_blocks/pallas_call | solution.py:99
  3.1 0.0 copy-start.4
  3.1 0.0 copy-start.5
  3.1 0.0 copy-start.6
  3.1 3.1 %collective-permute-start.2 = (bf16[256,256]{1,0:T(8,128)(2,1)S(1)}, bf16[256,256]{1,0:T(8,128)(2,1)S(1)}, u32[]{:S(2)}, u32[]{:S(2)}) collective-permute-start(bf16[256,256]{1,0:T(8,128)(2,1)S(1)} %get-tuple-element.18), channel_id=1, source_target_pairs={{0,4},{4,0},{8,12},{12,8},{1,5},{5,1},{9,13},{13,9},{2,6},{6,2},{1... | collective-permute-start | bytes 393224 | tf_op jit(solution)/shard_map/ppermute | solution.py:43
  6.2 2.5 %collective-permute-start = (bf16[256,256]{1,0:T(8,128)(2,1)S(1)}, bf16[256,256]{1,0:T(8,128)(2,1)S(1)}, u32[]{:S(2)}, u32[]{:S(2)}) collective-permute-start(bf16[256,256]{1,0:T(8,128)(2,1)S(1)} %get-tuple-element.14), channel_id=1, source_target_pairs={{0,12},{4,8},{8,4},{12,0},{1,13},{5,9},{9,5},{13,1},{2,14},{6,10},... | collective-permute-start | bytes 393224 | tf_op jit(solution)/shard_map/ppermute | solution.py:43
  8.7 0.1 collective-permute-start.1
  8.8 2.1 %project.1 = (f32[48,128]{1,0:T(8,128)S(1)}, f32[48,128]{1,0:T(8,128)S(1)}, f32[48,128]{1,0:T(8,128)S(1)}, f32[48,128]{1,0:T(8,128)S(1)}) custom-call(bf16[256,256]{1,0:T(8,128)(2,1)S(1)} %get-tuple-element.16.after_ref.refs_3_, bf16[2,4,2048]{2,1,0:T(4,128)(2,1)S(1)} %copy-done.2, bf16[16,128]{1,0:T(8,128)(2,1)S(1)} %bitcast.4, ...), custom_call_target="tpu_custom_call" | custom-call | flops 83886080 | bytes 10485760 | tf_op jit(solution)/shard_map/project/pallas_call | solution.py:193
  10.9 3.0 %collective-permute-start.3 = (f32[48,128]{1,0:T(8,128)S(1)}, f32[48,128]{1,0:T(8,128)S(1)}, u32[]{:S(2)}, u32[]{:S(2)}) collective-permute-start(f32[48,128]{1,0:T(8,128)S(1)} %get-tuple-element.20), channel_id=1, source_target_pairs={{0,12},{4,8},{8,4},{12,0},{1,13},{5,9},{9,5},{13,1},{2,14},{6,10},... | collective-permute-start | bytes 73736 | tf_op jit(solution)/shard_map/ppermute | solution.py:43
  13.9 0.3 collective-permute-start.4
  14.3 1.1 %collective-permute-start.5 = (f32[48,128]{1,0:T(8,128)S(1)}, f32[48,128]{1,0:T(8,128)S(1)}, u32[]{:S(2)}, u32[]{:S(2)}) collective-permute-start(f32[48,128]{1,0:T(8,128)S(1)} %get-tuple-element.22), channel_id=1, source_target_pairs={{0,4},{4,0},{8,12},{12,8},{1,5},{5,1},{9,13},{13,9},{2,6},{6,2},{1... | collective-permute-start | bytes 73736 | tf_op jit(solution)/shard_map/ppermute | solution.py:43
  15.4 3.2 %collective-permute-done.3.refs_4_ = f32[48,128]{1,0:T(8,128)S(1)} collective-permute-done((f32[48,128]{1,0:T(8,128)S(1)}, f32[48,128]{1,0:T(8,128)S(1)}, u32[]{:S(2)}, u32[]{:S(2)}) %collective-permute-start.3) | collective-permute-done | bytes 24608 | tf_op jit(solution)/shard_map/ppermute | solution.py:43
  18.6 3.9 %collective-permute-done.4.refs_5_ = f32[48,128]{1,0:T(8,128)S(1)} collective-permute-done((f32[48,128]{1,0:T(8,128)S(1)}, f32[48,128]{1,0:T(8,128)S(1)}, u32[]{:S(2)}, u32[]{:S(2)}) %collective-permute-start.4) | collective-permute-done | bytes 24608 | tf_op jit(solution)/shard_map/ppermute | solution.py:43
  22.6 1.6 %attend.1 = (bf16[1,1,512,256]{3,2,1,0:T(8,128)(2,1)}, bf16[32,128]{1,0:T(8,128)(2,1)S(1)}) custom-call(s32[2,4,8]{2,1,0:T(4,128)S(1)} %bitcast.6, f32[8,128]{1,0:T(8,128)S(1)} %copy-done.6, f32[8,128]{1,0:T(8,128)S(1)} %copy-done.5, bf16[256,256]{1,0:T(8,128)(2,1)S(1)} %collective-permute-done.refs_0_, bf16[256,256]{1,0:T(8,128)(2,1)S(1)} %collective-permute-done.1.refs_1_, ...), custom_call_target="tpu_custom_call" | custom-call | tf_op jit(solution)/shard_map/attend/pallas_call | solution.py:314
  24.2 2.6 %collective-permute-start.8 = (bf16[32,128]{1,0:T(8,128)(2,1)S(1)}, bf16[32,128]{1,0:T(8,128)(2,1)S(1)}, u32[]{:S(2)}, u32[]{:S(2)}) collective-permute-start(bf16[32,128]{1,0:T(8,128)(2,1)S(1)} %get-tuple-element.25.refs_0_), channel_id=1, source_target_pairs={{0,12},{4,8},{8,4},{12,0},{1,13},{5,9},{9,5},{13,1},{2,14},{6,10},... | collective-permute-start | bytes 24584 | tf_op jit(solution)/shard_map/ppermute | solution.py:43
  26.7 1.9 %collective-permute-start.6 = (bf16[32,128]{1,0:T(8,128)(2,1)S(1)}, bf16[32,128]{1,0:T(8,128)(2,1)S(1)}, u32[]{:S(2)}, u32[]{:S(2)}) collective-permute-start(bf16[32,128]{1,0:T(8,128)(2,1)S(1)} %get-tuple-element.25.refs_0_), channel_id=1, source_target_pairs={{0,4},{4,0},{8,12},{12,8},{1,5},{5,1},{9,13},{13,9},{2,6},{6,2},{1... | collective-permute-start | bytes 24584 | tf_op jit(solution)/shard_map/ppermute | solution.py:43
  28.6 1.1 %collective-permute-done.8.refs_3_ = bf16[32,128]{1,0:T(8,128)(2,1)S(1)} collective-permute-done((bf16[32,128]{1,0:T(8,128)(2,1)S(1)}, bf16[32,128]{1,0:T(8,128)(2,1)S(1)}, u32[]{:S(2)}, u32[]{:S(2)}) %collective-permute-start.8) | collective-permute-done | bytes 8224 | tf_op jit(solution)/shard_map/ppermute | solution.py:43
  29.7 1.6 %collective-permute-done.7.refs_2_ = bf16[32,128]{1,0:T(8,128)(2,1)S(1)} collective-permute-done((bf16[32,128]{1,0:T(8,128)(2,1)S(1)}, bf16[32,128]{1,0:T(8,128)(2,1)S(1)}, u32[]{:S(2)}, u32[]{:S(2)}) %collective-permute-start.7) | collective-permute-done | bytes 8224 | tf_op jit(solution)/shard_map/ppermute | solution.py:43
  31.3 1.2 %output_projection.1 = f32[8,2048]{1,0:T(8,128)S(1)} custom-call(bf16[2048,2048]{1,0:T(8,128)(2,1)S(1)} %bitcast.3, bf16[32,128]{1,0:T(8,128)(2,1)S(1)} %get-tuple-element.25.refs_0_, bf16[32,128]{1,0:T(8,128)(2,1)S(1)} %collective-permute-done.6.refs_1_, bf16[32,128]{1,0:T(8,128)(2,1)S(1)} %collective-permute-done.7.refs_2_, ...), custom_call_target="tpu_custom_call" | custom-call | tf_op jit(solution)/shard_map/output_projection/pallas_call | solution.py:371
  32.5 1.5 %collective-permute-start.9 = (f32[8,2048]{1,0:T(8,128)S(1)}, f32[8,2048]{1,0:T(8,128)S(1)}, u32[]{:S(2)}, u32[]{:S(2)}) collective-permute-start(f32[8,2048]{1,0:T(8,128)S(1)} %output_projection.1), channel_id=1, source_target_pairs={{0,2},{1,3},{2,0},{3,1},{4,6},{5,7},{6,4},{7,5},{8,10},{9,11},{10,... | collective-permute-start | bytes 196616 | tf_op jit(solution)/shard_map/ppermute | solution.py:43
  34.0 2.8 %collective-permute-done.9 = f32[8,2048]{1,0:T(8,128)S(1)} collective-permute-done((f32[8,2048]{1,0:T(8,128)S(1)}, f32[8,2048]{1,0:T(8,128)S(1)}, u32[]{:S(2)}, u32[]{:S(2)}) %collective-permute-start.9) | collective-permute-done | bytes 65568 | tf_op jit(solution)/shard_map/ppermute | solution.py:43
  36.8 0.1 collective-permute-start.10
  36.9 1.2 %collective-permute-done.10 = f32[8,2048]{1,0:T(8,128)S(1)} collective-permute-done((f32[8,2048]{1,0:T(8,128)S(1)}, f32[8,2048]{1,0:T(8,128)S(1)}, u32[]{:S(2)}, u32[]{:S(2)}) %collective-permute-start.10) | collective-permute-done | bytes 65568 | tf_op jit(solution)/shard_map/ppermute | solution.py:43
  38.2 0.6 %add_convert_fusion = bf16[2,4,2048]{2,1,0:T(4,128)(2,1)} fusion(f32[2,4,2048]{2,1,0:T(4,128)S(1)} %reshape.11, bf16[2,4,2048]{2,1,0:T(4,128)(2,1)S(1)} %copy-done.2), kind=kLoop, calls=%fused_computation | loop fusion | flops 49152 | bytes 131072 | tf_op jit(solution)/shard_map/convert_element_type | solution.py:418
  (25 shorter events, 0.1 us)
Async XLA Ops:
  0.6 30.7 %slice-start = ((s8[8388608]{0:T(1024)(128)(4,1)}), s8[4194304]{0:T(1024)(128)(4,1)S(1)}, s32[]{:S(2)}) async-start(s8[8388608]{0:T(1024)(128)(4,1)} %bitcast.2), calls=%async_computation | async-start | bytes 8388608
  0.6 8.1 %copy-start = (bf16[2048,2048]{1,0:T(8,128)(2,1)S(1)}, bf16[2048,2048]{1,0:T(8,128)(2,1)}, u32[]{:S(2)}) copy-start(bf16[2048,2048]{1,0:T(8,128)(2,1)} %wq_ref.1) | copy-start | bytes 25165828
  0.7 8.1 %copy-start.1 = (bf16[2048,2,256]{2,1,0:T(2,128)(2,1)S(1)}, bf16[2048,2,256]{2,1,0:T(2,128)(2,1)}, u32[]{:S(2)}) copy-start(bf16[2048,2,256]{2,1,0:T(2,128)(2,1)} %wkv_ref.1) | copy-start | bytes 6291460
  0.7 8.1 %copy-start.2 = (bf16[2,4,2048]{2,1,0:T(4,128)(2,1)S(1)}, bf16[2,4,2048]{2,1,0:T(4,128)(2,1)}, u32[]{:S(2)}) copy-start(bf16[2,4,2048]{2,1,0:T(4,128)(2,1)} %hidden_ref.1) | copy-start | bytes 98308
  0.7 8.1 %copy-start.3 = (bf16[2048]{0:T(1024)(128)(2,1)S(1)}, bf16[2048]{0:T(1024)(128)(2,1)}, u32[]{:S(2)}) copy-start(bf16[2048]{0:T(1024)(128)(2,1)} %param.12) | copy-start | bytes 12292
  0.7 30.6 %slice-start.1 = ((s8[8388608]{0:T(1024)(128)(4,1)}), s8[4194304]{0:T(1024)(128)(4,1)S(1)}, s32[]{:S(2)}) async-start(s8[8388608]{0:T(1024)(128)(4,1)} %bitcast.2), calls=%async_computation.1 | async-start | bytes 8388608
  3.1 19.5 %copy-start.4 = (s32[2,8,4]{1,2,0:T(4,128)S(1)}, s32[2,8,4]{1,2,0:T(4,128)}, u32[]{:S(2)}) copy-start(s32[2,8,4]{1,2,0:T(4,128)} %param.10) | copy-start | bytes 772
  3.1 19.5 %copy-start.5 = (f32[8,128]{1,0:T(8,128)S(1)}, f32[8,128]{1,0:T(8,128)}, u32[]{:S(2)}) copy-start(f32[8,128]{1,0:T(8,128)} %constant.5.clone.sin_ref) | copy-start | bytes 12292
  3.1 19.5 %copy-start.6 = (f32[8,128]{1,0:T(8,128)S(1)}, f32[8,128]{1,0:T(8,128)}, u32[]{:S(2)}) copy-start(f32[8,128]{1,0:T(8,128)} %constant.4.clone.cos_ref) | copy-start | bytes 12292
  3.1 11.2 %collective-permute-start.2 = (bf16[256,256]{1,0:T(8,128)(2,1)S(1)}, bf16[256,256]{1,0:T(8,128)(2,1)S(1)}, u32[]{:S(2)}, u32[]{:S(2)}) collective-permute-start(bf16[256,256]{1,0:T(8,128)(2,1)S(1)} %get-tuple-element.18), channel_id=1, source_target_pairs={{0,4},{4,0},{8,12},{12,8},{1,5},{5,1},{9,13},{13,9},{2,6},{6,2},{1... | collective-permute-start | bytes 393224 | tf_op jit(solution)/shard_map/ppermute | solution.py:43
  6.2 16.3 %collective-permute-start = (bf16[256,256]{1,0:T(8,128)(2,1)S(1)}, bf16[256,256]{1,0:T(8,128)(2,1)S(1)}, u32[]{:S(2)}, u32[]{:S(2)}) collective-permute-start(bf16[256,256]{1,0:T(8,128)(2,1)S(1)} %get-tuple-element.14), channel_id=1, source_target_pairs={{0,12},{4,8},{8,4},{12,0},{1,13},{5,9},{9,5},{13,1},{2,14},{6,10},... | collective-permute-start | bytes 393224 | tf_op jit(solution)/shard_map/ppermute | solution.py:43
  8.7 13.9 %collective-permute-start.1 = (bf16[256,256]{1,0:T(8,128)(2,1)S(1)}, bf16[256,256]{1,0:T(8,128)(2,1)S(1)}, u32[]{:S(2)}, u32[]{:S(2)}) collective-permute-start(bf16[256,256]{1,0:T(8,128)(2,1)S(1)} %get-tuple-element.15), channel_id=1, source_target_pairs={{0,8},{4,12},{8,0},{12,4},{1,9},{5,13},{9,1},{13,5},{2,10},{6,14},... | collective-permute-start | bytes 393224 | tf_op jit(solution)/shard_map/ppermute | solution.py:43
  10.9 7.7 %collective-permute-start.3 = (f32[48,128]{1,0:T(8,128)S(1)}, f32[48,128]{1,0:T(8,128)S(1)}, u32[]{:S(2)}, u32[]{:S(2)}) collective-permute-start(f32[48,128]{1,0:T(8,128)S(1)} %get-tuple-element.20), channel_id=1, source_target_pairs={{0,12},{4,8},{8,4},{12,0},{1,13},{5,9},{9,5},{13,1},{2,14},{6,10},... | collective-permute-start | bytes 73736 | tf_op jit(solution)/shard_map/ppermute | solution.py:43
  13.9 8.6 %collective-permute-start.4 = (f32[48,128]{1,0:T(8,128)S(1)}, f32[48,128]{1,0:T(8,128)S(1)}, u32[]{:S(2)}, u32[]{:S(2)}) collective-permute-start(f32[48,128]{1,0:T(8,128)S(1)} %get-tuple-element.21), channel_id=1, source_target_pairs={{0,8},{4,12},{8,0},{12,4},{1,9},{5,13},{9,1},{13,5},{2,10},{6,14},... | collective-permute-start | bytes 73736 | tf_op jit(solution)/shard_map/ppermute | solution.py:43
  14.3 8.3 %collective-permute-start.5 = (f32[48,128]{1,0:T(8,128)S(1)}, f32[48,128]{1,0:T(8,128)S(1)}, u32[]{:S(2)}, u32[]{:S(2)}) collective-permute-start(f32[48,128]{1,0:T(8,128)S(1)} %get-tuple-element.22), channel_id=1, source_target_pairs={{0,4},{4,0},{8,12},{12,8},{1,5},{5,1},{9,13},{13,9},{2,6},{6,2},{1... | collective-permute-start | bytes 73736 | tf_op jit(solution)/shard_map/ppermute | solution.py:43
  24.2 5.5 %collective-permute-start.8 = (bf16[32,128]{1,0:T(8,128)(2,1)S(1)}, bf16[32,128]{1,0:T(8,128)(2,1)S(1)}, u32[]{:S(2)}, u32[]{:S(2)}) collective-permute-start(bf16[32,128]{1,0:T(8,128)(2,1)S(1)} %get-tuple-element.25.refs_0_), channel_id=1, source_target_pairs={{0,12},{4,8},{8,4},{12,0},{1,13},{5,9},{9,5},{13,1},{2,14},{6,10},... | collective-permute-start | bytes 24584 | tf_op jit(solution)/shard_map/ppermute | solution.py:43
  26.7 4.5 %collective-permute-start.7 = (bf16[32,128]{1,0:T(8,128)(2,1)S(1)}, bf16[32,128]{1,0:T(8,128)(2,1)S(1)}, u32[]{:S(2)}, u32[]{:S(2)}) collective-permute-start(bf16[32,128]{1,0:T(8,128)(2,1)S(1)} %get-tuple-element.25.refs_0_), channel_id=1, source_target_pairs={{0,8},{4,12},{8,0},{12,4},{1,9},{5,13},{9,1},{13,5},{2,10},{6,14},... | collective-permute-start | bytes 24584 | tf_op jit(solution)/shard_map/ppermute | solution.py:43
  26.7 4.5 %collective-permute-start.6 = (bf16[32,128]{1,0:T(8,128)(2,1)S(1)}, bf16[32,128]{1,0:T(8,128)(2,1)S(1)}, u32[]{:S(2)}, u32[]{:S(2)}) collective-permute-start(bf16[32,128]{1,0:T(8,128)(2,1)S(1)} %get-tuple-element.25.refs_0_), channel_id=1, source_target_pairs={{0,4},{4,0},{8,12},{12,8},{1,5},{5,1},{9,13},{13,9},{2,6},{6,2},{1... | collective-permute-start | bytes 24584 | tf_op jit(solution)/shard_map/ppermute | solution.py:43
  32.5 4.3 %collective-permute-start.9 = (f32[8,2048]{1,0:T(8,128)S(1)}, f32[8,2048]{1,0:T(8,128)S(1)}, u32[]{:S(2)}, u32[]{:S(2)}) collective-permute-start(f32[8,2048]{1,0:T(8,128)S(1)} %output_projection.1), channel_id=1, source_target_pairs={{0,2},{1,3},{2,0},{3,1},{4,6},{5,7},{6,4},{7,5},{8,10},{9,11},{10,... | collective-permute-start | bytes 196616 | tf_op jit(solution)/shard_map/ppermute | solution.py:43
  36.8 1.3 %collective-permute-start.10 = (f32[8,2048]{1,0:T(8,128)S(1)}, f32[8,2048]{1,0:T(8,128)S(1)}, u32[]{:S(2)}, u32[]{:S(2)}) collective-permute-start(f32[8,2048]{1,0:T(8,128)S(1)} %add.9), channel_id=1, source_target_pairs={{0,1},{1,0},{2,3},{3,2},{4,5},{5,4},{6,7},{7,6},{8,9},{9,8},{10,11... | collective-permute-start | bytes 196616 | tf_op jit(solution)/shard_map/ppermute | solution.py:43

commit v7 on v6

--- a/solution.py
+++ b/solution.py
@@ -394,7 +394,7 @@
         blocks = pick(kept_blocks, source_cache, range(seq_count))
         parts = list(project(blocks[0], *weights, pair_count, direct))
         blocks = [blocks[0]] + [swap(blocks[k], "seq", k) for k in partners]
-        parts[1], blocks[1] = lax.optimization_barrier((parts[1], blocks[1]))
+        parts[1], blocks[3] = lax.optimization_barrier((parts[1], blocks[3]))
         parts = [parts[0]] + [swap(parts[k], "seq", k) for k in partners]
         arrivals = blocks[::-1] + parts[::-1]
     else:

time: 39 us -> 37.7 us (0.967)
  waiting for transfers between devices: 13.8 us -> 9.37 us
  starting transfers between devices: 16.2 us -> 19.3 us
    ppermute x11, waiting for transfers between devices: 13.8 us -> 9.37 us  [swap(): return lax.ppermute(outgoing, axis, [(i, i ^ offset) for i in range(count)])]
    ppermute x11, starting transfers between devices: 16.2 us -> 19.3 us  [swap(): return lax.ppermute(outgoing, axis, [(i, i ^ offset) for i in range(count)])]
  transfers between devices with their start and end apart: 11 -> 11, of which waited for: 6 -> 5; matrix products, arithmetic and copies ran while one was open for 0% -> 0% of each run, Pallas kernels for 5% -> 6%
where the time goes in v7:
time: 37.7 us; the launch traced here: 37.5 us
  starting transfers between devices  19.3 us (51%)
  waiting for transfers between devices  9.37 us (25%)
  Pallas kernels  7.28 us (19%)
  between operations  0.8 us (2%)
  other arithmetic  0.65 us (2%)
    ppermute x11, starting transfers between devices, swap(): return lax.ppermute(outgoing, axis, [(i, i ^ offset) for i in range(count)])  19.3 us
    ppermute x11, waiting for transfers between devices, swap(): return lax.ppermute(outgoing, axis, [(i, i ^ offset) for i in range(count)])  9.37 us
    pallas_call x1, Pallas kernels, pick(): pl.pallas_call(functools.partial(pick_kernel, offsets), out_shape=shapes,...  2.36 us
    pallas_call x1, Pallas kernels, project(): pl.pallas_call(functools.partial(project_kernel, direct), out_shape=shape...  2.12 us
    pallas_call x1, Pallas kernels, attend(): pl.pallas_call(functools.partial(attend_kernel, direct, source_blocks, he...  1.62 us
    pallas_call x1, Pallas kernels, output(): pl.pallas_call(functools.partial(output_kernel, heads_local), out_shape=j...  1.19 us
  transfers between devices with their start and end apart: 11, of which 5 were waited for; matrix products, arithmetic and copies ran while one was open for 0% of the time, Pallas kernels for 6%

profile of v7, /device:TPU:0, one launch (start us, length us, event | category | flops | bytes accessed | tf_op | source)
XLA Modules:
  0.0 37.5 jit_solution(13859358540358470420)
XLA Ops:
  0.6 0.0 slice-start
  0.7 0.0 slice-start.1
  0.7 2.4 %pick_blocks.1 = (bf16[256,256]{1,0:T(8,128)(2,1)S(1)}, bf16[256,256]{1,0:T(8,128)(2,1)S(1)}, bf16[256,256]{1,0:T(8,128)(2,1)S(1)}, bf16[256,256]{1,0:T(8,128)(2,1)S(1)}) custom-call(s32[2,4,8]{2,1,0:T(4,128)} %bitcast.5, bf16[2,2,512,256]{3,2,1,0:T(8,128)(2,1)} %cache_ref.1), custom_call_target="tpu_custom_call" | custom-call | flops 10000000000 | tf_op jit(solution)/shard_map/pick_blocks/pallas_call | solution.py:99
  3.1 0.0 copy-start.4
  3.1 0.0 copy-start.5
  3.1 0.0 copy-start.6
  3.1 5.1 %collective-permute-start = (bf16[256,256]{1,0:T(8,128)(2,1)S(1)}, bf16[256,256]{1,0:T(8,128)(2,1)S(1)}, u32[]{:S(2)}, u32[]{:S(2)}) collective-permute-start(bf16[256,256]{1,0:T(8,128)(2,1)S(1)} %get-tuple-element.16), channel_id=1, source_target_pairs={{0,12},{4,8},{8,4},{12,0},{1,13},{5,9},{9,5},{13,1},{2,14},{6,10},... | collective-permute-start | bytes 393224 | tf_op jit(solution)/shard_map/ppermute | solution.py:43
  8.2 0.6 %collective-permute-start.2 = (bf16[256,256]{1,0:T(8,128)(2,1)S(1)}, bf16[256,256]{1,0:T(8,128)(2,1)S(1)}, u32[]{:S(2)}, u32[]{:S(2)}) collective-permute-start(bf16[256,256]{1,0:T(8,128)(2,1)S(1)} %get-tuple-element.19), channel_id=1, source_target_pairs={{0,4},{4,0},{8,12},{12,8},{1,5},{5,1},{9,13},{13,9},{2,6},{6,2},{1... | collective-permute-start | bytes 393224 | tf_op jit(solution)/shard_map/ppermute | solution.py:43
  8.9 2.1 %project.1 = (f32[48,128]{1,0:T(8,128)S(1)}, f32[48,128]{1,0:T(8,128)S(1)}, f32[48,128]{1,0:T(8,128)S(1)}, f32[48,128]{1,0:T(8,128)S(1)}) custom-call(bf16[256,256]{1,0:T(8,128)(2,1)S(1)} %get-tuple-element.14.after_ref.refs_3_, bf16[2,4,2048]{2,1,0:T(4,128)(2,1)S(1)} %copy-done.2, bf16[16,128]{1,0:T(8,128)(2,1)S(1)} %bitcast.4, ...), custom_call_target="tpu_custom_call" | custom-call | flops 83886080 | bytes 10485760 | tf_op jit(solution)/shard_map/project/pallas_call | solution.py:193
  11.0 3.8 %collective-permute-start.3 = (f32[48,128]{1,0:T(8,128)S(1)}, f32[48,128]{1,0:T(8,128)S(1)}, u32[]{:S(2)}, u32[]{:S(2)}) collective-permute-start(f32[48,128]{1,0:T(8,128)S(1)} %get-tuple-element.20), channel_id=1, source_target_pairs={{0,12},{4,8},{8,4},{12,0},{1,13},{5,9},{9,5},{13,1},{2,14},{6,10},... | collective-permute-start | bytes 73736 | tf_op jit(solution)/shard_map/ppermute | solution.py:43
  14.8 0.0 collective-permute-start.4
  14.8 3.7 %collective-permute-start.5 = (f32[48,128]{1,0:T(8,128)S(1)}, f32[48,128]{1,0:T(8,128)S(1)}, u32[]{:S(2)}, u32[]{:S(2)}) collective-permute-start(f32[48,128]{1,0:T(8,128)S(1)} %get-tuple-element.22), channel_id=1, source_target_pairs={{0,4},{4,0},{8,12},{12,8},{1,5},{5,1},{9,13},{13,9},{2,6},{6,2},{1... | collective-permute-start | bytes 73736 | tf_op jit(solution)/shard_map/ppermute | solution.py:43
  18.5 2.8 %collective-permute-done.4.refs_5_ = f32[48,128]{1,0:T(8,128)S(1)} collective-permute-done((f32[48,128]{1,0:T(8,128)S(1)}, f32[48,128]{1,0:T(8,128)S(1)}, u32[]{:S(2)}, u32[]{:S(2)}) %collective-permute-start.4) | collective-permute-done | bytes 24608 | tf_op jit(solution)/shard_map/ppermute | solution.py:43
  21.4 1.6 %attend.1 = (bf16[1,1,512,256]{3,2,1,0:T(8,128)(2,1)}, bf16[32,128]{1,0:T(8,128)(2,1)S(1)}) custom-call(s32[2,4,8]{2,1,0:T(4,128)S(1)} %bitcast.6, f32[8,128]{1,0:T(8,128)S(1)} %copy-done.6, f32[8,128]{1,0:T(8,128)S(1)} %copy-done.5, bf16[256,256]{1,0:T(8,128)(2,1)S(1)} %collective-permute-done.refs_0_, bf16[256,256]{1,0:T(8,128)(2,1)S(1)} %collective-permute-done.1.refs_1_, ...), custom_call_target="tpu_custom_call" | custom-call | tf_op jit(solution)/shard_map/attend/pallas_call | solution.py:314
  23.1 2.4 %collective-permute-start.8 = (bf16[32,128]{1,0:T(8,128)(2,1)S(1)}, bf16[32,128]{1,0:T(8,128)(2,1)S(1)}, u32[]{:S(2)}, u32[]{:S(2)}) collective-permute-start(bf16[32,128]{1,0:T(8,128)(2,1)S(1)} %get-tuple-element.25.refs_0_), channel_id=1, source_target_pairs={{0,12},{4,8},{8,4},{12,0},{1,13},{5,9},{9,5},{13,1},{2,14},{6,10},... | collective-permute-start | bytes 24584 | tf_op jit(solution)/shard_map/ppermute | solution.py:43
  25.5 2.1 %collective-permute-start.6 = (bf16[32,128]{1,0:T(8,128)(2,1)S(1)}, bf16[32,128]{1,0:T(8,128)(2,1)S(1)}, u32[]{:S(2)}, u32[]{:S(2)}) collective-permute-start(bf16[32,128]{1,0:T(8,128)(2,1)S(1)} %get-tuple-element.25.refs_0_), channel_id=1, source_target_pairs={{0,4},{4,0},{8,12},{12,8},{1,5},{5,1},{9,13},{13,9},{2,6},{6,2},{1... | collective-permute-start | bytes 24584 | tf_op jit(solution)/shard_map/ppermute | solution.py:43
  27.5 1.1 %collective-permute-done.8.refs_3_ = bf16[32,128]{1,0:T(8,128)(2,1)S(1)} collective-permute-done((bf16[32,128]{1,0:T(8,128)(2,1)S(1)}, bf16[32,128]{1,0:T(8,128)(2,1)S(1)}, u32[]{:S(2)}, u32[]{:S(2)}) %collective-permute-start.8) | collective-permute-done | bytes 8224 | tf_op jit(solution)/shard_map/ppermute | solution.py:43
  28.6 1.4 %collective-permute-done.7.refs_2_ = bf16[32,128]{1,0:T(8,128)(2,1)S(1)} collective-permute-done((bf16[32,128]{1,0:T(8,128)(2,1)S(1)}, bf16[32,128]{1,0:T(8,128)(2,1)S(1)}, u32[]{:S(2)}, u32[]{:S(2)}) %collective-permute-start.7) | collective-permute-done | bytes 8224 | tf_op jit(solution)/shard_map/ppermute | solution.py:43
  30.0 1.2 %output_projection.1 = f32[8,2048]{1,0:T(8,128)S(1)} custom-call(bf16[2048,2048]{1,0:T(8,128)(2,1)S(1)} %bitcast.3, bf16[32,128]{1,0:T(8,128)(2,1)S(1)} %get-tuple-element.25.refs_0_, bf16[32,128]{1,0:T(8,128)(2,1)S(1)} %collective-permute-done.6.refs_1_, bf16[32,128]{1,0:T(8,128)(2,1)S(1)} %collective-permute-done.7.refs_2_, ...), custom_call_target="tpu_custom_call" | custom-call | tf_op jit(solution)/shard_map/output_projection/pallas_call | solution.py:371
  31.2 1.5 %collective-permute-start.9 = (f32[8,2048]{1,0:T(8,128)S(1)}, f32[8,2048]{1,0:T(8,128)S(1)}, u32[]{:S(2)}, u32[]{:S(2)}) collective-permute-start(f32[8,2048]{1,0:T(8,128)S(1)} %output_projection.1), channel_id=1, source_target_pairs={{0,2},{1,3},{2,0},{3,1},{4,6},{5,7},{6,4},{7,5},{8,10},{9,11},{10,... | collective-permute-start | bytes 196616 | tf_op jit(solution)/shard_map/ppermute | solution.py:43
  32.7 2.8 %collective-permute-done.9 = f32[8,2048]{1,0:T(8,128)S(1)} collective-permute-done((f32[8,2048]{1,0:T(8,128)S(1)}, f32[8,2048]{1,0:T(8,128)S(1)}, u32[]{:S(2)}, u32[]{:S(2)}) %collective-permute-start.9) | collective-permute-done | bytes 65568 | tf_op jit(solution)/shard_map/ppermute | solution.py:43
  35.5 0.1 collective-permute-start.10
  35.6 1.2 %collective-permute-done.10 = f32[8,2048]{1,0:T(8,128)S(1)} collective-permute-done((f32[8,2048]{1,0:T(8,128)S(1)}, f32[8,2048]{1,0:T(8,128)S(1)}, u32[]{:S(2)}, u32[]{:S(2)}) %collective-permute-start.10) | collective-permute-done | bytes 65568 | tf_op jit(solution)/shard_map/ppermute | solution.py:43
  36.9 0.6 %add_convert_fusion = bf16[2,4,2048]{2,1,0:T(4,128)(2,1)} fusion(f32[2,4,2048]{2,1,0:T(4,128)S(1)} %reshape.11, bf16[2,4,2048]{2,1,0:T(4,128)(2,1)S(1)} %copy-done.2), kind=kLoop, calls=%fused_computation | loop fusion | flops 49152 | bytes 131072 | tf_op jit(solution)/shard_map/convert_element_type | solution.py:418
  (25 shorter events, 0.1 us)
Async XLA Ops:
  0.6 29.4 %slice-start = ((s8[8388608]{0:T(1024)(128)(4,1)}), s8[4194304]{0:T(1024)(128)(4,1)S(1)}, s32[]{:S(2)}) async-start(s8[8388608]{0:T(1024)(128)(4,1)} %bitcast.2), calls=%async_computation | async-start | bytes 8388608
  0.6 8.2 %copy-start = (bf16[2048,2048]{1,0:T(8,128)(2,1)S(1)}, bf16[2048,2048]{1,0:T(8,128)(2,1)}, u32[]{:S(2)}) copy-start(bf16[2048,2048]{1,0:T(8,128)(2,1)} %wq_ref.1) | copy-start | bytes 25165828
  0.7 8.2 %copy-start.1 = (bf16[2048,2,256]{2,1,0:T(2,128)(2,1)S(1)}, bf16[2048,2,256]{2,1,0:T(2,128)(2,1)}, u32[]{:S(2)}) copy-start(bf16[2048,2,256]{2,1,0:T(2,128)(2,1)} %wkv_ref.1) | copy-start | bytes 6291460
  0.7 8.2 %copy-start.2 = (bf16[2,4,2048]{2,1,0:T(4,128)(2,1)S(1)}, bf16[2,4,2048]{2,1,0:T(4,128)(2,1)}, u32[]{:S(2)}) copy-start(bf16[2,4,2048]{2,1,0:T(4,128)(2,1)} %hidden_ref.1) | copy-start | bytes 98308
  0.7 8.2 %copy-start.3 = (bf16[2048]{0:T(1024)(128)(2,1)S(1)}, bf16[2048]{0:T(1024)(128)(2,1)}, u32[]{:S(2)}) copy-start(bf16[2048]{0:T(1024)(128)(2,1)} %param.12) | copy-start | bytes 12292
  0.7 29.3 %slice-start.1 = ((s8[8388608]{0:T(1024)(128)(4,1)}), s8[4194304]{0:T(1024)(128)(4,1)S(1)}, s32[]{:S(2)}) async-start(s8[8388608]{0:T(1024)(128)(4,1)} %bitcast.2), calls=%async_computation.1 | async-start | bytes 8388608
  3.1 18.3 %copy-start.4 = (s32[2,8,4]{1,2,0:T(4,128)S(1)}, s32[2,8,4]{1,2,0:T(4,128)}, u32[]{:S(2)}) copy-start(s32[2,8,4]{1,2,0:T(4,128)} %param.10) | copy-start | bytes 772
  3.1 18.3 %copy-start.5 = (f32[8,128]{1,0:T(8,128)S(1)}, f32[8,128]{1,0:T(8,128)}, u32[]{:S(2)}) copy-start(f32[8,128]{1,0:T(8,128)} %constant.5.clone.sin_ref) | copy-start | bytes 12292
  3.1 18.3 %copy-start.6 = (f32[8,128]{1,0:T(8,128)S(1)}, f32[8,128]{1,0:T(8,128)}, u32[]{:S(2)}) copy-start(f32[8,128]{1,0:T(8,128)} %constant.4.clone.cos_ref) | copy-start | bytes 12292
  3.1 11.7 %collective-permute-start = (bf16[256,256]{1,0:T(8,128)(2,1)S(1)}, bf16[256,256]{1,0:T(8,128)(2,1)S(1)}, u32[]{:S(2)}, u32[]{:S(2)}) collective-permute-start(bf16[256,256]{1,0:T(8,128)(2,1)S(1)} %get-tuple-element.16), channel_id=1, source_target_pairs={{0,12},{4,8},{8,4},{12,0},{1,13},{5,9},{9,5},{13,1},{2,14},{6,10},... | collective-permute-start | bytes 393224 | tf_op jit(solution)/shard_map/ppermute | solution.py:43
  8.2 13.2 %collective-permute-start.1 = (bf16[256,256]{1,0:T(8,128)(2,1)S(1)}, bf16[256,256]{1,0:T(8,128)(2,1)S(1)}, u32[]{:S(2)}, u32[]{:S(2)}) collective-permute-start(bf16[256,256]{1,0:T(8,128)(2,1)S(1)} %get-tuple-element.18), channel_id=1, source_target_pairs={{0,8},{4,12},{8,0},{12,4},{1,9},{5,13},{9,1},{13,5},{2,10},{6,14},... | collective-permute-start | bytes 393224 | tf_op jit(solution)/shard_map/ppermute | solution.py:43
  8.2 13.2 %collective-permute-start.2 = (bf16[256,256]{1,0:T(8,128)(2,1)S(1)}, bf16[256,256]{1,0:T(8,128)(2,1)S(1)}, u32[]{:S(2)}, u32[]{:S(2)}) collective-permute-start(bf16[256,256]{1,0:T(8,128)(2,1)S(1)} %get-tuple-element.19), channel_id=1, source_target_pairs={{0,4},{4,0},{8,12},{12,8},{1,5},{5,1},{9,13},{13,9},{2,6},{6,2},{1... | collective-permute-start | bytes 393224 | tf_op jit(solution)/shard_map/ppermute | solution.py:43
  11.0 7.5 %collective-permute-start.3 = (f32[48,128]{1,0:T(8,128)S(1)}, f32[48,128]{1,0:T(8,128)S(1)}, u32[]{:S(2)}, u32[]{:S(2)}) collective-permute-start(f32[48,128]{1,0:T(8,128)S(1)} %get-tuple-element.20), channel_id=1, source_target_pairs={{0,12},{4,8},{8,4},{12,0},{1,13},{5,9},{9,5},{13,1},{2,14},{6,10},... | collective-permute-start | bytes 73736 | tf_op jit(solution)/shard_map/ppermute | solution.py:43
  14.8 6.6 %collective-permute-start.4 = (f32[48,128]{1,0:T(8,128)S(1)}, f32[48,128]{1,0:T(8,128)S(1)}, u32[]{:S(2)}, u32[]{:S(2)}) collective-permute-start(f32[48,128]{1,0:T(8,128)S(1)} %get-tuple-element.21), channel_id=1, source_target_pairs={{0,8},{4,12},{8,0},{12,4},{1,9},{5,13},{9,1},{13,5},{2,10},{6,14},... | collective-permute-start | bytes 73736 | tf_op jit(solution)/shard_map/ppermute | solution.py:43
  14.8 6.6 %collective-permute-start.5 = (f32[48,128]{1,0:T(8,128)S(1)}, f32[48,128]{1,0:T(8,128)S(1)}, u32[]{:S(2)}, u32[]{:S(2)}) collective-permute-start(f32[48,128]{1,0:T(8,128)S(1)} %get-tuple-element.22), channel_id=1, source_target_pairs={{0,4},{4,0},{8,12},{12,8},{1,5},{5,1},{9,13},{13,9},{2,6},{6,2},{1... | collective-permute-start | bytes 73736 | tf_op jit(solution)/shard_map/ppermute | solution.py:43
  23.1 5.5 %collective-permute-start.8 = (bf16[32,128]{1,0:T(8,128)(2,1)S(1)}, bf16[32,128]{1,0:T(8,128)(2,1)S(1)}, u32[]{:S(2)}, u32[]{:S(2)}) collective-permute-start(bf16[32,128]{1,0:T(8,128)(2,1)S(1)} %get-tuple-element.25.refs_0_), channel_id=1, source_target_pairs={{0,12},{4,8},{8,4},{12,0},{1,13},{5,9},{9,5},{13,1},{2,14},{6,10},... | collective-permute-start | bytes 24584 | tf_op jit(solution)/shard_map/ppermute | solution.py:43
  25.4 4.5 %collective-permute-start.7 = (bf16[32,128]{1,0:T(8,128)(2,1)S(1)}, bf16[32,128]{1,0:T(8,128)(2,1)S(1)}, u32[]{:S(2)}, u32[]{:S(2)}) collective-permute-start(bf16[32,128]{1,0:T(8,128)(2,1)S(1)} %get-tuple-element.25.refs_0_), channel_id=1, source_target_pairs={{0,8},{4,12},{8,0},{12,4},{1,9},{5,13},{9,1},{13,5},{2,10},{6,14},... | collective-permute-start | bytes 24584 | tf_op jit(solution)/shard_map/ppermute | solution.py:43
  25.5 4.5 %collective-permute-start.6 = (bf16[32,128]{1,0:T(8,128)(2,1)S(1)}, bf16[32,128]{1,0:T(8,128)(2,1)S(1)}, u32[]{:S(2)}, u32[]{:S(2)}) collective-permute-start(bf16[32,128]{1,0:T(8,128)(2,1)S(1)} %get-tuple-element.25.refs_0_), channel_id=1, source_target_pairs={{0,4},{4,0},{8,12},{12,8},{1,5},{5,1},{9,13},{13,9},{2,6},{6,2},{1... | collective-permute-start | bytes 24584 | tf_op jit(solution)/shard_map/ppermute | solution.py:43
  31.2 4.3 %collective-permute-start.9 = (f32[8,2048]{1,0:T(8,128)S(1)}, f32[8,2048]{1,0:T(8,128)S(1)}, u32[]{:S(2)}, u32[]{:S(2)}) collective-permute-start(f32[8,2048]{1,0:T(8,128)S(1)} %output_projection.1), channel_id=1, source_target_pairs={{0,2},{1,3},{2,0},{3,1},{4,6},{5,7},{6,4},{7,5},{8,10},{9,11},{10,... | collective-permute-start | bytes 196616 | tf_op jit(solution)/shard_map/ppermute | solution.py:43
  35.5 1.3 %collective-permute-start.10 = (f32[8,2048]{1,0:T(8,128)S(1)}, f32[8,2048]{1,0:T(8,128)S(1)}, u32[]{:S(2)}, u32[]{:S(2)}) collective-permute-start(f32[8,2048]{1,0:T(8,128)S(1)} %add.9), channel_id=1, source_target_pairs={{0,1},{1,0},{2,3},{3,2},{4,5},{5,4},{6,7},{7,6},{8,9},{9,8},{10,11... | collective-permute-start | bytes 196616 | tf_op jit(solution)/shard_map/ppermute | solution.py:43

commit v8 on v7

--- a/solution.py
+++ b/solution.py
@@ -47,64 +47,81 @@
     return lax.all_to_all(outgoing, axis, split_axis=0, concat_axis=0, tiled=True)
 
 
-def start_picks(kept_ref, cache_ref, pair, out_ref, sem):
-    _, heads_local, source_tokens, _ = cache_ref.shape
+def picked_rows(kept_ref, cache_shape, pair, slot):
+    _, heads_local, source_tokens, _ = cache_shape
     source_blocks = source_tokens // BLK
     kept_count = kept_ref.shape[1]
-    me = lax.axis_index("seq")
+    first_block = lax.axis_index("seq") * source_blocks
     request = lax.div(pair, heads_local)
     local = lax.rem(pair, heads_local)
     head = lax.axis_index("head") * heads_local + local
 
     def count(k, total):
-        block = kept_ref[request, k, head]
-        return total + (block < me * source_blocks).astype(jnp.int32)
+        return total + (kept_ref[request, k, head] < first_block).astype(jnp.int32)
 
     start = lax.fori_loop(0, kept_count, count, jnp.int32(0), unroll=kept_count <= 8)
-    for slot in range(MOST):
-        rank = jnp.minimum(start + slot, kept_count - 1)
-        block = kept_ref[request, rank, head] - me * source_blocks
-        block = jnp.clip(block, 0, source_blocks - 1)
-        rows = pl.ds(pl.multiple_of(block * BLK, BLK), BLK)
-        pltpu.make_async_copy(
-            cache_ref.at[request, local, rows], out_ref.at[pl.ds(slot * BLK, BLK)], sem
-        ).start()
-
-
-def pick_kernel(offsets, kept_hbm_ref, cache_ref, *refs):
-    outs, kept_ref, sem = refs[:-2], refs[-2], refs[-1]
+    rank = jnp.minimum(start + slot, kept_count - 1)
+    block = jnp.clip(kept_ref[request, rank, head] - first_block, 0, source_blocks - 1)
+    return request, local, pl.ds(pl.multiple_of(block * BLK, BLK), BLK)
+
+
+def pick_near_kernel(kept_hbm_ref, cache_ref, *refs):
+    *outs, kept_ref, cache, kept_sem, sem = refs
+    kept_copy = pltpu.make_async_copy(kept_hbm_ref, kept_ref, kept_sem)
+    cache_copy = pltpu.make_async_copy(cache_ref, cache, sem)
+    kept_copy.start()
+    cache_copy.start()
+    kept_copy.wait()
+    me = lax.axis_index("seq")
+    places = [
+        [picked_rows(kept_ref, cache.shape, jnp.bitwise_xor(me, k), slot) for slot in range(MOST)]
+        for k in range(len(outs))
+    ]
+    cache_copy.wait()
+    for out_ref, slots in zip(outs, places):
+        for slot, (request, local, rows) in enumerate(slots):
+            out_ref[slot * BLK : (slot + 1) * BLK, :] = cache[request, local, rows, :]
+
+
+def pick_all_kernel(kept_hbm_ref, cache_ref, out_ref, kept_ref, sem):
     pltpu.sync_copy(kept_hbm_ref, kept_ref)
-    if offsets:
-        me = lax.axis_index("seq")
-        for offset, out_ref in zip(offsets, outs):
-            start_picks(kept_ref, cache_ref, jnp.bitwise_xor(me, offset), out_ref, sem)
-    else:
-
-        def pair_body(pair, carry):
-            start_picks(kept_ref, cache_ref, pair, outs[0].at[pair], sem)
-            return carry
-
-        lax.fori_loop(0, outs[0].shape[0], pair_body, 0)
-    for out_ref in outs:
-        pltpu.make_async_copy(out_ref, out_ref, sem).wait()
-
-
-def pick(kept_blocks, source_cache, offsets):
+
+    def pair_body(pair, carry):
+        for slot in range(MOST):
+            request, local, rows = picked_rows(kept_ref, cache_ref.shape, pair, slot)
+            pltpu.make_async_copy(
+                cache_ref.at[request, local, rows],
+                out_ref.at[pair, pl.ds(slot * BLK, BLK)],
+                sem,
+            ).start()
+        return carry
+
+    lax.fori_loop(0, out_ref.shape[0], pair_body, 0)
+    pltpu.make_async_copy(out_ref, out_ref, sem).wait()
+
+
+def pick(kept_blocks, source_cache, direct):
     requests, heads_local, _, row_width = source_cache.shape
+    pair_count = requests * heads_local
     block = (MOST * BLK, row_width)
-    if offsets:
-        shapes = [jax.ShapeDtypeStruct(block, jnp.bfloat16)] * len(offsets)
-    else:
-        shapes = [jax.ShapeDtypeStruct((requests * heads_local,) + block, jnp.bfloat16)]
+    kept_scratch = pltpu.SMEM(kept_blocks.shape, jnp.int32)
+    if direct:
+        shapes = [jax.ShapeDtypeStruct(block, jnp.bfloat16)] * pair_count
+        scratch = [
+            kept_scratch,
+            pltpu.VMEM(source_cache.shape, jnp.bfloat16),
+            pltpu.SemaphoreType.DMA,
+            pltpu.SemaphoreType.DMA,
+        ]
+    else:
+        shapes = [jax.ShapeDtypeStruct((pair_count,) + block, jnp.bfloat16)]
+        scratch = [kept_scratch, pltpu.SemaphoreType.DMA]
     return pl.pallas_call(
-        functools.partial(pick_kernel, offsets),
+        pick_near_kernel if direct else pick_all_kernel,
         out_shape=shapes,
         in_specs=[pl.BlockSpec(memory_space=pl.ANY)] * 2,
         out_specs=[pl.BlockSpec(memory_space=pltpu.VMEM)] * len(shapes),
-        scratch_shapes=[
-            pltpu.SMEM(kept_blocks.shape, jnp.int32),
-            pltpu.SemaphoreType.DMA,
-        ],
+        scratch_shapes=scratch,
         compiler_params=pltpu.CompilerParams(vmem_limit_bytes=8 * 1024 * 1024),
         cost_estimate=pl.CostEstimate(flops=10**10, bytes_accessed=0, transcendentals=0),
         name="pick_blocks",
@@ -321,6 +338,7 @@
         out_specs=(pl.BlockSpec(memory_space=pl.ANY), vmem),
         scratch_shapes=scratch,
         compiler_params=pltpu.CompilerParams(vmem_limit_bytes=16 * 1024 * 1024),
+        cost_estimate=pl.CostEstimate(flops=10**10, bytes_accessed=0, transcendentals=0),
         name="attend",
     )(kept_blocks, jnp.asarray(cosine), jnp.asarray(sine), *arrivals)
 
@@ -391,14 +409,14 @@
     weights = (new_hidden, norm_gain, w_query, w_keyval)
     if direct:
         partners = range(1, seq_count)
-        blocks = pick(kept_blocks, source_cache, range(seq_count))
+        blocks = pick(kept_blocks, source_cache, direct)
         parts = list(project(blocks[0], *weights, pair_count, direct))
         blocks = [blocks[0]] + [swap(blocks[k], "seq", k) for k in partners]
         parts[1], blocks[3] = lax.optimization_barrier((parts[1], blocks[3]))
         parts = [parts[0]] + [swap(parts[k], "seq", k) for k in partners]
         arrivals = blocks[::-1] + parts[::-1]
     else:
-        (blocks,) = pick(kept_blocks, source_cache, ())
+        (blocks,) = pick(kept_blocks, source_cache, direct)
         (parts,) = project(blocks, *weights, pair_count, direct)
         arrivals = [all_to_all(parts, "seq"), all_to_all(blocks, "seq")]
     kept_cache, attended = attend(

time: 37.7 us -> 36.7 us (0.973)
  Pallas kernels: 7.28 us -> 6.36 us
    pallas_call x1, Pallas kernels: 2.36 us -> 1.43 us  [pick(): pl.pallas_call(pick_near_kernel if direct else pick_all_kernel, out_shape...]
where the time goes in v8:
time: 36.7 us; the launch traced here: 36.6 us
  starting transfers between devices  19.5 us (53%)
  waiting for transfers between devices  9.21 us (25%)
  Pallas kernels  6.36 us (17%)
  between operations  0.8 us (2%)
  other arithmetic  0.65 us (2%)
    ppermute x11, starting transfers between devices, swap(): return lax.ppermute(outgoing, axis, [(i, i ^ offset) for i in range(count)])  19.5 us
    ppermute x11, waiting for transfers between devices, swap(): return lax.ppermute(outgoing, axis, [(i, i ^ offset) for i in range(count)])  9.21 us
    pallas_call x1, Pallas kernels, project(): pl.pallas_call(functools.partial(project_kernel, direct), out_shape=shape...  2.12 us
    pallas_call x1, Pallas kernels, attend(): pl.pallas_call(functools.partial(attend_kernel, direct, source_blocks, he...  1.62 us
    pallas_call x1, Pallas kernels, pick(): pl.pallas_call(pick_near_kernel if direct else pick_all_kernel, out_shape...  1.43 us
    pallas_call x1, Pallas kernels, output(): pl.pallas_call(functools.partial(output_kernel, heads_local), out_shape=j...  1.19 us
  transfers between devices with their start and end apart: 11, of which 5 were waited for; matrix products, arithmetic and copies ran while one was open for 0% of the time, Pallas kernels for 6%

profile of v8, /device:TPU:0, one launch (start us, length us, event | category | flops | bytes accessed | tf_op | source)
XLA Modules:
  0.0 36.6 jit_solution(8947769559102174923)
XLA Ops:
  0.7 1.4 %pick_blocks.1 = (bf16[256,256]{1,0:T(8,128)(2,1)S(1)}, bf16[256,256]{1,0:T(8,128)(2,1)S(1)}, bf16[256,256]{1,0:T(8,128)(2,1)S(1)}, bf16[256,256]{1,0:T(8,128)(2,1)S(1)}) custom-call(s32[2,4,8]{2,1,0:T(4,128)} %bitcast.5, bf16[2,2,512,256]{3,2,1,0:T(8,128)(2,1)} %cache_ref.1), custom_call_target="tpu_custom_call" | custom-call | flops 10000000000 | tf_op jit(solution)/shard_map/pick_blocks/pallas_call | solution.py:119
  2.1 0.0 copy-start.4
  2.1 0.0 copy-start.5
  2.1 0.0 copy-start.6
  2.1 5.1 %collective-permute-start = (bf16[256,256]{1,0:T(8,128)(2,1)S(1)}, bf16[256,256]{1,0:T(8,128)(2,1)S(1)}, u32[]{:S(2)}, u32[]{:S(2)}) collective-permute-start(bf16[256,256]{1,0:T(8,128)(2,1)S(1)} %get-tuple-element.16), channel_id=1, source_target_pairs={{0,12},{4,8},{8,4},{12,0},{1,13},{5,9},{9,5},{13,1},{2,14},{6,10},... | collective-permute-start | bytes 393224 | tf_op jit(solution)/shard_map/ppermute | solution.py:43
  7.3 0.6 %collective-permute-start.2 = (bf16[256,256]{1,0:T(8,128)(2,1)S(1)}, bf16[256,256]{1,0:T(8,128)(2,1)S(1)}, u32[]{:S(2)}, u32[]{:S(2)}) collective-permute-start(bf16[256,256]{1,0:T(8,128)(2,1)S(1)} %get-tuple-element.19), channel_id=1, source_target_pairs={{0,4},{4,0},{8,12},{12,8},{1,5},{5,1},{9,13},{13,9},{2,6},{6,2},{1... | collective-permute-start | bytes 393224 | tf_op jit(solution)/shard_map/ppermute | solution.py:43
  7.9 0.0 slice-start
  7.9 2.1 %project.1 = (f32[48,128]{1,0:T(8,128)S(1)}, f32[48,128]{1,0:T(8,128)S(1)}, f32[48,128]{1,0:T(8,128)S(1)}, f32[48,128]{1,0:T(8,128)S(1)}) custom-call(bf16[256,256]{1,0:T(8,128)(2,1)S(1)} %get-tuple-element.14.after_ref.refs_3_, bf16[2,4,2048]{2,1,0:T(4,128)(2,1)S(1)} %copy-done.2, bf16[16,128]{1,0:T(8,128)(2,1)S(1)} %bitcast.4, ...), custom_call_target="tpu_custom_call" | custom-call | flops 83886080 | bytes 10485760 | tf_op jit(solution)/shard_map/project/pallas_call | solution.py:210
  10.1 3.8 %collective-permute-start.3 = (f32[48,128]{1,0:T(8,128)S(1)}, f32[48,128]{1,0:T(8,128)S(1)}, u32[]{:S(2)}, u32[]{:S(2)}) collective-permute-start(f32[48,128]{1,0:T(8,128)S(1)} %get-tuple-element.20), channel_id=1, source_target_pairs={{0,12},{4,8},{8,4},{12,0},{1,13},{5,9},{9,5},{13,1},{2,14},{6,10},... | collective-permute-start | bytes 73736 | tf_op jit(solution)/shard_map/ppermute | solution.py:43
  13.9 3.7 %collective-permute-start.5 = (f32[48,128]{1,0:T(8,128)S(1)}, f32[48,128]{1,0:T(8,128)S(1)}, u32[]{:S(2)}, u32[]{:S(2)}) collective-permute-start(f32[48,128]{1,0:T(8,128)S(1)} %get-tuple-element.22), channel_id=1, source_target_pairs={{0,4},{4,0},{8,12},{12,8},{1,5},{5,1},{9,13},{13,9},{2,6},{6,2},{1... | collective-permute-start | bytes 73736 | tf_op jit(solution)/shard_map/ppermute | solution.py:43
  17.6 2.8 %collective-permute-done.4.refs_5_ = f32[48,128]{1,0:T(8,128)S(1)} collective-permute-done((f32[48,128]{1,0:T(8,128)S(1)}, f32[48,128]{1,0:T(8,128)S(1)}, u32[]{:S(2)}, u32[]{:S(2)}) %collective-permute-start.4) | collective-permute-done | bytes 24608 | tf_op jit(solution)/shard_map/ppermute | solution.py:43
  20.5 0.0 slice-start.1
  20.5 1.6 %attend.1 = (bf16[1,1,512,256]{3,2,1,0:T(8,128)(2,1)}, bf16[32,128]{1,0:T(8,128)(2,1)S(1)}) custom-call(s32[2,4,8]{2,1,0:T(4,128)S(1)} %bitcast.6, f32[8,128]{1,0:T(8,128)S(1)} %copy-done.6, f32[8,128]{1,0:T(8,128)S(1)} %copy-done.5, bf16[256,256]{1,0:T(8,128)(2,1)S(1)} %collective-permute-done.refs_0_, bf16[256,256]{1,0:T(8,128)(2,1)S(1)} %collective-permute-done.1.refs_1_, ...), custom_call_target="tpu_custom_call" | custom-call | flops 10000000000 | tf_op jit(solution)/shard_map/attend/pallas_call | solution.py:331
  22.1 2.4 %collective-permute-start.8 = (bf16[32,128]{1,0:T(8,128)(2,1)S(1)}, bf16[32,128]{1,0:T(8,128)(2,1)S(1)}, u32[]{:S(2)}, u32[]{:S(2)}) collective-permute-start(bf16[32,128]{1,0:T(8,128)(2,1)S(1)} %get-tuple-element.25.refs_0_), channel_id=1, source_target_pairs={{0,12},{4,8},{8,4},{12,0},{1,13},{5,9},{9,5},{13,1},{2,14},{6,10},... | collective-permute-start | bytes 24584 | tf_op jit(solution)/shard_map/ppermute | solution.py:43
  24.5 0.1 collective-permute-start.7
  24.6 2.0 %collective-permute-start.6 = (bf16[32,128]{1,0:T(8,128)(2,1)S(1)}, bf16[32,128]{1,0:T(8,128)(2,1)S(1)}, u32[]{:S(2)}, u32[]{:S(2)}) collective-permute-start(bf16[32,128]{1,0:T(8,128)(2,1)S(1)} %get-tuple-element.25.refs_0_), channel_id=1, source_target_pairs={{0,4},{4,0},{8,12},{12,8},{1,5},{5,1},{9,13},{13,9},{2,6},{6,2},{1... | collective-permute-start | bytes 24584 | tf_op jit(solution)/shard_map/ppermute | solution.py:43
  26.6 1.1 %collective-permute-done.8.refs_3_ = bf16[32,128]{1,0:T(8,128)(2,1)S(1)} collective-permute-done((bf16[32,128]{1,0:T(8,128)(2,1)S(1)}, bf16[32,128]{1,0:T(8,128)(2,1)S(1)}, u32[]{:S(2)}, u32[]{:S(2)}) %collective-permute-start.8) | collective-permute-done | bytes 8224 | tf_op jit(solution)/shard_map/ppermute | solution.py:43
  27.6 1.4 %collective-permute-done.7.refs_2_ = bf16[32,128]{1,0:T(8,128)(2,1)S(1)} collective-permute-done((bf16[32,128]{1,0:T(8,128)(2,1)S(1)}, bf16[32,128]{1,0:T(8,128)(2,1)S(1)}, u32[]{:S(2)}, u32[]{:S(2)}) %collective-permute-start.7) | collective-permute-done | bytes 8224 | tf_op jit(solution)/shard_map/ppermute | solution.py:43
  29.1 1.2 %output_projection.1 = f32[8,2048]{1,0:T(8,128)S(1)} custom-call(bf16[2048,2048]{1,0:T(8,128)(2,1)S(1)} %bitcast.3, bf16[32,128]{1,0:T(8,128)(2,1)S(1)} %get-tuple-element.25.refs_0_, bf16[32,128]{1,0:T(8,128)(2,1)S(1)} %collective-permute-done.6.refs_1_, bf16[32,128]{1,0:T(8,128)(2,1)S(1)} %collective-permute-done.7.refs_2_, ...), custom_call_target="tpu_custom_call" | custom-call | tf_op jit(solution)/shard_map/output_projection/pallas_call | solution.py:389
  30.3 1.7 %collective-permute-start.9 = (f32[8,2048]{1,0:T(8,128)S(1)}, f32[8,2048]{1,0:T(8,128)S(1)}, u32[]{:S(2)}, u32[]{:S(2)}) collective-permute-start(f32[8,2048]{1,0:T(8,128)S(1)} %output_projection.1), channel_id=1, source_target_pairs={{0,2},{1,3},{2,0},{3,1},{4,6},{5,7},{6,4},{7,5},{8,10},{9,11},{10,... | collective-permute-start | bytes 196616 | tf_op jit(solution)/shard_map/ppermute | solution.py:43
  31.9 2.6 %collective-permute-done.9 = f32[8,2048]{1,0:T(8,128)S(1)} collective-permute-done((f32[8,2048]{1,0:T(8,128)S(1)}, f32[8,2048]{1,0:T(8,128)S(1)}, u32[]{:S(2)}, u32[]{:S(2)}) %collective-permute-start.9) | collective-permute-done | bytes 65568 | tf_op jit(solution)/shard_map/ppermute | solution.py:43
  34.6 0.1 collective-permute-start.10
  34.6 1.2 %collective-permute-done.10 = f32[8,2048]{1,0:T(8,128)S(1)} collective-permute-done((f32[8,2048]{1,0:T(8,128)S(1)}, f32[8,2048]{1,0:T(8,128)S(1)}, u32[]{:S(2)}, u32[]{:S(2)}) %collective-permute-start.10) | collective-permute-done | bytes 65568 | tf_op jit(solution)/shard_map/ppermute | solution.py:43
  35.9 0.6 %add_convert_fusion = bf16[2,4,2048]{2,1,0:T(4,128)(2,1)} fusion(f32[2,4,2048]{2,1,0:T(4,128)S(1)} %reshape.11, bf16[2,4,2048]{2,1,0:T(4,128)(2,1)S(1)} %copy-done.2), kind=kLoop, calls=%fused_computation | loop fusion | flops 49152 | bytes 131072 | tf_op jit(solution)/shard_map/convert_element_type | solution.py:436
  (25 shorter events, 0.1 us)
Async XLA Ops:
  0.6 7.3 %copy-start = (bf16[2048,2048]{1,0:T(8,128)(2,1)S(1)}, bf16[2048,2048]{1,0:T(8,128)(2,1)}, u32[]{:S(2)}) copy-start(bf16[2048,2048]{1,0:T(8,128)(2,1)} %wq_ref.1) | copy-start | bytes 25165828
  0.6 7.3 %copy-start.1 = (bf16[2048,2,256]{2,1,0:T(2,128)(2,1)S(1)}, bf16[2048,2,256]{2,1,0:T(2,128)(2,1)}, u32[]{:S(2)}) copy-start(bf16[2048,2,256]{2,1,0:T(2,128)(2,1)} %wkv_ref.1) | copy-start | bytes 6291460
  0.7 7.3 %copy-start.2 = (bf16[2,4,2048]{2,1,0:T(4,128)(2,1)S(1)}, bf16[2,4,2048]{2,1,0:T(4,128)(2,1)}, u32[]{:S(2)}) copy-start(bf16[2,4,2048]{2,1,0:T(4,128)(2,1)} %hidden_ref.1) | copy-start | bytes 98308
  0.7 7.3 %copy-start.3 = (bf16[2048]{0:T(1024)(128)(2,1)S(1)}, bf16[2048]{0:T(1024)(128)(2,1)}, u32[]{:S(2)}) copy-start(bf16[2048]{0:T(1024)(128)(2,1)} %param.12) | copy-start | bytes 12292
  2.1 18.3 %copy-start.4 = (s32[2,8,4]{1,2,0:T(4,128)S(1)}, s32[2,8,4]{1,2,0:T(4,128)}, u32[]{:S(2)}) copy-start(s32[2,8,4]{1,2,0:T(4,128)} %param.10) | copy-start | bytes 772
  2.1 18.3 %copy-start.5 = (f32[8,128]{1,0:T(8,128)S(1)}, f32[8,128]{1,0:T(8,128)}, u32[]{:S(2)}) copy-start(f32[8,128]{1,0:T(8,128)} %constant.5.clone.sin_ref) | copy-start | bytes 12292
  2.1 18.3 %copy-start.6 = (f32[8,128]{1,0:T(8,128)S(1)}, f32[8,128]{1,0:T(8,128)}, u32[]{:S(2)}) copy-start(f32[8,128]{1,0:T(8,128)} %constant.4.clone.cos_ref) | copy-start | bytes 12292
  2.1 11.7 %collective-permute-start = (bf16[256,256]{1,0:T(8,128)(2,1)S(1)}, bf16[256,256]{1,0:T(8,128)(2,1)S(1)}, u32[]{:S(2)}, u32[]{:S(2)}) collective-permute-start(bf16[256,256]{1,0:T(8,128)(2,1)S(1)} %get-tuple-element.16), channel_id=1, source_target_pairs={{0,12},{4,8},{8,4},{12,0},{1,13},{5,9},{9,5},{13,1},{2,14},{6,10},... | collective-permute-start | bytes 393224 | tf_op jit(solution)/shard_map/ppermute | solution.py:43
  7.3 13.2 %collective-permute-start.1 = (bf16[256,256]{1,0:T(8,128)(2,1)S(1)}, bf16[256,256]{1,0:T(8,128)(2,1)S(1)}, u32[]{:S(2)}, u32[]{:S(2)}) collective-permute-start(bf16[256,256]{1,0:T(8,128)(2,1)S(1)} %get-tuple-element.18), channel_id=1, source_target_pairs={{0,8},{4,12},{8,0},{12,4},{1,9},{5,13},{9,1},{13,5},{2,10},{6,14},... | collective-permute-start | bytes 393224 | tf_op jit(solution)/shard_map/ppermute | solution.py:43
  7.3 13.2 %collective-permute-start.2 = (bf16[256,256]{1,0:T(8,128)(2,1)S(1)}, bf16[256,256]{1,0:T(8,128)(2,1)S(1)}, u32[]{:S(2)}, u32[]{:S(2)}) collective-permute-start(bf16[256,256]{1,0:T(8,128)(2,1)S(1)} %get-tuple-element.19), channel_id=1, source_target_pairs={{0,4},{4,0},{8,12},{12,8},{1,5},{5,1},{9,13},{13,9},{2,6},{6,2},{1... | collective-permute-start | bytes 393224 | tf_op jit(solution)/shard_map/ppermute | solution.py:43
  7.9 21.2 %slice-start = ((s8[8388608]{0:T(1024)(128)(4,1)}), s8[4194304]{0:T(1024)(128)(4,1)S(1)}, s32[]{:S(2)}) async-start(s8[8388608]{0:T(1024)(128)(4,1)} %bitcast.2), calls=%async_computation | async-start | bytes 8388608
  10.1 7.5 %collective-permute-start.3 = (f32[48,128]{1,0:T(8,128)S(1)}, f32[48,128]{1,0:T(8,128)S(1)}, u32[]{:S(2)}, u32[]{:S(2)}) collective-permute-start(f32[48,128]{1,0:T(8,128)S(1)} %get-tuple-element.20), channel_id=1, source_target_pairs={{0,12},{4,8},{8,4},{12,0},{1,13},{5,9},{9,5},{13,1},{2,14},{6,10},... | collective-permute-start | bytes 73736 | tf_op jit(solution)/shard_map/ppermute | solution.py:43
  13.9 6.6 %collective-permute-start.4 = (f32[48,128]{1,0:T(8,128)S(1)}, f32[48,128]{1,0:T(8,128)S(1)}, u32[]{:S(2)}, u32[]{:S(2)}) collective-permute-start(f32[48,128]{1,0:T(8,128)S(1)} %get-tuple-element.21), channel_id=1, source_target_pairs={{0,8},{4,12},{8,0},{12,4},{1,9},{5,13},{9,1},{13,5},{2,10},{6,14},... | collective-permute-start | bytes 73736 | tf_op jit(solution)/shard_map/ppermute | solution.py:43
  13.9 6.6 %collective-permute-start.5 = (f32[48,128]{1,0:T(8,128)S(1)}, f32[48,128]{1,0:T(8,128)S(1)}, u32[]{:S(2)}, u32[]{:S(2)}) collective-permute-start(f32[48,128]{1,0:T(8,128)S(1)} %get-tuple-element.22), channel_id=1, source_target_pairs={{0,4},{4,0},{8,12},{12,8},{1,5},{5,1},{9,13},{13,9},{2,6},{6,2},{1... | collective-permute-start | bytes 73736 | tf_op jit(solution)/shard_map/ppermute | solution.py:43
  20.5 8.6 %slice-start.1 = ((s8[8388608]{0:T(1024)(128)(4,1)}), s8[4194304]{0:T(1024)(128)(4,1)S(1)}, s32[]{:S(2)}) async-start(s8[8388608]{0:T(1024)(128)(4,1)} %bitcast.2), calls=%async_computation.1 | async-start | bytes 8388608
  22.1 5.5 %collective-permute-start.8 = (bf16[32,128]{1,0:T(8,128)(2,1)S(1)}, bf16[32,128]{1,0:T(8,128)(2,1)S(1)}, u32[]{:S(2)}, u32[]{:S(2)}) collective-permute-start(bf16[32,128]{1,0:T(8,128)(2,1)S(1)} %get-tuple-element.25.refs_0_), channel_id=1, source_target_pairs={{0,12},{4,8},{8,4},{12,0},{1,13},{5,9},{9,5},{13,1},{2,14},{6,10},... | collective-permute-start | bytes 24584 | tf_op jit(solution)/shard_map/ppermute | solution.py:43
  24.5 4.5 %collective-permute-start.7 = (bf16[32,128]{1,0:T(8,128)(2,1)S(1)}, bf16[32,128]{1,0:T(8,128)(2,1)S(1)}, u32[]{:S(2)}, u32[]{:S(2)}) collective-permute-start(bf16[32,128]{1,0:T(8,128)(2,1)S(1)} %get-tuple-element.25.refs_0_), channel_id=1, source_target_pairs={{0,8},{4,12},{8,0},{12,4},{1,9},{5,13},{9,1},{13,5},{2,10},{6,14},... | collective-permute-start | bytes 24584 | tf_op jit(solution)/shard_map/ppermute | solution.py:43
  24.6 4.5 %collective-permute-start.6 = (bf16[32,128]{1,0:T(8,128)(2,1)S(1)}, bf16[32,128]{1,0:T(8,128)(2,1)S(1)}, u32[]{:S(2)}, u32[]{:S(2)}) collective-permute-start(bf16[32,128]{1,0:T(8,128)(2,1)S(1)} %get-tuple-element.25.refs_0_), channel_id=1, source_target_pairs={{0,4},{4,0},{8,12},{12,8},{1,5},{5,1},{9,13},{13,9},{2,6},{6,2},{1... | collective-permute-start | bytes 24584 | tf_op jit(solution)/shard_map/ppermute | solution.py:43
  30.3 4.3 %collective-permute-start.9 = (f32[8,2048]{1,0:T(8,128)S(1)}, f32[8,2048]{1,0:T(8,128)S(1)}, u32[]{:S(2)}, u32[]{:S(2)}) collective-permute-start(f32[8,2048]{1,0:T(8,128)S(1)} %output_projection.1), channel_id=1, source_target_pairs={{0,2},{1,3},{2,0},{3,1},{4,6},{5,7},{6,4},{7,5},{8,10},{9,11},{10,... | collective-permute-start | bytes 196616 | tf_op jit(solution)/shard_map/ppermute | solution.py:43
  34.6 1.3 %collective-permute-start.10 = (f32[8,2048]{1,0:T(8,128)S(1)}, f32[8,2048]{1,0:T(8,128)S(1)}, u32[]{:S(2)}, u32[]{:S(2)}) collective-permute-start(f32[8,2048]{1,0:T(8,128)S(1)} %add.9), channel_id=1, source_target_pairs={{0,1},{1,0},{2,3},{3,2},{4,5},{5,4},{6,7},{7,6},{8,9},{9,8},{10,11... | collective-permute-start | bytes 196616 | tf_op jit(solution)/shard_map/ppermute | solution.py:43

commit v9 on v8

--- a/solution.py
+++ b/solution.py
@@ -228,6 +228,41 @@
     )
 
 
+def place_kernel(source_blocks, heads_local, kept_ref, after_ref, *refs):
+    del after_ref
+    *by_offset, cache_ref, sem = refs
+    me = lax.axis_index("seq")
+    request = lax.div(me, heads_local)
+    head = lax.axis_index("head") * heads_local + lax.rem(me, heads_local)
+    previous, slot = jnp.int32(-1), jnp.int32(0)
+    for k in range(kept_ref.shape[1]):
+        source = lax.div(kept_ref[request, k, head], source_blocks)
+        slot = jnp.where(source == previous, jnp.minimum(slot + 1, MOST - 1), 0)
+        previous = source
+        rows = pl.ds(pl.multiple_of(slot * BLK, BLK), BLK)
+        target = cache_ref.at[0, 0, pl.ds(k * BLK, BLK)]
+        for offset, ref in enumerate(by_offset):
+            pl.when(jnp.bitwise_xor(me, offset) == source)(
+                pltpu.make_async_copy(ref.at[rows], target, sem).start
+            )
+    pltpu.make_async_copy(cache_ref, cache_ref, sem).wait()
+
+
+def place(kept_blocks, after, blocks, source_blocks, heads_local):
+    kept_count = kept_blocks.shape[1]
+    anywhere = pl.BlockSpec(memory_space=pl.ANY)
+    return pl.pallas_call(
+        functools.partial(place_kernel, source_blocks, heads_local),
+        out_shape=jax.ShapeDtypeStruct((1, 1, kept_count * BLK, 2 * HD), jnp.bfloat16),
+        in_specs=[pl.BlockSpec(memory_space=pltpu.SMEM)] + [anywhere] * (1 + len(blocks)),
+        out_specs=anywhere,
+        scratch_shapes=[pltpu.SemaphoreType.DMA],
+        compiler_params=pltpu.CompilerParams(vmem_limit_bytes=8 * 1024 * 1024),
+        cost_estimate=pl.CostEstimate(flops=10**9, bytes_accessed=0, transcendentals=0),
+        name="place",
+    )(kept_blocks, after, *blocks)
+
+
 def attend_kernel(direct, source_blocks, heads_local, kept_ref, cos_ref, sin_ref, *refs):
     kept_count = kept_ref.shape[1]
     step_count = cos_ref.shape[0] // 2
@@ -235,33 +270,21 @@
     request = lax.div(me, heads_local)
     head = lax.axis_index("head") * heads_local + lax.rem(me, heads_local)
     if direct:
-        cache_ref, attended_ref, sem = refs[-3:]
-        by_offset, parts_refs = refs[:4][::-1], refs[4:8][::-1]
-        kept = cache_ref.at[0, 0]
-    else:
-        parts_ref, blocks_ref, cache_ref, attended_ref, sem, kept = refs
-
-    def start_copy(k, carry):
-        previous, slot = carry
-        source = lax.div(kept_ref[request, k, head], source_blocks)
-        slot = jnp.where(source == previous, jnp.minimum(slot + 1, MOST - 1), 0)
-        target = kept.at[pl.ds(pl.multiple_of(k * BLK, BLK), BLK)]
-        rows = pl.ds(pl.multiple_of(slot * BLK, BLK), BLK)
-        if direct:
-            for offset, ref in enumerate(by_offset):
-                pl.when(jnp.bitwise_xor(me, offset) == source)(
-                    pltpu.make_async_copy(ref.at[rows], target, sem).start
-                )
-        else:
+        by_offset, parts_refs, attended_ref = refs[:4][::-1], refs[4:8][::-1], refs[8]
+        total = sum(ref[...] for ref in parts_refs)
+    else:
+        parts_ref, blocks_ref, attended_ref, cache_ref, sem, kept = refs
+
+        def start_copy(k, carry):
+            previous, slot = carry
+            source = lax.div(kept_ref[request, k, head], source_blocks)
+            slot = jnp.where(source == previous, jnp.minimum(slot + 1, MOST - 1), 0)
+            target = kept.at[pl.ds(pl.multiple_of(k * BLK, BLK), BLK)]
+            rows = pl.ds(pl.multiple_of(slot * BLK, BLK), BLK)
             pltpu.make_async_copy(blocks_ref.at[source, rows], target, sem).start()
-        return source, slot
-
-    lax.fori_loop(
-        0, kept_count, start_copy, (jnp.int32(-1), jnp.int32(0)), unroll=kept_count <= 8
-    )
-    if direct:
-        total = sum(ref[...] for ref in parts_refs)
-    else:
+            return source, slot
+
+        lax.fori_loop(0, kept_count, start_copy, (jnp.int32(-1), jnp.int32(0)))
         total = jnp.sum(parts_ref[...], axis=0)
         pltpu.make_async_copy(kept, kept, sem).wait()
         pltpu.make_async_copy(kept, cache_ref.at[0, 0], sem).start()
@@ -315,27 +338,31 @@
     else:
         for i in range(attended_ref.shape[0]):
             attended_ref[i] = attended
-    pltpu.make_async_copy(cache_ref, cache_ref, sem).wait()
+        pltpu.make_async_copy(cache_ref, cache_ref, sem).wait()
 
 
 def attend(kept_blocks, arrivals, source_blocks, heads_local, step_count, seq_count, direct):
     kept_count = kept_blocks.shape[1]
-    row_width = 2 * HD
     cosine, sine = rope_tables(source_blocks * BLK * seq_count, step_count)
     shape = (QPK * step_count, HD)
-    scratch = [pltpu.SemaphoreType.DMA]
-    if not direct:
-        shape = (seq_count,) + shape
-        scratch.append(pltpu.VMEM((kept_count * BLK, row_width), jnp.bfloat16))
     vmem = pl.BlockSpec(memory_space=pltpu.VMEM)
+    if direct:
+        shapes = [jax.ShapeDtypeStruct(shape, jnp.bfloat16)]
+        out_specs = [vmem]
+        scratch = []
+    else:
+        cache = (1, 1, kept_count * BLK, 2 * HD)
+        shapes = [
+            jax.ShapeDtypeStruct((seq_count,) + shape, jnp.bfloat16),
+            jax.ShapeDtypeStruct(cache, jnp.bfloat16),
+        ]
+        out_specs = [vmem, pl.BlockSpec(memory_space=pl.ANY)]
+        scratch = [pltpu.SemaphoreType.DMA, pltpu.VMEM(cache[2:], jnp.bfloat16)]
     return pl.pallas_call(
         functools.partial(attend_kernel, direct, source_blocks, heads_local),
-        out_shape=(
-            jax.ShapeDtypeStruct((1, 1, kept_count * BLK, row_width), jnp.bfloat16),
-            jax.ShapeDtypeStruct(shape, jnp.bfloat16),
-        ),
+        out_shape=shapes,
         in_specs=[pl.BlockSpec(memory_space=pltpu.SMEM)] + [vmem] * (2 + len(arrivals)),
-        out_specs=(pl.BlockSpec(memory_space=pl.ANY), vmem),
+        out_specs=out_specs,
         scratch_shapes=scratch,
         compiler_params=pltpu.CompilerParams(vmem_limit_bytes=16 * 1024 * 1024),
         cost_estimate=pl.CostEstimate(flops=10**10, bytes_accessed=0, transcendentals=0),
@@ -343,23 +370,51 @@
     )(kept_blocks, jnp.asarray(cosine), jnp.asarray(sine), *arrivals)
 
 
-def output_kernel(heads_local, w_ref, *refs):
-    gathered_refs, out_ref = refs[:-1], refs[-1]
-    query_rows = gathered_refs[0].shape[-2]
+def merge_heads(first, second, step_count):
+    pieces = []
+    for h in range(QPK):
+        rows = slice(h * step_count, (h + 1) * step_count)
+        pieces.append(jnp.concatenate([first[rows], second[rows]], axis=0))
+    return jnp.concatenate(pieces, axis=1).astype(jnp.bfloat16)
+
+
+def output_half_kernel(flip, w_ref, same_ref, other_ref, *refs):
+    out_ref = refs[-1]
+    query_rows = same_ref.shape[0]
+    me = lax.axis_index("seq")
+    local = jnp.bitwise_and(me, 1)
+    if flip:
+        local = 1 - local
+    second = me >= 2
+    same = same_ref[...].astype(jnp.float32)
+    other = other_ref[...].astype(jnp.float32)
+    merged = merge_heads(
+        jnp.where(second, other, same), jnp.where(second, same, other), query_rows // QPK
+    )
+    depth = w_ref.shape[0] // 2
+    weights = w_ref[pl.ds(pl.multiple_of(local * depth, depth), depth), :]
+    total = jnp.dot(merged, weights, preferred_element_type=jnp.float32)
+    out_ref[...] = total if len(refs) == 1 else total + refs[0][...]
+
+
+def output_half(flip, w_out, same, other, *addend):
+    rows = 2 * same.shape[0] // QPK
+    vmem = pl.BlockSpec(memory_space=pltpu.VMEM)
+    return pl.pallas_call(
+        functools.partial(output_half_kernel, flip),
+        out_shape=jax.ShapeDtypeStruct((rows, w_out.shape[1]), jnp.float32),
+        in_specs=[vmem] * (3 + len(addend)),
+        out_specs=vmem,
+        compiler_params=pltpu.CompilerParams(vmem_limit_bytes=8 * 1024 * 1024),
+        cost_estimate=pl.CostEstimate(flops=10**9, bytes_accessed=0, transcendentals=0),
+        name="output_half",
+    )(w_out, same, other, *addend)
+
+
+def output_kernel(heads_local, w_ref, gathered_ref, out_ref):
+    pair_count, query_rows, _ = gathered_ref.shape
     step_count = query_rows // QPK
-    if len(gathered_refs) == 1:
-        pair_count = gathered_refs[0].shape[0]
-        pairs = [gathered_refs[0][p].astype(jnp.float32) for p in range(pair_count)]
-    else:
-        pair_count = len(gathered_refs)
-        me = lax.axis_index("seq")
-        arrived = [ref[...].astype(jnp.float32) for ref in gathered_refs]
-        pairs = arrived
-        bit = 1
-        while bit < pair_count:
-            swap = jnp.bitwise_and(me, bit) != 0
-            pairs = [jnp.where(swap, pairs[p ^ bit], pairs[p]) for p in range(pair_count)]
-            bit *= 2
+    pairs = [gathered_ref[p].astype(jnp.float32) for p in range(pair_count)]
     requests = pair_count // heads_local
     pieces = []
     for l in range(heads_local):
@@ -371,30 +426,21 @@
                 )
             )
     merged = jnp.concatenate(pieces, axis=1).astype(jnp.bfloat16)
-    total = jnp.dot(merged, w_ref[...], preferred_element_type=jnp.float32)
-    if len(out_ref.shape) == 2:
-        out_ref[...] = total
-    else:
-        for i in range(out_ref.shape[0]):
-            out_ref[i] = total
-
-
-def output(gathered, w_out, heads_local, pair_count, head_count):
-    query_rows = gathered[0].shape[-2]
-    total_rows = pair_count // heads_local * (query_rows // QPK)
-    shape = (total_rows, w_out.shape[1])
-    if not is_direct(head_count):
-        shape = (head_count,) + shape
+    out_ref[...] = jnp.dot(merged, w_ref[...], preferred_element_type=jnp.float32)
+
+
+def output(gathered, w_out, heads_local):
+    pair_count, query_rows, _ = gathered.shape
+    rows = pair_count // heads_local * (query_rows // QPK)
     vmem = pl.BlockSpec(memory_space=pltpu.VMEM)
-    terms = pl.pallas_call(
+    return pl.pallas_call(
         functools.partial(output_kernel, heads_local),
-        out_shape=jax.ShapeDtypeStruct(shape, jnp.float32),
-        in_specs=[vmem] * (1 + len(gathered)),
+        out_shape=jax.ShapeDtypeStruct((rows, w_out.shape[1]), jnp.float32),
+        in_specs=[vmem] * 2,
         out_specs=vmem,
         compiler_params=pltpu.CompilerParams(vmem_limit_bytes=8 * 1024 * 1024),
         name="output_projection",
-    )(pltpu.with_memory_space_constraint(w_out, pltpu.VMEM), *gathered)
-    return terms
+    )(w_out, gathered)
 
 
 def shards(source_cache, kept_blocks, new_hidden, norm_gain, w_query, w_keyval, w_out):
@@ -405,33 +451,35 @@
     pair_count = requests * heads_local
 
     kept_blocks = kept_blocks.transpose(0, 2, 1)
-    direct = is_direct(seq_count)
+    source_blocks = source_tokens // BLK
+    direct = is_direct(seq_count) and heads_local == 2
     weights = (new_hidden, norm_gain, w_query, w_keyval)
+    w_out = pltpu.with_memory_space_constraint(w_out, pltpu.VMEM)
+    shape = (source_blocks, heads_local, step_count, seq_count, direct)
     if direct:
         partners = range(1, seq_count)
-        blocks = pick(kept_blocks, source_cache, direct)
+        blocks = list(pick(kept_blocks, source_cache, direct))
         parts = list(project(blocks[0], *weights, pair_count, direct))
         blocks = [blocks[0]] + [swap(blocks[k], "seq", k) for k in partners]
         parts[1], blocks[3] = lax.optimization_barrier((parts[1], blocks[3]))
         parts = [parts[0]] + [swap(parts[k], "seq", k) for k in partners]
-        arrivals = blocks[::-1] + parts[::-1]
+        (attended,) = attend(kept_blocks, blocks[::-1] + parts[::-1], *shape)
+        kept_cache = place(kept_blocks, attended, blocks, source_blocks, heads_local)
+        first, second, third = [swap(attended, "seq", k) for k in partners]
+        first, kept_cache = lax.optimization_barrier((first, kept_cache))
+        terms = output_half(True, w_out, first, third)
+        terms = output_half(False, w_out, attended, second, terms)
     else:
         (blocks,) = pick(kept_blocks, source_cache, direct)
         (parts,) = project(blocks, *weights, pair_count, direct)
         arrivals = [all_to_all(parts, "seq"), all_to_all(blocks, "seq")]
-    kept_cache, attended = attend(
-        kept_blocks, arrivals, source_tokens // BLK, heads_local, step_count, seq_count, direct
-    )
-    if direct:
-        gathered = [attended] + [swap(attended, "seq", k) for k in range(1, seq_count)]
-    else:
-        gathered = [all_to_all(attended, "seq")]
-    terms = output(gathered, w_out, heads_local, pair_count, head_count)
+        attended, kept_cache = attend(kept_blocks, arrivals, *shape)
+        terms = output(all_to_all(attended, "seq"), w_out, heads_local)
     if is_direct(head_count):
         terms = terms + swap(terms, "head", 2)
         summed = terms + swap(terms, "head", 1)
     else:
-        summed = jnp.sum(all_to_all(terms, "head"), axis=0)
+        summed = lax.psum(terms, "head")
     summed = summed.reshape(requests, step_count, width)
     decoded = (new_hidden.astype(jnp.float32) + summed).astype(jnp.bfloat16)
     return (kept_cache, decoded)

time: 36.7 us -> 35.8 us (0.975)
  waiting for transfers between devices: 9.21 us -> 7.51 us
  Pallas kernels: 6.36 us -> 7.31 us
    ppermute x11, waiting for transfers between devices: 9.21 us -> 7.51 us  [swap(): return lax.ppermute(outgoing, axis, [(i, i ^ offset) for i in range(count)])]
    pallas_call x1 -> x3, Pallas kernels: 1.19 us -> 2.63 us  [the longest x1 1.32 us: place(): pl.pallas_call(functools.partial(place_kernel, source_blocks, heads_local...]
    pallas_call x1, Pallas kernels: 1.62 us -> 1.12 us  [attend(): pl.pallas_call(functools.partial(attend_kernel, direct, source_blocks, he...]
  transfers between devices with their start and end apart: 11 -> 11, of which waited for: 5 -> 5; matrix products, arithmetic and copies ran while one was open for 0% -> 0% of each run, Pallas kernels for 6% -> 11%
where the time goes in v9:
time: 35.8 us; the launch traced here: 35.7 us
  starting transfers between devices  19.3 us (54%)
  waiting for transfers between devices  7.51 us (21%)
  Pallas kernels  7.31 us (20%)
  between operations  0.8 us (2%)
  other arithmetic  0.65 us (2%)
    ppermute x11, starting transfers between devices, swap(): return lax.ppermute(outgoing, axis, [(i, i ^ offset) for i in range(count)])  19.3 us
    ppermute x11, waiting for transfers between devices, swap(): return lax.ppermute(outgoing, axis, [(i, i ^ offset) for i in range(count)])  7.51 us
    pallas_call x1, Pallas kernels, project(): pl.pallas_call(functools.partial(project_kernel, direct), out_shape=shape...  2.12 us
    pallas_call x1, Pallas kernels, pick(): pl.pallas_call(pick_near_kernel if direct else pick_all_kernel, out_shape...  1.43 us
    pallas_call x1, Pallas kernels, place(): pl.pallas_call(functools.partial(place_kernel, source_blocks, heads_local...  1.32 us
    pallas_call x2, Pallas kernels, output_half(): pl.pallas_call(functools.partial(output_half_kernel, flip), out_shape=jax...  1.31 us
    pallas_call x1, Pallas kernels, attend(): pl.pallas_call(functools.partial(attend_kernel, direct, source_blocks, he...  1.12 us
  transfers between devices with their start and end apart: 11, of which 5 were waited for; matrix products, arithmetic and copies ran while one was open for 0% of the time, Pallas kernels for 11%

profile of v9, /device:TPU:0, one launch (start us, length us, event | category | flops | bytes accessed | tf_op | source)
XLA Modules:
  0.0 35.7 jit_solution(10476965729596324908)
XLA Ops:
  0.7 1.4 %pick_blocks.1 = (bf16[256,256]{1,0:T(8,128)(2,1)S(1)}, bf16[256,256]{1,0:T(8,128)(2,1)S(1)}, bf16[256,256]{1,0:T(8,128)(2,1)S(1)}, bf16[256,256]{1,0:T(8,128)(2,1)S(1)}) custom-call(s32[2,4,8]{2,1,0:T(4,128)} %bitcast.5, bf16[2,2,512,256]{3,2,1,0:T(8,128)(2,1)} %cache_ref.1), custom_call_target="tpu_custom_call" | custom-call | flops 10000000000 | tf_op jit(solution)/shard_map/pick_blocks/pallas_call | solution.py:119
  2.1 0.0 copy-start.4
  2.1 0.0 copy-start.5
  2.1 0.0 copy-start.6
  2.1 5.1 %collective-permute-start = (bf16[256,256]{1,0:T(8,128)(2,1)S(1)}, bf16[256,256]{1,0:T(8,128)(2,1)S(1)}, u32[]{:S(2)}, u32[]{:S(2)}) collective-permute-start(bf16[256,256]{1,0:T(8,128)(2,1)S(1)} %get-tuple-element.16), channel_id=1, source_target_pairs={{0,12},{4,8},{8,4},{12,0},{1,13},{5,9},{9,5},{13,1},{2,14},{6,10},... | collective-permute-start | bytes 393224 | tf_op jit(solution)/shard_map/ppermute | solution.py:43
  7.3 0.6 %collective-permute-start.2 = (bf16[256,256]{1,0:T(8,128)(2,1)S(1)}, bf16[256,256]{1,0:T(8,128)(2,1)S(1)}, u32[]{:S(2)}, u32[]{:S(2)}) collective-permute-start(bf16[256,256]{1,0:T(8,128)(2,1)S(1)} %get-tuple-element.19), channel_id=1, source_target_pairs={{0,4},{4,0},{8,12},{12,8},{1,5},{5,1},{9,13},{13,9},{2,6},{6,2},{1... | collective-permute-start | bytes 393224 | tf_op jit(solution)/shard_map/ppermute | solution.py:43
  7.9 2.1 %project.1 = (f32[48,128]{1,0:T(8,128)S(1)}, f32[48,128]{1,0:T(8,128)S(1)}, f32[48,128]{1,0:T(8,128)S(1)}, f32[48,128]{1,0:T(8,128)S(1)}) custom-call(bf16[256,256]{1,0:T(8,128)(2,1)S(1)} %get-tuple-element.14.after_ref.refs_3_.refs_0_, bf16[2,4,2048]{2,1,0:T(4,128)(2,1)S(1)} %copy-done.2, bf16[16,128]{1,0:T(8,128)(2,1)S(1)} %bitcast.4, ...), custom_call_target="tpu_custom_call" | custom-call | flops 83886080 | bytes 10485760 | tf_op jit(solution)/shard_map/project/pallas_call | solution.py:210
  10.0 3.8 %collective-permute-start.3 = (f32[48,128]{1,0:T(8,128)S(1)}, f32[48,128]{1,0:T(8,128)S(1)}, u32[]{:S(2)}, u32[]{:S(2)}) collective-permute-start(f32[48,128]{1,0:T(8,128)S(1)} %get-tuple-element.20), channel_id=1, source_target_pairs={{0,12},{4,8},{8,4},{12,0},{1,13},{5,9},{9,5},{13,1},{2,14},{6,10},... | collective-permute-start | bytes 73736 | tf_op jit(solution)/shard_map/ppermute | solution.py:43
  13.9 3.7 %collective-permute-start.5 = (f32[48,128]{1,0:T(8,128)S(1)}, f32[48,128]{1,0:T(8,128)S(1)}, u32[]{:S(2)}, u32[]{:S(2)}) collective-permute-start(f32[48,128]{1,0:T(8,128)S(1)} %get-tuple-element.22), channel_id=1, source_target_pairs={{0,4},{4,0},{8,12},{12,8},{1,5},{5,1},{9,13},{13,9},{2,6},{6,2},{1... | collective-permute-start | bytes 73736 | tf_op jit(solution)/shard_map/ppermute | solution.py:43
  17.6 2.8 %collective-permute-done.4.refs_5_ = f32[48,128]{1,0:T(8,128)S(1)} collective-permute-done((f32[48,128]{1,0:T(8,128)S(1)}, f32[48,128]{1,0:T(8,128)S(1)}, u32[]{:S(2)}, u32[]{:S(2)}) %collective-permute-start.4) | collective-permute-done | bytes 24608 | tf_op jit(solution)/shard_map/ppermute | solution.py:43
  20.5 0.0 slice-start
  20.5 1.1 %attend.1.after_ref.same_ref = bf16[32,128]{1,0:T(8,128)(2,1)S(1)} custom-call(s32[2,4,8]{2,1,0:T(4,128)S(1)} %bitcast.6, f32[8,128]{1,0:T(8,128)S(1)} %copy-done.6, f32[8,128]{1,0:T(8,128)S(1)} %copy-done.5, bf16[256,256]{1,0:T(8,128)(2,1)S(1)} %collective-permute-done.refs_0_.refs_3_, bf16[256,256]{1,0:T(8,128)(2,1)S(1)} %collective-permute-done.1.refs_1_.refs_2_, ...), custom_call_target="tpu_custom_call" | custom-call | flops 10000000000 | tf_op jit(solution)/shard_map/attend/pallas_call | solution.py:361
  21.6 2.5 %collective-permute-start.8 = (bf16[32,128]{1,0:T(8,128)(2,1)S(1)}, bf16[32,128]{1,0:T(8,128)(2,1)S(1)}, u32[]{:S(2)}, u32[]{:S(2)}) collective-permute-start(bf16[32,128]{1,0:T(8,128)(2,1)S(1)} %attend.1.after_ref.same_ref), channel_id=1, source_target_pairs={{0,12},{4,8},{8,4},{12,0},{1,13},{5,9},{9,5},{13,1},{2,14},{6,10},... | collective-permute-start | bytes 24584 | tf_op jit(solution)/shard_map/ppermute | solution.py:43
  24.2 1.9 %collective-permute-start.6 = (bf16[32,128]{1,0:T(8,128)(2,1)S(1)}, bf16[32,128]{1,0:T(8,128)(2,1)S(1)}, u32[]{:S(2)}, u32[]{:S(2)}) collective-permute-start(bf16[32,128]{1,0:T(8,128)(2,1)S(1)} %attend.1.after_ref.same_ref), channel_id=1, source_target_pairs={{0,4},{4,0},{8,12},{12,8},{1,5},{5,1},{9,13},{13,9},{2,6},{6,2},{1... | collective-permute-start | bytes 24584 | tf_op jit(solution)/shard_map/ppermute | solution.py:43
  26.1 1.3 %place.1 = bf16[1,1,512,256]{3,2,1,0:T(8,128)(2,1)} custom-call(s32[2,4,8]{2,1,0:T(4,128)S(1)} %bitcast.7, bf16[32,128]{1,0:T(8,128)(2,1)S(1)} %attend.1.after_ref.same_ref, bf16[256,256]{1,0:T(8,128)(2,1)S(1)} %get-tuple-element.14.after_ref.refs_3_.refs_0_, bf16[256,256]{1,0:T(8,128)(2,1)S(1)} %collective-permute-done.2.refs_2_.refs_1_, ...), custom_call_target="tpu_custom_call" | custom-call | flops 1000000000 | tf_op jit(solution)/shard_map/place/pallas_call | solution.py:254
  27.4 0.4 %collective-permute-done.6.same_ref = bf16[32,128]{1,0:T(8,128)(2,1)S(1)} collective-permute-done((bf16[32,128]{1,0:T(8,128)(2,1)S(1)}, bf16[32,128]{1,0:T(8,128)(2,1)S(1)}, u32[]{:S(2)}, u32[]{:S(2)}) %collective-permute-start.6) | collective-permute-done | bytes 8224 | tf_op jit(solution)/shard_map/ppermute | solution.py:43
  27.9 0.7 %output_half.2.refs_0_ = f32[8,2048]{1,0:T(8,128)S(1)} custom-call(bf16[2048,2048]{1,0:T(8,128)(2,1)S(1)} %bitcast.3, bf16[32,128]{1,0:T(8,128)(2,1)S(1)} %collective-permute-done.6.same_ref, bf16[32,128]{1,0:T(8,128)(2,1)S(1)} %collective-permute-done.8.other_ref), custom_call_target="tpu_custom_call" | custom-call | flops 1000000000 | tf_op jit(solution)/shard_map/output_half/pallas_call | solution.py:403
  28.5 0.2 collective-permute-done.7.other_ref
  28.7 0.6 %output_half.3 = f32[8,2048]{1,0:T(8,128)S(1)} custom-call(bf16[2048,2048]{1,0:T(8,128)(2,1)S(1)} %bitcast.3, bf16[32,128]{1,0:T(8,128)(2,1)S(1)} %attend.1.after_ref.same_ref, bf16[32,128]{1,0:T(8,128)(2,1)S(1)} %collective-permute-done.7.other_ref, f32[8,2048]{1,0:T(8,128)S(1)} %output_half.2.refs_0_), custom_call_target="tpu_custom_call" | custom-call | flops 1000000000 | tf_op jit(solution)/shard_map/output_half/pallas_call | solution.py:403
  29.4 1.5 %collective-permute-start.9 = (f32[8,2048]{1,0:T(8,128)S(1)}, f32[8,2048]{1,0:T(8,128)S(1)}, u32[]{:S(2)}, u32[]{:S(2)}) collective-permute-start(f32[8,2048]{1,0:T(8,128)S(1)} %output_half.3), channel_id=1, source_target_pairs={{0,2},{1,3},{2,0},{3,1},{4,6},{5,7},{6,4},{7,5},{8,10},{9,11},{10,... | collective-permute-start | bytes 196616 | tf_op jit(solution)/shard_map/ppermute | solution.py:43
  30.9 2.8 %collective-permute-done.9 = f32[8,2048]{1,0:T(8,128)S(1)} collective-permute-done((f32[8,2048]{1,0:T(8,128)S(1)}, f32[8,2048]{1,0:T(8,128)S(1)}, u32[]{:S(2)}, u32[]{:S(2)}) %collective-permute-start.9) | collective-permute-done | bytes 65568 | tf_op jit(solution)/shard_map/ppermute | solution.py:43
  33.7 0.1 collective-permute-start.10
  33.8 1.2 %collective-permute-done.10 = f32[8,2048]{1,0:T(8,128)S(1)} collective-permute-done((f32[8,2048]{1,0:T(8,128)S(1)}, f32[8,2048]{1,0:T(8,128)S(1)}, u32[]{:S(2)}, u32[]{:S(2)}) %collective-permute-start.10) | collective-permute-done | bytes 65568 | tf_op jit(solution)/shard_map/ppermute | solution.py:43
  35.0 0.6 %add_convert_fusion = bf16[2,4,2048]{2,1,0:T(4,128)(2,1)} fusion(f32[2,4,2048]{2,1,0:T(4,128)S(1)} %reshape.11, bf16[2,4,2048]{2,1,0:T(4,128)(2,1)S(1)} %copy-done.2), kind=kLoop, calls=%fused_computation | loop fusion | flops 49152 | bytes 131072 | tf_op jit(solution)/shard_map/convert_element_type | solution.py:484
  (27 shorter events, 0.1 us)
Async XLA Ops:
  0.6 7.3 %copy-start = (bf16[2048,2048]{1,0:T(8,128)(2,1)S(1)}, bf16[2048,2048]{1,0:T(8,128)(2,1)}, u32[]{:S(2)}) copy-start(bf16[2048,2048]{1,0:T(8,128)(2,1)} %wq_ref.1) | copy-start | bytes 25165828
  0.6 7.3 %copy-start.1 = (bf16[2048,2,256]{2,1,0:T(2,128)(2,1)S(1)}, bf16[2048,2,256]{2,1,0:T(2,128)(2,1)}, u32[]{:S(2)}) copy-start(bf16[2048,2,256]{2,1,0:T(2,128)(2,1)} %wkv_ref.1) | copy-start | bytes 6291460
  0.7 7.3 %copy-start.2 = (bf16[2,4,2048]{2,1,0:T(4,128)(2,1)S(1)}, bf16[2,4,2048]{2,1,0:T(4,128)(2,1)}, u32[]{:S(2)}) copy-start(bf16[2,4,2048]{2,1,0:T(4,128)(2,1)} %hidden_ref.1) | copy-start | bytes 98308
  0.7 7.3 %copy-start.3 = (bf16[2048]{0:T(1024)(128)(2,1)S(1)}, bf16[2048]{0:T(1024)(128)(2,1)}, u32[]{:S(2)}) copy-start(bf16[2048]{0:T(1024)(128)(2,1)} %param.12) | copy-start | bytes 12292
  2.1 18.4 %copy-start.4 = (s32[2,8,4]{1,2,0:T(4,128)S(1)}, s32[2,8,4]{1,2,0:T(4,128)}, u32[]{:S(2)}) copy-start(s32[2,8,4]{1,2,0:T(4,128)} %param.10) | copy-start | bytes 772
  2.1 18.4 %copy-start.5 = (f32[8,128]{1,0:T(8,128)S(1)}, f32[8,128]{1,0:T(8,128)}, u32[]{:S(2)}) copy-start(f32[8,128]{1,0:T(8,128)} %constant.5.clone.sin_ref) | copy-start | bytes 12292
  2.1 18.4 %copy-start.6 = (f32[8,128]{1,0:T(8,128)S(1)}, f32[8,128]{1,0:T(8,128)}, u32[]{:S(2)}) copy-start(f32[8,128]{1,0:T(8,128)} %constant.4.clone.cos_ref) | copy-start | bytes 12292
  2.1 11.7 %collective-permute-start = (bf16[256,256]{1,0:T(8,128)(2,1)S(1)}, bf16[256,256]{1,0:T(8,128)(2,1)S(1)}, u32[]{:S(2)}, u32[]{:S(2)}) collective-permute-start(bf16[256,256]{1,0:T(8,128)(2,1)S(1)} %get-tuple-element.16), channel_id=1, source_target_pairs={{0,12},{4,8},{8,4},{12,0},{1,13},{5,9},{9,5},{13,1},{2,14},{6,10},... | collective-permute-start | bytes 393224 | tf_op jit(solution)/shard_map/ppermute | solution.py:43
  7.3 13.2 %collective-permute-start.1 = (bf16[256,256]{1,0:T(8,128)(2,1)S(1)}, bf16[256,256]{1,0:T(8,128)(2,1)S(1)}, u32[]{:S(2)}, u32[]{:S(2)}) collective-permute-start(bf16[256,256]{1,0:T(8,128)(2,1)S(1)} %get-tuple-element.18), channel_id=1, source_target_pairs={{0,8},{4,12},{8,0},{12,4},{1,9},{5,13},{9,1},{13,5},{2,10},{6,14},... | collective-permute-start | bytes 393224 | tf_op jit(solution)/shard_map/ppermute | solution.py:43
  7.3 13.2 %collective-permute-start.2 = (bf16[256,256]{1,0:T(8,128)(2,1)S(1)}, bf16[256,256]{1,0:T(8,128)(2,1)S(1)}, u32[]{:S(2)}, u32[]{:S(2)}) collective-permute-start(bf16[256,256]{1,0:T(8,128)(2,1)S(1)} %get-tuple-element.19), channel_id=1, source_target_pairs={{0,4},{4,0},{8,12},{12,8},{1,5},{5,1},{9,13},{13,9},{2,6},{6,2},{1... | collective-permute-start | bytes 393224 | tf_op jit(solution)/shard_map/ppermute | solution.py:43
  10.0 7.5 %collective-permute-start.3 = (f32[48,128]{1,0:T(8,128)S(1)}, f32[48,128]{1,0:T(8,128)S(1)}, u32[]{:S(2)}, u32[]{:S(2)}) collective-permute-start(f32[48,128]{1,0:T(8,128)S(1)} %get-tuple-element.20), channel_id=1, source_target_pairs={{0,12},{4,8},{8,4},{12,0},{1,13},{5,9},{9,5},{13,1},{2,14},{6,10},... | collective-permute-start | bytes 73736 | tf_op jit(solution)/shard_map/ppermute | solution.py:43
  13.9 6.6 %collective-permute-start.4 = (f32[48,128]{1,0:T(8,128)S(1)}, f32[48,128]{1,0:T(8,128)S(1)}, u32[]{:S(2)}, u32[]{:S(2)}) collective-permute-start(f32[48,128]{1,0:T(8,128)S(1)} %get-tuple-element.21), channel_id=1, source_target_pairs={{0,8},{4,12},{8,0},{12,4},{1,9},{5,13},{9,1},{13,5},{2,10},{6,14},... | collective-permute-start | bytes 73736 | tf_op jit(solution)/shard_map/ppermute | solution.py:43
  13.9 6.6 %collective-permute-start.5 = (f32[48,128]{1,0:T(8,128)S(1)}, f32[48,128]{1,0:T(8,128)S(1)}, u32[]{:S(2)}, u32[]{:S(2)}) collective-permute-start(f32[48,128]{1,0:T(8,128)S(1)} %get-tuple-element.22), channel_id=1, source_target_pairs={{0,4},{4,0},{8,12},{12,8},{1,5},{5,1},{9,13},{13,9},{2,6},{6,2},{1... | collective-permute-start | bytes 73736 | tf_op jit(solution)/shard_map/ppermute | solution.py:43
  20.5 7.4 %slice-start = ((s8[8388608]{0:T(1024)(128)(4,1)}), s8[4194304]{0:T(1024)(128)(4,1)S(1)}, s32[]{:S(2)}) async-start(s8[8388608]{0:T(1024)(128)(4,1)} %bitcast.2), calls=%async_computation | async-start | bytes 8388608
  20.5 7.3 %slice-start.1 = ((s8[8388608]{0:T(1024)(128)(4,1)}), s8[4194304]{0:T(1024)(128)(4,1)S(1)}, s32[]{:S(2)}) async-start(s8[8388608]{0:T(1024)(128)(4,1)} %bitcast.2), calls=%async_computation.1 | async-start | bytes 8388608
  21.6 6.2 %collective-permute-start.8 = (bf16[32,128]{1,0:T(8,128)(2,1)S(1)}, bf16[32,128]{1,0:T(8,128)(2,1)S(1)}, u32[]{:S(2)}, u32[]{:S(2)}) collective-permute-start(bf16[32,128]{1,0:T(8,128)(2,1)S(1)} %attend.1.after_ref.same_ref), channel_id=1, source_target_pairs={{0,12},{4,8},{8,4},{12,0},{1,13},{5,9},{9,5},{13,1},{2,14},{6,10},... | collective-permute-start | bytes 24584 | tf_op jit(solution)/shard_map/ppermute | solution.py:43
  24.2 4.5 %collective-permute-start.7 = (bf16[32,128]{1,0:T(8,128)(2,1)S(1)}, bf16[32,128]{1,0:T(8,128)(2,1)S(1)}, u32[]{:S(2)}, u32[]{:S(2)}) collective-permute-start(bf16[32,128]{1,0:T(8,128)(2,1)S(1)} %attend.1.after_ref.same_ref), channel_id=1, source_target_pairs={{0,8},{4,12},{8,0},{12,4},{1,9},{5,13},{9,1},{13,5},{2,10},{6,14},... | collective-permute-start | bytes 24584 | tf_op jit(solution)/shard_map/ppermute | solution.py:43
  24.2 3.7 %collective-permute-start.6 = (bf16[32,128]{1,0:T(8,128)(2,1)S(1)}, bf16[32,128]{1,0:T(8,128)(2,1)S(1)}, u32[]{:S(2)}, u32[]{:S(2)}) collective-permute-start(bf16[32,128]{1,0:T(8,128)(2,1)S(1)} %attend.1.after_ref.same_ref), channel_id=1, source_target_pairs={{0,4},{4,0},{8,12},{12,8},{1,5},{5,1},{9,13},{13,9},{2,6},{6,2},{1... | collective-permute-start | bytes 24584 | tf_op jit(solution)/shard_map/ppermute | solution.py:43
  29.4 4.3 %collective-permute-start.9 = (f32[8,2048]{1,0:T(8,128)S(1)}, f32[8,2048]{1,0:T(8,128)S(1)}, u32[]{:S(2)}, u32[]{:S(2)}) collective-permute-start(f32[8,2048]{1,0:T(8,128)S(1)} %output_half.3), channel_id=1, source_target_pairs={{0,2},{1,3},{2,0},{3,1},{4,6},{5,7},{6,4},{7,5},{8,10},{9,11},{10,... | collective-permute-start | bytes 196616 | tf_op jit(solution)/shard_map/ppermute | solution.py:43
  33.7 1.3 %collective-permute-start.10 = (f32[8,2048]{1,0:T(8,128)S(1)}, f32[8,2048]{1,0:T(8,128)S(1)}, u32[]{:S(2)}, u32[]{:S(2)}) collective-permute-start(f32[8,2048]{1,0:T(8,128)S(1)} %add.9), channel_id=1, source_target_pairs={{0,1},{1,0},{2,3},{3,2},{4,5},{5,4},{6,7},{7,6},{8,9},{9,8},{10,11... | collective-permute-start | bytes 196616 | tf_op jit(solution)/shard_map/ppermute | solution.py:43

commit v10 on v9

--- a/solution.py
+++ b/solution.py
@@ -177,13 +177,13 @@
     def pieces_of(r, l):
         steps = slice(r * step_count, (r + 1) * step_count)
         square_rows = jnp.broadcast_to(square[steps], (step_count, HD))
+        high = square_rows.astype(jnp.bfloat16).astype(jnp.float32)
         own = keyval[l * row_count + r * step_count : l * row_count + (r + 1) * step_count]
         heads = [query[steps, (l * QPK + h) * HD : (l * QPK + h + 1) * HD] for h in range(QPK)]
-        return heads + [own[:, :HD], own[:, HD:], square_rows, square_rows]
+        return heads + [own[:, :HD], own[:, HD:], high, square_rows - high]
 
     def write_pair(out_ref, pieces):
-        for j, piece in enumerate(pieces):
-            out_ref[j * step_count : (j + 1) * step_count, :] = piece
+        out_ref[...] = jnp.concatenate(pieces, axis=0).astype(out_ref.dtype)
 
     for r in range(requests):
         for l in range(heads_local):
@@ -202,7 +202,8 @@
     requests, step_count, width = new_hidden.shape
     terms = ((QPK + 4) * step_count, HD)
     if direct:
-        shapes = [jax.ShapeDtypeStruct(terms, jnp.float32)] * pair_count
+        shapes = [jax.ShapeDtypeStruct(terms, jnp.float32)]
+        shapes += [jax.ShapeDtypeStruct(terms, jnp.bfloat16)] * (pair_count - 1)
     else:
         shapes = [jax.ShapeDtypeStruct((pair_count,) + terms, jnp.float32)]
     vmem = pl.BlockSpec(memory_space=pltpu.VMEM)
@@ -271,7 +272,7 @@
     head = lax.axis_index("head") * heads_local + lax.rem(me, heads_local)
     if direct:
         by_offset, parts_refs, attended_ref = refs[:4][::-1], refs[4:8][::-1], refs[8]
-        total = sum(ref[...] for ref in parts_refs)
+        total = sum(ref[...].astype(jnp.float32) for ref in parts_refs)
     else:
         parts_ref, blocks_ref, attended_ref, cache_ref, sem, kept = refs
 
@@ -289,7 +290,9 @@
         pltpu.make_async_copy(kept, kept, sem).wait()
         pltpu.make_async_copy(kept, cache_ref.at[0, 0], sem).start()
     query_rows = QPK * step_count
-    inverse = lax.rsqrt(total[query_rows + 2 * step_count :] * (1.0 / D) + EPS)
+    high, low = total[-2 * step_count : -step_count], total[-step_count:]
+    inverse = lax.rsqrt((high + low) * (1.0 / D) + EPS)
+    inverse = jnp.concatenate([inverse, inverse], axis=0)
     cosine, sine = cos_ref[...], sin_ref[...]
     query = total[:query_rows].reshape(QPK // 2, 2 * step_count, HD) * inverse[None]
     query = rotate(query, cosine[None], sine[None]).reshape(query_rows, HD).astype(jnp.bfloat16)

time: 35.8 us -> 35.2 us (0.983)
  waiting for transfers between devices: 7.51 us -> 7.08 us
    ppermute x11, waiting for transfers between devices: 7.51 us -> 7.08 us  [swap(): return lax.ppermute(outgoing, axis, [(i, i ^ offset) for i in range(count)])]
  transfers between devices with their start and end apart: 11 -> 11, of which waited for: 5 -> 4; matrix products, arithmetic and copies ran while one was open for 0% -> 0% of each run, Pallas kernels for 11% -> 12%
where the time goes in v10:
time: 35.2 us; the launch traced here: 35 us
  starting transfers between devices  19.1 us (54%)
  Pallas kernels  7.34 us (21%)
  waiting for transfers between devices  7.08 us (20%)
  between operations  0.8 us (2%)
  other arithmetic  0.65 us (2%)
    ppermute x11, starting transfers between devices, swap(): return lax.ppermute(outgoing, axis, [(i, i ^ offset) for i in range(count)])  19.1 us
    ppermute x11, waiting for transfers between devices, swap(): return lax.ppermute(outgoing, axis, [(i, i ^ offset) for i in range(count)])  7.08 us
    pallas_call x1, Pallas kernels, project(): pl.pallas_call(functools.partial(project_kernel, direct), out_shape=shape...  2.13 us
    pallas_call x1, Pallas kernels, pick(): pl.pallas_call(pick_near_kernel if direct else pick_all_kernel, out_shape...  1.43 us
    pallas_call x2, Pallas kernels, output_half(): pl.pallas_call(functools.partial(output_half_kernel, flip), out_shape=jax...  1.32 us
    pallas_call x1, Pallas kernels, place(): pl.pallas_call(functools.partial(place_kernel, source_blocks, heads_local...  1.32 us
    pallas_call x1, Pallas kernels, attend(): pl.pallas_call(functools.partial(attend_kernel, direct, source_blocks, he...  1.13 us
  transfers between devices with their start and end apart: 11, of which 4 were waited for; matrix products, arithmetic and copies ran while one was open for 0% of the time, Pallas kernels for 12%

profile of v10, /device:TPU:0, one launch (start us, length us, event | category | flops | bytes accessed | tf_op | source)
XLA Modules:
  0.0 35.0 jit_solution(11496116595288311118)
XLA Ops:
  0.7 1.4 %pick_blocks.1 = (bf16[256,256]{1,0:T(8,128)(2,1)S(1)}, bf16[256,256]{1,0:T(8,128)(2,1)S(1)}, bf16[256,256]{1,0:T(8,128)(2,1)S(1)}, bf16[256,256]{1,0:T(8,128)(2,1)S(1)}) custom-call(s32[2,4,8]{2,1,0:T(4,128)} %bitcast.5, bf16[2,2,512,256]{3,2,1,0:T(8,128)(2,1)} %cache_ref.1), custom_call_target="tpu_custom_call" | custom-call | flops 10000000000 | tf_op jit(solution)/shard_map/pick_blocks/pallas_call | solution.py:119
  2.1 0.0 copy-start.4
  2.1 0.0 copy-start.5
  2.1 0.0 copy-start.6
  2.1 5.1 %collective-permute-start = (bf16[256,256]{1,0:T(8,128)(2,1)S(1)}, bf16[256,256]{1,0:T(8,128)(2,1)S(1)}, u32[]{:S(2)}, u32[]{:S(2)}) collective-permute-start(bf16[256,256]{1,0:T(8,128)(2,1)S(1)} %get-tuple-element.16), channel_id=1, source_target_pairs={{0,12},{4,8},{8,4},{12,0},{1,13},{5,9},{9,5},{13,1},{2,14},{6,10},... | collective-permute-start | bytes 393224 | tf_op jit(solution)/shard_map/ppermute | solution.py:43
  7.3 0.6 %collective-permute-start.2 = (bf16[256,256]{1,0:T(8,128)(2,1)S(1)}, bf16[256,256]{1,0:T(8,128)(2,1)S(1)}, u32[]{:S(2)}, u32[]{:S(2)}) collective-permute-start(bf16[256,256]{1,0:T(8,128)(2,1)S(1)} %get-tuple-element.19), channel_id=1, source_target_pairs={{0,4},{4,0},{8,12},{12,8},{1,5},{5,1},{9,13},{13,9},{2,6},{6,2},{1... | collective-permute-start | bytes 393224 | tf_op jit(solution)/shard_map/ppermute | solution.py:43
  7.9 2.1 %project.1 = (f32[48,128]{1,0:T(8,128)S(1)}, bf16[48,128]{1,0:T(8,128)(2,1)S(1)}, bf16[48,128]{1,0:T(8,128)(2,1)S(1)}, bf16[48,128]{1,0:T(8,128)(2,1)S(1)}) custom-call(bf16[256,256]{1,0:T(8,128)(2,1)S(1)} %get-tuple-element.14.after_ref.refs_3_.refs_0_, bf16[2,4,2048]{2,1,0:T(4,128)(2,1)S(1)} %copy-done.2, bf16[16,128]{1,0:T(8,128)(2,1)S(1)} %bitcast.4, ...), custom_call_target="tpu_custom_call" | custom-call | flops 83886080 | bytes 10485760 | tf_op jit(solution)/shard_map/project/pallas_call | solution.py:211
  10.1 3.8 %collective-permute-start.3 = (bf16[48,128]{1,0:T(8,128)(2,1)S(1)}, bf16[48,128]{1,0:T(8,128)(2,1)S(1)}, u32[]{:S(2)}, u32[]{:S(2)}) collective-permute-start(bf16[48,128]{1,0:T(8,128)(2,1)S(1)} %get-tuple-element.20), channel_id=1, source_target_pairs={{0,12},{4,8},{8,4},{12,0},{1,13},{5,9},{9,5},{13,1},{2,14},{6,10},... | collective-permute-start | bytes 36872 | tf_op jit(solution)/shard_map/ppermute | solution.py:43
  13.9 3.4 %collective-permute-start.5 = (bf16[48,128]{1,0:T(8,128)(2,1)S(1)}, bf16[48,128]{1,0:T(8,128)(2,1)S(1)}, u32[]{:S(2)}, u32[]{:S(2)}) collective-permute-start(bf16[48,128]{1,0:T(8,128)(2,1)S(1)} %get-tuple-element.22), channel_id=1, source_target_pairs={{0,4},{4,0},{8,12},{12,8},{1,5},{5,1},{9,13},{13,9},{2,6},{6,2},{1... | collective-permute-start | bytes 36872 | tf_op jit(solution)/shard_map/ppermute | solution.py:43
  17.3 2.1 %collective-permute-done.4.refs_5_ = bf16[48,128]{1,0:T(8,128)(2,1)S(1)} collective-permute-done((bf16[48,128]{1,0:T(8,128)(2,1)S(1)}, bf16[48,128]{1,0:T(8,128)(2,1)S(1)}, u32[]{:S(2)}, u32[]{:S(2)}) %collective-permute-start.4) | collective-permute-done | bytes 12320 | tf_op jit(solution)/shard_map/ppermute | solution.py:43
  19.4 0.0 slice-start
  19.5 1.1 %attend.1.after_ref.same_ref = bf16[32,128]{1,0:T(8,128)(2,1)S(1)} custom-call(s32[2,4,8]{2,1,0:T(4,128)S(1)} %bitcast.6, f32[8,128]{1,0:T(8,128)S(1)} %copy-done.6, f32[8,128]{1,0:T(8,128)S(1)} %copy-done.5, bf16[256,256]{1,0:T(8,128)(2,1)S(1)} %collective-permute-done.refs_0_.refs_3_, bf16[256,256]{1,0:T(8,128)(2,1)S(1)} %collective-permute-done.1.refs_1_.refs_2_, ...), custom_call_target="tpu_custom_call" | custom-call | flops 10000000000 | tf_op jit(solution)/shard_map/attend/pallas_call | solution.py:364
  20.6 2.5 %collective-permute-start.8 = (bf16[32,128]{1,0:T(8,128)(2,1)S(1)}, bf16[32,128]{1,0:T(8,128)(2,1)S(1)}, u32[]{:S(2)}, u32[]{:S(2)}) collective-permute-start(bf16[32,128]{1,0:T(8,128)(2,1)S(1)} %attend.1.after_ref.same_ref), channel_id=1, source_target_pairs={{0,12},{4,8},{8,4},{12,0},{1,13},{5,9},{9,5},{13,1},{2,14},{6,10},... | collective-permute-start | bytes 24584 | tf_op jit(solution)/shard_map/ppermute | solution.py:43
  23.1 0.6 %collective-permute-start.7 = (bf16[32,128]{1,0:T(8,128)(2,1)S(1)}, bf16[32,128]{1,0:T(8,128)(2,1)S(1)}, u32[]{:S(2)}, u32[]{:S(2)}) collective-permute-start(bf16[32,128]{1,0:T(8,128)(2,1)S(1)} %attend.1.after_ref.same_ref), channel_id=1, source_target_pairs={{0,8},{4,12},{8,0},{12,4},{1,9},{5,13},{9,1},{13,5},{2,10},{6,14},... | collective-permute-start | bytes 24584 | tf_op jit(solution)/shard_map/ppermute | solution.py:43
  23.7 1.3 %collective-permute-start.6 = (bf16[32,128]{1,0:T(8,128)(2,1)S(1)}, bf16[32,128]{1,0:T(8,128)(2,1)S(1)}, u32[]{:S(2)}, u32[]{:S(2)}) collective-permute-start(bf16[32,128]{1,0:T(8,128)(2,1)S(1)} %attend.1.after_ref.same_ref), channel_id=1, source_target_pairs={{0,4},{4,0},{8,12},{12,8},{1,5},{5,1},{9,13},{13,9},{2,6},{6,2},{1... | collective-permute-start | bytes 24584 | tf_op jit(solution)/shard_map/ppermute | solution.py:43
  25.0 1.3 %place.1 = bf16[1,1,512,256]{3,2,1,0:T(8,128)(2,1)} custom-call(s32[2,4,8]{2,1,0:T(4,128)S(1)} %bitcast.7, bf16[32,128]{1,0:T(8,128)(2,1)S(1)} %attend.1.after_ref.same_ref, bf16[256,256]{1,0:T(8,128)(2,1)S(1)} %get-tuple-element.14.after_ref.refs_3_.refs_0_, bf16[256,256]{1,0:T(8,128)(2,1)S(1)} %collective-permute-done.2.refs_2_.refs_1_, ...), custom_call_target="tpu_custom_call" | custom-call | flops 1000000000 | tf_op jit(solution)/shard_map/place/pallas_call | solution.py:255
  26.4 1.0 %collective-permute-done.6.same_ref = bf16[32,128]{1,0:T(8,128)(2,1)S(1)} collective-permute-done((bf16[32,128]{1,0:T(8,128)(2,1)S(1)}, bf16[32,128]{1,0:T(8,128)(2,1)S(1)}, u32[]{:S(2)}, u32[]{:S(2)}) %collective-permute-start.6) | collective-permute-done | bytes 8224 | tf_op jit(solution)/shard_map/ppermute | solution.py:43
  27.4 0.7 %output_half.2.refs_0_ = f32[8,2048]{1,0:T(8,128)S(1)} custom-call(bf16[2048,2048]{1,0:T(8,128)(2,1)S(1)} %bitcast.3, bf16[32,128]{1,0:T(8,128)(2,1)S(1)} %collective-permute-done.6.same_ref, bf16[32,128]{1,0:T(8,128)(2,1)S(1)} %collective-permute-done.8.other_ref), custom_call_target="tpu_custom_call" | custom-call | flops 1000000000 | tf_op jit(solution)/shard_map/output_half/pallas_call | solution.py:406
  28.0 0.7 %output_half.3 = f32[8,2048]{1,0:T(8,128)S(1)} custom-call(bf16[2048,2048]{1,0:T(8,128)(2,1)S(1)} %bitcast.3, bf16[32,128]{1,0:T(8,128)(2,1)S(1)} %attend.1.after_ref.same_ref, bf16[32,128]{1,0:T(8,128)(2,1)S(1)} %collective-permute-done.7.other_ref, f32[8,2048]{1,0:T(8,128)S(1)} %output_half.2.refs_0_), custom_call_target="tpu_custom_call" | custom-call | flops 1000000000 | tf_op jit(solution)/shard_map/output_half/pallas_call | solution.py:406
  28.7 1.5 %collective-permute-start.9 = (f32[8,2048]{1,0:T(8,128)S(1)}, f32[8,2048]{1,0:T(8,128)S(1)}, u32[]{:S(2)}, u32[]{:S(2)}) collective-permute-start(f32[8,2048]{1,0:T(8,128)S(1)} %output_half.3), channel_id=1, source_target_pairs={{0,2},{1,3},{2,0},{3,1},{4,6},{5,7},{6,4},{7,5},{8,10},{9,11},{10,... | collective-permute-start | bytes 196616 | tf_op jit(solution)/shard_map/ppermute | solution.py:43
  30.2 2.8 %collective-permute-done.9 = f32[8,2048]{1,0:T(8,128)S(1)} collective-permute-done((f32[8,2048]{1,0:T(8,128)S(1)}, f32[8,2048]{1,0:T(8,128)S(1)}, u32[]{:S(2)}, u32[]{:S(2)}) %collective-permute-start.9) | collective-permute-done | bytes 65568 | tf_op jit(solution)/shard_map/ppermute | solution.py:43
  33.0 0.1 collective-permute-start.10
  33.1 1.2 %collective-permute-done.10 = f32[8,2048]{1,0:T(8,128)S(1)} collective-permute-done((f32[8,2048]{1,0:T(8,128)S(1)}, f32[8,2048]{1,0:T(8,128)S(1)}, u32[]{:S(2)}, u32[]{:S(2)}) %collective-permute-start.10) | collective-permute-done | bytes 65568 | tf_op jit(solution)/shard_map/ppermute | solution.py:43
  34.4 0.6 %add_convert_fusion = bf16[2,4,2048]{2,1,0:T(4,128)(2,1)} fusion(f32[2,4,2048]{2,1,0:T(4,128)S(1)} %reshape.11, bf16[2,4,2048]{2,1,0:T(4,128)(2,1)S(1)} %copy-done.2), kind=kLoop, calls=%fused_computation | loop fusion | flops 49152 | bytes 131072 | tf_op jit(solution)/shard_map/convert_element_type | solution.py:487
  (27 shorter events, 0.1 us)
Async XLA Ops:
  0.6 7.3 %copy-start = (bf16[2048,2048]{1,0:T(8,128)(2,1)S(1)}, bf16[2048,2048]{1,0:T(8,128)(2,1)}, u32[]{:S(2)}) copy-start(bf16[2048,2048]{1,0:T(8,128)(2,1)} %wq_ref.1) | copy-start | bytes 25165828
  0.6 7.3 %copy-start.1 = (bf16[2048,2,256]{2,1,0:T(2,128)(2,1)S(1)}, bf16[2048,2,256]{2,1,0:T(2,128)(2,1)}, u32[]{:S(2)}) copy-start(bf16[2048,2,256]{2,1,0:T(2,128)(2,1)} %wkv_ref.1) | copy-start | bytes 6291460
  0.7 7.3 %copy-start.2 = (bf16[2,4,2048]{2,1,0:T(4,128)(2,1)S(1)}, bf16[2,4,2048]{2,1,0:T(4,128)(2,1)}, u32[]{:S(2)}) copy-start(bf16[2,4,2048]{2,1,0:T(4,128)(2,1)} %hidden_ref.1) | copy-start | bytes 98308
  0.7 7.3 %copy-start.3 = (bf16[2048]{0:T(1024)(128)(2,1)S(1)}, bf16[2048]{0:T(1024)(128)(2,1)}, u32[]{:S(2)}) copy-start(bf16[2048]{0:T(1024)(128)(2,1)} %param.12) | copy-start | bytes 12292
  2.1 17.3 %copy-start.4 = (s32[2,8,4]{1,2,0:T(4,128)S(1)}, s32[2,8,4]{1,2,0:T(4,128)}, u32[]{:S(2)}) copy-start(s32[2,8,4]{1,2,0:T(4,128)} %param.10) | copy-start | bytes 772
  2.1 17.3 %copy-start.5 = (f32[8,128]{1,0:T(8,128)S(1)}, f32[8,128]{1,0:T(8,128)}, u32[]{:S(2)}) copy-start(f32[8,128]{1,0:T(8,128)} %constant.5.clone.sin_ref) | copy-start | bytes 12292
  2.1 17.3 %copy-start.6 = (f32[8,128]{1,0:T(8,128)S(1)}, f32[8,128]{1,0:T(8,128)}, u32[]{:S(2)}) copy-start(f32[8,128]{1,0:T(8,128)} %constant.4.clone.cos_ref) | copy-start | bytes 12292
  2.1 11.7 %collective-permute-start = (bf16[256,256]{1,0:T(8,128)(2,1)S(1)}, bf16[256,256]{1,0:T(8,128)(2,1)S(1)}, u32[]{:S(2)}, u32[]{:S(2)}) collective-permute-start(bf16[256,256]{1,0:T(8,128)(2,1)S(1)} %get-tuple-element.16), channel_id=1, source_target_pairs={{0,12},{4,8},{8,4},{12,0},{1,13},{5,9},{9,5},{13,1},{2,14},{6,10},... | collective-permute-start | bytes 393224 | tf_op jit(solution)/shard_map/ppermute | solution.py:43
  7.3 12.1 %collective-permute-start.1 = (bf16[256,256]{1,0:T(8,128)(2,1)S(1)}, bf16[256,256]{1,0:T(8,128)(2,1)S(1)}, u32[]{:S(2)}, u32[]{:S(2)}) collective-permute-start(bf16[256,256]{1,0:T(8,128)(2,1)S(1)} %get-tuple-element.18), channel_id=1, source_target_pairs={{0,8},{4,12},{8,0},{12,4},{1,9},{5,13},{9,1},{13,5},{2,10},{6,14},... | collective-permute-start | bytes 393224 | tf_op jit(solution)/shard_map/ppermute | solution.py:43
  7.3 12.1 %collective-permute-start.2 = (bf16[256,256]{1,0:T(8,128)(2,1)S(1)}, bf16[256,256]{1,0:T(8,128)(2,1)S(1)}, u32[]{:S(2)}, u32[]{:S(2)}) collective-permute-start(bf16[256,256]{1,0:T(8,128)(2,1)S(1)} %get-tuple-element.19), channel_id=1, source_target_pairs={{0,4},{4,0},{8,12},{12,8},{1,5},{5,1},{9,13},{13,9},{2,6},{6,2},{1... | collective-permute-start | bytes 393224 | tf_op jit(solution)/shard_map/ppermute | solution.py:43
  10.1 7.3 %collective-permute-start.3 = (bf16[48,128]{1,0:T(8,128)(2,1)S(1)}, bf16[48,128]{1,0:T(8,128)(2,1)S(1)}, u32[]{:S(2)}, u32[]{:S(2)}) collective-permute-start(bf16[48,128]{1,0:T(8,128)(2,1)S(1)} %get-tuple-element.20), channel_id=1, source_target_pairs={{0,12},{4,8},{8,4},{12,0},{1,13},{5,9},{9,5},{13,1},{2,14},{6,10},... | collective-permute-start | bytes 36872 | tf_op jit(solution)/shard_map/ppermute | solution.py:43
  13.9 5.5 %collective-permute-start.4 = (bf16[48,128]{1,0:T(8,128)(2,1)S(1)}, bf16[48,128]{1,0:T(8,128)(2,1)S(1)}, u32[]{:S(2)}, u32[]{:S(2)}) collective-permute-start(bf16[48,128]{1,0:T(8,128)(2,1)S(1)} %get-tuple-element.21), channel_id=1, source_target_pairs={{0,8},{4,12},{8,0},{12,4},{1,9},{5,13},{9,1},{13,5},{2,10},{6,14},... | collective-permute-start | bytes 36872 | tf_op jit(solution)/shard_map/ppermute | solution.py:43
  13.9 5.5 %collective-permute-start.5 = (bf16[48,128]{1,0:T(8,128)(2,1)S(1)}, bf16[48,128]{1,0:T(8,128)(2,1)S(1)}, u32[]{:S(2)}, u32[]{:S(2)}) collective-permute-start(bf16[48,128]{1,0:T(8,128)(2,1)S(1)} %get-tuple-element.22), channel_id=1, source_target_pairs={{0,4},{4,0},{8,12},{12,8},{1,5},{5,1},{9,13},{13,9},{2,6},{6,2},{1... | collective-permute-start | bytes 36872 | tf_op jit(solution)/shard_map/ppermute | solution.py:43
  19.4 8.0 %slice-start = ((s8[8388608]{0:T(1024)(128)(4,1)}), s8[4194304]{0:T(1024)(128)(4,1)S(1)}, s32[]{:S(2)}) async-start(s8[8388608]{0:T(1024)(128)(4,1)} %bitcast.2), calls=%async_computation | async-start | bytes 8388608
  19.4 7.9 %slice-start.1 = ((s8[8388608]{0:T(1024)(128)(4,1)}), s8[4194304]{0:T(1024)(128)(4,1)S(1)}, s32[]{:S(2)}) async-start(s8[8388608]{0:T(1024)(128)(4,1)} %bitcast.2), calls=%async_computation.1 | async-start | bytes 8388608
  20.6 6.8 %collective-permute-start.8 = (bf16[32,128]{1,0:T(8,128)(2,1)S(1)}, bf16[32,128]{1,0:T(8,128)(2,1)S(1)}, u32[]{:S(2)}, u32[]{:S(2)}) collective-permute-start(bf16[32,128]{1,0:T(8,128)(2,1)S(1)} %attend.1.after_ref.same_ref), channel_id=1, source_target_pairs={{0,12},{4,8},{8,4},{12,0},{1,13},{5,9},{9,5},{13,1},{2,14},{6,10},... | collective-permute-start | bytes 24584 | tf_op jit(solution)/shard_map/ppermute | solution.py:43
  23.1 4.9 %collective-permute-start.7 = (bf16[32,128]{1,0:T(8,128)(2,1)S(1)}, bf16[32,128]{1,0:T(8,128)(2,1)S(1)}, u32[]{:S(2)}, u32[]{:S(2)}) collective-permute-start(bf16[32,128]{1,0:T(8,128)(2,1)S(1)} %attend.1.after_ref.same_ref), channel_id=1, source_target_pairs={{0,8},{4,12},{8,0},{12,4},{1,9},{5,13},{9,1},{13,5},{2,10},{6,14},... | collective-permute-start | bytes 24584 | tf_op jit(solution)/shard_map/ppermute | solution.py:43
  23.7 3.7 %collective-permute-start.6 = (bf16[32,128]{1,0:T(8,128)(2,1)S(1)}, bf16[32,128]{1,0:T(8,128)(2,1)S(1)}, u32[]{:S(2)}, u32[]{:S(2)}) collective-permute-start(bf16[32,128]{1,0:T(8,128)(2,1)S(1)} %attend.1.after_ref.same_ref), channel_id=1, source_target_pairs={{0,4},{4,0},{8,12},{12,8},{1,5},{5,1},{9,13},{13,9},{2,6},{6,2},{1... | collective-permute-start | bytes 24584 | tf_op jit(solution)/shard_map/ppermute | solution.py:43
  28.7 4.3 %collective-permute-start.9 = (f32[8,2048]{1,0:T(8,128)S(1)}, f32[8,2048]{1,0:T(8,128)S(1)}, u32[]{:S(2)}, u32[]{:S(2)}) collective-permute-start(f32[8,2048]{1,0:T(8,128)S(1)} %output_half.3), channel_id=1, source_target_pairs={{0,2},{1,3},{2,0},{3,1},{4,6},{5,7},{6,4},{7,5},{8,10},{9,11},{10,... | collective-permute-start | bytes 196616 | tf_op jit(solution)/shard_map/ppermute | solution.py:43
  33.0 1.3 %collective-permute-start.10 = (f32[8,2048]{1,0:T(8,128)S(1)}, f32[8,2048]{1,0:T(8,128)S(1)}, u32[]{:S(2)}, u32[]{:S(2)}) collective-permute-start(f32[8,2048]{1,0:T(8,128)S(1)} %add.9), channel_id=1, source_target_pairs={{0,1},{1,0},{2,3},{3,2},{4,5},{5,4},{6,7},{7,6},{8,9},{9,8},{10,11... | collective-permute-start | bytes 196616 | tf_op jit(solution)/shard_map/ppermute | solution.py:43

commit v11 on v9

--- a/solution.py
+++ b/solution.py
@@ -394,15 +394,18 @@
     depth = w_ref.shape[0] // 2
     weights = w_ref[pl.ds(pl.multiple_of(local * depth, depth), depth), :]
     total = jnp.dot(merged, weights, preferred_element_type=jnp.float32)
-    out_ref[...] = total if len(refs) == 1 else total + refs[0][...]
+    if len(refs) > 1:
+        total += refs[0][...]
+    out_ref[...] = total.astype(out_ref.dtype)
 
 
 def output_half(flip, w_out, same, other, *addend):
     rows = 2 * same.shape[0] // QPK
+    dtype = jnp.bfloat16 if addend else jnp.float32
     vmem = pl.BlockSpec(memory_space=pltpu.VMEM)
     return pl.pallas_call(
         functools.partial(output_half_kernel, flip),
-        out_shape=jax.ShapeDtypeStruct((rows, w_out.shape[1]), jnp.float32),
+        out_shape=jax.ShapeDtypeStruct((rows, w_out.shape[1]), dtype),
         in_specs=[vmem] * (3 + len(addend)),
         out_specs=vmem,
         compiler_params=pltpu.CompilerParams(vmem_limit_bytes=8 * 1024 * 1024),
@@ -476,8 +479,10 @@
         attended, kept_cache = attend(kept_blocks, arrivals, *shape)
         terms = output(all_to_all(attended, "seq"), w_out, heads_local)
     if is_direct(head_count):
-        terms = terms + swap(terms, "head", 2)
-        summed = terms + swap(terms, "head", 1)
+        terms = terms.astype(jnp.bfloat16)
+        others = [swap(terms, "head", k) for k in range(1, head_count)]
+        own, core, along, across = [t.astype(jnp.float32) for t in [terms] + others]
+        summed = (own + core) + (along + across)
     else:
         summed = lax.psum(terms, "head")
     summed = summed.reshape(requests, step_count, width)

time: 35.8 us -> 34.3 us (0.958)
  waiting for transfers between devices: 7.51 us -> 5.68 us
    ppermute x11 -> x12, waiting for transfers between devices: 7.51 us -> 5.68 us  [swap(): return lax.ppermute(outgoing, axis, [(i, i ^ offset) for i in range(count)])]
    ppermute x11 -> x12, starting transfers between devices: 19.3 us -> 19.6 us  [swap(): return lax.ppermute(outgoing, axis, [(i, i ^ offset) for i in range(count)])]
  transfers between devices with their start and end apart: 11 -> 12, of which waited for: 5 -> 5; matrix products, arithmetic and copies ran while one was open for 0% -> 0% of each run, Pallas kernels for 11% -> 12%
where the time goes in v11:
time: 34.3 us; the launch traced here: 34.1 us
  starting transfers between devices  19.6 us (57%)
  Pallas kernels  7.31 us (21%)
  waiting for transfers between devices  5.68 us (17%)
  between operations  0.8 us (2%)
  other arithmetic  0.65 us (2%)
    ppermute x12, starting transfers between devices, swap(): return lax.ppermute(outgoing, axis, [(i, i ^ offset) for i in range(count)])  19.6 us
    ppermute x12, waiting for transfers between devices, swap(): return lax.ppermute(outgoing, axis, [(i, i ^ offset) for i in range(count)])  5.68 us
    pallas_call x1, Pallas kernels, project(): pl.pallas_call(functools.partial(project_kernel, direct), out_shape=shape...  2.12 us
    pallas_call x1, Pallas kernels, pick(): pl.pallas_call(pick_near_kernel if direct else pick_all_kernel, out_shape...  1.43 us
    pallas_call x1, Pallas kernels, place(): pl.pallas_call(functools.partial(place_kernel, source_blocks, heads_local...  1.32 us
    pallas_call x2, Pallas kernels, output_half(): pl.pallas_call(functools.partial(output_half_kernel, flip), out_shape=jax...  1.31 us
    pallas_call x1, Pallas kernels, attend(): pl.pallas_call(functools.partial(attend_kernel, direct, source_blocks, he...  1.12 us
  transfers between devices with their start and end apart: 12, of which 5 were waited for; matrix products, arithmetic and copies ran while one was open for 0% of the time, Pallas kernels for 12%

profile of v11, /device:TPU:0, one launch (start us, length us, event | category | flops | bytes accessed | tf_op | source)
XLA Modules:
  0.0 34.1 jit_solution(2567134158727667260)
XLA Ops:
  0.7 1.4 %pick_blocks.1 = (bf16[256,256]{1,0:T(8,128)(2,1)S(1)}, bf16[256,256]{1,0:T(8,128)(2,1)S(1)}, bf16[256,256]{1,0:T(8,128)(2,1)S(1)}, bf16[256,256]{1,0:T(8,128)(2,1)S(1)}) custom-call(s32[2,4,8]{2,1,0:T(4,128)} %bitcast.5, bf16[2,2,512,256]{3,2,1,0:T(8,128)(2,1)} %cache_ref.1), custom_call_target="tpu_custom_call" | custom-call | flops 10000000000 | tf_op jit(solution)/shard_map/pick_blocks/pallas_call | solution.py:119
  2.1 0.0 copy-start.4
  2.1 0.0 copy-start.5
  2.1 0.0 copy-start.6
  2.1 5.1 %collective-permute-start = (bf16[256,256]{1,0:T(8,128)(2,1)S(1)}, bf16[256,256]{1,0:T(8,128)(2,1)S(1)}, u32[]{:S(2)}, u32[]{:S(2)}) collective-permute-start(bf16[256,256]{1,0:T(8,128)(2,1)S(1)} %get-tuple-element.16), channel_id=1, source_target_pairs={{0,12},{4,8},{8,4},{12,0},{1,13},{5,9},{9,5},{13,1},{2,14},{6,10},... | collective-permute-start | bytes 393224 | tf_op jit(solution)/shard_map/ppermute | solution.py:43
  7.3 0.6 %collective-permute-start.2 = (bf16[256,256]{1,0:T(8,128)(2,1)S(1)}, bf16[256,256]{1,0:T(8,128)(2,1)S(1)}, u32[]{:S(2)}, u32[]{:S(2)}) collective-permute-start(bf16[256,256]{1,0:T(8,128)(2,1)S(1)} %get-tuple-element.19), channel_id=1, source_target_pairs={{0,4},{4,0},{8,12},{12,8},{1,5},{5,1},{9,13},{13,9},{2,6},{6,2},{1... | collective-permute-start | bytes 393224 | tf_op jit(solution)/shard_map/ppermute | solution.py:43
  7.9 2.1 %project.1 = (f32[48,128]{1,0:T(8,128)S(1)}, f32[48,128]{1,0:T(8,128)S(1)}, f32[48,128]{1,0:T(8,128)S(1)}, f32[48,128]{1,0:T(8,128)S(1)}) custom-call(bf16[256,256]{1,0:T(8,128)(2,1)S(1)} %get-tuple-element.14.after_ref.refs_3_.refs_0_, bf16[2,4,2048]{2,1,0:T(4,128)(2,1)S(1)} %copy-done.2, bf16[16,128]{1,0:T(8,128)(2,1)S(1)} %bitcast.4, ...), custom_call_target="tpu_custom_call" | custom-call | flops 83886080 | bytes 10485760 | tf_op jit(solution)/shard_map/project/pallas_call | solution.py:210
  10.0 3.8 %collective-permute-start.3 = (f32[48,128]{1,0:T(8,128)S(1)}, f32[48,128]{1,0:T(8,128)S(1)}, u32[]{:S(2)}, u32[]{:S(2)}) collective-permute-start(f32[48,128]{1,0:T(8,128)S(1)} %get-tuple-element.20), channel_id=1, source_target_pairs={{0,12},{4,8},{8,4},{12,0},{1,13},{5,9},{9,5},{13,1},{2,14},{6,10},... | collective-permute-start | bytes 73736 | tf_op jit(solution)/shard_map/ppermute | solution.py:43
  13.9 3.7 %collective-permute-start.5 = (f32[48,128]{1,0:T(8,128)S(1)}, f32[48,128]{1,0:T(8,128)S(1)}, u32[]{:S(2)}, u32[]{:S(2)}) collective-permute-start(f32[48,128]{1,0:T(8,128)S(1)} %get-tuple-element.22), channel_id=1, source_target_pairs={{0,4},{4,0},{8,12},{12,8},{1,5},{5,1},{9,13},{13,9},{2,6},{6,2},{1... | collective-permute-start | bytes 73736 | tf_op jit(solution)/shard_map/ppermute | solution.py:43
  17.6 2.8 %collective-permute-done.4.refs_5_ = f32[48,128]{1,0:T(8,128)S(1)} collective-permute-done((f32[48,128]{1,0:T(8,128)S(1)}, f32[48,128]{1,0:T(8,128)S(1)}, u32[]{:S(2)}, u32[]{:S(2)}) %collective-permute-start.4) | collective-permute-done | bytes 24608 | tf_op jit(solution)/shard_map/ppermute | solution.py:43
  20.5 0.0 slice-start
  20.5 1.1 %attend.1.after_ref.same_ref = bf16[32,128]{1,0:T(8,128)(2,1)S(1)} custom-call(s32[2,4,8]{2,1,0:T(4,128)S(1)} %bitcast.6, f32[8,128]{1,0:T(8,128)S(1)} %copy-done.6, f32[8,128]{1,0:T(8,128)S(1)} %copy-done.5, bf16[256,256]{1,0:T(8,128)(2,1)S(1)} %collective-permute-done.refs_0_.refs_3_, bf16[256,256]{1,0:T(8,128)(2,1)S(1)} %collective-permute-done.1.refs_1_.refs_2_, ...), custom_call_target="tpu_custom_call" | custom-call | flops 10000000000 | tf_op jit(solution)/shard_map/attend/pallas_call | solution.py:361
  21.6 2.5 %collective-permute-start.8 = (bf16[32,128]{1,0:T(8,128)(2,1)S(1)}, bf16[32,128]{1,0:T(8,128)(2,1)S(1)}, u32[]{:S(2)}, u32[]{:S(2)}) collective-permute-start(bf16[32,128]{1,0:T(8,128)(2,1)S(1)} %attend.1.after_ref.same_ref), channel_id=1, source_target_pairs={{0,12},{4,8},{8,4},{12,0},{1,13},{5,9},{9,5},{13,1},{2,14},{6,10},... | collective-permute-start | bytes 24584 | tf_op jit(solution)/shard_map/ppermute | solution.py:43
  24.2 1.9 %collective-permute-start.6 = (bf16[32,128]{1,0:T(8,128)(2,1)S(1)}, bf16[32,128]{1,0:T(8,128)(2,1)S(1)}, u32[]{:S(2)}, u32[]{:S(2)}) collective-permute-start(bf16[32,128]{1,0:T(8,128)(2,1)S(1)} %attend.1.after_ref.same_ref), channel_id=1, source_target_pairs={{0,4},{4,0},{8,12},{12,8},{1,5},{5,1},{9,13},{13,9},{2,6},{6,2},{1... | collective-permute-start | bytes 24584 | tf_op jit(solution)/shard_map/ppermute | solution.py:43
  26.1 1.3 %place.1 = bf16[1,1,512,256]{3,2,1,0:T(8,128)(2,1)} custom-call(s32[2,4,8]{2,1,0:T(4,128)S(1)} %bitcast.7, bf16[32,128]{1,0:T(8,128)(2,1)S(1)} %attend.1.after_ref.same_ref, bf16[256,256]{1,0:T(8,128)(2,1)S(1)} %get-tuple-element.14.after_ref.refs_3_.refs_0_, bf16[256,256]{1,0:T(8,128)(2,1)S(1)} %collective-permute-done.2.refs_2_.refs_1_, ...), custom_call_target="tpu_custom_call" | custom-call | flops 1000000000 | tf_op jit(solution)/shard_map/place/pallas_call | solution.py:254
  27.4 0.4 %collective-permute-done.6.same_ref = bf16[32,128]{1,0:T(8,128)(2,1)S(1)} collective-permute-done((bf16[32,128]{1,0:T(8,128)(2,1)S(1)}, bf16[32,128]{1,0:T(8,128)(2,1)S(1)}, u32[]{:S(2)}, u32[]{:S(2)}) %collective-permute-start.6) | collective-permute-done | bytes 8224 | tf_op jit(solution)/shard_map/ppermute | solution.py:43
  27.9 0.7 %output_half.2.refs_0_ = f32[8,2048]{1,0:T(8,128)S(1)} custom-call(bf16[2048,2048]{1,0:T(8,128)(2,1)S(1)} %bitcast.3, bf16[32,128]{1,0:T(8,128)(2,1)S(1)} %collective-permute-done.6.same_ref, bf16[32,128]{1,0:T(8,128)(2,1)S(1)} %collective-permute-done.8.other_ref), custom_call_target="tpu_custom_call" | custom-call | flops 1000000000 | tf_op jit(solution)/shard_map/output_half/pallas_call | solution.py:406
  28.5 0.2 collective-permute-done.7.other_ref
  28.7 0.7 %output_half.3 = bf16[8,2048]{1,0:T(8,128)(2,1)S(1)} custom-call(bf16[2048,2048]{1,0:T(8,128)(2,1)S(1)} %bitcast.3, bf16[32,128]{1,0:T(8,128)(2,1)S(1)} %attend.1.after_ref.same_ref, bf16[32,128]{1,0:T(8,128)(2,1)S(1)} %collective-permute-done.7.other_ref, f32[8,2048]{1,0:T(8,128)S(1)} %output_half.2.refs_0_), custom_call_target="tpu_custom_call" | custom-call | flops 1000000000 | tf_op jit(solution)/shard_map/output_half/pallas_call | solution.py:406
  29.4 1.5 %collective-permute-start.10 = (bf16[8,2048]{1,0:T(8,128)(2,1)S(1)}, bf16[8,2048]{1,0:T(8,128)(2,1)S(1)}, u32[]{:S(2)}, u32[]{:S(2)}) collective-permute-start(bf16[8,2048]{1,0:T(8,128)(2,1)S(1)} %output_half.3), channel_id=1, source_target_pairs={{0,2},{1,3},{2,0},{3,1},{4,6},{5,7},{6,4},{7,5},{8,10},{9,11},{10,... | collective-permute-start | bytes 98312 | tf_op jit(solution)/shard_map/ppermute | solution.py:43
  30.9 0.3 collective-permute-start.9
  31.3 1.8 %collective-permute-done.11 = bf16[8,2048]{1,0:T(8,128)(2,1)S(1)} collective-permute-done((bf16[8,2048]{1,0:T(8,128)(2,1)S(1)}, bf16[8,2048]{1,0:T(8,128)(2,1)S(1)}, u32[]{:S(2)}, u32[]{:S(2)}) %collective-permute-start.11) | collective-permute-done | bytes 32800 | tf_op jit(solution)/shard_map/ppermute | solution.py:43
  33.0 0.4 %collective-permute-done.10 = bf16[8,2048]{1,0:T(8,128)(2,1)S(1)} collective-permute-done((bf16[8,2048]{1,0:T(8,128)(2,1)S(1)}, bf16[8,2048]{1,0:T(8,128)(2,1)S(1)}, u32[]{:S(2)}, u32[]{:S(2)}) %collective-permute-start.10) | collective-permute-done | bytes 32800 | tf_op jit(solution)/shard_map/ppermute | solution.py:43
  33.5 0.6 %add_convert_fusion = bf16[2,4,2048]{2,1,0:T(4,128)(2,1)} fusion(f32[2,4,2048]{2,1,0:T(4,128)S(1)} %reshape.11, bf16[2,4,2048]{2,1,0:T(4,128)(2,1)S(1)} %copy-done.2), kind=kLoop, calls=%fused_computation | loop fusion | flops 49152 | bytes 131072 | tf_op jit(solution)/shard_map/convert_element_type | solution.py:489
  (28 shorter events, 0.1 us)
Async XLA Ops:
  0.6 7.3 %copy-start = (bf16[2048,2048]{1,0:T(8,128)(2,1)S(1)}, bf16[2048,2048]{1,0:T(8,128)(2,1)}, u32[]{:S(2)}) copy-start(bf16[2048,2048]{1,0:T(8,128)(2,1)} %wq_ref.1) | copy-start | bytes 25165828
  0.6 7.3 %copy-start.1 = (bf16[2048,2,256]{2,1,0:T(2,128)(2,1)S(1)}, bf16[2048,2,256]{2,1,0:T(2,128)(2,1)}, u32[]{:S(2)}) copy-start(bf16[2048,2,256]{2,1,0:T(2,128)(2,1)} %wkv_ref.1) | copy-start | bytes 6291460
  0.7 7.3 %copy-start.2 = (bf16[2,4,2048]{2,1,0:T(4,128)(2,1)S(1)}, bf16[2,4,2048]{2,1,0:T(4,128)(2,1)}, u32[]{:S(2)}) copy-start(bf16[2,4,2048]{2,1,0:T(4,128)(2,1)} %hidden_ref.1) | copy-start | bytes 98308
  0.7 7.3 %copy-start.3 = (bf16[2048]{0:T(1024)(128)(2,1)S(1)}, bf16[2048]{0:T(1024)(128)(2,1)}, u32[]{:S(2)}) copy-start(bf16[2048]{0:T(1024)(128)(2,1)} %param.12) | copy-start | bytes 12292
  2.1 18.4 %copy-start.4 = (s32[2,8,4]{1,2,0:T(4,128)S(1)}, s32[2,8,4]{1,2,0:T(4,128)}, u32[]{:S(2)}) copy-start(s32[2,8,4]{1,2,0:T(4,128)} %param.10) | copy-start | bytes 772
  2.1 18.4 %copy-start.5 = (f32[8,128]{1,0:T(8,128)S(1)}, f32[8,128]{1,0:T(8,128)}, u32[]{:S(2)}) copy-start(f32[8,128]{1,0:T(8,128)} %constant.5.clone.sin_ref) | copy-start | bytes 12292
  2.1 18.4 %copy-start.6 = (f32[8,128]{1,0:T(8,128)S(1)}, f32[8,128]{1,0:T(8,128)}, u32[]{:S(2)}) copy-start(f32[8,128]{1,0:T(8,128)} %constant.4.clone.cos_ref) | copy-start | bytes 12292
  2.1 11.7 %collective-permute-start = (bf16[256,256]{1,0:T(8,128)(2,1)S(1)}, bf16[256,256]{1,0:T(8,128)(2,1)S(1)}, u32[]{:S(2)}, u32[]{:S(2)}) collective-permute-start(bf16[256,256]{1,0:T(8,128)(2,1)S(1)} %get-tuple-element.16), channel_id=1, source_target_pairs={{0,12},{4,8},{8,4},{12,0},{1,13},{5,9},{9,5},{13,1},{2,14},{6,10},... | collective-permute-start | bytes 393224 | tf_op jit(solution)/shard_map/ppermute | solution.py:43
  7.3 13.2 %collective-permute-start.1 = (bf16[256,256]{1,0:T(8,128)(2,1)S(1)}, bf16[256,256]{1,0:T(8,128)(2,1)S(1)}, u32[]{:S(2)}, u32[]{:S(2)}) collective-permute-start(bf16[256,256]{1,0:T(8,128)(2,1)S(1)} %get-tuple-element.18), channel_id=1, source_target_pairs={{0,8},{4,12},{8,0},{12,4},{1,9},{5,13},{9,1},{13,5},{2,10},{6,14},... | collective-permute-start | bytes 393224 | tf_op jit(solution)/shard_map/ppermute | solution.py:43
  7.3 13.2 %collective-permute-start.2 = (bf16[256,256]{1,0:T(8,128)(2,1)S(1)}, bf16[256,256]{1,0:T(8,128)(2,1)S(1)}, u32[]{:S(2)}, u32[]{:S(2)}) collective-permute-start(bf16[256,256]{1,0:T(8,128)(2,1)S(1)} %get-tuple-element.19), channel_id=1, source_target_pairs={{0,4},{4,0},{8,12},{12,8},{1,5},{5,1},{9,13},{13,9},{2,6},{6,2},{1... | collective-permute-start | bytes 393224 | tf_op jit(solution)/shard_map/ppermute | solution.py:43
  10.0 7.5 %collective-permute-start.3 = (f32[48,128]{1,0:T(8,128)S(1)}, f32[48,128]{1,0:T(8,128)S(1)}, u32[]{:S(2)}, u32[]{:S(2)}) collective-permute-start(f32[48,128]{1,0:T(8,128)S(1)} %get-tuple-element.20), channel_id=1, source_target_pairs={{0,12},{4,8},{8,4},{12,0},{1,13},{5,9},{9,5},{13,1},{2,14},{6,10},... | collective-permute-start | bytes 73736 | tf_op jit(solution)/shard_map/ppermute | solution.py:43
  13.9 6.6 %collective-permute-start.4 = (f32[48,128]{1,0:T(8,128)S(1)}, f32[48,128]{1,0:T(8,128)S(1)}, u32[]{:S(2)}, u32[]{:S(2)}) collective-permute-start(f32[48,128]{1,0:T(8,128)S(1)} %get-tuple-element.21), channel_id=1, source_target_pairs={{0,8},{4,12},{8,0},{12,4},{1,9},{5,13},{9,1},{13,5},{2,10},{6,14},... | collective-permute-start | bytes 73736 | tf_op jit(solution)/shard_map/ppermute | solution.py:43
  13.9 6.6 %collective-permute-start.5 = (f32[48,128]{1,0:T(8,128)S(1)}, f32[48,128]{1,0:T(8,128)S(1)}, u32[]{:S(2)}, u32[]{:S(2)}) collective-permute-start(f32[48,128]{1,0:T(8,128)S(1)} %get-tuple-element.22), channel_id=1, source_target_pairs={{0,4},{4,0},{8,12},{12,8},{1,5},{5,1},{9,13},{13,9},{2,6},{6,2},{1... | collective-permute-start | bytes 73736 | tf_op jit(solution)/shard_map/ppermute | solution.py:43
  20.5 7.4 %slice-start = ((s8[8388608]{0:T(1024)(128)(4,1)}), s8[4194304]{0:T(1024)(128)(4,1)S(1)}, s32[]{:S(2)}) async-start(s8[8388608]{0:T(1024)(128)(4,1)} %bitcast.2), calls=%async_computation | async-start | bytes 8388608
  20.5 7.3 %slice-start.1 = ((s8[8388608]{0:T(1024)(128)(4,1)}), s8[4194304]{0:T(1024)(128)(4,1)S(1)}, s32[]{:S(2)}) async-start(s8[8388608]{0:T(1024)(128)(4,1)} %bitcast.2), calls=%async_computation.1 | async-start | bytes 8388608
  21.6 6.2 %collective-permute-start.8 = (bf16[32,128]{1,0:T(8,128)(2,1)S(1)}, bf16[32,128]{1,0:T(8,128)(2,1)S(1)}, u32[]{:S(2)}, u32[]{:S(2)}) collective-permute-start(bf16[32,128]{1,0:T(8,128)(2,1)S(1)} %attend.1.after_ref.same_ref), channel_id=1, source_target_pairs={{0,12},{4,8},{8,4},{12,0},{1,13},{5,9},{9,5},{13,1},{2,14},{6,10},... | collective-permute-start | bytes 24584 | tf_op jit(solution)/shard_map/ppermute | solution.py:43
  24.2 4.5 %collective-permute-start.7 = (bf16[32,128]{1,0:T(8,128)(2,1)S(1)}, bf16[32,128]{1,0:T(8,128)(2,1)S(1)}, u32[]{:S(2)}, u32[]{:S(2)}) collective-permute-start(bf16[32,128]{1,0:T(8,128)(2,1)S(1)} %attend.1.after_ref.same_ref), channel_id=1, source_target_pairs={{0,8},{4,12},{8,0},{12,4},{1,9},{5,13},{9,1},{13,5},{2,10},{6,14},... | collective-permute-start | bytes 24584 | tf_op jit(solution)/shard_map/ppermute | solution.py:43
  24.2 3.7 %collective-permute-start.6 = (bf16[32,128]{1,0:T(8,128)(2,1)S(1)}, bf16[32,128]{1,0:T(8,128)(2,1)S(1)}, u32[]{:S(2)}, u32[]{:S(2)}) collective-permute-start(bf16[32,128]{1,0:T(8,128)(2,1)S(1)} %attend.1.after_ref.same_ref), channel_id=1, source_target_pairs={{0,4},{4,0},{8,12},{12,8},{1,5},{5,1},{9,13},{13,9},{2,6},{6,2},{1... | collective-permute-start | bytes 24584 | tf_op jit(solution)/shard_map/ppermute | solution.py:43
  29.4 3.7 %collective-permute-start.11 = (bf16[8,2048]{1,0:T(8,128)(2,1)S(1)}, bf16[8,2048]{1,0:T(8,128)(2,1)S(1)}, u32[]{:S(2)}, u32[]{:S(2)}) collective-permute-start(bf16[8,2048]{1,0:T(8,128)(2,1)S(1)} %output_half.3), channel_id=1, source_target_pairs={{0,3},{1,2},{2,1},{3,0},{4,7},{5,6},{6,5},{7,4},{8,11},{9,10},{10,... | collective-permute-start | bytes 98312 | tf_op jit(solution)/shard_map/ppermute | solution.py:43
  29.4 4.1 %collective-permute-start.10 = (bf16[8,2048]{1,0:T(8,128)(2,1)S(1)}, bf16[8,2048]{1,0:T(8,128)(2,1)S(1)}, u32[]{:S(2)}, u32[]{:S(2)}) collective-permute-start(bf16[8,2048]{1,0:T(8,128)(2,1)S(1)} %output_half.3), channel_id=1, source_target_pairs={{0,2},{1,3},{2,0},{3,1},{4,6},{5,7},{6,4},{7,5},{8,10},{9,11},{10,... | collective-permute-start | bytes 98312 | tf_op jit(solution)/shard_map/ppermute | solution.py:43
  30.9 2.5 %collective-permute-start.9 = (bf16[8,2048]{1,0:T(8,128)(2,1)S(1)}, bf16[8,2048]{1,0:T(8,128)(2,1)S(1)}, u32[]{:S(2)}, u32[]{:S(2)}) collective-permute-start(bf16[8,2048]{1,0:T(8,128)(2,1)S(1)} %output_half.3), channel_id=1, source_target_pairs={{0,1},{1,0},{2,3},{3,2},{4,5},{5,4},{6,7},{7,6},{8,9},{9,8},{10,11... | collective-permute-start | bytes 98312 | tf_op jit(solution)/shard_map/ppermute | solution.py:43

commit v12 on v11

--- a/solution.py
+++ b/solution.py
@@ -41,6 +41,26 @@
 def swap(outgoing, axis, offset):
     count = lax.axis_size(axis)
     return lax.ppermute(outgoing, axis, [(i, i ^ offset) for i in range(count)])
+
+
+KEPT_ORDER = ((3, 2, 1), (1, 3, 2))
+
+
+def kept_offset(step):
+    if step == 0:
+        return 0
+    even, odd = (order[step - 1] for order in KEPT_ORDER)
+    return jnp.where(jnp.bitwise_and(lax.axis_index("head"), 1) == 0, even, odd)
+
+
+def swap_kept(outgoing, step):
+    seq_count, head_count = lax.axis_size("seq"), lax.axis_size("head")
+    pairs = [
+        (s * head_count + h, (s ^ KEPT_ORDER[h & 1][step - 1]) * head_count + h)
+        for s in range(seq_count)
+        for h in range(head_count)
+    ]
+    return lax.ppermute(outgoing, ("seq", "head"), pairs)
 
 
 def all_to_all(outgoing, axis):
@@ -74,8 +94,11 @@
     kept_copy.wait()
     me = lax.axis_index("seq")
     places = [
-        [picked_rows(kept_ref, cache.shape, jnp.bitwise_xor(me, k), slot) for slot in range(MOST)]
-        for k in range(len(outs))
+        [
+            picked_rows(kept_ref, cache.shape, jnp.bitwise_xor(me, kept_offset(step)), slot)
+            for slot in range(MOST)
+        ]
+        for step in range(len(outs))
     ]
     cache_copy.wait()
     for out_ref, slots in zip(outs, places):
@@ -230,7 +253,7 @@
 
 def place_kernel(source_blocks, heads_local, kept_ref, after_ref, *refs):
     del after_ref
-    *by_offset, cache_ref, sem = refs
+    *by_step, cache_ref, sem = refs
     me = lax.axis_index("seq")
     request = lax.div(me, heads_local)
     head = lax.axis_index("head") * heads_local + lax.rem(me, heads_local)
@@ -241,8 +264,8 @@
         previous = source
         rows = pl.ds(pl.multiple_of(slot * BLK, BLK), BLK)
         target = cache_ref.at[0, 0, pl.ds(k * BLK, BLK)]
-        for offset, ref in enumerate(by_offset):
-            pl.when(jnp.bitwise_xor(me, offset) == source)(
+        for step, ref in enumerate(by_step):
+            pl.when(jnp.bitwise_xor(me, kept_offset(step)) == source)(
                 pltpu.make_async_copy(ref.at[rows], target, sem).start
             )
     pltpu.make_async_copy(cache_ref, cache_ref, sem).wait()
@@ -270,7 +293,7 @@
     request = lax.div(me, heads_local)
     head = lax.axis_index("head") * heads_local + lax.rem(me, heads_local)
     if direct:
-        by_offset, parts_refs, attended_ref = refs[:4][::-1], refs[4:8][::-1], refs[8]
+        by_step, parts_refs, attended_ref = refs[:4], refs[4:8][::-1], refs[8]
         total = sum(ref[...] for ref in parts_refs)
     else:
         parts_ref, blocks_ref, attended_ref, cache_ref, sem, kept = refs
@@ -312,8 +335,8 @@
         values.append(block[:, HD:])
 
     if direct:
-        for offset, ref in enumerate(by_offset):
-            source = jnp.bitwise_xor(me, offset)
+        for step, ref in enumerate(by_step):
+            source = jnp.bitwise_xor(me, kept_offset(step))
             filled = jnp.int32(0)
             for k in range(kept_count):
                 here = lax.div(kept_ref[request, k, head], source_blocks) == source
@@ -463,10 +486,10 @@
         partners = range(1, seq_count)
         blocks = list(pick(kept_blocks, source_cache, direct))
         parts = list(project(blocks[0], *weights, pair_count, direct))
-        blocks = [blocks[0]] + [swap(blocks[k], "seq", k) for k in partners]
-        parts[1], blocks[3] = lax.optimization_barrier((parts[1], blocks[3]))
+        blocks = [blocks[0]] + [swap_kept(blocks[step], step) for step in partners]
+        parts[1], blocks[1] = lax.optimization_barrier((parts[1], blocks[1]))
         parts = [parts[0]] + [swap(parts[k], "seq", k) for k in partners]
-        (attended,) = attend(kept_blocks, blocks[::-1] + parts[::-1], *shape)
+        (attended,) = attend(kept_blocks, blocks + parts[::-1], *shape)
         kept_cache = place(kept_blocks, attended, blocks, source_blocks, heads_local)
         first, second, third = [swap(attended, "seq", k) for k in partners]
         first, kept_cache = lax.optimization_barrier((first, kept_cache))

time: 34.3 us -> 35.3 us (1.029)
  waiting for transfers between devices: 5.68 us -> 6.48 us
    ppermute x0 -> x3, starting transfers between devices: none -> 5.76 us  [swap_kept(): return lax.ppermute(outgoing, ('seq', 'head'), pairs)]
    ppermute x12 -> x9, starting transfers between devices: 19.6 us -> 14 us  [swap(): return lax.ppermute(outgoing, axis, [(i, i ^ offset) for i in range(count)])]
    ppermute x12 -> x9, waiting for transfers between devices: 5.68 us -> 6.48 us  [swap(): return lax.ppermute(outgoing, axis, [(i, i ^ offset) for i in range(count)])]
where the time goes in v12:
time: 35.3 us; the launch traced here: 35.1 us
  starting transfers between devices  19.8 us (56%)
  Pallas kernels  7.31 us (21%)
  waiting for transfers between devices  6.48 us (18%)
  between operations  0.8 us (2%)
  other arithmetic  0.65 us (2%)
    ppermute x9, starting transfers between devices, swap(): return lax.ppermute(outgoing, axis, [(i, i ^ offset) for i in range(count)])  14 us
    ppermute x9, waiting for transfers between devices, swap(): return lax.ppermute(outgoing, axis, [(i, i ^ offset) for i in range(count)])  6.48 us
    ppermute x3, starting transfers between devices, swap_kept(): return lax.ppermute(outgoing, ('seq', 'head'), pairs)  5.76 us
    pallas_call x1, Pallas kernels, project(): pl.pallas_call(functools.partial(project_kernel, direct), out_shape=shape...  2.12 us
    pallas_call x1, Pallas kernels, pick(): pl.pallas_call(pick_near_kernel if direct else pick_all_kernel, out_shape...  1.43 us
    pallas_call x1, Pallas kernels, place(): pl.pallas_call(functools.partial(place_kernel, source_blocks, heads_local...  1.33 us
    pallas_call x2, Pallas kernels, output_half(): pl.pallas_call(functools.partial(output_half_kernel, flip), out_shape=jax...  1.31 us
    pallas_call x1, Pallas kernels, attend(): pl.pallas_call(functools.partial(attend_kernel, direct, source_blocks, he...  1.12 us
  transfers between devices with their start and end apart: 12, of which 5 were waited for; matrix products, arithmetic and copies ran while one was open for 0% of the time, Pallas kernels for 12%

profile of v12, /device:TPU:0, one launch (start us, length us, event | category | flops | bytes accessed | tf_op | source)
XLA Modules:
  0.0 35.1 jit_solution(26738918773848393)
XLA Ops:
  0.7 1.4 %pick_blocks.1 = (bf16[256,256]{1,0:T(8,128)(2,1)S(1)}, bf16[256,256]{1,0:T(8,128)(2,1)S(1)}, bf16[256,256]{1,0:T(8,128)(2,1)S(1)}, bf16[256,256]{1,0:T(8,128)(2,1)S(1)}) custom-call(s32[2,4,8]{2,1,0:T(4,128)} %bitcast.5, bf16[2,2,512,256]{3,2,1,0:T(8,128)(2,1)} %cache_ref.1), custom_call_target="tpu_custom_call" | custom-call | flops 10000000000 | tf_op jit(solution)/shard_map/pick_blocks/pallas_call | solution.py:142
  2.1 0.0 copy-start.4
  2.1 0.0 copy-start.5
  2.1 0.0 copy-start.6
  2.1 5.1 %collective-permute-start = (bf16[256,256]{1,0:T(8,128)(2,1)S(1)}, bf16[256,256]{1,0:T(8,128)(2,1)S(1)}, u32[]{:S(2)}, u32[]{:S(2)}) collective-permute-start(bf16[256,256]{1,0:T(8,128)(2,1)S(1)} %get-tuple-element.16), channel_id=1, source_target_pairs={{0,12},{1,5},{2,14},{3,7},{4,8},{5,1},{6,10},{7,3},{8,4},{9,13},{1... | collective-permute-start | bytes 393224 | tf_op jit(solution)/shard_map/ppermute | solution.py:63
  7.3 0.6 %collective-permute-start.2 = (bf16[256,256]{1,0:T(8,128)(2,1)S(1)}, bf16[256,256]{1,0:T(8,128)(2,1)S(1)}, u32[]{:S(2)}, u32[]{:S(2)}) collective-permute-start(bf16[256,256]{1,0:T(8,128)(2,1)S(1)} %get-tuple-element.19), channel_id=1, source_target_pairs={{0,4},{1,9},{2,6},{3,11},{4,0},{5,13},{6,2},{7,15},{8,12},{9,1},{1... | collective-permute-start | bytes 393224 | tf_op jit(solution)/shard_map/ppermute | solution.py:63
  7.9 2.1 %project.1 = (f32[48,128]{1,0:T(8,128)S(1)}, f32[48,128]{1,0:T(8,128)S(1)}, f32[48,128]{1,0:T(8,128)S(1)}, f32[48,128]{1,0:T(8,128)S(1)}) custom-call(bf16[256,256]{1,0:T(8,128)(2,1)S(1)} %get-tuple-element.14.after_ref.refs_0_, bf16[2,4,2048]{2,1,0:T(4,128)(2,1)S(1)} %copy-done.2, bf16[16,128]{1,0:T(8,128)(2,1)S(1)} %bitcast.4, ...), custom_call_target="tpu_custom_call" | custom-call | flops 83886080 | bytes 10485760 | tf_op jit(solution)/shard_map/project/pallas_call | solution.py:233
  10.0 3.8 %collective-permute-start.3 = (f32[48,128]{1,0:T(8,128)S(1)}, f32[48,128]{1,0:T(8,128)S(1)}, u32[]{:S(2)}, u32[]{:S(2)}) collective-permute-start(f32[48,128]{1,0:T(8,128)S(1)} %get-tuple-element.20), channel_id=1, source_target_pairs={{0,12},{4,8},{8,4},{12,0},{1,13},{5,9},{9,5},{13,1},{2,14},{6,10},... | collective-permute-start | bytes 73736 | tf_op jit(solution)/shard_map/ppermute | solution.py:43
  13.9 3.9 %collective-permute-start.5 = (f32[48,128]{1,0:T(8,128)S(1)}, f32[48,128]{1,0:T(8,128)S(1)}, u32[]{:S(2)}, u32[]{:S(2)}) collective-permute-start(f32[48,128]{1,0:T(8,128)S(1)} %get-tuple-element.22), channel_id=1, source_target_pairs={{0,4},{4,0},{8,12},{12,8},{1,5},{5,1},{9,13},{13,9},{2,6},{6,2},{1... | collective-permute-start | bytes 73736 | tf_op jit(solution)/shard_map/ppermute | solution.py:43
  17.8 3.8 %collective-permute-done.4.refs_5_ = f32[48,128]{1,0:T(8,128)S(1)} collective-permute-done((f32[48,128]{1,0:T(8,128)S(1)}, f32[48,128]{1,0:T(8,128)S(1)}, u32[]{:S(2)}, u32[]{:S(2)}) %collective-permute-start.4) | collective-permute-done | bytes 24608 | tf_op jit(solution)/shard_map/ppermute | solution.py:43
  21.6 0.0 slice-start
  21.6 1.1 %attend.1.after_ref.same_ref = bf16[32,128]{1,0:T(8,128)(2,1)S(1)} custom-call(s32[2,4,8]{2,1,0:T(4,128)S(1)} %bitcast.6, f32[8,128]{1,0:T(8,128)S(1)} %copy-done.6, f32[8,128]{1,0:T(8,128)S(1)} %copy-done.5, bf16[256,256]{1,0:T(8,128)(2,1)S(1)} %get-tuple-element.14.after_ref.refs_0_, bf16[256,256]{1,0:T(8,128)(2,1)S(1)} %collective-permute-done.refs_1_, ...), custom_call_target="tpu_custom_call" | custom-call | flops 10000000000 | tf_op jit(solution)/shard_map/attend/pallas_call | solution.py:384
  22.8 2.4 %collective-permute-start.8 = (bf16[32,128]{1,0:T(8,128)(2,1)S(1)}, bf16[32,128]{1,0:T(8,128)(2,1)S(1)}, u32[]{:S(2)}, u32[]{:S(2)}) collective-permute-start(bf16[32,128]{1,0:T(8,128)(2,1)S(1)} %attend.1.after_ref.same_ref), channel_id=1, source_target_pairs={{0,12},{4,8},{8,4},{12,0},{1,13},{5,9},{9,5},{13,1},{2,14},{6,10},... | collective-permute-start | bytes 24584 | tf_op jit(solution)/shard_map/ppermute | solution.py:43
  25.2 2.1 %collective-permute-start.6 = (bf16[32,128]{1,0:T(8,128)(2,1)S(1)}, bf16[32,128]{1,0:T(8,128)(2,1)S(1)}, u32[]{:S(2)}, u32[]{:S(2)}) collective-permute-start(bf16[32,128]{1,0:T(8,128)(2,1)S(1)} %attend.1.after_ref.same_ref), channel_id=1, source_target_pairs={{0,4},{4,0},{8,12},{12,8},{1,5},{5,1},{9,13},{13,9},{2,6},{6,2},{1... | collective-permute-start | bytes 24584 | tf_op jit(solution)/shard_map/ppermute | solution.py:43
  27.2 1.3 %place.1 = bf16[1,1,512,256]{3,2,1,0:T(8,128)(2,1)} custom-call(s32[2,4,8]{2,1,0:T(4,128)S(1)} %bitcast.7, bf16[32,128]{1,0:T(8,128)(2,1)S(1)} %attend.1.after_ref.same_ref, bf16[256,256]{1,0:T(8,128)(2,1)S(1)} %get-tuple-element.14.after_ref.refs_0_, bf16[256,256]{1,0:T(8,128)(2,1)S(1)} %collective-permute-done.refs_1_, ...), custom_call_target="tpu_custom_call" | custom-call | flops 1000000000 | tf_op jit(solution)/shard_map/place/pallas_call | solution.py:277
  28.6 0.3 collective-permute-done.6.same_ref
  28.9 0.7 %output_half.2.refs_0_ = f32[8,2048]{1,0:T(8,128)S(1)} custom-call(bf16[2048,2048]{1,0:T(8,128)(2,1)S(1)} %bitcast.3, bf16[32,128]{1,0:T(8,128)(2,1)S(1)} %collective-permute-done.6.same_ref, bf16[32,128]{1,0:T(8,128)(2,1)S(1)} %collective-permute-done.8.other_ref), custom_call_target="tpu_custom_call" | custom-call | flops 1000000000 | tf_op jit(solution)/shard_map/output_half/pallas_call | solution.py:429
  29.5 0.2 collective-permute-done.7.other_ref
  29.7 0.7 %output_half.3 = bf16[8,2048]{1,0:T(8,128)(2,1)S(1)} custom-call(bf16[2048,2048]{1,0:T(8,128)(2,1)S(1)} %bitcast.3, bf16[32,128]{1,0:T(8,128)(2,1)S(1)} %attend.1.after_ref.same_ref, bf16[32,128]{1,0:T(8,128)(2,1)S(1)} %collective-permute-done.7.other_ref, f32[8,2048]{1,0:T(8,128)S(1)} %output_half.2.refs_0_), custom_call_target="tpu_custom_call" | custom-call | flops 1000000000 | tf_op jit(solution)/shard_map/output_half/pallas_call | solution.py:429
  30.4 1.5 %collective-permute-start.10 = (bf16[8,2048]{1,0:T(8,128)(2,1)S(1)}, bf16[8,2048]{1,0:T(8,128)(2,1)S(1)}, u32[]{:S(2)}, u32[]{:S(2)}) collective-permute-start(bf16[8,2048]{1,0:T(8,128)(2,1)S(1)} %output_half.3), channel_id=1, source_target_pairs={{0,2},{1,3},{2,0},{3,1},{4,6},{5,7},{6,4},{7,5},{8,10},{9,11},{10,... | collective-permute-start | bytes 98312 | tf_op jit(solution)/shard_map/ppermute | solution.py:43
  31.9 0.3 collective-permute-start.9
  32.2 1.8 %collective-permute-done.11 = bf16[8,2048]{1,0:T(8,128)(2,1)S(1)} collective-permute-done((bf16[8,2048]{1,0:T(8,128)(2,1)S(1)}, bf16[8,2048]{1,0:T(8,128)(2,1)S(1)}, u32[]{:S(2)}, u32[]{:S(2)}) %collective-permute-start.11) | collective-permute-done | bytes 32800 | tf_op jit(solution)/shard_map/ppermute | solution.py:43
  34.0 0.4 %collective-permute-done.10 = bf16[8,2048]{1,0:T(8,128)(2,1)S(1)} collective-permute-done((bf16[8,2048]{1,0:T(8,128)(2,1)S(1)}, bf16[8,2048]{1,0:T(8,128)(2,1)S(1)}, u32[]{:S(2)}, u32[]{:S(2)}) %collective-permute-start.10) | collective-permute-done | bytes 32800 | tf_op jit(solution)/shard_map/ppermute | solution.py:43
  34.5 0.6 %add_convert_fusion = bf16[2,4,2048]{2,1,0:T(4,128)(2,1)} fusion(f32[2,4,2048]{2,1,0:T(4,128)S(1)} %reshape.11, bf16[2,4,2048]{2,1,0:T(4,128)(2,1)S(1)} %copy-done.2), kind=kLoop, calls=%fused_computation | loop fusion | flops 49152 | bytes 131072 | tf_op jit(solution)/shard_map/convert_element_type | solution.py:512
  (28 shorter events, 0.1 us)
Async XLA Ops:
  0.6 7.3 %copy-start = (bf16[2048,2048]{1,0:T(8,128)(2,1)S(1)}, bf16[2048,2048]{1,0:T(8,128)(2,1)}, u32[]{:S(2)}) copy-start(bf16[2048,2048]{1,0:T(8,128)(2,1)} %wq_ref.1) | copy-start | bytes 25165828
  0.6 7.3 %copy-start.1 = (bf16[2048,2,256]{2,1,0:T(2,128)(2,1)S(1)}, bf16[2048,2,256]{2,1,0:T(2,128)(2,1)}, u32[]{:S(2)}) copy-start(bf16[2048,2,256]{2,1,0:T(2,128)(2,1)} %wkv_ref.1) | copy-start | bytes 6291460
  0.7 7.3 %copy-start.2 = (bf16[2,4,2048]{2,1,0:T(4,128)(2,1)S(1)}, bf16[2,4,2048]{2,1,0:T(4,128)(2,1)}, u32[]{:S(2)}) copy-start(bf16[2,4,2048]{2,1,0:T(4,128)(2,1)} %hidden_ref.1) | copy-start | bytes 98308
  0.7 7.3 %copy-start.3 = (bf16[2048]{0:T(1024)(128)(2,1)S(1)}, bf16[2048]{0:T(1024)(128)(2,1)}, u32[]{:S(2)}) copy-start(bf16[2048]{0:T(1024)(128)(2,1)} %param.12) | copy-start | bytes 12292
  2.1 19.5 %copy-start.4 = (s32[2,8,4]{1,2,0:T(4,128)S(1)}, s32[2,8,4]{1,2,0:T(4,128)}, u32[]{:S(2)}) copy-start(s32[2,8,4]{1,2,0:T(4,128)} %param.10) | copy-start | bytes 772
  2.1 19.5 %copy-start.5 = (f32[8,128]{1,0:T(8,128)S(1)}, f32[8,128]{1,0:T(8,128)}, u32[]{:S(2)}) copy-start(f32[8,128]{1,0:T(8,128)} %constant.5.clone.sin_ref) | copy-start | bytes 12292
  2.1 19.5 %copy-start.6 = (f32[8,128]{1,0:T(8,128)S(1)}, f32[8,128]{1,0:T(8,128)}, u32[]{:S(2)}) copy-start(f32[8,128]{1,0:T(8,128)} %constant.4.clone.cos_ref) | copy-start | bytes 12292
  2.1 11.7 %collective-permute-start = (bf16[256,256]{1,0:T(8,128)(2,1)S(1)}, bf16[256,256]{1,0:T(8,128)(2,1)S(1)}, u32[]{:S(2)}, u32[]{:S(2)}) collective-permute-start(bf16[256,256]{1,0:T(8,128)(2,1)S(1)} %get-tuple-element.16), channel_id=1, source_target_pairs={{0,12},{1,5},{2,14},{3,7},{4,8},{5,1},{6,10},{7,3},{8,4},{9,13},{1... | collective-permute-start | bytes 393224 | tf_op jit(solution)/shard_map/ppermute | solution.py:63
  7.3 14.3 %collective-permute-start.1 = (bf16[256,256]{1,0:T(8,128)(2,1)S(1)}, bf16[256,256]{1,0:T(8,128)(2,1)S(1)}, u32[]{:S(2)}, u32[]{:S(2)}) collective-permute-start(bf16[256,256]{1,0:T(8,128)(2,1)S(1)} %get-tuple-element.18), channel_id=1, source_target_pairs={{0,8},{1,13},{2,10},{3,15},{4,12},{5,9},{6,14},{7,11},{8,0},{9,5},... | collective-permute-start | bytes 393224 | tf_op jit(solution)/shard_map/ppermute | solution.py:63
  7.3 14.3 %collective-permute-start.2 = (bf16[256,256]{1,0:T(8,128)(2,1)S(1)}, bf16[256,256]{1,0:T(8,128)(2,1)S(1)}, u32[]{:S(2)}, u32[]{:S(2)}) collective-permute-start(bf16[256,256]{1,0:T(8,128)(2,1)S(1)} %get-tuple-element.19), channel_id=1, source_target_pairs={{0,4},{1,9},{2,6},{3,11},{4,0},{5,13},{6,2},{7,15},{8,12},{9,1},{1... | collective-permute-start | bytes 393224 | tf_op jit(solution)/shard_map/ppermute | solution.py:63
  10.0 7.7 %collective-permute-start.3 = (f32[48,128]{1,0:T(8,128)S(1)}, f32[48,128]{1,0:T(8,128)S(1)}, u32[]{:S(2)}, u32[]{:S(2)}) collective-permute-start(f32[48,128]{1,0:T(8,128)S(1)} %get-tuple-element.20), channel_id=1, source_target_pairs={{0,12},{4,8},{8,4},{12,0},{1,13},{5,9},{9,5},{13,1},{2,14},{6,10},... | collective-permute-start | bytes 73736 | tf_op jit(solution)/shard_map/ppermute | solution.py:43
  13.9 7.7 %collective-permute-start.4 = (f32[48,128]{1,0:T(8,128)S(1)}, f32[48,128]{1,0:T(8,128)S(1)}, u32[]{:S(2)}, u32[]{:S(2)}) collective-permute-start(f32[48,128]{1,0:T(8,128)S(1)} %get-tuple-element.21), channel_id=1, source_target_pairs={{0,8},{4,12},{8,0},{12,4},{1,9},{5,13},{9,1},{13,5},{2,10},{6,14},... | collective-permute-start | bytes 73736 | tf_op jit(solution)/shard_map/ppermute | solution.py:43
  13.9 7.7 %collective-permute-start.5 = (f32[48,128]{1,0:T(8,128)S(1)}, f32[48,128]{1,0:T(8,128)S(1)}, u32[]{:S(2)}, u32[]{:S(2)}) collective-permute-start(f32[48,128]{1,0:T(8,128)S(1)} %get-tuple-element.22), channel_id=1, source_target_pairs={{0,4},{4,0},{8,12},{12,8},{1,5},{5,1},{9,13},{13,9},{2,6},{6,2},{1... | collective-permute-start | bytes 73736 | tf_op jit(solution)/shard_map/ppermute | solution.py:43
  21.6 7.3 %slice-start = ((s8[8388608]{0:T(1024)(128)(4,1)}), s8[4194304]{0:T(1024)(128)(4,1)S(1)}, s32[]{:S(2)}) async-start(s8[8388608]{0:T(1024)(128)(4,1)} %bitcast.2), calls=%async_computation | async-start | bytes 8388608
  21.6 7.2 %slice-start.1 = ((s8[8388608]{0:T(1024)(128)(4,1)}), s8[4194304]{0:T(1024)(128)(4,1)S(1)}, s32[]{:S(2)}) async-start(s8[8388608]{0:T(1024)(128)(4,1)} %bitcast.2), calls=%async_computation.1 | async-start | bytes 8388608
  22.8 6.1 %collective-permute-start.8 = (bf16[32,128]{1,0:T(8,128)(2,1)S(1)}, bf16[32,128]{1,0:T(8,128)(2,1)S(1)}, u32[]{:S(2)}, u32[]{:S(2)}) collective-permute-start(bf16[32,128]{1,0:T(8,128)(2,1)S(1)} %attend.1.after_ref.same_ref), channel_id=1, source_target_pairs={{0,12},{4,8},{8,4},{12,0},{1,13},{5,9},{9,5},{13,1},{2,14},{6,10},... | collective-permute-start | bytes 24584 | tf_op jit(solution)/shard_map/ppermute | solution.py:43
  25.2 4.5 %collective-permute-start.7 = (bf16[32,128]{1,0:T(8,128)(2,1)S(1)}, bf16[32,128]{1,0:T(8,128)(2,1)S(1)}, u32[]{:S(2)}, u32[]{:S(2)}) collective-permute-start(bf16[32,128]{1,0:T(8,128)(2,1)S(1)} %attend.1.after_ref.same_ref), channel_id=1, source_target_pairs={{0,8},{4,12},{8,0},{12,4},{1,9},{5,13},{9,1},{13,5},{2,10},{6,14},... | collective-permute-start | bytes 24584 | tf_op jit(solution)/shard_map/ppermute | solution.py:43
  25.2 3.7 %collective-permute-start.6 = (bf16[32,128]{1,0:T(8,128)(2,1)S(1)}, bf16[32,128]{1,0:T(8,128)(2,1)S(1)}, u32[]{:S(2)}, u32[]{:S(2)}) collective-permute-start(bf16[32,128]{1,0:T(8,128)(2,1)S(1)} %attend.1.after_ref.same_ref), channel_id=1, source_target_pairs={{0,4},{4,0},{8,12},{12,8},{1,5},{5,1},{9,13},{13,9},{2,6},{6,2},{1... | collective-permute-start | bytes 24584 | tf_op jit(solution)/shard_map/ppermute | solution.py:43
  30.4 3.7 %collective-permute-start.11 = (bf16[8,2048]{1,0:T(8,128)(2,1)S(1)}, bf16[8,2048]{1,0:T(8,128)(2,1)S(1)}, u32[]{:S(2)}, u32[]{:S(2)}) collective-permute-start(bf16[8,2048]{1,0:T(8,128)(2,1)S(1)} %output_half.3), channel_id=1, source_target_pairs={{0,3},{1,2},{2,1},{3,0},{4,7},{5,6},{6,5},{7,4},{8,11},{9,10},{10,... | collective-permute-start | bytes 98312 | tf_op jit(solution)/shard_map/ppermute | solution.py:43
  30.4 4.1 %collective-permute-start.10 = (bf16[8,2048]{1,0:T(8,128)(2,1)S(1)}, bf16[8,2048]{1,0:T(8,128)(2,1)S(1)}, u32[]{:S(2)}, u32[]{:S(2)}) collective-permute-start(bf16[8,2048]{1,0:T(8,128)(2,1)S(1)} %output_half.3), channel_id=1, source_target_pairs={{0,2},{1,3},{2,0},{3,1},{4,6},{5,7},{6,4},{7,5},{8,10},{9,11},{10,... | collective-permute-start | bytes 98312 | tf_op jit(solution)/shard_map/ppermute | solution.py:43
  31.9 2.5 %collective-permute-start.9 = (bf16[8,2048]{1,0:T(8,128)(2,1)S(1)}, bf16[8,2048]{1,0:T(8,128)(2,1)S(1)}, u32[]{:S(2)}, u32[]{:S(2)}) collective-permute-start(bf16[8,2048]{1,0:T(8,128)(2,1)S(1)} %output_half.3), channel_id=1, source_target_pairs={{0,1},{1,0},{2,3},{3,2},{4,5},{5,4},{6,7},{7,6},{8,9},{9,8},{10,11... | collective-permute-start | bytes 98312 | tf_op jit(solution)/shard_map/ppermute | solution.py:43

commit v13 on v11

--- a/solution.py
+++ b/solution.py
@@ -16,6 +16,9 @@
 MOST = 2
 ROPE_BASE = 500000.0
 EPS = 1e-05
+LEAST = -1e30
+TINY = 1e-30
+ATTEND_COST = 10**10
 
 CONTRACT_LAST = (((1,), (1,)), ((), ()))
 
@@ -181,8 +184,8 @@
         heads = [query[steps, (l * QPK + h) * HD : (l * QPK + h + 1) * HD] for h in range(QPK)]
         return heads + [own[:, :HD], own[:, HD:], square_rows, square_rows]
 
-    def write_pair(out_ref, pieces):
-        for j, piece in enumerate(pieces):
+    def write_pair(out_ref, first_piece, pieces):
+        for j, piece in enumerate(pieces, first_piece):
             out_ref[j * step_count : (j + 1) * step_count, :] = piece
 
     for r in range(requests):
@@ -190,11 +193,16 @@
             pair = r * heads_local + l
             pieces = pieces_of(r, l)
             if not direct:
-                write_pair(outs[0].at[pair], pieces)
+                write_pair(outs[0].at[pair], 0, pieces)
                 continue
             for offset, out_ref in enumerate(outs):
                 pl.when(jnp.bitwise_xor(me, offset) == pair)(
-                    functools.partial(write_pair, out_ref, pieces)
+                    functools.partial(write_pair, out_ref, 0, pieces)
+                )
+                pl.when(jnp.bitwise_xor(me, offset ^ 2) == pair)(
+                    functools.partial(
+                        write_pair, out_ref, len(pieces), pieces[:QPK] + pieces[-2:]
+                    )
                 )
 
 
@@ -202,7 +210,8 @@
     requests, step_count, width = new_hidden.shape
     terms = ((QPK + 4) * step_count, HD)
     if direct:
-        shapes = [jax.ShapeDtypeStruct(terms, jnp.float32)] * pair_count
+        two_pairs = (terms[0] + (QPK + 2) * step_count, HD)
+        shapes = [jax.ShapeDtypeStruct(two_pairs, jnp.float32)] * pair_count
     else:
         shapes = [jax.ShapeDtypeStruct((pair_count,) + terms, jnp.float32)]
     vmem = pl.BlockSpec(memory_space=pltpu.VMEM)
@@ -263,111 +272,202 @@
     )(kept_blocks, after, *blocks)
 
 
-def attend_kernel(direct, source_blocks, heads_local, kept_ref, cos_ref, sin_ref, *refs):
-    kept_count = kept_ref.shape[1]
-    step_count = cos_ref.shape[0] // 2
-    me = lax.axis_index("seq")
-    request = lax.div(me, heads_local)
-    head = lax.axis_index("head") * heads_local + lax.rem(me, heads_local)
-    if direct:
-        by_offset, parts_refs, attended_ref = refs[:4][::-1], refs[4:8][::-1], refs[8]
-        total = sum(ref[...] for ref in parts_refs)
-    else:
-        parts_ref, blocks_ref, attended_ref, cache_ref, sem, kept = refs
-
-        def start_copy(k, carry):
-            previous, slot = carry
-            source = lax.div(kept_ref[request, k, head], source_blocks)
-            slot = jnp.where(source == previous, jnp.minimum(slot + 1, MOST - 1), 0)
-            target = kept.at[pl.ds(pl.multiple_of(k * BLK, BLK), BLK)]
-            rows = pl.ds(pl.multiple_of(slot * BLK, BLK), BLK)
-            pltpu.make_async_copy(blocks_ref.at[source, rows], target, sem).start()
-            return source, slot
-
-        lax.fori_loop(0, kept_count, start_copy, (jnp.int32(-1), jnp.int32(0)))
-        total = jnp.sum(parts_ref[...], axis=0)
-        pltpu.make_async_copy(kept, kept, sem).wait()
-        pltpu.make_async_copy(kept, cache_ref.at[0, 0], sem).start()
-    query_rows = QPK * step_count
-    inverse = lax.rsqrt(total[query_rows + 2 * step_count :] * (1.0 / D) + EPS)
-    cosine, sine = cos_ref[...], sin_ref[...]
-    query = total[:query_rows].reshape(QPK // 2, 2 * step_count, HD) * inverse[None]
-    query = rotate(query, cosine[None], sine[None]).reshape(query_rows, HD).astype(jnp.bfloat16)
-    keyval = total[query_rows : query_rows + 2 * step_count] * inverse
+def split_three(value):
+    parts = []
+    for _ in range(3):
+        parts.append(value.astype(jnp.bfloat16))
+        value = value - parts[-1].astype(jnp.float32)
+    return parts
+
+
+def norm_of(square_rows):
+    return lax.rsqrt(square_rows * (1.0 / D) + EPS)
+
+
+def rotated_queries(terms, inverse, cosine, sine):
+    rows = terms.shape[0]
+    query = terms.reshape(rows // inverse.shape[0], inverse.shape[0], HD) * inverse[None]
+    return rotate(query, cosine[None], sine[None]).reshape(rows, HD).astype(jnp.bfloat16)
+
+
+def new_steps(terms, inverse, cosine, sine, step_count):
+    keyval = terms * inverse
     new_key = rotate(keyval, cosine, sine).astype(jnp.bfloat16)
     new_value = jnp.concatenate([keyval[step_count:], keyval[:step_count]], axis=0)
-    new_value = new_value.astype(jnp.bfloat16)
-    scale = 1.0 / math.sqrt(HD)
-    score = lax.dot_general(query, new_key, CONTRACT_LAST, preferred_element_type=jnp.float32)
+    return new_key, new_value.astype(jnp.bfloat16)
+
+
+def scores_of(query, keys, filled=None, step_count=None):
+    score = lax.dot_general(query, keys, CONTRACT_LAST, preferred_element_type=jnp.float32)
+    score = score * (1.0 / math.sqrt(HD))
+    column = lax.broadcasted_iota(jnp.int32, score.shape, 1)
+    if step_count is None:
+        return jnp.where(column < filled * BLK, score, -jnp.inf)
     row = lax.broadcasted_iota(jnp.int32, score.shape, 0)
-    column = lax.broadcasted_iota(jnp.int32, score.shape, 1)
-    scores = [jnp.where(column <= lax.rem(row, step_count), score * scale, -jnp.inf)]
-    values = [new_value]
-    def add_block(block, filled):
-        score = lax.dot_general(
-            query, block[:, :HD], CONTRACT_LAST, preferred_element_type=jnp.float32
-        )
-        column = lax.broadcasted_iota(jnp.int32, score.shape, 1)
-        scores.append(jnp.where(column < filled * BLK, score * scale, -jnp.inf))
-        values.append(block[:, HD:])
-
-    if direct:
-        for offset, ref in enumerate(by_offset):
-            source = jnp.bitwise_xor(me, offset)
-            filled = jnp.int32(0)
-            for k in range(kept_count):
-                here = lax.div(kept_ref[request, k, head], source_blocks) == source
-                filled += here.astype(jnp.int32)
-            add_block(ref[: MOST * BLK, :], filled)
-    else:
-        add_block(kept[...], kept_count)
+    return jnp.where(column <= lax.rem(row, step_count), score, -jnp.inf)
+
+
+def softmax_values(scores, values):
     row_max = functools.reduce(
         jnp.maximum, [jnp.max(score, axis=1, keepdims=True) for score in scores]
     )
-    denominator = jnp.zeros((query_rows, 1), jnp.float32)
-    numerator = jnp.zeros((query_rows, HD), jnp.float32)
+    row_max = jnp.maximum(row_max, LEAST)
+    denominator = jnp.zeros(row_max.shape, jnp.float32)
+    numerator = jnp.zeros((row_max.shape[0], HD), jnp.float32)
     for score, value in zip(scores, values):
         weight = jnp.exp(score - row_max)
         denominator += jnp.sum(weight, axis=1, keepdims=True)
         numerator += jnp.dot(
             weight.astype(jnp.bfloat16), value, preferred_element_type=jnp.float32
         )
-    attended = (numerator / denominator).astype(jnp.bfloat16)
-    if direct:
-        attended_ref[...] = attended
-    else:
-        for i in range(attended_ref.shape[0]):
-            attended_ref[i] = attended
-        pltpu.make_async_copy(cache_ref, cache_ref, sem).wait()
+    attended = numerator / jnp.maximum(denominator, TINY)
+    return attended, row_max, denominator
+
+
+def attend_near_kernel(source_blocks, heads_local, kept_ref, cos_ref, sin_ref, *refs):
+    own_ref, near_ref, far_ref, other_ref = refs[:4]
+    parts_refs, out_ref = refs[4:8], refs[8]
+    kept_count = kept_ref.shape[1]
+    step_count = cos_ref.shape[0] // 2
+    me = lax.axis_index("seq")
+    request = lax.div(me, heads_local)
+    head = lax.axis_index("head") * heads_local + lax.rem(me, heads_local)
+    cosine, sine = cos_ref[...], sin_ref[...]
+    total = (parts_refs[0][...] + parts_refs[1][...]) + (parts_refs[2][...] + parts_refs[3][...])
+    query_rows = QPK * step_count
+    pair_rows = (QPK + 4) * step_count
+
+    def filled_blocks(request, source):
+        filled = jnp.int32(0)
+        for k in range(kept_count):
+            here = lax.div(kept_ref[request, k, head], source_blocks) == source
+            filled += here.astype(jnp.int32)
+        return filled
+
+    inverse = norm_of(total[pair_rows - 2 * step_count : pair_rows])
+    query = rotated_queries(total[:query_rows], inverse, cosine, sine)
+    new_key, new_value = new_steps(
+        total[query_rows : query_rows + 2 * step_count], inverse, cosine, sine, step_count
+    )
+    scores = [scores_of(query, new_key, step_count=step_count)]
+    values = [new_value]
+    for offset, ref in ((0, own_ref), (1, near_ref), (3, far_ref)):
+        filled = filled_blocks(request, jnp.bitwise_xor(me, offset))
+        scores.append(scores_of(query, ref[:, :HD], filled))
+        values.append(ref[:, HD:])
+
+    other_inverse = norm_of(total[-2 * step_count :])
+    other_query = rotated_queries(
+        total[pair_rows : pair_rows + query_rows], other_inverse, cosine, sine
+    )
+    filled = filled_blocks(1 - request, me)
+    other_scores = [scores_of(other_query, other_ref[:, :HD], filled)]
+
+    attended, row_max, denominator = softmax_values(scores, values)
+    other, other_max, other_denominator = softmax_values(other_scores, [other_ref[:, HD:]])
+    out_ref[:query_rows, :] = attended.astype(jnp.bfloat16)
+    out_ref[query_rows : 2 * query_rows, :] = other.astype(jnp.bfloat16)
+    row_max = jnp.concatenate([row_max, other_max], axis=0)
+    denominator = jnp.concatenate([denominator, other_denominator], axis=0)
+    log_sum = row_max + jnp.log(jnp.maximum(denominator, TINY))
+    columns = jnp.concatenate(
+        [jnp.broadcast_to(log_sum, (2 * query_rows, HD)), jnp.zeros((HD - 2 * query_rows, HD))],
+        axis=0,
+    )
+    across = jnp.transpose(columns)[:16]
+    row = lax.broadcasted_iota(jnp.int32, across.shape, 0)
+    high, middle, low = [part.astype(jnp.float32) for part in split_three(across)]
+    stats = jnp.where(row == 0, high, jnp.where(row == 1, middle, low))
+    out_ref[2 * query_rows :, :] = stats.astype(jnp.bfloat16)
+
+
+def attend_all_kernel(
+    source_blocks, heads_local, kept_ref, cos_ref, sin_ref, parts_ref, blocks_ref,
+    attended_ref, cache_ref, sem, kept,
+):
+    kept_count = kept_ref.shape[1]
+    step_count = cos_ref.shape[0] // 2
+    me = lax.axis_index("seq")
+    request = lax.div(me, heads_local)
+    head = lax.axis_index("head") * heads_local + lax.rem(me, heads_local)
+
+    def start_copy(k, carry):
+        previous, slot = carry
+        source = lax.div(kept_ref[request, k, head], source_blocks)
+        slot = jnp.where(source == previous, jnp.minimum(slot + 1, MOST - 1), 0)
+        target = kept.at[pl.ds(pl.multiple_of(k * BLK, BLK), BLK)]
+        rows = pl.ds(pl.multiple_of(slot * BLK, BLK), BLK)
+        pltpu.make_async_copy(blocks_ref.at[source, rows], target, sem).start()
+        return source, slot
+
+    lax.fori_loop(0, kept_count, start_copy, (jnp.int32(-1), jnp.int32(0)))
+    total = jnp.sum(parts_ref[...], axis=0)
+    pltpu.make_async_copy(kept, kept, sem).wait()
+    pltpu.make_async_copy(kept, cache_ref.at[0, 0], sem).start()
+    query_rows = QPK * step_count
+    cosine, sine = cos_ref[...], sin_ref[...]
+    inverse = norm_of(total[-2 * step_count :])
+    query = rotated_queries(total[:query_rows], inverse, cosine, sine)
+    new_key, new_value = new_steps(
+        total[query_rows : query_rows + 2 * step_count], inverse, cosine, sine, step_count
+    )
+    scores = [
+        scores_of(query, new_key, step_count=step_count),
+        scores_of(query, kept[:, :HD], kept_count),
+    ]
+    attended, _, _ = softmax_values(scores, [new_value, kept[:, HD:]])
+    for i in range(attended_ref.shape[0]):
+        attended_ref[i] = attended.astype(jnp.bfloat16)
+    pltpu.make_async_copy(cache_ref, cache_ref, sem).wait()
 
 
 def attend(kept_blocks, arrivals, source_blocks, heads_local, step_count, seq_count, direct):
     kept_count = kept_blocks.shape[1]
     cosine, sine = rope_tables(source_blocks * BLK * seq_count, step_count)
-    shape = (QPK * step_count, HD)
+    query_rows = QPK * step_count
     vmem = pl.BlockSpec(memory_space=pltpu.VMEM)
     if direct:
-        shapes = [jax.ShapeDtypeStruct(shape, jnp.bfloat16)]
+        shapes = [jax.ShapeDtypeStruct((2 * query_rows + 16, HD), jnp.bfloat16)]
         out_specs = [vmem]
         scratch = []
     else:
         cache = (1, 1, kept_count * BLK, 2 * HD)
         shapes = [
-            jax.ShapeDtypeStruct((seq_count,) + shape, jnp.bfloat16),
+            jax.ShapeDtypeStruct((seq_count, query_rows, HD), jnp.bfloat16),
             jax.ShapeDtypeStruct(cache, jnp.bfloat16),
         ]
         out_specs = [vmem, pl.BlockSpec(memory_space=pl.ANY)]
         scratch = [pltpu.SemaphoreType.DMA, pltpu.VMEM(cache[2:], jnp.bfloat16)]
     return pl.pallas_call(
-        functools.partial(attend_kernel, direct, source_blocks, heads_local),
+        functools.partial(
+            attend_near_kernel if direct else attend_all_kernel, source_blocks, heads_local
+        ),
         out_shape=shapes,
         in_specs=[pl.BlockSpec(memory_space=pltpu.SMEM)] + [vmem] * (2 + len(arrivals)),
         out_specs=out_specs,
         scratch_shapes=scratch,
         compiler_params=pltpu.CompilerParams(vmem_limit_bytes=16 * 1024 * 1024),
-        cost_estimate=pl.CostEstimate(flops=10**10, bytes_accessed=0, transcendentals=0),
+        cost_estimate=pl.CostEstimate(flops=ATTEND_COST, bytes_accessed=0, transcendentals=0),
         name="attend",
     )(kept_blocks, jnp.asarray(cosine), jnp.asarray(sine), *arrivals)
+
+
+def join(values, log_sum, other_values, other_log_sum):
+    largest = jnp.maximum(log_sum, other_log_sum)
+    weight = jnp.exp(log_sum - largest)
+    other_weight = jnp.exp(other_log_sum - largest)
+    return (weight * values + other_weight * other_values) / (weight + other_weight)
+
+
+def read_values(ref, query_rows):
+    values = ref[: 2 * query_rows, :].astype(jnp.float32)
+    stats = ref[2 * query_rows :, :].astype(jnp.float32)
+    log_sum = (stats[0:1] + stats[1:2]) + stats[2:3]
+    columns = jnp.transpose(jnp.broadcast_to(log_sum, (HD, HD)))
+    return (
+        (values[:query_rows], columns[:query_rows]),
+        (values[query_rows:], columns[query_rows : 2 * query_rows]),
+    )
 
 
 def merge_heads(first, second, step_count):
@@ -380,14 +480,16 @@
 
 def output_half_kernel(flip, w_ref, same_ref, other_ref, *refs):
     out_ref = refs[-1]
-    query_rows = same_ref.shape[0]
+    query_rows = (same_ref.shape[0] - 16) // 2
     me = lax.axis_index("seq")
     local = jnp.bitwise_and(me, 1)
     if flip:
         local = 1 - local
     second = me >= 2
-    same = same_ref[...].astype(jnp.float32)
-    other = other_ref[...].astype(jnp.float32)
+    same_first, other_second = read_values(same_ref, query_rows)
+    other_first, same_second = read_values(other_ref, query_rows)
+    same = join(*same_first, *same_second)
+    other = join(*other_first, *other_second)
     merged = merge_heads(
         jnp.where(second, other, same), jnp.where(second, same, other), query_rows // QPK
     )
@@ -400,7 +502,7 @@
 
 
 def output_half(flip, w_out, same, other, *addend):
-    rows = 2 * same.shape[0] // QPK
+    rows = (same.shape[0] - 16) // QPK
     dtype = jnp.bfloat16 if addend else jnp.float32
     vmem = pl.BlockSpec(memory_space=pltpu.VMEM)
     return pl.pallas_call(
@@ -461,17 +563,19 @@
     shape = (source_blocks, heads_local, step_count, seq_count, direct)
     if direct:
         partners = range(1, seq_count)
-        blocks = list(pick(kept_blocks, source_cache, direct))
-        parts = list(project(blocks[0], *weights, pair_count, direct))
-        blocks = [blocks[0]] + [swap(blocks[k], "seq", k) for k in partners]
-        parts[1], blocks[3] = lax.optimization_barrier((parts[1], blocks[3]))
+        sent = list(pick(kept_blocks, source_cache, direct))
+        parts = list(project(sent[0], *weights, pair_count, direct))
+        far, near = swap(sent[3], "seq", 3), swap(sent[1], "seq", 1)
         parts = [parts[0]] + [swap(parts[k], "seq", k) for k in partners]
-        (attended,) = attend(kept_blocks, blocks[::-1] + parts[::-1], *shape)
-        kept_cache = place(kept_blocks, attended, blocks, source_blocks, heads_local)
-        first, second, third = [swap(attended, "seq", k) for k in partners]
-        first, kept_cache = lax.optimization_barrier((first, kept_cache))
-        terms = output_half(True, w_out, first, third)
-        terms = output_half(False, w_out, attended, second, terms)
+        late, near = lax.optimization_barrier((sent[2], near))
+        late = swap(late, "seq", 2)
+        (values,) = attend(kept_blocks, [sent[0], near, far, sent[2]] + parts[::-1], *shape)
+        first, second, third = [swap(values, "seq", k) for k in partners]
+        third, late = lax.optimization_barrier((third, late))
+        terms = output_half(False, w_out, values, second)
+        terms = output_half(True, w_out, first, third, terms)
+        blocks = [sent[0], near, late, far]
+        kept_cache = place(kept_blocks, values, blocks, source_blocks, heads_local)
     else:
         (blocks,) = pick(kept_blocks, source_cache, direct)
         (parts,) = project(blocks, *weights, pair_count, direct)
@@ -481,6 +585,7 @@
     if is_direct(head_count):
         terms = terms.astype(jnp.bfloat16)
         others = [swap(terms, "head", k) for k in range(1, head_count)]
+        others[1], kept_cache = lax.optimization_barrier((others[1], kept_cache))
         own, core, along, across = [t.astype(jnp.float32) for t in [terms] + others]
         summed = (own + core) + (along + across)
     else:

time: 34.3 us -> 36 us (1.050)
  waiting for transfers between devices: 5.68 us -> 9.37 us
  starting transfers between devices: 19.6 us -> 17.3 us
    ppermute x12, waiting for transfers between devices: 5.68 us -> 9.37 us  [swap(): return lax.ppermute(outgoing, axis, [(i, i ^ offset) for i in range(count)])]
    ppermute x12, starting transfers between devices: 19.6 us -> 17.3 us  [swap(): return lax.ppermute(outgoing, axis, [(i, i ^ offset) for i in range(count)])]
  transfers between devices with their start and end apart: 12 -> 12, of which waited for: 5 -> 7; matrix products, arithmetic and copies ran while one was open for 0% -> 0% of each run, Pallas kernels for 12% -> 15%
where the time goes in v13:
time: 36 us; the launch traced here: 35.8 us
  starting transfers between devices  17.3 us (48%)
  waiting for transfers between devices  9.37 us (26%)
  Pallas kernels  7.65 us (21%)
  between operations  0.77 us (2%)
  other arithmetic  0.65 us (2%)
    ppermute x12, starting transfers between devices, swap(): return lax.ppermute(outgoing, axis, [(i, i ^ offset) for i in range(count)])  17.3 us
    ppermute x12, waiting for transfers between devices, swap(): return lax.ppermute(outgoing, axis, [(i, i ^ offset) for i in range(count)])  9.37 us
    pallas_call x1, Pallas kernels, project(): pl.pallas_call(functools.partial(project_kernel, direct), out_shape=shape...  2.19 us
    pallas_call x2, Pallas kernels, output_half(): pl.pallas_call(functools.partial(output_half_kernel, flip), out_shape=jax...  1.45 us
    pallas_call x1, Pallas kernels, pick(): pl.pallas_call(pick_near_kernel if direct else pick_all_kernel, out_shape...  1.43 us
    pallas_call x1, Pallas kernels, place(): pl.pallas_call(functools.partial(place_kernel, source_blocks, heads_local...  1.32 us
    pallas_call x1, Pallas kernels, attend(): pl.pallas_call(functools.partial(attend_near_kernel if direct else attend...  1.25 us
  transfers between devices with their start and end apart: 12, of which 7 were waited for; matrix products, arithmetic and copies ran while one was open for 0% of the time, Pallas kernels for 15%

profile of v13, /device:TPU:0, one launch (start us, length us, event | category | flops | bytes accessed | tf_op | source)
XLA Modules:
  0.0 35.8 jit_solution(13078378202007770010)
XLA Ops:
  0.7 1.4 %pick_blocks.1 = (bf16[256,256]{1,0:T(8,128)(2,1)S(1)}, bf16[256,256]{1,0:T(8,128)(2,1)S(1)}, bf16[256,256]{1,0:T(8,128)(2,1)S(1)}, bf16[256,256]{1,0:T(8,128)(2,1)S(1)}) custom-call(s32[2,4,8]{2,1,0:T(4,128)} %bitcast.5, bf16[2,2,512,256]{3,2,1,0:T(8,128)(2,1)} %cache_ref.1), custom_call_target="tpu_custom_call" | custom-call | flops 10000000000 | tf_op jit(solution)/shard_map/pick_blocks/pallas_call | solution.py:122
  2.1 3.1 %collective-permute-start = (bf16[256,256]{1,0:T(8,128)(2,1)S(1)}, bf16[256,256]{1,0:T(8,128)(2,1)S(1)}, u32[]{:S(2)}, u32[]{:S(2)}) collective-permute-start(bf16[256,256]{1,0:T(8,128)(2,1)S(1)} %get-tuple-element.18), channel_id=1, source_target_pairs={{0,4},{4,0},{8,12},{12,8},{1,5},{5,1},{9,13},{13,9},{2,6},{6,2},{1... | collective-permute-start | bytes 393224 | tf_op jit(solution)/shard_map/ppermute | solution.py:46
  5.2 2.5 %collective-permute-start.1 = (bf16[256,256]{1,0:T(8,128)(2,1)S(1)}, bf16[256,256]{1,0:T(8,128)(2,1)S(1)}, u32[]{:S(2)}, u32[]{:S(2)}) collective-permute-start(bf16[256,256]{1,0:T(8,128)(2,1)S(1)} %get-tuple-element.20), channel_id=1, source_target_pairs={{0,12},{4,8},{8,4},{12,0},{1,13},{5,9},{9,5},{13,1},{2,14},{6,10},... | collective-permute-start | bytes 393224 | tf_op jit(solution)/shard_map/ppermute | solution.py:46
  7.7 2.2 %project.1 = (f32[88,128]{1,0:T(8,128)S(1)}, f32[88,128]{1,0:T(8,128)S(1)}, f32[88,128]{1,0:T(8,128)S(1)}, f32[88,128]{1,0:T(8,128)S(1)}) custom-call(bf16[256,256]{1,0:T(8,128)(2,1)S(1)} %get-tuple-element.16.after_ref.refs_0_, bf16[2,4,2048]{2,1,0:T(4,128)(2,1)S(1)} %copy-done.2, bf16[16,128]{1,0:T(8,128)(2,1)S(1)} %bitcast.4, ...), custom_call_target="tpu_custom_call" | custom-call | flops 83886080 | bytes 10485760 | tf_op jit(solution)/shard_map/project/pallas_call | solution.py:219
  9.9 2.3 %collective-permute-start.2 = (f32[88,128]{1,0:T(8,128)S(1)}, f32[88,128]{1,0:T(8,128)S(1)}, u32[]{:S(2)}, u32[]{:S(2)}) collective-permute-start(f32[88,128]{1,0:T(8,128)S(1)} %get-tuple-element.21), channel_id=1, source_target_pairs={{0,12},{4,8},{8,4},{12,0},{1,13},{5,9},{9,5},{13,1},{2,14},{6,10},... | collective-permute-start | bytes 135176 | tf_op jit(solution)/shard_map/ppermute | solution.py:46
  12.3 2.1 %collective-permute-start.4 = (f32[88,128]{1,0:T(8,128)S(1)}, f32[88,128]{1,0:T(8,128)S(1)}, u32[]{:S(2)}, u32[]{:S(2)}) collective-permute-start(f32[88,128]{1,0:T(8,128)S(1)} %get-tuple-element.23), channel_id=1, source_target_pairs={{0,4},{4,0},{8,12},{12,8},{1,5},{5,1},{9,13},{13,9},{2,6},{6,2},{1... | collective-permute-start | bytes 135176 | tf_op jit(solution)/shard_map/ppermute | solution.py:46
  14.4 0.8 %collective-permute-start.7 = (bf16[256,256]{1,0:T(8,128)(2,1)S(1)}, bf16[256,256]{1,0:T(8,128)(2,1)S(1)}, u32[]{:S(2)}, u32[]{:S(2)}) collective-permute-start(bf16[256,256]{1,0:T(8,128)(2,1)S(1)} %get-tuple-element.25.refs_3_), channel_id=1, source_target_pairs={{0,8},{4,12},{8,0},{12,4},{1,9},{5,13},{9,1},{13,5},{2,10},{6,14},... | collective-permute-start | bytes 393224 | tf_op jit(solution)/shard_map/ppermute | solution.py:46
  15.2 0.8 %collective-permute-done.2.refs_4_ = f32[88,128]{1,0:T(8,128)S(1)} collective-permute-done((f32[88,128]{1,0:T(8,128)S(1)}, f32[88,128]{1,0:T(8,128)S(1)}, u32[]{:S(2)}, u32[]{:S(2)}) %collective-permute-start.2) | collective-permute-done | bytes 45088 | tf_op jit(solution)/shard_map/ppermute | solution.py:46
  16.0 4.6 %collective-permute-done.3.refs_5_ = f32[88,128]{1,0:T(8,128)S(1)} collective-permute-done((f32[88,128]{1,0:T(8,128)S(1)}, f32[88,128]{1,0:T(8,128)S(1)}, u32[]{:S(2)}, u32[]{:S(2)}) %collective-permute-start.3) | collective-permute-done | bytes 45088 | tf_op jit(solution)/shard_map/ppermute | solution.py:46
  20.6 1.3 %attend.1.same_ref.after_ref = bf16[80,128]{1,0:T(8,128)(2,1)S(1)} custom-call(s32[2,4,8]{2,1,0:T(4,128)S(1)} %bitcast.6, f32[8,128]{1,0:T(8,128)S(1)} %copy-done.5, f32[8,128]{1,0:T(8,128)S(1)} %copy-done.6, bf16[256,256]{1,0:T(8,128)(2,1)S(1)} %get-tuple-element.16.after_ref.refs_0_, bf16[256,256]{1,0:T(8,128)(2,1)S(1)} %collective-permute-done.refs_1_, ...), custom_call_target="tpu_custom_call" | custom-call | flops 10000000000 | tf_op jit(solution)/shard_map/attend/pallas_call | solution.py:441
  21.8 1.9 %collective-permute-start.8 = (bf16[80,128]{1,0:T(8,128)(2,1)S(1)}, bf16[80,128]{1,0:T(8,128)(2,1)S(1)}, u32[]{:S(2)}, u32[]{:S(2)}) collective-permute-start(bf16[80,128]{1,0:T(8,128)(2,1)S(1)} %attend.1.same_ref.after_ref), channel_id=1, source_target_pairs={{0,8},{4,12},{8,0},{12,4},{1,9},{5,13},{9,1},{13,5},{2,10},{6,14},... | collective-permute-start | bytes 61448 | tf_op jit(solution)/shard_map/ppermute | solution.py:46
  23.7 1.9 %collective-permute-start.6 = (bf16[80,128]{1,0:T(8,128)(2,1)S(1)}, bf16[80,128]{1,0:T(8,128)(2,1)S(1)}, u32[]{:S(2)}, u32[]{:S(2)}) collective-permute-start(bf16[80,128]{1,0:T(8,128)(2,1)S(1)} %attend.1.same_ref.after_ref), channel_id=1, source_target_pairs={{0,12},{4,8},{8,4},{12,0},{1,13},{5,9},{9,5},{13,1},{2,14},{6,10},... | collective-permute-start | bytes 61448 | tf_op jit(solution)/shard_map/ppermute | solution.py:46
  25.6 0.5 %collective-permute-start.5 = (bf16[80,128]{1,0:T(8,128)(2,1)S(1)}, bf16[80,128]{1,0:T(8,128)(2,1)S(1)}, u32[]{:S(2)}, u32[]{:S(2)}) collective-permute-start(bf16[80,128]{1,0:T(8,128)(2,1)S(1)} %attend.1.same_ref.after_ref), channel_id=1, source_target_pairs={{0,4},{4,0},{8,12},{12,8},{1,5},{5,1},{9,13},{13,9},{2,6},{6,2},{1... | collective-permute-start | bytes 61448 | tf_op jit(solution)/shard_map/ppermute | solution.py:46
  26.1 0.6 %collective-permute-done.8.other_ref = bf16[80,128]{1,0:T(8,128)(2,1)S(1)} collective-permute-done((bf16[80,128]{1,0:T(8,128)(2,1)S(1)}, bf16[80,128]{1,0:T(8,128)(2,1)S(1)}, u32[]{:S(2)}, u32[]{:S(2)}) %collective-permute-start.8) | collective-permute-done | bytes 20512 | tf_op jit(solution)/shard_map/ppermute | solution.py:46
  26.8 0.7 %output_half.2.refs_0_ = f32[8,2048]{1,0:T(8,128)S(1)} custom-call(bf16[2048,2048]{1,0:T(8,128)(2,1)S(1)} %bitcast.3, bf16[80,128]{1,0:T(8,128)(2,1)S(1)} %attend.1.same_ref.after_ref, bf16[80,128]{1,0:T(8,128)(2,1)S(1)} %collective-permute-done.8.other_ref), custom_call_target="tpu_custom_call" | custom-call | flops 1000000000 | tf_op jit(solution)/shard_map/output_half/pallas_call | solution.py:508
  27.5 1.8 %collective-permute-done.6.other_ref = bf16[80,128]{1,0:T(8,128)(2,1)S(1)} collective-permute-done((bf16[80,128]{1,0:T(8,128)(2,1)S(1)}, bf16[80,128]{1,0:T(8,128)(2,1)S(1)}, u32[]{:S(2)}, u32[]{:S(2)}) %collective-permute-start.6) | collective-permute-done | bytes 20512 | tf_op jit(solution)/shard_map/ppermute | solution.py:46
  29.3 0.2 collective-permute-done.5.same_ref
  29.5 0.7 %output_half.3 = bf16[8,2048]{1,0:T(8,128)(2,1)S(1)} custom-call(bf16[2048,2048]{1,0:T(8,128)(2,1)S(1)} %bitcast.3, bf16[80,128]{1,0:T(8,128)(2,1)S(1)} %collective-permute-done.5.same_ref, bf16[80,128]{1,0:T(8,128)(2,1)S(1)} %collective-permute-done.6.other_ref, f32[8,2048]{1,0:T(8,128)S(1)} %output_half.2.refs_0_), custom_call_target="tpu_custom_call" | custom-call | flops 1000000000 | tf_op jit(solution)/shard_map/output_half/pallas_call | solution.py:508
  30.2 1.5 %collective-permute-start.9 = (bf16[8,2048]{1,0:T(8,128)(2,1)S(1)}, bf16[8,2048]{1,0:T(8,128)(2,1)S(1)}, u32[]{:S(2)}, u32[]{:S(2)}) collective-permute-start(bf16[8,2048]{1,0:T(8,128)(2,1)S(1)} %output_half.3), channel_id=1, source_target_pairs={{0,2},{1,3},{2,0},{3,1},{4,6},{5,7},{6,4},{7,5},{8,10},{9,11},{10,... | collective-permute-start | bytes 98312 | tf_op jit(solution)/shard_map/ppermute | solution.py:46
  31.7 0.6 %collective-permute-start.11 = (bf16[8,2048]{1,0:T(8,128)(2,1)S(1)}, bf16[8,2048]{1,0:T(8,128)(2,1)S(1)}, u32[]{:S(2)}, u32[]{:S(2)}) collective-permute-start(bf16[8,2048]{1,0:T(8,128)(2,1)S(1)} %output_half.3), channel_id=1, source_target_pairs={{0,3},{1,2},{2,1},{3,0},{4,7},{5,6},{6,5},{7,4},{8,11},{9,10},{10,... | collective-permute-start | bytes 98312 | tf_op jit(solution)/shard_map/ppermute | solution.py:46
  32.4 1.3 %place.1 = bf16[1,1,512,256]{3,2,1,0:T(8,128)(2,1)} custom-call(s32[2,4,8]{2,1,0:T(4,128)S(1)} %bitcast.7, bf16[80,128]{1,0:T(8,128)(2,1)S(1)} %attend.1.same_ref.after_ref, bf16[256,256]{1,0:T(8,128)(2,1)S(1)} %get-tuple-element.16.after_ref.refs_0_, bf16[256,256]{1,0:T(8,128)(2,1)S(1)} %collective-permute-done.refs_1_, ...), custom_call_target="tpu_custom_call" | custom-call | flops 1000000000 | tf_op jit(solution)/shard_map/place/pallas_call | solution.py:263
  33.7 0.4 %collective-permute-done.9 = bf16[8,2048]{1,0:T(8,128)(2,1)S(1)} collective-permute-done((bf16[8,2048]{1,0:T(8,128)(2,1)S(1)}, bf16[8,2048]{1,0:T(8,128)(2,1)S(1)}, u32[]{:S(2)}, u32[]{:S(2)}) %collective-permute-start.9) | collective-permute-done | bytes 32800 | tf_op jit(solution)/shard_map/ppermute | solution.py:46
  34.2 0.9 %collective-permute-done.11 = bf16[8,2048]{1,0:T(8,128)(2,1)S(1)} collective-permute-done((bf16[8,2048]{1,0:T(8,128)(2,1)S(1)}, bf16[8,2048]{1,0:T(8,128)(2,1)S(1)}, u32[]{:S(2)}, u32[]{:S(2)}) %collective-permute-start.11) | collective-permute-done | bytes 32800 | tf_op jit(solution)/shard_map/ppermute | solution.py:46
  35.1 0.6 %add_convert_fusion = bf16[2,4,2048]{2,1,0:T(4,128)(2,1)} fusion(f32[2,4,2048]{2,1,0:T(4,128)S(1)} %reshape.11, bf16[2,4,2048]{2,1,0:T(4,128)(2,1)S(1)} %copy-done.2), kind=kLoop, calls=%fused_computation | loop fusion | flops 49152 | bytes 131072 | tf_op jit(solution)/shard_map/convert_element_type | solution.py:594
  (28 shorter events, 0.1 us)
Async XLA Ops:
  0.6 7.1 %copy-start = (bf16[2048,2048]{1,0:T(8,128)(2,1)S(1)}, bf16[2048,2048]{1,0:T(8,128)(2,1)}, u32[]{:S(2)}) copy-start(bf16[2048,2048]{1,0:T(8,128)(2,1)} %wq_ref.1) | copy-start | bytes 25165828
  0.6 7.1 %copy-start.1 = (bf16[2048,2,256]{2,1,0:T(2,128)(2,1)S(1)}, bf16[2048,2,256]{2,1,0:T(2,128)(2,1)}, u32[]{:S(2)}) copy-start(bf16[2048,2,256]{2,1,0:T(2,128)(2,1)} %wkv_ref.1) | copy-start | bytes 6291460
  0.7 7.1 %copy-start.2 = (bf16[2,4,2048]{2,1,0:T(4,128)(2,1)S(1)}, bf16[2,4,2048]{2,1,0:T(4,128)(2,1)}, u32[]{:S(2)}) copy-start(bf16[2,4,2048]{2,1,0:T(4,128)(2,1)} %hidden_ref.1) | copy-start | bytes 98308
  0.7 7.1 %copy-start.3 = (bf16[2048]{0:T(1024)(128)(2,1)S(1)}, bf16[2048]{0:T(1024)(128)(2,1)}, u32[]{:S(2)}) copy-start(bf16[2048]{0:T(1024)(128)(2,1)} %param.12) | copy-start | bytes 12292
  2.1 18.4 %copy-start.4 = (s32[2,8,4]{1,2,0:T(4,128)S(1)}, s32[2,8,4]{1,2,0:T(4,128)}, u32[]{:S(2)}) copy-start(s32[2,8,4]{1,2,0:T(4,128)} %param.10) | copy-start | bytes 772
  2.1 18.4 %copy-start.5 = (f32[8,128]{1,0:T(8,128)S(1)}, f32[8,128]{1,0:T(8,128)}, u32[]{:S(2)}) copy-start(f32[8,128]{1,0:T(8,128)} %constant.4.clone.cos_ref) | copy-start | bytes 12292
  2.1 18.4 %copy-start.6 = (f32[8,128]{1,0:T(8,128)S(1)}, f32[8,128]{1,0:T(8,128)}, u32[]{:S(2)}) copy-start(f32[8,128]{1,0:T(8,128)} %constant.5.clone.sin_ref) | copy-start | bytes 12292
  2.1 12.2 %collective-permute-start = (bf16[256,256]{1,0:T(8,128)(2,1)S(1)}, bf16[256,256]{1,0:T(8,128)(2,1)S(1)}, u32[]{:S(2)}, u32[]{:S(2)}) collective-permute-start(bf16[256,256]{1,0:T(8,128)(2,1)S(1)} %get-tuple-element.18), channel_id=1, source_target_pairs={{0,4},{4,0},{8,12},{12,8},{1,5},{5,1},{9,13},{13,9},{2,6},{6,2},{1... | collective-permute-start | bytes 393224 | tf_op jit(solution)/shard_map/ppermute | solution.py:46
  5.2 15.3 %collective-permute-start.1 = (bf16[256,256]{1,0:T(8,128)(2,1)S(1)}, bf16[256,256]{1,0:T(8,128)(2,1)S(1)}, u32[]{:S(2)}, u32[]{:S(2)}) collective-permute-start(bf16[256,256]{1,0:T(8,128)(2,1)S(1)} %get-tuple-element.20), channel_id=1, source_target_pairs={{0,12},{4,8},{8,4},{12,0},{1,13},{5,9},{9,5},{13,1},{2,14},{6,10},... | collective-permute-start | bytes 393224 | tf_op jit(solution)/shard_map/ppermute | solution.py:46
  7.7 19.0 %slice-start = ((s8[8388608]{0:T(1024)(128)(4,1)}), s8[4194304]{0:T(1024)(128)(4,1)S(1)}, s32[]{:S(2)}) async-start(s8[8388608]{0:T(1024)(128)(4,1)} %bitcast.2), calls=%async_computation | async-start | bytes 8388608
  9.9 6.0 %collective-permute-start.2 = (f32[88,128]{1,0:T(8,128)S(1)}, f32[88,128]{1,0:T(8,128)S(1)}, u32[]{:S(2)}, u32[]{:S(2)}) collective-permute-start(f32[88,128]{1,0:T(8,128)S(1)} %get-tuple-element.21), channel_id=1, source_target_pairs={{0,12},{4,8},{8,4},{12,0},{1,13},{5,9},{9,5},{13,1},{2,14},{6,10},... | collective-permute-start | bytes 135176 | tf_op jit(solution)/shard_map/ppermute | solution.py:46
  12.3 8.3 %collective-permute-start.3 = (f32[88,128]{1,0:T(8,128)S(1)}, f32[88,128]{1,0:T(8,128)S(1)}, u32[]{:S(2)}, u32[]{:S(2)}) collective-permute-start(f32[88,128]{1,0:T(8,128)S(1)} %get-tuple-element.22), channel_id=1, source_target_pairs={{0,8},{4,12},{8,0},{12,4},{1,9},{5,13},{9,1},{13,5},{2,10},{6,14},... | collective-permute-start | bytes 135176 | tf_op jit(solution)/shard_map/ppermute | solution.py:46
  12.3 8.3 %collective-permute-start.4 = (f32[88,128]{1,0:T(8,128)S(1)}, f32[88,128]{1,0:T(8,128)S(1)}, u32[]{:S(2)}, u32[]{:S(2)}) collective-permute-start(f32[88,128]{1,0:T(8,128)S(1)} %get-tuple-element.23), channel_id=1, source_target_pairs={{0,4},{4,0},{8,12},{12,8},{1,5},{5,1},{9,13},{13,9},{2,6},{6,2},{1... | collective-permute-start | bytes 135176 | tf_op jit(solution)/shard_map/ppermute | solution.py:46
  14.4 14.9 %collective-permute-start.7 = (bf16[256,256]{1,0:T(8,128)(2,1)S(1)}, bf16[256,256]{1,0:T(8,128)(2,1)S(1)}, u32[]{:S(2)}, u32[]{:S(2)}) collective-permute-start(bf16[256,256]{1,0:T(8,128)(2,1)S(1)} %get-tuple-element.25.refs_3_), channel_id=1, source_target_pairs={{0,8},{4,12},{8,0},{12,4},{1,9},{5,13},{9,1},{13,5},{2,10},{6,14},... | collective-permute-start | bytes 393224 | tf_op jit(solution)/shard_map/ppermute | solution.py:46
  20.6 6.2 %slice-start.1 = ((s8[8388608]{0:T(1024)(128)(4,1)}), s8[4194304]{0:T(1024)(128)(4,1)S(1)}, s32[]{:S(2)}) async-start(s8[8388608]{0:T(1024)(128)(4,1)} %bitcast.2), calls=%async_computation.1 | async-start | bytes 8388608
  21.8 4.9 %collective-permute-start.8 = (bf16[80,128]{1,0:T(8,128)(2,1)S(1)}, bf16[80,128]{1,0:T(8,128)(2,1)S(1)}, u32[]{:S(2)}, u32[]{:S(2)}) collective-permute-start(bf16[80,128]{1,0:T(8,128)(2,1)S(1)} %attend.1.same_ref.after_ref), channel_id=1, source_target_pairs={{0,8},{4,12},{8,0},{12,4},{1,9},{5,13},{9,1},{13,5},{2,10},{6,14},... | collective-permute-start | bytes 61448 | tf_op jit(solution)/shard_map/ppermute | solution.py:46
  23.7 5.6 %collective-permute-start.6 = (bf16[80,128]{1,0:T(8,128)(2,1)S(1)}, bf16[80,128]{1,0:T(8,128)(2,1)S(1)}, u32[]{:S(2)}, u32[]{:S(2)}) collective-permute-start(bf16[80,128]{1,0:T(8,128)(2,1)S(1)} %attend.1.same_ref.after_ref), channel_id=1, source_target_pairs={{0,12},{4,8},{8,4},{12,0},{1,13},{5,9},{9,5},{13,1},{2,14},{6,10},... | collective-permute-start | bytes 61448 | tf_op jit(solution)/shard_map/ppermute | solution.py:46
  25.6 3.9 %collective-permute-start.5 = (bf16[80,128]{1,0:T(8,128)(2,1)S(1)}, bf16[80,128]{1,0:T(8,128)(2,1)S(1)}, u32[]{:S(2)}, u32[]{:S(2)}) collective-permute-start(bf16[80,128]{1,0:T(8,128)(2,1)S(1)} %attend.1.same_ref.after_ref), channel_id=1, source_target_pairs={{0,4},{4,0},{8,12},{12,8},{1,5},{5,1},{9,13},{13,9},{2,6},{6,2},{1... | collective-permute-start | bytes 61448 | tf_op jit(solution)/shard_map/ppermute | solution.py:46
  30.2 3.9 %collective-permute-start.9 = (bf16[8,2048]{1,0:T(8,128)(2,1)S(1)}, bf16[8,2048]{1,0:T(8,128)(2,1)S(1)}, u32[]{:S(2)}, u32[]{:S(2)}) collective-permute-start(bf16[8,2048]{1,0:T(8,128)(2,1)S(1)} %output_half.3), channel_id=1, source_target_pairs={{0,2},{1,3},{2,0},{3,1},{4,6},{5,7},{6,4},{7,5},{8,10},{9,11},{10,... | collective-permute-start | bytes 98312 | tf_op jit(solution)/shard_map/ppermute | solution.py:46
  31.7 2.4 %collective-permute-start.10 = (bf16[8,2048]{1,0:T(8,128)(2,1)S(1)}, bf16[8,2048]{1,0:T(8,128)(2,1)S(1)}, u32[]{:S(2)}, u32[]{:S(2)}) collective-permute-start(bf16[8,2048]{1,0:T(8,128)(2,1)S(1)} %output_half.3), channel_id=1, source_target_pairs={{0,1},{1,0},{2,3},{3,2},{4,5},{5,4},{6,7},{7,6},{8,9},{9,8},{10,11... | collective-permute-start | bytes 98312 | tf_op jit(solution)/shard_map/ppermute | solution.py:46
  31.7 3.3 %collective-permute-start.11 = (bf16[8,2048]{1,0:T(8,128)(2,1)S(1)}, bf16[8,2048]{1,0:T(8,128)(2,1)S(1)}, u32[]{:S(2)}, u32[]{:S(2)}) collective-permute-start(bf16[8,2048]{1,0:T(8,128)(2,1)S(1)} %output_half.3), channel_id=1, source_target_pairs={{0,3},{1,2},{2,1},{3,0},{4,7},{5,6},{6,5},{7,4},{8,11},{9,10},{10,... | collective-permute-start | bytes 98312 | tf_op jit(solution)/shard_map/ppermute | solution.py:46

commit v14 on v11

--- a/solution.py
+++ b/solution.py
@@ -41,6 +41,15 @@
 def swap(outgoing, axis, offset):
     count = lax.axis_size(axis)
     return lax.ppermute(outgoing, axis, [(i, i ^ offset) for i in range(count)])
+
+
+VALUE_PAIRS = (
+    ((2, 1), (3, 0)),
+    ((1, 0), (3, 2)),
+    ((0, 2), (1, 3), (2, 0), (3, 1)),
+    ((0, 1), (1, 2), (2, 3)),
+    ((0, 3),),
+)
 
 
 def all_to_all(outgoing, axis):
@@ -378,40 +387,47 @@
     return jnp.concatenate(pieces, axis=1).astype(jnp.bfloat16)
 
 
-def output_half_kernel(flip, w_ref, same_ref, other_ref, *refs):
-    out_ref = refs[-1]
-    query_rows = same_ref.shape[0]
+def output_same_kernel(w_ref, own_ref, second_ref, out_ref):
     me = lax.axis_index("seq")
-    local = jnp.bitwise_and(me, 1)
-    if flip:
-        local = 1 - local
-    second = me >= 2
-    same = same_ref[...].astype(jnp.float32)
-    other = other_ref[...].astype(jnp.float32)
+    out_ref[...] = output_terms(w_ref, jnp.bitwise_and(me, 1), me >= 2, own_ref, second_ref)
+
+
+def output_other_kernel(w_ref, *refs):
+    transfers, addend_ref, out_ref = refs[:4], refs[4], refs[5]
+    me = lax.axis_index("seq")
+    five, four, two, one = [ref[...].astype(jnp.float32) for ref in transfers]
+    even = jnp.bitwise_and(me, 1) == 0
+    first = jnp.where(even, two, four)
+    third = jnp.where(me < 2, one, jnp.where(even, four, five))
+    terms = output_terms(w_ref, 1 - jnp.bitwise_and(me, 1), me >= 2, first, third)
+    out_ref[...] = (terms + addend_ref[...]).astype(out_ref.dtype)
+
+
+def output_terms(w_ref, local, second, same, other):
+    same = same[...].astype(jnp.float32)
+    other = other[...].astype(jnp.float32)
     merged = merge_heads(
-        jnp.where(second, other, same), jnp.where(second, same, other), query_rows // QPK
+        jnp.where(second, other, same),
+        jnp.where(second, same, other),
+        same.shape[0] // QPK,
     )
     depth = w_ref.shape[0] // 2
     weights = w_ref[pl.ds(pl.multiple_of(local * depth, depth), depth), :]
-    total = jnp.dot(merged, weights, preferred_element_type=jnp.float32)
-    if len(refs) > 1:
-        total += refs[0][...]
-    out_ref[...] = total.astype(out_ref.dtype)
-
-
-def output_half(flip, w_out, same, other, *addend):
-    rows = 2 * same.shape[0] // QPK
-    dtype = jnp.bfloat16 if addend else jnp.float32
+    return jnp.dot(merged, weights, preferred_element_type=jnp.float32)
+
+
+def output_half(kernel, dtype, w_out, values, *arrivals):
+    rows = 2 * values.shape[0] // QPK
     vmem = pl.BlockSpec(memory_space=pltpu.VMEM)
     return pl.pallas_call(
-        functools.partial(output_half_kernel, flip),
+        kernel,
         out_shape=jax.ShapeDtypeStruct((rows, w_out.shape[1]), dtype),
-        in_specs=[vmem] * (3 + len(addend)),
+        in_specs=[vmem] * (2 + len(arrivals)),
         out_specs=vmem,
         compiler_params=pltpu.CompilerParams(vmem_limit_bytes=8 * 1024 * 1024),
         cost_estimate=pl.CostEstimate(flops=10**9, bytes_accessed=0, transcendentals=0),
         name="output_half",
-    )(w_out, same, other, *addend)
+    )(w_out, values, *arrivals)
 
 
 def output_kernel(heads_local, w_ref, gathered_ref, out_ref):
@@ -467,11 +483,13 @@
         parts[1], blocks[3] = lax.optimization_barrier((parts[1], blocks[3]))
         parts = [parts[0]] + [swap(parts[k], "seq", k) for k in partners]
         (attended,) = attend(kept_blocks, blocks[::-1] + parts[::-1], *shape)
+        one, two, three, four, five = [lax.ppermute(attended, "seq", p) for p in VALUE_PAIRS]
+        three, two, one = lax.optimization_barrier((three, two, one))
+        terms = output_half(output_same_kernel, jnp.float32, w_out, attended, three)
+        terms = output_half(
+            output_other_kernel, jnp.bfloat16, w_out, five, four, two, one, terms
+        )
         kept_cache = place(kept_blocks, attended, blocks, source_blocks, heads_local)
-        first, second, third = [swap(attended, "seq", k) for k in partners]
-        first, kept_cache = lax.optimization_barrier((first, kept_cache))
-        terms = output_half(True, w_out, first, third)
-        terms = output_half(False, w_out, attended, second, terms)
     else:
         (blocks,) = pick(kept_blocks, source_cache, direct)
         (parts,) = project(blocks, *weights, pair_count, direct)
@@ -481,6 +499,7 @@
     if is_direct(head_count):
         terms = terms.astype(jnp.bfloat16)
         others = [swap(terms, "head", k) for k in range(1, head_count)]
+        others[2], kept_cache = lax.optimization_barrier((others[2], kept_cache))
         own, core, along, across = [t.astype(jnp.float32) for t in [terms] + others]
         summed = (own + core) + (along + across)
     else:

time: 34.3 us -> 41.1 us (1.20)
  starting transfers between devices: 19.6 us -> 27 us
  waiting for transfers between devices: 5.68 us -> 4.86 us
    ppermute x0 -> x5, starting transfers between devices: none -> 11.6 us  [shards(): lax.ppermute(attended, 'seq', p)]
    ppermute x12 -> x9, starting transfers between devices: 19.6 us -> 15.4 us  [swap(): return lax.ppermute(outgoing, axis, [(i, i ^ offset) for i in range(count)])]
    ppermute x12 -> x9, waiting for transfers between devices: 5.68 us -> 4.23 us  [swap(): return lax.ppermute(outgoing, axis, [(i, i ^ offset) for i in range(count)])]
    ppermute x0 -> x5, waiting for transfers between devices: none -> 0.64 us  [shards(): lax.ppermute(attended, 'seq', p)]
  transfers between devices with their start and end apart: 12 -> 14, of which waited for: 5 -> 3; matrix products, arithmetic and copies ran while one was open for 0% -> 0% of each run, Pallas kernels for 12% -> 10%
where the time goes in v14:
time: 41.1 us; the launch traced here: 40.8 us
  starting transfers between devices  27 us (66%)
  Pallas kernels  7.33 us (18%)
  waiting for transfers between devices  4.86 us (12%)
  between operations  0.86 us (2%)
  other arithmetic  0.65 us (2%)
    ppermute x9, starting transfers between devices, swap(): return lax.ppermute(outgoing, axis, [(i, i ^ offset) for i in range(count)])  15.4 us
    ppermute x5, starting transfers between devices, shards(): lax.ppermute(attended, 'seq', p)  11.6 us
    ppermute x9, waiting for transfers between devices, swap(): return lax.ppermute(outgoing, axis, [(i, i ^ offset) for i in range(count)])  4.23 us
    pallas_call x1, Pallas kernels, project(): pl.pallas_call(functools.partial(project_kernel, direct), out_shape=shape...  2.13 us
    pallas_call x1, Pallas kernels, pick(): pl.pallas_call(pick_near_kernel if direct else pick_all_kernel, out_shape...  1.43 us
    pallas_call x1, Pallas kernels, place(): pl.pallas_call(functools.partial(place_kernel, source_blocks, heads_local...  1.33 us
    pallas_call x2, Pallas kernels, output_half(): pl.pallas_call(kernel, out_shape=jax.ShapeDtypeStruct((rows, w_out.shape[...  1.31 us
    pallas_call x1, Pallas kernels, attend(): pl.pallas_call(functools.partial(attend_kernel, direct, source_blocks, he...  1.13 us
  transfers between devices with their start and end apart: 14, of which 3 were waited for; matrix products, arithmetic and copies ran while one was open for 0% of the time, Pallas kernels for 10%

profile of v14, /device:TPU:0, one launch (start us, length us, event | category | flops | bytes accessed | tf_op | source)
XLA Modules:
  0.0 40.8 jit_solution(5358321005481104957)
XLA Ops:
  0.7 1.4 %pick_blocks.1 = (bf16[256,256]{1,0:T(8,128)(2,1)S(1)}, bf16[256,256]{1,0:T(8,128)(2,1)S(1)}, bf16[256,256]{1,0:T(8,128)(2,1)S(1)}, bf16[256,256]{1,0:T(8,128)(2,1)S(1)}) custom-call(s32[2,4,8]{2,1,0:T(4,128)} %bitcast.5, bf16[2,2,512,256]{3,2,1,0:T(8,128)(2,1)} %cache_ref.1), custom_call_target="tpu_custom_call" | custom-call | flops 10000000000 | tf_op jit(solution)/shard_map/pick_blocks/pallas_call | solution.py:128
  2.1 0.0 copy-start.5
  2.1 5.1 %collective-permute-start = (bf16[256,256]{1,0:T(8,128)(2,1)S(1)}, bf16[256,256]{1,0:T(8,128)(2,1)S(1)}, u32[]{:S(2)}, u32[]{:S(2)}) collective-permute-start(bf16[256,256]{1,0:T(8,128)(2,1)S(1)} %get-tuple-element.19), channel_id=1, source_target_pairs={{0,12},{4,8},{8,4},{12,0},{1,13},{5,9},{9,5},{13,1},{2,14},{6,10},... | collective-permute-start | bytes 393224 | tf_op jit(solution)/shard_map/ppermute | solution.py:43
  7.3 0.6 %collective-permute-start.2 = (bf16[256,256]{1,0:T(8,128)(2,1)S(1)}, bf16[256,256]{1,0:T(8,128)(2,1)S(1)}, u32[]{:S(2)}, u32[]{:S(2)}) collective-permute-start(bf16[256,256]{1,0:T(8,128)(2,1)S(1)} %get-tuple-element.22), channel_id=1, source_target_pairs={{0,4},{4,0},{8,12},{12,8},{1,5},{5,1},{9,13},{13,9},{2,6},{6,2},{1... | collective-permute-start | bytes 393224 | tf_op jit(solution)/shard_map/ppermute | solution.py:43
  7.9 0.0 slice-start
  7.9 2.1 %project.1 = (f32[48,128]{1,0:T(8,128)S(1)}, f32[48,128]{1,0:T(8,128)S(1)}, f32[48,128]{1,0:T(8,128)S(1)}, f32[48,128]{1,0:T(8,128)S(1)}) custom-call(bf16[256,256]{1,0:T(8,128)(2,1)S(1)} %get-tuple-element.17.after_ref.refs_3_.refs_0_, bf16[2,4,2048]{2,1,0:T(4,128)(2,1)S(1)} %copy-done.2, bf16[16,128]{1,0:T(8,128)(2,1)S(1)} %bitcast.4, ...), custom_call_target="tpu_custom_call" | custom-call | flops 83886080 | bytes 10485760 | tf_op jit(solution)/shard_map/project/pallas_call | solution.py:219
  10.1 3.8 %collective-permute-start.3 = (f32[48,128]{1,0:T(8,128)S(1)}, f32[48,128]{1,0:T(8,128)S(1)}, u32[]{:S(2)}, u32[]{:S(2)}) collective-permute-start(f32[48,128]{1,0:T(8,128)S(1)} %get-tuple-element.23), channel_id=1, source_target_pairs={{0,12},{4,8},{8,4},{12,0},{1,13},{5,9},{9,5},{13,1},{2,14},{6,10},... | collective-permute-start | bytes 73736 | tf_op jit(solution)/shard_map/ppermute | solution.py:43
  13.9 3.7 %collective-permute-start.5 = (f32[48,128]{1,0:T(8,128)S(1)}, f32[48,128]{1,0:T(8,128)S(1)}, u32[]{:S(2)}, u32[]{:S(2)}) collective-permute-start(f32[48,128]{1,0:T(8,128)S(1)} %get-tuple-element.25), channel_id=1, source_target_pairs={{0,4},{4,0},{8,12},{12,8},{1,5},{5,1},{9,13},{13,9},{2,6},{6,2},{1... | collective-permute-start | bytes 73736 | tf_op jit(solution)/shard_map/ppermute | solution.py:43
  17.6 2.8 %collective-permute-done.4.refs_5_ = f32[48,128]{1,0:T(8,128)S(1)} collective-permute-done((f32[48,128]{1,0:T(8,128)S(1)}, f32[48,128]{1,0:T(8,128)S(1)}, u32[]{:S(2)}, u32[]{:S(2)}) %collective-permute-start.4) | collective-permute-done | bytes 24608 | tf_op jit(solution)/shard_map/ppermute | solution.py:43
  20.5 0.0 slice-start.1
  20.5 1.1 %attend.1.own_ref.after_ref = bf16[32,128]{1,0:T(8,128)(2,1)S(1)} custom-call(s32[2,4,8]{2,1,0:T(4,128)S(1)} %bitcast.6, f32[8,128]{1,0:T(8,128)S(1)} %copy-done.6, f32[8,128]{1,0:T(8,128)S(1)} %copy-done.5, bf16[256,256]{1,0:T(8,128)(2,1)S(1)} %collective-permute-done.refs_0_.refs_3_, bf16[256,256]{1,0:T(8,128)(2,1)S(1)} %collective-permute-done.1.refs_1_.refs_2_, ...), custom_call_target="tpu_custom_call" | custom-call | flops 10000000000 | tf_op jit(solution)/shard_map/attend/pallas_call | solution.py:370
  21.6 1.4 %collective-permute-start.10 = (bf16[32,128]{1,0:T(8,128)(2,1)S(1)}, bf16[32,128]{1,0:T(8,128)(2,1)S(1)}, u32[]{:S(2)}, u32[]{:S(2)}) collective-permute-start(bf16[32,128]{1,0:T(8,128)(2,1)S(1)} %attend.1.own_ref.after_ref), channel_id=1, source_target_pairs={{8,4},{12,0},{9,5},{13,1},{10,6},{14,2},{11,7},{15,3},{24,20},{28,... | collective-permute-start | bytes 24584 | tf_op jit(solution)/shard_map/ppermute | solution.py:486
  23.1 1.3 %collective-permute-start.9 = (bf16[32,128]{1,0:T(8,128)(2,1)S(1)}, bf16[32,128]{1,0:T(8,128)(2,1)S(1)}, u32[]{:S(2)}, u32[]{:S(2)}) collective-permute-start(bf16[32,128]{1,0:T(8,128)(2,1)S(1)} %attend.1.own_ref.after_ref), channel_id=1, source_target_pairs={{4,0},{12,8},{5,1},{13,9},{6,2},{14,10},{7,3},{15,11},{20,16},{28,... | collective-permute-start | bytes 24584 | tf_op jit(solution)/shard_map/ppermute | solution.py:486
  24.4 3.1 %collective-permute-start.8 = (bf16[32,128]{1,0:T(8,128)(2,1)S(1)}, bf16[32,128]{1,0:T(8,128)(2,1)S(1)}, u32[]{:S(2)}, u32[]{:S(2)}) collective-permute-start(bf16[32,128]{1,0:T(8,128)(2,1)S(1)} %attend.1.own_ref.after_ref), channel_id=1, source_target_pairs={{0,8},{4,12},{8,0},{12,4},{1,9},{5,13},{9,1},{13,5},{2,10},{6,14},... | collective-permute-start | bytes 24584 | tf_op jit(solution)/shard_map/ppermute | solution.py:486
  27.4 4.5 %collective-permute-start.7 = (bf16[32,128]{1,0:T(8,128)(2,1)S(1)}, bf16[32,128]{1,0:T(8,128)(2,1)S(1)}, u32[]{:S(2)}, u32[]{:S(2)}) collective-permute-start(bf16[32,128]{1,0:T(8,128)(2,1)S(1)} %attend.1.own_ref.after_ref), channel_id=1, source_target_pairs={{0,4},{4,8},{8,12},{1,5},{5,9},{9,13},{2,6},{6,10},{10,14},{3,7},{... | collective-permute-start | bytes 24584 | tf_op jit(solution)/shard_map/ppermute | solution.py:486
  32.0 1.3 %collective-permute-start.6 = (bf16[32,128]{1,0:T(8,128)(2,1)S(1)}, bf16[32,128]{1,0:T(8,128)(2,1)S(1)}, u32[]{:S(2)}, u32[]{:S(2)}) collective-permute-start(bf16[32,128]{1,0:T(8,128)(2,1)S(1)} %attend.1.own_ref.after_ref), channel_id=1, source_target_pairs={{0,12},{1,13},{2,14},{3,15},{16,28},{17,29},{18,30},{19,31}} | collective-permute-start | bytes 24584 | tf_op jit(solution)/shard_map/ppermute | solution.py:486
  33.3 0.7 %output_half.2.refs_4_ = f32[8,2048]{1,0:T(8,128)S(1)} custom-call(bf16[2048,2048]{1,0:T(8,128)(2,1)S(1)} %bitcast.3, bf16[32,128]{1,0:T(8,128)(2,1)S(1)} %attend.1.own_ref.after_ref, bf16[32,128]{1,0:T(8,128)(2,1)S(1)} %collective-permute-done.8.second_ref), custom_call_target="tpu_custom_call" | custom-call | flops 1000000000 | tf_op jit(solution)/shard_map/output_half/pallas_call | solution.py:422
  34.0 0.6 %collective-permute-done.6.refs_0_ = bf16[32,128]{1,0:T(8,128)(2,1)S(1)} collective-permute-done((bf16[32,128]{1,0:T(8,128)(2,1)S(1)}, bf16[32,128]{1,0:T(8,128)(2,1)S(1)}, u32[]{:S(2)}, u32[]{:S(2)}) %collective-permute-start.6) | collective-permute-done | bytes 8224 | tf_op jit(solution)/shard_map/ppermute | solution.py:486
  34.6 0.7 %output_half.3 = bf16[8,2048]{1,0:T(8,128)(2,1)S(1)} custom-call(bf16[2048,2048]{1,0:T(8,128)(2,1)S(1)} %bitcast.3, bf16[32,128]{1,0:T(8,128)(2,1)S(1)} %collective-permute-done.6.refs_0_, bf16[32,128]{1,0:T(8,128)(2,1)S(1)} %collective-permute-done.7.refs_1_, bf16[32,128]{1,0:T(8,128)(2,1)S(1)} %collective-permute-done.9.refs_2_, ...), custom_call_target="tpu_custom_call" | custom-call | flops 1000000000 | tf_op jit(solution)/shard_map/output_half/pallas_call | solution.py:422
  35.3 1.5 %collective-permute-start.13 = (bf16[8,2048]{1,0:T(8,128)(2,1)S(1)}, bf16[8,2048]{1,0:T(8,128)(2,1)S(1)}, u32[]{:S(2)}, u32[]{:S(2)}) collective-permute-start(bf16[8,2048]{1,0:T(8,128)(2,1)S(1)} %output_half.3), channel_id=1, source_target_pairs={{0,2},{1,3},{2,0},{3,1},{4,6},{5,7},{6,4},{7,5},{8,10},{9,11},{10,... | collective-permute-start | bytes 98312 | tf_op jit(solution)/shard_map/ppermute | solution.py:43
  36.8 0.6 %collective-permute-start.11 = (bf16[8,2048]{1,0:T(8,128)(2,1)S(1)}, bf16[8,2048]{1,0:T(8,128)(2,1)S(1)}, u32[]{:S(2)}, u32[]{:S(2)}) collective-permute-start(bf16[8,2048]{1,0:T(8,128)(2,1)S(1)} %output_half.3), channel_id=1, source_target_pairs={{0,3},{1,2},{2,1},{3,0},{4,7},{5,6},{6,5},{7,4},{8,11},{9,10},{10,... | collective-permute-start | bytes 98312 | tf_op jit(solution)/shard_map/ppermute | solution.py:43
  37.4 1.3 %place.1 = bf16[1,1,512,256]{3,2,1,0:T(8,128)(2,1)} custom-call(s32[2,4,8]{2,1,0:T(4,128)S(1)} %bitcast.7, bf16[32,128]{1,0:T(8,128)(2,1)S(1)} %attend.1.own_ref.after_ref, bf16[256,256]{1,0:T(8,128)(2,1)S(1)} %get-tuple-element.17.after_ref.refs_3_.refs_0_, bf16[256,256]{1,0:T(8,128)(2,1)S(1)} %collective-permute-done.2.refs_2_.refs_1_, ...), custom_call_target="tpu_custom_call" | custom-call | flops 1000000000 | tf_op jit(solution)/shard_map/place/pallas_call | solution.py:263
  38.8 1.4 %collective-permute-done.11 = bf16[8,2048]{1,0:T(8,128)(2,1)S(1)} collective-permute-done((bf16[8,2048]{1,0:T(8,128)(2,1)S(1)}, bf16[8,2048]{1,0:T(8,128)(2,1)S(1)}, u32[]{:S(2)}, u32[]{:S(2)}) %collective-permute-start.11) | collective-permute-done | bytes 32800 | tf_op jit(solution)/shard_map/ppermute | solution.py:43
  40.2 0.6 %add_convert_fusion = bf16[2,4,2048]{2,1,0:T(4,128)(2,1)} fusion(f32[2,4,2048]{2,1,0:T(4,128)S(1)} %reshape.11, bf16[2,4,2048]{2,1,0:T(4,128)(2,1)S(1)} %copy-done.2), kind=kLoop, calls=%fused_computation | loop fusion | flops 49152 | bytes 131072 | tf_op jit(solution)/shard_map/convert_element_type | solution.py:508
  (32 shorter events, 0.1 us)
Async XLA Ops:
  0.6 7.3 %copy-start = (bf16[2048,2048]{1,0:T(8,128)(2,1)S(1)}, bf16[2048,2048]{1,0:T(8,128)(2,1)}, u32[]{:S(2)}) copy-start(bf16[2048,2048]{1,0:T(8,128)(2,1)} %wq_ref.1) | copy-start | bytes 25165828
  0.6 7.3 %copy-start.1 = (bf16[2048,2,256]{2,1,0:T(2,128)(2,1)S(1)}, bf16[2048,2,256]{2,1,0:T(2,128)(2,1)}, u32[]{:S(2)}) copy-start(bf16[2048,2,256]{2,1,0:T(2,128)(2,1)} %wkv_ref.1) | copy-start | bytes 6291460
  0.7 7.3 %copy-start.2 = (bf16[2,4,2048]{2,1,0:T(4,128)(2,1)S(1)}, bf16[2,4,2048]{2,1,0:T(4,128)(2,1)}, u32[]{:S(2)}) copy-start(bf16[2,4,2048]{2,1,0:T(4,128)(2,1)} %hidden_ref.1) | copy-start | bytes 98308
  0.7 7.3 %copy-start.3 = (bf16[2048]{0:T(1024)(128)(2,1)S(1)}, bf16[2048]{0:T(1024)(128)(2,1)}, u32[]{:S(2)}) copy-start(bf16[2048]{0:T(1024)(128)(2,1)} %param.12) | copy-start | bytes 12292
  2.1 18.3 %copy-start.4 = (s32[2,8,4]{1,2,0:T(4,128)S(1)}, s32[2,8,4]{1,2,0:T(4,128)}, u32[]{:S(2)}) copy-start(s32[2,8,4]{1,2,0:T(4,128)} %param.10) | copy-start | bytes 772
  2.1 18.3 %copy-start.5 = (f32[8,128]{1,0:T(8,128)S(1)}, f32[8,128]{1,0:T(8,128)}, u32[]{:S(2)}) copy-start(f32[8,128]{1,0:T(8,128)} %constant.5.clone.sin_ref) | copy-start | bytes 12292
  2.1 18.3 %copy-start.6 = (f32[8,128]{1,0:T(8,128)S(1)}, f32[8,128]{1,0:T(8,128)}, u32[]{:S(2)}) copy-start(f32[8,128]{1,0:T(8,128)} %constant.4.clone.cos_ref) | copy-start | bytes 12292
  2.1 11.8 %collective-permute-start = (bf16[256,256]{1,0:T(8,128)(2,1)S(1)}, bf16[256,256]{1,0:T(8,128)(2,1)S(1)}, u32[]{:S(2)}, u32[]{:S(2)}) collective-permute-start(bf16[256,256]{1,0:T(8,128)(2,1)S(1)} %get-tuple-element.19), channel_id=1, source_target_pairs={{0,12},{4,8},{8,4},{12,0},{1,13},{5,9},{9,5},{13,1},{2,14},{6,10},... | collective-permute-start | bytes 393224 | tf_op jit(solution)/shard_map/ppermute | solution.py:43
  7.3 13.2 %collective-permute-start.1 = (bf16[256,256]{1,0:T(8,128)(2,1)S(1)}, bf16[256,256]{1,0:T(8,128)(2,1)S(1)}, u32[]{:S(2)}, u32[]{:S(2)}) collective-permute-start(bf16[256,256]{1,0:T(8,128)(2,1)S(1)} %get-tuple-element.21), channel_id=1, source_target_pairs={{0,8},{4,12},{8,0},{12,4},{1,9},{5,13},{9,1},{13,5},{2,10},{6,14},... | collective-permute-start | bytes 393224 | tf_op jit(solution)/shard_map/ppermute | solution.py:43
  7.3 13.2 %collective-permute-start.2 = (bf16[256,256]{1,0:T(8,128)(2,1)S(1)}, bf16[256,256]{1,0:T(8,128)(2,1)S(1)}, u32[]{:S(2)}, u32[]{:S(2)}) collective-permute-start(bf16[256,256]{1,0:T(8,128)(2,1)S(1)} %get-tuple-element.22), channel_id=1, source_target_pairs={{0,4},{4,0},{8,12},{12,8},{1,5},{5,1},{9,13},{13,9},{2,6},{6,2},{1... | collective-permute-start | bytes 393224 | tf_op jit(solution)/shard_map/ppermute | solution.py:43
  7.9 25.4 %slice-start = ((s8[8388608]{0:T(1024)(128)(4,1)}), s8[4194304]{0:T(1024)(128)(4,1)S(1)}, s32[]{:S(2)}) async-start(s8[8388608]{0:T(1024)(128)(4,1)} %bitcast.2), calls=%async_computation | async-start | bytes 8388608
  10.1 7.5 %collective-permute-start.3 = (f32[48,128]{1,0:T(8,128)S(1)}, f32[48,128]{1,0:T(8,128)S(1)}, u32[]{:S(2)}, u32[]{:S(2)}) collective-permute-start(f32[48,128]{1,0:T(8,128)S(1)} %get-tuple-element.23), channel_id=1, source_target_pairs={{0,12},{4,8},{8,4},{12,0},{1,13},{5,9},{9,5},{13,1},{2,14},{6,10},... | collective-permute-start | bytes 73736 | tf_op jit(solution)/shard_map/ppermute | solution.py:43
  13.9 6.5 %collective-permute-start.4 = (f32[48,128]{1,0:T(8,128)S(1)}, f32[48,128]{1,0:T(8,128)S(1)}, u32[]{:S(2)}, u32[]{:S(2)}) collective-permute-start(f32[48,128]{1,0:T(8,128)S(1)} %get-tuple-element.24), channel_id=1, source_target_pairs={{0,8},{4,12},{8,0},{12,4},{1,9},{5,13},{9,1},{13,5},{2,10},{6,14},... | collective-permute-start | bytes 73736 | tf_op jit(solution)/shard_map/ppermute | solution.py:43
  13.9 6.5 %collective-permute-start.5 = (f32[48,128]{1,0:T(8,128)S(1)}, f32[48,128]{1,0:T(8,128)S(1)}, u32[]{:S(2)}, u32[]{:S(2)}) collective-permute-start(f32[48,128]{1,0:T(8,128)S(1)} %get-tuple-element.25), channel_id=1, source_target_pairs={{0,4},{4,0},{8,12},{12,8},{1,5},{5,1},{9,13},{13,9},{2,6},{6,2},{1... | collective-permute-start | bytes 73736 | tf_op jit(solution)/shard_map/ppermute | solution.py:43
  20.5 12.8 %slice-start.1 = ((s8[8388608]{0:T(1024)(128)(4,1)}), s8[4194304]{0:T(1024)(128)(4,1)S(1)}, s32[]{:S(2)}) async-start(s8[8388608]{0:T(1024)(128)(4,1)} %bitcast.2), calls=%async_computation.1 | async-start | bytes 8388608
  21.6 11.6 %collective-permute-start.10 = (bf16[32,128]{1,0:T(8,128)(2,1)S(1)}, bf16[32,128]{1,0:T(8,128)(2,1)S(1)}, u32[]{:S(2)}, u32[]{:S(2)}) collective-permute-start(bf16[32,128]{1,0:T(8,128)(2,1)S(1)} %attend.1.own_ref.after_ref), channel_id=1, source_target_pairs={{8,4},{12,0},{9,5},{13,1},{10,6},{14,2},{11,7},{15,3},{24,20},{28,... | collective-permute-start | bytes 24584 | tf_op jit(solution)/shard_map/ppermute | solution.py:486
  23.1 10.2 %collective-permute-start.9 = (bf16[32,128]{1,0:T(8,128)(2,1)S(1)}, bf16[32,128]{1,0:T(8,128)(2,1)S(1)}, u32[]{:S(2)}, u32[]{:S(2)}) collective-permute-start(bf16[32,128]{1,0:T(8,128)(2,1)S(1)} %attend.1.own_ref.after_ref), channel_id=1, source_target_pairs={{4,0},{12,8},{5,1},{13,9},{6,2},{14,10},{7,3},{15,11},{20,16},{28,... | collective-permute-start | bytes 24584 | tf_op jit(solution)/shard_map/ppermute | solution.py:486
  24.4 8.9 %collective-permute-start.8 = (bf16[32,128]{1,0:T(8,128)(2,1)S(1)}, bf16[32,128]{1,0:T(8,128)(2,1)S(1)}, u32[]{:S(2)}, u32[]{:S(2)}) collective-permute-start(bf16[32,128]{1,0:T(8,128)(2,1)S(1)} %attend.1.own_ref.after_ref), channel_id=1, source_target_pairs={{0,8},{4,12},{8,0},{12,4},{1,9},{5,13},{9,1},{13,5},{2,10},{6,14},... | collective-permute-start | bytes 24584 | tf_op jit(solution)/shard_map/ppermute | solution.py:486
  27.4 6.6 %collective-permute-start.7 = (bf16[32,128]{1,0:T(8,128)(2,1)S(1)}, bf16[32,128]{1,0:T(8,128)(2,1)S(1)}, u32[]{:S(2)}, u32[]{:S(2)}) collective-permute-start(bf16[32,128]{1,0:T(8,128)(2,1)S(1)} %attend.1.own_ref.after_ref), channel_id=1, source_target_pairs={{0,4},{4,8},{8,12},{1,5},{5,9},{9,13},{2,6},{6,10},{10,14},{3,7},{... | collective-permute-start | bytes 24584 | tf_op jit(solution)/shard_map/ppermute | solution.py:486
  32.0 2.6 %collective-permute-start.6 = (bf16[32,128]{1,0:T(8,128)(2,1)S(1)}, bf16[32,128]{1,0:T(8,128)(2,1)S(1)}, u32[]{:S(2)}, u32[]{:S(2)}) collective-permute-start(bf16[32,128]{1,0:T(8,128)(2,1)S(1)} %attend.1.own_ref.after_ref), channel_id=1, source_target_pairs={{0,12},{1,13},{2,14},{3,15},{16,28},{17,29},{18,30},{19,31}} | collective-permute-start | bytes 24584 | tf_op jit(solution)/shard_map/ppermute | solution.py:486
  35.3 4.9 %collective-permute-start.13 = (bf16[8,2048]{1,0:T(8,128)(2,1)S(1)}, bf16[8,2048]{1,0:T(8,128)(2,1)S(1)}, u32[]{:S(2)}, u32[]{:S(2)}) collective-permute-start(bf16[8,2048]{1,0:T(8,128)(2,1)S(1)} %output_half.3), channel_id=1, source_target_pairs={{0,2},{1,3},{2,0},{3,1},{4,6},{5,7},{6,4},{7,5},{8,10},{9,11},{10,... | collective-permute-start | bytes 98312 | tf_op jit(solution)/shard_map/ppermute | solution.py:43
  36.8 3.3 %collective-permute-start.12 = (bf16[8,2048]{1,0:T(8,128)(2,1)S(1)}, bf16[8,2048]{1,0:T(8,128)(2,1)S(1)}, u32[]{:S(2)}, u32[]{:S(2)}) collective-permute-start(bf16[8,2048]{1,0:T(8,128)(2,1)S(1)} %output_half.3), channel_id=1, source_target_pairs={{0,1},{1,0},{2,3},{3,2},{4,5},{5,4},{6,7},{7,6},{8,9},{9,8},{10,11... | collective-permute-start | bytes 98312 | tf_op jit(solution)/shard_map/ppermute | solution.py:43
  36.8 3.3 %collective-permute-start.11 = (bf16[8,2048]{1,0:T(8,128)(2,1)S(1)}, bf16[8,2048]{1,0:T(8,128)(2,1)S(1)}, u32[]{:S(2)}, u32[]{:S(2)}) collective-permute-start(bf16[8,2048]{1,0:T(8,128)(2,1)S(1)} %output_half.3), channel_id=1, source_target_pairs={{0,3},{1,2},{2,1},{3,0},{4,7},{5,6},{6,5},{7,4},{8,11},{9,10},{10,... | collective-permute-start | bytes 98312 | tf_op jit(solution)/shard_map/ppermute | solution.py:43

commit v15 on v14

--- a/solution.py
+++ b/solution.py
@@ -43,13 +43,9 @@
     return lax.ppermute(outgoing, axis, [(i, i ^ offset) for i in range(count)])
 
 
-VALUE_PAIRS = (
-    ((2, 1), (3, 0)),
-    ((1, 0), (3, 2)),
-    ((0, 2), (1, 3), (2, 0), (3, 1)),
-    ((0, 1), (1, 2), (2, 3)),
-    ((0, 3),),
-)
+def shift(outgoing, axis, step):
+    count = lax.axis_size(axis)
+    return lax.ppermute(outgoing, axis, [(i, (i + step) % count) for i in range(count)])
 
 
 def all_to_all(outgoing, axis):
@@ -392,13 +388,13 @@
     out_ref[...] = output_terms(w_ref, jnp.bitwise_and(me, 1), me >= 2, own_ref, second_ref)
 
 
-def output_other_kernel(w_ref, *refs):
-    transfers, addend_ref, out_ref = refs[:4], refs[4], refs[5]
+def output_other_kernel(w_ref, above_ref, below_ref, addend_ref, out_ref):
     me = lax.axis_index("seq")
-    five, four, two, one = [ref[...].astype(jnp.float32) for ref in transfers]
     even = jnp.bitwise_and(me, 1) == 0
-    first = jnp.where(even, two, four)
-    third = jnp.where(me < 2, one, jnp.where(even, four, five))
+    below = below_ref[...].astype(jnp.float32)
+    above = above_ref[...].astype(jnp.float32)
+    first = jnp.where(even, above, below)
+    third = jnp.where(even, below, above)
     terms = output_terms(w_ref, 1 - jnp.bitwise_and(me, 1), me >= 2, first, third)
     out_ref[...] = (terms + addend_ref[...]).astype(out_ref.dtype)
 
@@ -483,13 +479,11 @@
         parts[1], blocks[3] = lax.optimization_barrier((parts[1], blocks[3]))
         parts = [parts[0]] + [swap(parts[k], "seq", k) for k in partners]
         (attended,) = attend(kept_blocks, blocks[::-1] + parts[::-1], *shape)
-        one, two, three, four, five = [lax.ppermute(attended, "seq", p) for p in VALUE_PAIRS]
-        three, two, one = lax.optimization_barrier((three, two, one))
-        terms = output_half(output_same_kernel, jnp.float32, w_out, attended, three)
-        terms = output_half(
-            output_other_kernel, jnp.bfloat16, w_out, five, four, two, one, terms
-        )
         kept_cache = place(kept_blocks, attended, blocks, source_blocks, heads_local)
+        below, second, above = [shift(attended, "seq", step) for step in (1, 2, -1)]
+        second, below = lax.optimization_barrier((second, below))
+        terms = output_half(output_same_kernel, jnp.float32, w_out, attended, second)
+        terms = output_half(output_other_kernel, jnp.bfloat16, w_out, above, below, terms)
     else:
         (blocks,) = pick(kept_blocks, source_cache, direct)
         (parts,) = project(blocks, *weights, pair_count, direct)
@@ -498,8 +492,8 @@
         terms = output(all_to_all(attended, "seq"), w_out, heads_local)
     if is_direct(head_count):
         terms = terms.astype(jnp.bfloat16)
+        terms, kept_cache = lax.optimization_barrier((terms, kept_cache))
         others = [swap(terms, "head", k) for k in range(1, head_count)]
-        others[2], kept_cache = lax.optimization_barrier((others[2], kept_cache))
         own, core, along, across = [t.astype(jnp.float32) for t in [terms] + others]
         summed = (own + core) + (along + across)
     else:

time: 41.1 us -> 34.1 us (0.83)
  starting transfers between devices: 27 us -> 20 us
    ppermute x5 -> x3, starting transfers between devices: 11.6 us -> 4.86 us  [shift(): lax.ppermute(outgoing, axis, [(i, (i + step) % count) for i in range(coun...]
    ppermute x9, waiting for transfers between devices: 4.23 us -> 5.04 us  [swap(): return lax.ppermute(outgoing, axis, [(i, i ^ offset) for i in range(count)])]
    ppermute x5 -> x3, waiting for transfers between devices: 0.64 us -> 0.01 us  [shift(): lax.ppermute(outgoing, axis, [(i, (i + step) % count) for i in range(coun...]
  transfers between devices with their start and end apart: 14 -> 12, of which waited for: 3 -> 3; matrix products, arithmetic and copies ran while one was open for 0% -> 0% of each run, Pallas kernels for 10% -> 12%
where the time goes in v15:
time: 34.1 us; the launch traced here: 34 us
  starting transfers between devices  20 us (59%)
  Pallas kernels  7.32 us (21%)
  waiting for transfers between devices  5.05 us (15%)
  between operations  0.82 us (2%)
  other arithmetic  0.65 us (2%)
    ppermute x9, starting transfers between devices, swap(): return lax.ppermute(outgoing, axis, [(i, i ^ offset) for i in range(count)])  15.2 us
    ppermute x9, waiting for transfers between devices, swap(): return lax.ppermute(outgoing, axis, [(i, i ^ offset) for i in range(count)])  5.04 us
    ppermute x3, starting transfers between devices, shift(): lax.ppermute(outgoing, axis, [(i, (i + step) % count) for i in range(coun...  4.86 us
    pallas_call x1, Pallas kernels, project(): pl.pallas_call(functools.partial(project_kernel, direct), out_shape=shape...  2.12 us
    pallas_call x1, Pallas kernels, pick(): pl.pallas_call(pick_near_kernel if direct else pick_all_kernel, out_shape...  1.43 us
    pallas_call x2, Pallas kernels, output_half(): pl.pallas_call(kernel, out_shape=jax.ShapeDtypeStruct((rows, w_out.shape[...  1.32 us
    pallas_call x1, Pallas kernels, place(): pl.pallas_call(functools.partial(place_kernel, source_blocks, heads_local...  1.32 us
    pallas_call x1, Pallas kernels, attend(): pl.pallas_call(functools.partial(attend_kernel, direct, source_blocks, he...  1.12 us
  transfers between devices with their start and end apart: 12, of which 3 were waited for; matrix products, arithmetic and copies ran while one was open for 0% of the time, Pallas kernels for 12%

profile of v15, /device:TPU:0, one launch (start us, length us, event | category | flops | bytes accessed | tf_op | source)
XLA Modules:
  0.0 34.0 jit_solution(15762317175890172936)
XLA Ops:
  0.7 1.4 %pick_blocks.1 = (bf16[256,256]{1,0:T(8,128)(2,1)S(1)}, bf16[256,256]{1,0:T(8,128)(2,1)S(1)}, bf16[256,256]{1,0:T(8,128)(2,1)S(1)}, bf16[256,256]{1,0:T(8,128)(2,1)S(1)}) custom-call(s32[2,4,8]{2,1,0:T(4,128)} %bitcast.5, bf16[2,2,512,256]{3,2,1,0:T(8,128)(2,1)} %cache_ref.1), custom_call_target="tpu_custom_call" | custom-call | flops 10000000000 | tf_op jit(solution)/shard_map/pick_blocks/pallas_call | solution.py:124
  2.1 0.0 copy-start.4
  2.1 0.0 copy-start.5
  2.1 0.0 copy-start.6
  2.1 5.1 %collective-permute-start = (bf16[256,256]{1,0:T(8,128)(2,1)S(1)}, bf16[256,256]{1,0:T(8,128)(2,1)S(1)}, u32[]{:S(2)}, u32[]{:S(2)}) collective-permute-start(bf16[256,256]{1,0:T(8,128)(2,1)S(1)} %get-tuple-element.18), channel_id=1, source_target_pairs={{0,12},{4,8},{8,4},{12,0},{1,13},{5,9},{9,5},{13,1},{2,14},{6,10},... | collective-permute-start | bytes 393224 | tf_op jit(solution)/shard_map/ppermute | solution.py:43
  7.3 0.6 %collective-permute-start.2 = (bf16[256,256]{1,0:T(8,128)(2,1)S(1)}, bf16[256,256]{1,0:T(8,128)(2,1)S(1)}, u32[]{:S(2)}, u32[]{:S(2)}) collective-permute-start(bf16[256,256]{1,0:T(8,128)(2,1)S(1)} %get-tuple-element.21), channel_id=1, source_target_pairs={{0,4},{4,0},{8,12},{12,8},{1,5},{5,1},{9,13},{13,9},{2,6},{6,2},{1... | collective-permute-start | bytes 393224 | tf_op jit(solution)/shard_map/ppermute | solution.py:43
  7.9 2.1 %project.1 = (f32[48,128]{1,0:T(8,128)S(1)}, f32[48,128]{1,0:T(8,128)S(1)}, f32[48,128]{1,0:T(8,128)S(1)}, f32[48,128]{1,0:T(8,128)S(1)}) custom-call(bf16[256,256]{1,0:T(8,128)(2,1)S(1)} %get-tuple-element.16.after_ref.refs_3_.refs_0_, bf16[2,4,2048]{2,1,0:T(4,128)(2,1)S(1)} %copy-done.2, bf16[16,128]{1,0:T(8,128)(2,1)S(1)} %bitcast.4, ...), custom_call_target="tpu_custom_call" | custom-call | flops 83886080 | bytes 10485760 | tf_op jit(solution)/shard_map/project/pallas_call | solution.py:215
  10.0 3.8 %collective-permute-start.3 = (f32[48,128]{1,0:T(8,128)S(1)}, f32[48,128]{1,0:T(8,128)S(1)}, u32[]{:S(2)}, u32[]{:S(2)}) collective-permute-start(f32[48,128]{1,0:T(8,128)S(1)} %get-tuple-element.22), channel_id=1, source_target_pairs={{0,12},{4,8},{8,4},{12,0},{1,13},{5,9},{9,5},{13,1},{2,14},{6,10},... | collective-permute-start | bytes 73736 | tf_op jit(solution)/shard_map/ppermute | solution.py:43
  13.9 0.0 collective-permute-start.4
  13.9 3.7 %collective-permute-start.5 = (f32[48,128]{1,0:T(8,128)S(1)}, f32[48,128]{1,0:T(8,128)S(1)}, u32[]{:S(2)}, u32[]{:S(2)}) collective-permute-start(f32[48,128]{1,0:T(8,128)S(1)} %get-tuple-element.24), channel_id=1, source_target_pairs={{0,4},{4,0},{8,12},{12,8},{1,5},{5,1},{9,13},{13,9},{2,6},{6,2},{1... | collective-permute-start | bytes 73736 | tf_op jit(solution)/shard_map/ppermute | solution.py:43
  17.6 2.8 %collective-permute-done.4.refs_5_ = f32[48,128]{1,0:T(8,128)S(1)} collective-permute-done((f32[48,128]{1,0:T(8,128)S(1)}, f32[48,128]{1,0:T(8,128)S(1)}, u32[]{:S(2)}, u32[]{:S(2)}) %collective-permute-start.4) | collective-permute-done | bytes 24608 | tf_op jit(solution)/shard_map/ppermute | solution.py:43
  20.5 0.0 slice-start
  20.5 1.1 %attend.1.own_ref.after_ref = bf16[32,128]{1,0:T(8,128)(2,1)S(1)} custom-call(s32[2,4,8]{2,1,0:T(4,128)S(1)} %bitcast.6, f32[8,128]{1,0:T(8,128)S(1)} %copy-done.6, f32[8,128]{1,0:T(8,128)S(1)} %copy-done.5, bf16[256,256]{1,0:T(8,128)(2,1)S(1)} %collective-permute-done.refs_0_.refs_3_, bf16[256,256]{1,0:T(8,128)(2,1)S(1)} %collective-permute-done.1.refs_1_.refs_2_, ...), custom_call_target="tpu_custom_call" | custom-call | flops 10000000000 | tf_op jit(solution)/shard_map/attend/pallas_call | solution.py:366
  21.6 1.0 %collective-permute-start.8 = (bf16[32,128]{1,0:T(8,128)(2,1)S(1)}, bf16[32,128]{1,0:T(8,128)(2,1)S(1)}, u32[]{:S(2)}, u32[]{:S(2)}) collective-permute-start(bf16[32,128]{1,0:T(8,128)(2,1)S(1)} %attend.1.own_ref.after_ref), channel_id=1, source_target_pairs={{0,4},{4,8},{8,12},{12,0},{1,5},{5,9},{9,13},{13,1},{2,6},{6,10},{... | collective-permute-start | bytes 24584 | tf_op jit(solution)/shard_map/ppermute | solution.py:48
  22.6 2.1 %collective-permute-start.7 = (bf16[32,128]{1,0:T(8,128)(2,1)S(1)}, bf16[32,128]{1,0:T(8,128)(2,1)S(1)}, u32[]{:S(2)}, u32[]{:S(2)}) collective-permute-start(bf16[32,128]{1,0:T(8,128)(2,1)S(1)} %attend.1.own_ref.after_ref), channel_id=1, source_target_pairs={{0,8},{4,12},{8,0},{12,4},{1,9},{5,13},{9,1},{13,5},{2,10},{6,14},... | collective-permute-start | bytes 24584 | tf_op jit(solution)/shard_map/ppermute | solution.py:48
  24.7 1.8 %collective-permute-start.6 = (bf16[32,128]{1,0:T(8,128)(2,1)S(1)}, bf16[32,128]{1,0:T(8,128)(2,1)S(1)}, u32[]{:S(2)}, u32[]{:S(2)}) collective-permute-start(bf16[32,128]{1,0:T(8,128)(2,1)S(1)} %attend.1.own_ref.after_ref), channel_id=1, source_target_pairs={{0,12},{4,0},{8,4},{12,8},{1,13},{5,1},{9,5},{13,9},{2,14},{6,2},{... | collective-permute-start | bytes 24584 | tf_op jit(solution)/shard_map/ppermute | solution.py:48
  26.5 1.3 %place.1 = bf16[1,1,512,256]{3,2,1,0:T(8,128)(2,1)} custom-call(s32[2,4,8]{2,1,0:T(4,128)S(1)} %bitcast.7, bf16[32,128]{1,0:T(8,128)(2,1)S(1)} %attend.1.own_ref.after_ref, bf16[256,256]{1,0:T(8,128)(2,1)S(1)} %get-tuple-element.16.after_ref.refs_3_.refs_0_, bf16[256,256]{1,0:T(8,128)(2,1)S(1)} %collective-permute-done.2.refs_2_.refs_1_, ...), custom_call_target="tpu_custom_call" | custom-call | flops 1000000000 | tf_op jit(solution)/shard_map/place/pallas_call | solution.py:259
  27.9 0.7 %output_half.2.addend_ref = f32[8,2048]{1,0:T(8,128)S(1)} custom-call(bf16[2048,2048]{1,0:T(8,128)(2,1)S(1)} %bitcast.3, bf16[32,128]{1,0:T(8,128)(2,1)S(1)} %attend.1.own_ref.after_ref, bf16[32,128]{1,0:T(8,128)(2,1)S(1)} %collective-permute-done.7.second_ref), custom_call_target="tpu_custom_call" | custom-call | flops 1000000000 | tf_op jit(solution)/shard_map/output_half/pallas_call | solution.py:418
  28.5 0.7 %output_half.3 = bf16[8,2048]{1,0:T(8,128)(2,1)S(1)} custom-call(bf16[2048,2048]{1,0:T(8,128)(2,1)S(1)} %bitcast.3, bf16[32,128]{1,0:T(8,128)(2,1)S(1)} %collective-permute-done.6.above_ref, bf16[32,128]{1,0:T(8,128)(2,1)S(1)} %collective-permute-done.8.below_ref, f32[8,2048]{1,0:T(8,128)S(1)} %output_half.2.addend_ref), custom_call_target="tpu_custom_call" | custom-call | flops 1000000000 | tf_op jit(solution)/shard_map/output_half/pallas_call | solution.py:418
  29.2 1.5 %collective-permute-start.10 = (bf16[8,2048]{1,0:T(8,128)(2,1)S(1)}, bf16[8,2048]{1,0:T(8,128)(2,1)S(1)}, u32[]{:S(2)}, u32[]{:S(2)}) collective-permute-start(bf16[8,2048]{1,0:T(8,128)(2,1)S(1)} %output_half.3), channel_id=1, source_target_pairs={{0,2},{1,3},{2,0},{3,1},{4,6},{5,7},{6,4},{7,5},{8,10},{9,11},{10,... | collective-permute-start | bytes 98312 | tf_op jit(solution)/shard_map/ppermute | solution.py:43
  30.8 0.3 collective-permute-start.9
  31.1 1.8 %collective-permute-done.11 = bf16[8,2048]{1,0:T(8,128)(2,1)S(1)} collective-permute-done((bf16[8,2048]{1,0:T(8,128)(2,1)S(1)}, bf16[8,2048]{1,0:T(8,128)(2,1)S(1)}, u32[]{:S(2)}, u32[]{:S(2)}) %collective-permute-start.11) | collective-permute-done | bytes 32800 | tf_op jit(solution)/shard_map/ppermute | solution.py:43
  32.9 0.4 %collective-permute-done.10 = bf16[8,2048]{1,0:T(8,128)(2,1)S(1)} collective-permute-done((bf16[8,2048]{1,0:T(8,128)(2,1)S(1)}, bf16[8,2048]{1,0:T(8,128)(2,1)S(1)}, u32[]{:S(2)}, u32[]{:S(2)}) %collective-permute-start.10) | collective-permute-done | bytes 32800 | tf_op jit(solution)/shard_map/ppermute | solution.py:43
  33.3 0.6 %add_convert_fusion = bf16[2,4,2048]{2,1,0:T(4,128)(2,1)} fusion(f32[2,4,2048]{2,1,0:T(4,128)S(1)} %reshape.11, bf16[2,4,2048]{2,1,0:T(4,128)(2,1)S(1)} %copy-done.2), kind=kLoop, calls=%fused_computation | loop fusion | flops 49152 | bytes 131072 | tf_op jit(solution)/shard_map/convert_element_type | solution.py:502
  (28 shorter events, 0.1 us)
Async XLA Ops:
  0.6 7.3 %copy-start = (bf16[2048,2048]{1,0:T(8,128)(2,1)S(1)}, bf16[2048,2048]{1,0:T(8,128)(2,1)}, u32[]{:S(2)}) copy-start(bf16[2048,2048]{1,0:T(8,128)(2,1)} %wq_ref.1) | copy-start | bytes 25165828
  0.6 7.3 %copy-start.1 = (bf16[2048,2,256]{2,1,0:T(2,128)(2,1)S(1)}, bf16[2048,2,256]{2,1,0:T(2,128)(2,1)}, u32[]{:S(2)}) copy-start(bf16[2048,2,256]{2,1,0:T(2,128)(2,1)} %wkv_ref.1) | copy-start | bytes 6291460
  0.7 7.3 %copy-start.2 = (bf16[2,4,2048]{2,1,0:T(4,128)(2,1)S(1)}, bf16[2,4,2048]{2,1,0:T(4,128)(2,1)}, u32[]{:S(2)}) copy-start(bf16[2,4,2048]{2,1,0:T(4,128)(2,1)} %hidden_ref.1) | copy-start | bytes 98308
  0.7 7.3 %copy-start.3 = (bf16[2048]{0:T(1024)(128)(2,1)S(1)}, bf16[2048]{0:T(1024)(128)(2,1)}, u32[]{:S(2)}) copy-start(bf16[2048]{0:T(1024)(128)(2,1)} %param.12) | copy-start | bytes 12292
  2.1 18.4 %copy-start.4 = (s32[2,8,4]{1,2,0:T(4,128)S(1)}, s32[2,8,4]{1,2,0:T(4,128)}, u32[]{:S(2)}) copy-start(s32[2,8,4]{1,2,0:T(4,128)} %param.10) | copy-start | bytes 772
  2.1 18.4 %copy-start.5 = (f32[8,128]{1,0:T(8,128)S(1)}, f32[8,128]{1,0:T(8,128)}, u32[]{:S(2)}) copy-start(f32[8,128]{1,0:T(8,128)} %constant.5.clone.sin_ref) | copy-start | bytes 12292
  2.1 18.4 %copy-start.6 = (f32[8,128]{1,0:T(8,128)S(1)}, f32[8,128]{1,0:T(8,128)}, u32[]{:S(2)}) copy-start(f32[8,128]{1,0:T(8,128)} %constant.4.clone.cos_ref) | copy-start | bytes 12292
  2.1 11.7 %collective-permute-start = (bf16[256,256]{1,0:T(8,128)(2,1)S(1)}, bf16[256,256]{1,0:T(8,128)(2,1)S(1)}, u32[]{:S(2)}, u32[]{:S(2)}) collective-permute-start(bf16[256,256]{1,0:T(8,128)(2,1)S(1)} %get-tuple-element.18), channel_id=1, source_target_pairs={{0,12},{4,8},{8,4},{12,0},{1,13},{5,9},{9,5},{13,1},{2,14},{6,10},... | collective-permute-start | bytes 393224 | tf_op jit(solution)/shard_map/ppermute | solution.py:43
  7.3 13.2 %collective-permute-start.1 = (bf16[256,256]{1,0:T(8,128)(2,1)S(1)}, bf16[256,256]{1,0:T(8,128)(2,1)S(1)}, u32[]{:S(2)}, u32[]{:S(2)}) collective-permute-start(bf16[256,256]{1,0:T(8,128)(2,1)S(1)} %get-tuple-element.20), channel_id=1, source_target_pairs={{0,8},{4,12},{8,0},{12,4},{1,9},{5,13},{9,1},{13,5},{2,10},{6,14},... | collective-permute-start | bytes 393224 | tf_op jit(solution)/shard_map/ppermute | solution.py:43
  7.3 13.2 %collective-permute-start.2 = (bf16[256,256]{1,0:T(8,128)(2,1)S(1)}, bf16[256,256]{1,0:T(8,128)(2,1)S(1)}, u32[]{:S(2)}, u32[]{:S(2)}) collective-permute-start(bf16[256,256]{1,0:T(8,128)(2,1)S(1)} %get-tuple-element.21), channel_id=1, source_target_pairs={{0,4},{4,0},{8,12},{12,8},{1,5},{5,1},{9,13},{13,9},{2,6},{6,2},{1... | collective-permute-start | bytes 393224 | tf_op jit(solution)/shard_map/ppermute | solution.py:43
  10.0 7.5 %collective-permute-start.3 = (f32[48,128]{1,0:T(8,128)S(1)}, f32[48,128]{1,0:T(8,128)S(1)}, u32[]{:S(2)}, u32[]{:S(2)}) collective-permute-start(f32[48,128]{1,0:T(8,128)S(1)} %get-tuple-element.22), channel_id=1, source_target_pairs={{0,12},{4,8},{8,4},{12,0},{1,13},{5,9},{9,5},{13,1},{2,14},{6,10},... | collective-permute-start | bytes 73736 | tf_op jit(solution)/shard_map/ppermute | solution.py:43
  13.9 6.6 %collective-permute-start.4 = (f32[48,128]{1,0:T(8,128)S(1)}, f32[48,128]{1,0:T(8,128)S(1)}, u32[]{:S(2)}, u32[]{:S(2)}) collective-permute-start(f32[48,128]{1,0:T(8,128)S(1)} %get-tuple-element.23), channel_id=1, source_target_pairs={{0,8},{4,12},{8,0},{12,4},{1,9},{5,13},{9,1},{13,5},{2,10},{6,14},... | collective-permute-start | bytes 73736 | tf_op jit(solution)/shard_map/ppermute | solution.py:43
  13.9 6.6 %collective-permute-start.5 = (f32[48,128]{1,0:T(8,128)S(1)}, f32[48,128]{1,0:T(8,128)S(1)}, u32[]{:S(2)}, u32[]{:S(2)}) collective-permute-start(f32[48,128]{1,0:T(8,128)S(1)} %get-tuple-element.24), channel_id=1, source_target_pairs={{0,4},{4,0},{8,12},{12,8},{1,5},{5,1},{9,13},{13,9},{2,6},{6,2},{1... | collective-permute-start | bytes 73736 | tf_op jit(solution)/shard_map/ppermute | solution.py:43
  20.5 7.4 %slice-start = ((s8[8388608]{0:T(1024)(128)(4,1)}), s8[4194304]{0:T(1024)(128)(4,1)S(1)}, s32[]{:S(2)}) async-start(s8[8388608]{0:T(1024)(128)(4,1)} %bitcast.2), calls=%async_computation | async-start | bytes 8388608
  20.5 7.4 %slice-start.1 = ((s8[8388608]{0:T(1024)(128)(4,1)}), s8[4194304]{0:T(1024)(128)(4,1)S(1)}, s32[]{:S(2)}) async-start(s8[8388608]{0:T(1024)(128)(4,1)} %bitcast.2), calls=%async_computation.1 | async-start | bytes 8388608
  21.6 6.2 %collective-permute-start.8 = (bf16[32,128]{1,0:T(8,128)(2,1)S(1)}, bf16[32,128]{1,0:T(8,128)(2,1)S(1)}, u32[]{:S(2)}, u32[]{:S(2)}) collective-permute-start(bf16[32,128]{1,0:T(8,128)(2,1)S(1)} %attend.1.own_ref.after_ref), channel_id=1, source_target_pairs={{0,4},{4,8},{8,12},{12,0},{1,5},{5,9},{9,13},{13,1},{2,6},{6,10},{... | collective-permute-start | bytes 24584 | tf_op jit(solution)/shard_map/ppermute | solution.py:48
  22.6 5.2 %collective-permute-start.7 = (bf16[32,128]{1,0:T(8,128)(2,1)S(1)}, bf16[32,128]{1,0:T(8,128)(2,1)S(1)}, u32[]{:S(2)}, u32[]{:S(2)}) collective-permute-start(bf16[32,128]{1,0:T(8,128)(2,1)S(1)} %attend.1.own_ref.after_ref), channel_id=1, source_target_pairs={{0,8},{4,12},{8,0},{12,4},{1,9},{5,13},{9,1},{13,5},{2,10},{6,14},... | collective-permute-start | bytes 24584 | tf_op jit(solution)/shard_map/ppermute | solution.py:48
  24.7 3.8 %collective-permute-start.6 = (bf16[32,128]{1,0:T(8,128)(2,1)S(1)}, bf16[32,128]{1,0:T(8,128)(2,1)S(1)}, u32[]{:S(2)}, u32[]{:S(2)}) collective-permute-start(bf16[32,128]{1,0:T(8,128)(2,1)S(1)} %attend.1.own_ref.after_ref), channel_id=1, source_target_pairs={{0,12},{4,0},{8,4},{12,8},{1,13},{5,1},{9,5},{13,9},{2,14},{6,2},{... | collective-permute-start | bytes 24584 | tf_op jit(solution)/shard_map/ppermute | solution.py:48
  29.2 3.7 %collective-permute-start.11 = (bf16[8,2048]{1,0:T(8,128)(2,1)S(1)}, bf16[8,2048]{1,0:T(8,128)(2,1)S(1)}, u32[]{:S(2)}, u32[]{:S(2)}) collective-permute-start(bf16[8,2048]{1,0:T(8,128)(2,1)S(1)} %output_half.3), channel_id=1, source_target_pairs={{0,3},{1,2},{2,1},{3,0},{4,7},{5,6},{6,5},{7,4},{8,11},{9,10},{10,... | collective-permute-start | bytes 98312 | tf_op jit(solution)/shard_map/ppermute | solution.py:43
  29.2 4.1 %collective-permute-start.10 = (bf16[8,2048]{1,0:T(8,128)(2,1)S(1)}, bf16[8,2048]{1,0:T(8,128)(2,1)S(1)}, u32[]{:S(2)}, u32[]{:S(2)}) collective-permute-start(bf16[8,2048]{1,0:T(8,128)(2,1)S(1)} %output_half.3), channel_id=1, source_target_pairs={{0,2},{1,3},{2,0},{3,1},{4,6},{5,7},{6,4},{7,5},{8,10},{9,11},{10,... | collective-permute-start | bytes 98312 | tf_op jit(solution)/shard_map/ppermute | solution.py:43
  30.8 2.5 %collective-permute-start.9 = (bf16[8,2048]{1,0:T(8,128)(2,1)S(1)}, bf16[8,2048]{1,0:T(8,128)(2,1)S(1)}, u32[]{:S(2)}, u32[]{:S(2)}) collective-permute-start(bf16[8,2048]{1,0:T(8,128)(2,1)S(1)} %output_half.3), channel_id=1, source_target_pairs={{0,1},{1,0},{2,3},{3,2},{4,5},{5,4},{6,7},{7,6},{8,9},{9,8},{10,11... | collective-permute-start | bytes 98312 | tf_op jit(solution)/shard_map/ppermute | solution.py:43

commit v16 on v15

--- a/solution.py
+++ b/solution.py
@@ -492,8 +492,8 @@
         terms = output(all_to_all(attended, "seq"), w_out, heads_local)
     if is_direct(head_count):
         terms = terms.astype(jnp.bfloat16)
-        terms, kept_cache = lax.optimization_barrier((terms, kept_cache))
         others = [swap(terms, "head", k) for k in range(1, head_count)]
+        others[0], others[1], others[2], kept_cache = lax.optimization_barrier((others[0], others[1], others[2], kept_cache))
         own, core, along, across = [t.astype(jnp.float32) for t in [terms] + others]
         summed = (own + core) + (along + across)
     else:

time: 34.1 us -> 33.9 us (level)
    ppermute x9, waiting for transfers between devices: 5.04 us -> 3.71 us  [swap(): return lax.ppermute(outgoing, axis, [(i, i ^ offset) for i in range(count)])]
    ppermute x3, waiting for transfers between devices: 0.01 us -> 1.21 us  [shift(): lax.ppermute(outgoing, axis, [(i, (i + step) % count) for i in range(coun...]
  transfers between devices with their start and end apart: 12 -> 12, of which waited for: 3 -> 6; matrix products, arithmetic and copies ran while one was open for 0% -> 0% of each run, Pallas kernels for 12% -> 12%
where the time goes in v16:
time: 33.9 us; the launch traced here: 33.8 us
  starting transfers between devices  20 us (59%)
  Pallas kernels  7.32 us (22%)
  waiting for transfers between devices  4.92 us (15%)
  between operations  0.79 us (2%)
  other arithmetic  0.65 us (2%)
    ppermute x9, starting transfers between devices, swap(): return lax.ppermute(outgoing, axis, [(i, i ^ offset) for i in range(count)])  15.1 us
    ppermute x3, starting transfers between devices, shift(): lax.ppermute(outgoing, axis, [(i, (i + step) % count) for i in range(coun...  4.87 us
    ppermute x9, waiting for transfers between devices, swap(): return lax.ppermute(outgoing, axis, [(i, i ^ offset) for i in range(count)])  3.71 us
    pallas_call x1, Pallas kernels, project(): pl.pallas_call(functools.partial(project_kernel, direct), out_shape=shape...  2.13 us
    pallas_call x1, Pallas kernels, pick(): pl.pallas_call(pick_near_kernel if direct else pick_all_kernel, out_shape...  1.43 us
    pallas_call x1, Pallas kernels, place(): pl.pallas_call(functools.partial(place_kernel, source_blocks, heads_local...  1.33 us
    pallas_call x2, Pallas kernels, output_half(): pl.pallas_call(kernel, out_shape=jax.ShapeDtypeStruct((rows, w_out.shape[...  1.3 us
    ppermute x3, waiting for transfers between devices, shift(): lax.ppermute(outgoing, axis, [(i, (i + step) % count) for i in range(coun...  1.21 us
  transfers between devices with their start and end apart: 12, of which 6 were waited for; matrix products, arithmetic and copies ran while one was open for 0% of the time, Pallas kernels for 12%

profile of v16, /device:TPU:0, one launch (start us, length us, event | category | flops | bytes accessed | tf_op | source)
XLA Modules:
  0.0 33.8 jit_solution(1461987123985840042)
XLA Ops:
  0.7 1.4 %pick_blocks.1 = (bf16[256,256]{1,0:T(8,128)(2,1)S(1)}, bf16[256,256]{1,0:T(8,128)(2,1)S(1)}, bf16[256,256]{1,0:T(8,128)(2,1)S(1)}, bf16[256,256]{1,0:T(8,128)(2,1)S(1)}) custom-call(s32[2,4,8]{2,1,0:T(4,128)} %bitcast.5, bf16[2,2,512,256]{3,2,1,0:T(8,128)(2,1)} %cache_ref.1), custom_call_target="tpu_custom_call" | custom-call | flops 10000000000 | tf_op jit(solution)/shard_map/pick_blocks/pallas_call | solution.py:124
  2.1 5.1 %collective-permute-start = (bf16[256,256]{1,0:T(8,128)(2,1)S(1)}, bf16[256,256]{1,0:T(8,128)(2,1)S(1)}, u32[]{:S(2)}, u32[]{:S(2)}) collective-permute-start(bf16[256,256]{1,0:T(8,128)(2,1)S(1)} %get-tuple-element.20), channel_id=1, source_target_pairs={{0,12},{4,8},{8,4},{12,0},{1,13},{5,9},{9,5},{13,1},{2,14},{6,10},... | collective-permute-start | bytes 393224 | tf_op jit(solution)/shard_map/ppermute | solution.py:43
  7.3 0.6 %collective-permute-start.2 = (bf16[256,256]{1,0:T(8,128)(2,1)S(1)}, bf16[256,256]{1,0:T(8,128)(2,1)S(1)}, u32[]{:S(2)}, u32[]{:S(2)}) collective-permute-start(bf16[256,256]{1,0:T(8,128)(2,1)S(1)} %get-tuple-element.23), channel_id=1, source_target_pairs={{0,4},{4,0},{8,12},{12,8},{1,5},{5,1},{9,13},{13,9},{2,6},{6,2},{1... | collective-permute-start | bytes 393224 | tf_op jit(solution)/shard_map/ppermute | solution.py:43
  7.9 0.0 slice-start
  7.9 2.1 %project.1 = (f32[48,128]{1,0:T(8,128)S(1)}, f32[48,128]{1,0:T(8,128)S(1)}, f32[48,128]{1,0:T(8,128)S(1)}, f32[48,128]{1,0:T(8,128)S(1)}) custom-call(bf16[256,256]{1,0:T(8,128)(2,1)S(1)} %get-tuple-element.18.after_ref.refs_3_.refs_0_, bf16[2,4,2048]{2,1,0:T(4,128)(2,1)S(1)} %copy-done.2, bf16[16,128]{1,0:T(8,128)(2,1)S(1)} %bitcast.4, ...), custom_call_target="tpu_custom_call" | custom-call | flops 83886080 | bytes 10485760 | tf_op jit(solution)/shard_map/project/pallas_call | solution.py:215
  10.1 3.8 %collective-permute-start.3 = (f32[48,128]{1,0:T(8,128)S(1)}, f32[48,128]{1,0:T(8,128)S(1)}, u32[]{:S(2)}, u32[]{:S(2)}) collective-permute-start(f32[48,128]{1,0:T(8,128)S(1)} %get-tuple-element.24), channel_id=1, source_target_pairs={{0,12},{4,8},{8,4},{12,0},{1,13},{5,9},{9,5},{13,1},{2,14},{6,10},... | collective-permute-start | bytes 73736 | tf_op jit(solution)/shard_map/ppermute | solution.py:43
  13.9 3.7 %collective-permute-start.5 = (f32[48,128]{1,0:T(8,128)S(1)}, f32[48,128]{1,0:T(8,128)S(1)}, u32[]{:S(2)}, u32[]{:S(2)}) collective-permute-start(f32[48,128]{1,0:T(8,128)S(1)} %get-tuple-element.26), channel_id=1, source_target_pairs={{0,4},{4,0},{8,12},{12,8},{1,5},{5,1},{9,13},{13,9},{2,6},{6,2},{1... | collective-permute-start | bytes 73736 | tf_op jit(solution)/shard_map/ppermute | solution.py:43
  17.6 2.8 %collective-permute-done.4.refs_5_ = f32[48,128]{1,0:T(8,128)S(1)} collective-permute-done((f32[48,128]{1,0:T(8,128)S(1)}, f32[48,128]{1,0:T(8,128)S(1)}, u32[]{:S(2)}, u32[]{:S(2)}) %collective-permute-start.4) | collective-permute-done | bytes 24608 | tf_op jit(solution)/shard_map/ppermute | solution.py:43
  20.5 0.0 slice-start.1
  20.5 1.1 %attend.1.own_ref.after_ref = bf16[32,128]{1,0:T(8,128)(2,1)S(1)} custom-call(s32[2,4,8]{2,1,0:T(4,128)S(1)} %bitcast.6, f32[8,128]{1,0:T(8,128)S(1)} %copy-done.6, f32[8,128]{1,0:T(8,128)S(1)} %copy-done.5, bf16[256,256]{1,0:T(8,128)(2,1)S(1)} %collective-permute-done.refs_0_.refs_3_, bf16[256,256]{1,0:T(8,128)(2,1)S(1)} %collective-permute-done.1.refs_1_.refs_2_, ...), custom_call_target="tpu_custom_call" | custom-call | flops 10000000000 | tf_op jit(solution)/shard_map/attend/pallas_call | solution.py:366
  21.6 1.0 %collective-permute-start.8 = (bf16[32,128]{1,0:T(8,128)(2,1)S(1)}, bf16[32,128]{1,0:T(8,128)(2,1)S(1)}, u32[]{:S(2)}, u32[]{:S(2)}) collective-permute-start(bf16[32,128]{1,0:T(8,128)(2,1)S(1)} %attend.1.own_ref.after_ref), channel_id=1, source_target_pairs={{0,4},{4,8},{8,12},{12,0},{1,5},{5,9},{9,13},{13,1},{2,6},{6,10},{... | collective-permute-start | bytes 24584 | tf_op jit(solution)/shard_map/ppermute | solution.py:48
  22.6 2.1 %collective-permute-start.7 = (bf16[32,128]{1,0:T(8,128)(2,1)S(1)}, bf16[32,128]{1,0:T(8,128)(2,1)S(1)}, u32[]{:S(2)}, u32[]{:S(2)}) collective-permute-start(bf16[32,128]{1,0:T(8,128)(2,1)S(1)} %attend.1.own_ref.after_ref), channel_id=1, source_target_pairs={{0,8},{4,12},{8,0},{12,4},{1,9},{5,13},{9,1},{13,5},{2,10},{6,14},... | collective-permute-start | bytes 24584 | tf_op jit(solution)/shard_map/ppermute | solution.py:48
  24.7 1.8 %collective-permute-start.6 = (bf16[32,128]{1,0:T(8,128)(2,1)S(1)}, bf16[32,128]{1,0:T(8,128)(2,1)S(1)}, u32[]{:S(2)}, u32[]{:S(2)}) collective-permute-start(bf16[32,128]{1,0:T(8,128)(2,1)S(1)} %attend.1.own_ref.after_ref), channel_id=1, source_target_pairs={{0,12},{4,0},{8,4},{12,8},{1,13},{5,1},{9,5},{13,9},{2,14},{6,2},{... | collective-permute-start | bytes 24584 | tf_op jit(solution)/shard_map/ppermute | solution.py:48
  26.5 0.6 %collective-permute-done.8.below_ref = bf16[32,128]{1,0:T(8,128)(2,1)S(1)} collective-permute-done((bf16[32,128]{1,0:T(8,128)(2,1)S(1)}, bf16[32,128]{1,0:T(8,128)(2,1)S(1)}, u32[]{:S(2)}, u32[]{:S(2)}) %collective-permute-start.8) | collective-permute-done | bytes 8224 | tf_op jit(solution)/shard_map/ppermute | solution.py:48
  27.1 0.1 collective-permute-done.7.second_ref
  27.2 0.7 %output_half.2.addend_ref = f32[8,2048]{1,0:T(8,128)S(1)} custom-call(bf16[2048,2048]{1,0:T(8,128)(2,1)S(1)} %bitcast.3, bf16[32,128]{1,0:T(8,128)(2,1)S(1)} %attend.1.own_ref.after_ref, bf16[32,128]{1,0:T(8,128)(2,1)S(1)} %collective-permute-done.7.second_ref), custom_call_target="tpu_custom_call" | custom-call | flops 1000000000 | tf_op jit(solution)/shard_map/output_half/pallas_call | solution.py:418
  27.9 0.5 %collective-permute-done.6.above_ref = bf16[32,128]{1,0:T(8,128)(2,1)S(1)} collective-permute-done((bf16[32,128]{1,0:T(8,128)(2,1)S(1)}, bf16[32,128]{1,0:T(8,128)(2,1)S(1)}, u32[]{:S(2)}, u32[]{:S(2)}) %collective-permute-start.6) | collective-permute-done | bytes 8224 | tf_op jit(solution)/shard_map/ppermute | solution.py:48
  28.4 0.7 %output_half.3 = bf16[8,2048]{1,0:T(8,128)(2,1)S(1)} custom-call(bf16[2048,2048]{1,0:T(8,128)(2,1)S(1)} %bitcast.3, bf16[32,128]{1,0:T(8,128)(2,1)S(1)} %collective-permute-done.6.above_ref, bf16[32,128]{1,0:T(8,128)(2,1)S(1)} %collective-permute-done.8.below_ref, f32[8,2048]{1,0:T(8,128)S(1)} %output_half.2.addend_ref), custom_call_target="tpu_custom_call" | custom-call | flops 1000000000 | tf_op jit(solution)/shard_map/output_half/pallas_call | solution.py:418
  29.0 1.5 %collective-permute-start.10 = (bf16[8,2048]{1,0:T(8,128)(2,1)S(1)}, bf16[8,2048]{1,0:T(8,128)(2,1)S(1)}, u32[]{:S(2)}, u32[]{:S(2)}) collective-permute-start(bf16[8,2048]{1,0:T(8,128)(2,1)S(1)} %output_half.3), channel_id=1, source_target_pairs={{0,2},{1,3},{2,0},{3,1},{4,6},{5,7},{6,4},{7,5},{8,10},{9,11},{10,... | collective-permute-start | bytes 98312 | tf_op jit(solution)/shard_map/ppermute | solution.py:43
  30.6 0.3 collective-permute-start.9
  30.9 1.3 %place.1 = bf16[1,1,512,256]{3,2,1,0:T(8,128)(2,1)} custom-call(s32[2,4,8]{2,1,0:T(4,128)S(1)} %bitcast.7, bf16[32,128]{1,0:T(8,128)(2,1)S(1)} %attend.1.own_ref.after_ref, bf16[256,256]{1,0:T(8,128)(2,1)S(1)} %get-tuple-element.18.after_ref.refs_3_.refs_0_, bf16[256,256]{1,0:T(8,128)(2,1)S(1)} %collective-permute-done.2.refs_2_.refs_1_, ...), custom_call_target="tpu_custom_call" | custom-call | flops 1000000000 | tf_op jit(solution)/shard_map/place/pallas_call | solution.py:259
  32.2 0.5 %collective-permute-done.11 = bf16[8,2048]{1,0:T(8,128)(2,1)S(1)} collective-permute-done((bf16[8,2048]{1,0:T(8,128)(2,1)S(1)}, bf16[8,2048]{1,0:T(8,128)(2,1)S(1)}, u32[]{:S(2)}, u32[]{:S(2)}) %collective-permute-start.11) | collective-permute-done | bytes 32800 | tf_op jit(solution)/shard_map/ppermute | solution.py:43
  32.7 0.4 %collective-permute-done.10 = bf16[8,2048]{1,0:T(8,128)(2,1)S(1)} collective-permute-done((bf16[8,2048]{1,0:T(8,128)(2,1)S(1)}, bf16[8,2048]{1,0:T(8,128)(2,1)S(1)}, u32[]{:S(2)}, u32[]{:S(2)}) %collective-permute-start.10) | collective-permute-done | bytes 32800 | tf_op jit(solution)/shard_map/ppermute | solution.py:43
  33.1 0.6 %add_convert_fusion = bf16[2,4,2048]{2,1,0:T(4,128)(2,1)} fusion(f32[2,4,2048]{2,1,0:T(4,128)S(1)} %reshape.11, bf16[2,4,2048]{2,1,0:T(4,128)(2,1)S(1)} %copy-done.2), kind=kLoop, calls=%fused_computation | loop fusion | flops 49152 | bytes 131072 | tf_op jit(solution)/shard_map/convert_element_type | solution.py:502
  (28 shorter events, 0.1 us)
Async XLA Ops:
  0.6 7.3 %copy-start = (bf16[2048,2048]{1,0:T(8,128)(2,1)S(1)}, bf16[2048,2048]{1,0:T(8,128)(2,1)}, u32[]{:S(2)}) copy-start(bf16[2048,2048]{1,0:T(8,128)(2,1)} %wq_ref.1) | copy-start | bytes 25165828
  0.6 7.3 %copy-start.1 = (bf16[2048,2,256]{2,1,0:T(2,128)(2,1)S(1)}, bf16[2048,2,256]{2,1,0:T(2,128)(2,1)}, u32[]{:S(2)}) copy-start(bf16[2048,2,256]{2,1,0:T(2,128)(2,1)} %wkv_ref.1) | copy-start | bytes 6291460
  0.7 7.3 %copy-start.2 = (bf16[2,4,2048]{2,1,0:T(4,128)(2,1)S(1)}, bf16[2,4,2048]{2,1,0:T(4,128)(2,1)}, u32[]{:S(2)}) copy-start(bf16[2,4,2048]{2,1,0:T(4,128)(2,1)} %hidden_ref.1) | copy-start | bytes 98308
  0.7 7.3 %copy-start.3 = (bf16[2048]{0:T(1024)(128)(2,1)S(1)}, bf16[2048]{0:T(1024)(128)(2,1)}, u32[]{:S(2)}) copy-start(bf16[2048]{0:T(1024)(128)(2,1)} %param.12) | copy-start | bytes 12292
  2.1 18.3 %copy-start.4 = (s32[2,8,4]{1,2,0:T(4,128)S(1)}, s32[2,8,4]{1,2,0:T(4,128)}, u32[]{:S(2)}) copy-start(s32[2,8,4]{1,2,0:T(4,128)} %param.10) | copy-start | bytes 772
  2.1 18.3 %copy-start.5 = (f32[8,128]{1,0:T(8,128)S(1)}, f32[8,128]{1,0:T(8,128)}, u32[]{:S(2)}) copy-start(f32[8,128]{1,0:T(8,128)} %constant.5.clone.sin_ref) | copy-start | bytes 12292
  2.1 18.3 %copy-start.6 = (f32[8,128]{1,0:T(8,128)S(1)}, f32[8,128]{1,0:T(8,128)}, u32[]{:S(2)}) copy-start(f32[8,128]{1,0:T(8,128)} %constant.4.clone.cos_ref) | copy-start | bytes 12292
  2.1 11.8 %collective-permute-start = (bf16[256,256]{1,0:T(8,128)(2,1)S(1)}, bf16[256,256]{1,0:T(8,128)(2,1)S(1)}, u32[]{:S(2)}, u32[]{:S(2)}) collective-permute-start(bf16[256,256]{1,0:T(8,128)(2,1)S(1)} %get-tuple-element.20), channel_id=1, source_target_pairs={{0,12},{4,8},{8,4},{12,0},{1,13},{5,9},{9,5},{13,1},{2,14},{6,10},... | collective-permute-start | bytes 393224 | tf_op jit(solution)/shard_map/ppermute | solution.py:43
  7.3 13.2 %collective-permute-start.1 = (bf16[256,256]{1,0:T(8,128)(2,1)S(1)}, bf16[256,256]{1,0:T(8,128)(2,1)S(1)}, u32[]{:S(2)}, u32[]{:S(2)}) collective-permute-start(bf16[256,256]{1,0:T(8,128)(2,1)S(1)} %get-tuple-element.22), channel_id=1, source_target_pairs={{0,8},{4,12},{8,0},{12,4},{1,9},{5,13},{9,1},{13,5},{2,10},{6,14},... | collective-permute-start | bytes 393224 | tf_op jit(solution)/shard_map/ppermute | solution.py:43
  7.3 13.2 %collective-permute-start.2 = (bf16[256,256]{1,0:T(8,128)(2,1)S(1)}, bf16[256,256]{1,0:T(8,128)(2,1)S(1)}, u32[]{:S(2)}, u32[]{:S(2)}) collective-permute-start(bf16[256,256]{1,0:T(8,128)(2,1)S(1)} %get-tuple-element.23), channel_id=1, source_target_pairs={{0,4},{4,0},{8,12},{12,8},{1,5},{5,1},{9,13},{13,9},{2,6},{6,2},{1... | collective-permute-start | bytes 393224 | tf_op jit(solution)/shard_map/ppermute | solution.py:43
  7.9 19.3 %slice-start = ((s8[8388608]{0:T(1024)(128)(4,1)}), s8[4194304]{0:T(1024)(128)(4,1)S(1)}, s32[]{:S(2)}) async-start(s8[8388608]{0:T(1024)(128)(4,1)} %bitcast.2), calls=%async_computation | async-start | bytes 8388608
  10.1 7.5 %collective-permute-start.3 = (f32[48,128]{1,0:T(8,128)S(1)}, f32[48,128]{1,0:T(8,128)S(1)}, u32[]{:S(2)}, u32[]{:S(2)}) collective-permute-start(f32[48,128]{1,0:T(8,128)S(1)} %get-tuple-element.24), channel_id=1, source_target_pairs={{0,12},{4,8},{8,4},{12,0},{1,13},{5,9},{9,5},{13,1},{2,14},{6,10},... | collective-permute-start | bytes 73736 | tf_op jit(solution)/shard_map/ppermute | solution.py:43
  13.9 6.5 %collective-permute-start.4 = (f32[48,128]{1,0:T(8,128)S(1)}, f32[48,128]{1,0:T(8,128)S(1)}, u32[]{:S(2)}, u32[]{:S(2)}) collective-permute-start(f32[48,128]{1,0:T(8,128)S(1)} %get-tuple-element.25), channel_id=1, source_target_pairs={{0,8},{4,12},{8,0},{12,4},{1,9},{5,13},{9,1},{13,5},{2,10},{6,14},... | collective-permute-start | bytes 73736 | tf_op jit(solution)/shard_map/ppermute | solution.py:43
  13.9 6.5 %collective-permute-start.5 = (f32[48,128]{1,0:T(8,128)S(1)}, f32[48,128]{1,0:T(8,128)S(1)}, u32[]{:S(2)}, u32[]{:S(2)}) collective-permute-start(f32[48,128]{1,0:T(8,128)S(1)} %get-tuple-element.26), channel_id=1, source_target_pairs={{0,4},{4,0},{8,12},{12,8},{1,5},{5,1},{9,13},{13,9},{2,6},{6,2},{1... | collective-permute-start | bytes 73736 | tf_op jit(solution)/shard_map/ppermute | solution.py:43
  20.5 6.7 %slice-start.1 = ((s8[8388608]{0:T(1024)(128)(4,1)}), s8[4194304]{0:T(1024)(128)(4,1)S(1)}, s32[]{:S(2)}) async-start(s8[8388608]{0:T(1024)(128)(4,1)} %bitcast.2), calls=%async_computation.1 | async-start | bytes 8388608
  21.6 5.5 %collective-permute-start.8 = (bf16[32,128]{1,0:T(8,128)(2,1)S(1)}, bf16[32,128]{1,0:T(8,128)(2,1)S(1)}, u32[]{:S(2)}, u32[]{:S(2)}) collective-permute-start(bf16[32,128]{1,0:T(8,128)(2,1)S(1)} %attend.1.own_ref.after_ref), channel_id=1, source_target_pairs={{0,4},{4,8},{8,12},{12,0},{1,5},{5,9},{9,13},{13,1},{2,6},{6,10},{... | collective-permute-start | bytes 24584 | tf_op jit(solution)/shard_map/ppermute | solution.py:48
  22.6 4.6 %collective-permute-start.7 = (bf16[32,128]{1,0:T(8,128)(2,1)S(1)}, bf16[32,128]{1,0:T(8,128)(2,1)S(1)}, u32[]{:S(2)}, u32[]{:S(2)}) collective-permute-start(bf16[32,128]{1,0:T(8,128)(2,1)S(1)} %attend.1.own_ref.after_ref), channel_id=1, source_target_pairs={{0,8},{4,12},{8,0},{12,4},{1,9},{5,13},{9,1},{13,5},{2,10},{6,14},... | collective-permute-start | bytes 24584 | tf_op jit(solution)/shard_map/ppermute | solution.py:48
  24.7 3.7 %collective-permute-start.6 = (bf16[32,128]{1,0:T(8,128)(2,1)S(1)}, bf16[32,128]{1,0:T(8,128)(2,1)S(1)}, u32[]{:S(2)}, u32[]{:S(2)}) collective-permute-start(bf16[32,128]{1,0:T(8,128)(2,1)S(1)} %attend.1.own_ref.after_ref), channel_id=1, source_target_pairs={{0,12},{4,0},{8,4},{12,8},{1,13},{5,1},{9,5},{13,9},{2,14},{6,2},{... | collective-permute-start | bytes 24584 | tf_op jit(solution)/shard_map/ppermute | solution.py:48
  29.0 3.7 %collective-permute-start.11 = (bf16[8,2048]{1,0:T(8,128)(2,1)S(1)}, bf16[8,2048]{1,0:T(8,128)(2,1)S(1)}, u32[]{:S(2)}, u32[]{:S(2)}) collective-permute-start(bf16[8,2048]{1,0:T(8,128)(2,1)S(1)} %output_half.3), channel_id=1, source_target_pairs={{0,3},{1,2},{2,1},{3,0},{4,7},{5,6},{6,5},{7,4},{8,11},{9,10},{10,... | collective-permute-start | bytes 98312 | tf_op jit(solution)/shard_map/ppermute | solution.py:43
  29.0 4.1 %collective-permute-start.10 = (bf16[8,2048]{1,0:T(8,128)(2,1)S(1)}, bf16[8,2048]{1,0:T(8,128)(2,1)S(1)}, u32[]{:S(2)}, u32[]{:S(2)}) collective-permute-start(bf16[8,2048]{1,0:T(8,128)(2,1)S(1)} %output_half.3), channel_id=1, source_target_pairs={{0,2},{1,3},{2,0},{3,1},{4,6},{5,7},{6,4},{7,5},{8,10},{9,11},{10,... | collective-permute-start | bytes 98312 | tf_op jit(solution)/shard_map/ppermute | solution.py:43
  30.6 2.5 %collective-permute-start.9 = (bf16[8,2048]{1,0:T(8,128)(2,1)S(1)}, bf16[8,2048]{1,0:T(8,128)(2,1)S(1)}, u32[]{:S(2)}, u32[]{:S(2)}) collective-permute-start(bf16[8,2048]{1,0:T(8,128)(2,1)S(1)} %output_half.3), channel_id=1, source_target_pairs={{0,1},{1,0},{2,3},{3,2},{4,5},{5,4},{6,7},{7,6},{8,9},{9,8},{10,11... | collective-permute-start | bytes 98312 | tf_op jit(solution)/shard_map/ppermute | solution.py:43

commit v17 on v16

--- a/solution.py
+++ b/solution.py
@@ -72,20 +72,31 @@
 
 def pick_near_kernel(kept_hbm_ref, cache_ref, *refs):
     *outs, kept_ref, cache, kept_sem, sem = refs
+    heads_local = cache.shape[1]
+    me = lax.axis_index("seq")
+
+    def pair_copy(pair):
+        place = (lax.div(pair, heads_local), lax.rem(pair, heads_local))
+        return pltpu.make_async_copy(cache_ref.at[place], cache.at[place], sem.at[pair])
+
     kept_copy = pltpu.make_async_copy(kept_hbm_ref, kept_ref, kept_sem)
-    cache_copy = pltpu.make_async_copy(cache_ref, cache, sem)
     kept_copy.start()
-    cache_copy.start()
+    offsets = list(reversed(range(len(outs))))
+    for offset in offsets:
+        pair_copy(jnp.bitwise_xor(me, offset)).start()
     kept_copy.wait()
-    me = lax.axis_index("seq")
-    places = [
-        [picked_rows(kept_ref, cache.shape, jnp.bitwise_xor(me, k), slot) for slot in range(MOST)]
-        for k in range(len(outs))
-    ]
-    cache_copy.wait()
-    for out_ref, slots in zip(outs, places):
-        for slot, (request, local, rows) in enumerate(slots):
-            out_ref[slot * BLK : (slot + 1) * BLK, :] = cache[request, local, rows, :]
+    places = {
+        offset: [
+            picked_rows(kept_ref, cache.shape, jnp.bitwise_xor(me, offset), slot)
+            for slot in range(MOST)
+        ]
+        for offset in offsets
+    }
+    for offset in offsets:
+        pair_copy(jnp.bitwise_xor(me, offset)).wait()
+        for slot, (request, local, rows) in enumerate(places[offset]):
+            out = outs[offset]
+            out[slot * BLK : (slot + 1) * BLK, :] = cache[request, local, rows, :]
 
 
 def pick_all_kernel(kept_hbm_ref, cache_ref, out_ref, kept_ref, sem):
@@ -116,7 +127,7 @@
             kept_scratch,
             pltpu.VMEM(source_cache.shape, jnp.bfloat16),
             pltpu.SemaphoreType.DMA,
-            pltpu.SemaphoreType.DMA,
+            pltpu.SemaphoreType.DMA((pair_count,)),
         ]
     else:
         shapes = [jax.ShapeDtypeStruct((pair_count,) + block, jnp.bfloat16)]
@@ -159,12 +170,24 @@
     ]
 
 
-def project_kernel(direct, after_ref, hidden_ref, gain_ref, wq_ref, wkv_ref, *outs):
+def project_kernel(direct, source_blocks, after_ref, hidden_ref, gain_ref, wq_ref, wkv_ref, *refs):
     del after_ref
+    outs = refs
     requests, step_count, width = hidden_ref.shape
     heads_local = wkv_ref.shape[1]
     row_count = requests * step_count
     me = lax.axis_index("seq")
+    if direct:
+        kept_ref, *outs, mask_ref = refs
+        request = lax.div(me, heads_local)
+        head = lax.axis_index("head") * heads_local + lax.rem(me, heads_local)
+        column = lax.broadcasted_iota(jnp.int32, mask_ref.shape[1:], 1)
+        for offset in range(mask_ref.shape[0]):
+            filled = jnp.int32(0)
+            for k in range(kept_ref.shape[1]):
+                source = lax.div(kept_ref[request, k, head], source_blocks)
+                filled += (source == jnp.bitwise_xor(me, offset)).astype(jnp.int32)
+            mask_ref[offset] = jnp.where(column < filled * BLK, 0.0, -jnp.inf)
     hidden = jnp.concatenate(
         [hidden_ref[r].astype(jnp.float32) for r in range(requests)], axis=0
     )
@@ -203,19 +226,23 @@
                 )
 
 
-def project(after, new_hidden, norm_gain, w_query, w_keyval, pair_count, direct):
+def project(after, new_hidden, norm_gain, w_query, w_keyval, kept_blocks, source_blocks, direct):
     requests, step_count, width = new_hidden.shape
+    pair_count = requests * w_keyval.shape[1]
     terms = ((QPK + 4) * step_count, HD)
     if direct:
         shapes = [jax.ShapeDtypeStruct(terms, jnp.float32)] * pair_count
+        shapes.append(jax.ShapeDtypeStruct((pair_count, 8, MOST * BLK), jnp.float32))
     else:
         shapes = [jax.ShapeDtypeStruct((pair_count,) + terms, jnp.float32)]
     vmem = pl.BlockSpec(memory_space=pltpu.VMEM)
     weights = w_query.size + w_keyval.size
     return pl.pallas_call(
-        functools.partial(project_kernel, direct),
+        functools.partial(project_kernel, direct, source_blocks),
         out_shape=shapes,
-        in_specs=[pl.BlockSpec(memory_space=pl.ANY)] + [vmem] * 4,
+        in_specs=[pl.BlockSpec(memory_space=pl.ANY)]
+        + [vmem] * 4
+        + [pl.BlockSpec(memory_space=pltpu.SMEM)] * direct,
         out_specs=[vmem] * len(shapes),
         compiler_params=pltpu.CompilerParams(vmem_limit_bytes=8 * 1024 * 1024),
         cost_estimate=pl.CostEstimate(
@@ -230,6 +257,7 @@
         norm_gain.reshape(width // HD, HD),
         pltpu.with_memory_space_constraint(w_query, pltpu.VMEM),
         pltpu.with_memory_space_constraint(w_keyval, pltpu.VMEM),
+        *([kept_blocks] if direct else []),
     )
 
 
@@ -268,21 +296,21 @@
     )(kept_blocks, after, *blocks)
 
 
-def attend_kernel(direct, source_blocks, heads_local, kept_ref, cos_ref, sin_ref, *refs):
-    kept_count = kept_ref.shape[1]
+def attend_kernel(direct, source_blocks, heads_local, which_ref, cos_ref, sin_ref, *refs):
     step_count = cos_ref.shape[0] // 2
-    me = lax.axis_index("seq")
-    request = lax.div(me, heads_local)
-    head = lax.axis_index("head") * heads_local + lax.rem(me, heads_local)
     if direct:
         by_offset, parts_refs, attended_ref = refs[:4][::-1], refs[4:8][::-1], refs[8]
         total = sum(ref[...] for ref in parts_refs)
     else:
         parts_ref, blocks_ref, attended_ref, cache_ref, sem, kept = refs
+        kept_count = which_ref.shape[1]
+        me = lax.axis_index("seq")
+        request = lax.div(me, heads_local)
+        head = lax.axis_index("head") * heads_local + lax.rem(me, heads_local)
 
         def start_copy(k, carry):
             previous, slot = carry
-            source = lax.div(kept_ref[request, k, head], source_blocks)
+            source = lax.div(which_ref[request, k, head], source_blocks)
             slot = jnp.where(source == previous, jnp.minimum(slot + 1, MOST - 1), 0)
             target = kept.at[pl.ds(pl.multiple_of(k * BLK, BLK), BLK)]
             rows = pl.ds(pl.multiple_of(slot * BLK, BLK), BLK)
@@ -308,24 +336,20 @@
     column = lax.broadcasted_iota(jnp.int32, score.shape, 1)
     scores = [jnp.where(column <= lax.rem(row, step_count), score * scale, -jnp.inf)]
     values = [new_value]
-    def add_block(block, filled):
+
+    def add_block(block):
         score = lax.dot_general(
             query, block[:, :HD], CONTRACT_LAST, preferred_element_type=jnp.float32
         )
-        column = lax.broadcasted_iota(jnp.int32, score.shape, 1)
-        scores.append(jnp.where(column < filled * BLK, score * scale, -jnp.inf))
+        scores.append(score * scale)
         values.append(block[:, HD:])
 
     if direct:
         for offset, ref in enumerate(by_offset):
-            source = jnp.bitwise_xor(me, offset)
-            filled = jnp.int32(0)
-            for k in range(kept_count):
-                here = lax.div(kept_ref[request, k, head], source_blocks) == source
-                filled += here.astype(jnp.int32)
-            add_block(ref[: MOST * BLK, :], filled)
-    else:
-        add_block(kept[...], kept_count)
+            add_block(ref[...])
+            scores[-1] += which_ref[offset, :1, :]
+    else:
+        add_block(kept[...])
     row_max = functools.reduce(
         jnp.maximum, [jnp.max(score, axis=1, keepdims=True) for score in scores]
     )
@@ -346,8 +370,7 @@
         pltpu.make_async_copy(cache_ref, cache_ref, sem).wait()
 
 
-def attend(kept_blocks, arrivals, source_blocks, heads_local, step_count, seq_count, direct):
-    kept_count = kept_blocks.shape[1]
+def attend(which, arrivals, source_blocks, heads_local, step_count, seq_count, direct):
     cosine, sine = rope_tables(source_blocks * BLK * seq_count, step_count)
     shape = (QPK * step_count, HD)
     vmem = pl.BlockSpec(memory_space=pltpu.VMEM)
@@ -356,7 +379,7 @@
         out_specs = [vmem]
         scratch = []
     else:
-        cache = (1, 1, kept_count * BLK, 2 * HD)
+        cache = (1, 1, which.shape[1] * BLK, 2 * HD)
         shapes = [
             jax.ShapeDtypeStruct((seq_count,) + shape, jnp.bfloat16),
             jax.ShapeDtypeStruct(cache, jnp.bfloat16),
@@ -366,13 +389,13 @@
     return pl.pallas_call(
         functools.partial(attend_kernel, direct, source_blocks, heads_local),
         out_shape=shapes,
-        in_specs=[pl.BlockSpec(memory_space=pltpu.SMEM)] + [vmem] * (2 + len(arrivals)),
+        in_specs=[vmem if direct else pl.BlockSpec(memory_space=pltpu.SMEM)] + [vmem] * (2 + len(arrivals)),
         out_specs=out_specs,
         scratch_shapes=scratch,
         compiler_params=pltpu.CompilerParams(vmem_limit_bytes=16 * 1024 * 1024),
         cost_estimate=pl.CostEstimate(flops=10**10, bytes_accessed=0, transcendentals=0),
         name="attend",
-    )(kept_blocks, jnp.asarray(cosine), jnp.asarray(sine), *arrivals)
+    )(which, jnp.asarray(cosine), jnp.asarray(sine), *arrivals)
 
 
 def merge_heads(first, second, step_count):
@@ -474,11 +497,11 @@
     if direct:
         partners = range(1, seq_count)
         blocks = list(pick(kept_blocks, source_cache, direct))
-        parts = list(project(blocks[0], *weights, pair_count, direct))
+        *parts, mask = project(blocks[0], *weights, kept_blocks, source_blocks, direct)
         blocks = [blocks[0]] + [swap(blocks[k], "seq", k) for k in partners]
         parts[1], blocks[3] = lax.optimization_barrier((parts[1], blocks[3]))
         parts = [parts[0]] + [swap(parts[k], "seq", k) for k in partners]
-        (attended,) = attend(kept_blocks, blocks[::-1] + parts[::-1], *shape)
+        (attended,) = attend(mask, blocks[::-1] + parts[::-1], *shape)
         kept_cache = place(kept_blocks, attended, blocks, source_blocks, heads_local)
         below, second, above = [shift(attended, "seq", step) for step in (1, 2, -1)]
         second, below = lax.optimization_barrier((second, below))
@@ -486,7 +509,7 @@
         terms = output_half(output_other_kernel, jnp.bfloat16, w_out, above, below, terms)
     else:
         (blocks,) = pick(kept_blocks, source_cache, direct)
-        (parts,) = project(blocks, *weights, pair_count, direct)
+        (parts,) = project(blocks, *weights, kept_blocks, source_blocks, direct)
         arrivals = [all_to_all(parts, "seq"), all_to_all(blocks, "seq")]
         attended, kept_cache = attend(kept_blocks, arrivals, *shape)
         terms = output(all_to_all(attended, "seq"), w_out, heads_local)

time: 33.9 us -> 33.3 us (0.982)
  starting transfers between devices: 20 us -> 19.4 us
    ppermute x9, starting transfers between devices: 15.1 us -> 14.5 us  [swap(): return lax.ppermute(outgoing, axis, [(i, i ^ offset) for i in range(count)])]
    pallas_call x1, Pallas kernels: 2.13 us -> 2.74 us  [project(): pl.pallas_call(functools.partial(project_kernel, direct, source_blocks),...]
    pallas_call x1, Pallas kernels: 1.13 us -> 0.52 us  [attend(): pl.pallas_call(functools.partial(attend_kernel, direct, source_blocks, he...]
  transfers between devices with their start and end apart: 12 -> 12, of which waited for: 6 -> 6; matrix products, arithmetic and copies ran while one was open for 0% -> 0% of each run, Pallas kernels for 12% -> 14%
where the time goes in v17:
time: 33.3 us; the launch traced here: 33.1 us
  starting transfers between devices  19.4 us (58%)
  Pallas kernels  7.3 us (22%)
  waiting for transfers between devices  4.93 us (15%)
  between operations  0.79 us (2%)
  other arithmetic  0.65 us (2%)
    ppermute x9, starting transfers between devices, swap(): return lax.ppermute(outgoing, axis, [(i, i ^ offset) for i in range(count)])  14.5 us
    ppermute x3, starting transfers between devices, shift(): lax.ppermute(outgoing, axis, [(i, (i + step) % count) for i in range(coun...  4.87 us
    ppermute x9, waiting for transfers between devices, swap(): return lax.ppermute(outgoing, axis, [(i, i ^ offset) for i in range(count)])  3.71 us
    pallas_call x1, Pallas kernels, project(): pl.pallas_call(functools.partial(project_kernel, direct, source_blocks),...  2.74 us
    pallas_call x1, Pallas kernels, pick(): pl.pallas_call(pick_near_kernel if direct else pick_all_kernel, out_shape...  1.41 us
    pallas_call x1, Pallas kernels, place(): pl.pallas_call(functools.partial(place_kernel, source_blocks, heads_local...  1.32 us
    pallas_call x2, Pallas kernels, output_half(): pl.pallas_call(kernel, out_shape=jax.ShapeDtypeStruct((rows, w_out.shape[...  1.3 us
    ppermute x3, waiting for transfers between devices, shift(): lax.ppermute(outgoing, axis, [(i, (i + step) % count) for i in range(coun...  1.22 us
  transfers between devices with their start and end apart: 12, of which 6 were waited for; matrix products, arithmetic and copies ran while one was open for 0% of the time, Pallas kernels for 14%

profile of v17, /device:TPU:0, one launch (start us, length us, event | category | flops | bytes accessed | tf_op | source)
XLA Modules:
  0.0 33.1 jit_solution(17567387691318584793)
XLA Ops:
  0.7 1.4 %pick_blocks.1 = (bf16[256,256]{1,0:T(8,128)(2,1)S(1)}, bf16[256,256]{1,0:T(8,128)(2,1)S(1)}, bf16[256,256]{1,0:T(8,128)(2,1)S(1)}, bf16[256,256]{1,0:T(8,128)(2,1)S(1)}) custom-call(s32[2,4,8]{2,1,0:T(4,128)} %bitcast.5, bf16[2,2,512,256]{3,2,1,0:T(8,128)(2,1)} %cache_ref.1), custom_call_target="tpu_custom_call" | custom-call | flops 10000000000 | tf_op jit(solution)/shard_map/pick_blocks/pallas_call | solution.py:135
  2.1 5.1 %collective-permute-start = (bf16[256,256]{1,0:T(8,128)(2,1)S(1)}, bf16[256,256]{1,0:T(8,128)(2,1)S(1)}, u32[]{:S(2)}, u32[]{:S(2)}) collective-permute-start(bf16[256,256]{1,0:T(8,128)(2,1)S(1)} %get-tuple-element.22), channel_id=1, source_target_pairs={{0,12},{4,8},{8,4},{12,0},{1,13},{5,9},{9,5},{13,1},{2,14},{6,10},... | collective-permute-start | bytes 393224 | tf_op jit(solution)/shard_map/ppermute | solution.py:43
  7.2 0.6 %collective-permute-start.2 = (bf16[256,256]{1,0:T(8,128)(2,1)S(1)}, bf16[256,256]{1,0:T(8,128)(2,1)S(1)}, u32[]{:S(2)}, u32[]{:S(2)}) collective-permute-start(bf16[256,256]{1,0:T(8,128)(2,1)S(1)} %get-tuple-element.25), channel_id=1, source_target_pairs={{0,4},{4,0},{8,12},{12,8},{1,5},{5,1},{9,13},{13,9},{2,6},{6,2},{1... | collective-permute-start | bytes 393224 | tf_op jit(solution)/shard_map/ppermute | solution.py:43
  7.9 0.0 slice-start
  7.9 2.7 %project.1 = (f32[48,128]{1,0:T(8,128)S(1)}, f32[48,128]{1,0:T(8,128)S(1)}, f32[48,128]{1,0:T(8,128)S(1)}, f32[48,128]{1,0:T(8,128)S(1)}, f32[4,8,256]{2,1,0:T(8,128)S(1)}) custom-call(bf16[256,256]{1,0:T(8,128)(2,1)S(1)} %get-tuple-element.19.after_ref.refs_3_.refs_0_, bf16[2,4,2048]{2,1,0:T(4,128)(2,1)S(1)} %copy-done.2, bf16[16,128]{1,0:T(8,128)(2,1)S(1)} %bitcast.4, ...), custom_call_target="tpu_custom_call" | custom-call | flops 83886080 | bytes 10485760 | tf_op jit(solution)/shard_map/project/pallas_call | solution.py:240
  10.7 3.8 %collective-permute-start.3 = (f32[48,128]{1,0:T(8,128)S(1)}, f32[48,128]{1,0:T(8,128)S(1)}, u32[]{:S(2)}, u32[]{:S(2)}) collective-permute-start(f32[48,128]{1,0:T(8,128)S(1)} %get-tuple-element.26), channel_id=1, source_target_pairs={{0,12},{4,8},{8,4},{12,0},{1,13},{5,9},{9,5},{13,1},{2,14},{6,10},... | collective-permute-start | bytes 73736 | tf_op jit(solution)/shard_map/ppermute | solution.py:43
  14.5 3.1 %collective-permute-start.5 = (f32[48,128]{1,0:T(8,128)S(1)}, f32[48,128]{1,0:T(8,128)S(1)}, u32[]{:S(2)}, u32[]{:S(2)}) collective-permute-start(f32[48,128]{1,0:T(8,128)S(1)} %get-tuple-element.28), channel_id=1, source_target_pairs={{0,4},{4,0},{8,12},{12,8},{1,5},{5,1},{9,13},{13,9},{2,6},{6,2},{1... | collective-permute-start | bytes 73736 | tf_op jit(solution)/shard_map/ppermute | solution.py:43
  17.6 2.8 %collective-permute-done.4.refs_5_ = f32[48,128]{1,0:T(8,128)S(1)} collective-permute-done((f32[48,128]{1,0:T(8,128)S(1)}, f32[48,128]{1,0:T(8,128)S(1)}, u32[]{:S(2)}, u32[]{:S(2)}) %collective-permute-start.4) | collective-permute-done | bytes 24608 | tf_op jit(solution)/shard_map/ppermute | solution.py:43
  20.4 0.0 slice-start.1
  20.5 0.5 %attend.1.own_ref.after_ref = bf16[32,128]{1,0:T(8,128)(2,1)S(1)} custom-call(f32[4,8,256]{2,1,0:T(8,128)S(1)} %get-tuple-element.20.which_ref, f32[8,128]{1,0:T(8,128)S(1)} %copy-done.6, f32[8,128]{1,0:T(8,128)S(1)} %copy-done.5, bf16[256,256]{1,0:T(8,128)(2,1)S(1)} %collective-permute-done.refs_0_.refs_3_, ...), custom_call_target="tpu_custom_call" | custom-call | flops 10000000000 | tf_op jit(solution)/shard_map/attend/pallas_call | solution.py:389
  21.0 1.0 %collective-permute-start.8 = (bf16[32,128]{1,0:T(8,128)(2,1)S(1)}, bf16[32,128]{1,0:T(8,128)(2,1)S(1)}, u32[]{:S(2)}, u32[]{:S(2)}) collective-permute-start(bf16[32,128]{1,0:T(8,128)(2,1)S(1)} %attend.1.own_ref.after_ref), channel_id=1, source_target_pairs={{0,4},{4,8},{8,12},{12,0},{1,5},{5,9},{9,13},{13,1},{2,6},{6,10},{... | collective-permute-start | bytes 24584 | tf_op jit(solution)/shard_map/ppermute | solution.py:48
  22.0 2.1 %collective-permute-start.7 = (bf16[32,128]{1,0:T(8,128)(2,1)S(1)}, bf16[32,128]{1,0:T(8,128)(2,1)S(1)}, u32[]{:S(2)}, u32[]{:S(2)}) collective-permute-start(bf16[32,128]{1,0:T(8,128)(2,1)S(1)} %attend.1.own_ref.after_ref), channel_id=1, source_target_pairs={{0,8},{4,12},{8,0},{12,4},{1,9},{5,13},{9,1},{13,5},{2,10},{6,14},... | collective-permute-start | bytes 24584 | tf_op jit(solution)/shard_map/ppermute | solution.py:48
  24.1 1.8 %collective-permute-start.6 = (bf16[32,128]{1,0:T(8,128)(2,1)S(1)}, bf16[32,128]{1,0:T(8,128)(2,1)S(1)}, u32[]{:S(2)}, u32[]{:S(2)}) collective-permute-start(bf16[32,128]{1,0:T(8,128)(2,1)S(1)} %attend.1.own_ref.after_ref), channel_id=1, source_target_pairs={{0,12},{4,0},{8,4},{12,8},{1,13},{5,1},{9,5},{13,9},{2,14},{6,2},{... | collective-permute-start | bytes 24584 | tf_op jit(solution)/shard_map/ppermute | solution.py:48
  25.9 0.6 %collective-permute-done.8.below_ref = bf16[32,128]{1,0:T(8,128)(2,1)S(1)} collective-permute-done((bf16[32,128]{1,0:T(8,128)(2,1)S(1)}, bf16[32,128]{1,0:T(8,128)(2,1)S(1)}, u32[]{:S(2)}, u32[]{:S(2)}) %collective-permute-start.8) | collective-permute-done | bytes 8224 | tf_op jit(solution)/shard_map/ppermute | solution.py:48
  26.5 0.1 collective-permute-done.7.second_ref
  26.6 0.7 %output_half.2.addend_ref = f32[8,2048]{1,0:T(8,128)S(1)} custom-call(bf16[2048,2048]{1,0:T(8,128)(2,1)S(1)} %bitcast.3, bf16[32,128]{1,0:T(8,128)(2,1)S(1)} %attend.1.own_ref.after_ref, bf16[32,128]{1,0:T(8,128)(2,1)S(1)} %collective-permute-done.7.second_ref), custom_call_target="tpu_custom_call" | custom-call | flops 1000000000 | tf_op jit(solution)/shard_map/output_half/pallas_call | solution.py:441
  27.2 0.5 %collective-permute-done.6.above_ref = bf16[32,128]{1,0:T(8,128)(2,1)S(1)} collective-permute-done((bf16[32,128]{1,0:T(8,128)(2,1)S(1)}, bf16[32,128]{1,0:T(8,128)(2,1)S(1)}, u32[]{:S(2)}, u32[]{:S(2)}) %collective-permute-start.6) | collective-permute-done | bytes 8224 | tf_op jit(solution)/shard_map/ppermute | solution.py:48
  27.7 0.7 %output_half.3 = bf16[8,2048]{1,0:T(8,128)(2,1)S(1)} custom-call(bf16[2048,2048]{1,0:T(8,128)(2,1)S(1)} %bitcast.3, bf16[32,128]{1,0:T(8,128)(2,1)S(1)} %collective-permute-done.6.above_ref, bf16[32,128]{1,0:T(8,128)(2,1)S(1)} %collective-permute-done.8.below_ref, f32[8,2048]{1,0:T(8,128)S(1)} %output_half.2.addend_ref), custom_call_target="tpu_custom_call" | custom-call | flops 1000000000 | tf_op jit(solution)/shard_map/output_half/pallas_call | solution.py:441
  28.4 1.5 %collective-permute-start.10 = (bf16[8,2048]{1,0:T(8,128)(2,1)S(1)}, bf16[8,2048]{1,0:T(8,128)(2,1)S(1)}, u32[]{:S(2)}, u32[]{:S(2)}) collective-permute-start(bf16[8,2048]{1,0:T(8,128)(2,1)S(1)} %output_half.3), channel_id=1, source_target_pairs={{0,2},{1,3},{2,0},{3,1},{4,6},{5,7},{6,4},{7,5},{8,10},{9,11},{10,... | collective-permute-start | bytes 98312 | tf_op jit(solution)/shard_map/ppermute | solution.py:43
  29.9 0.3 collective-permute-start.9
  30.3 1.3 %place.1 = bf16[1,1,512,256]{3,2,1,0:T(8,128)(2,1)} custom-call(s32[2,4,8]{2,1,0:T(4,128)S(1)} %bitcast.7, bf16[32,128]{1,0:T(8,128)(2,1)S(1)} %attend.1.own_ref.after_ref, bf16[256,256]{1,0:T(8,128)(2,1)S(1)} %get-tuple-element.19.after_ref.refs_3_.refs_0_, bf16[256,256]{1,0:T(8,128)(2,1)S(1)} %collective-permute-done.2.refs_2_.refs_1_, ...), custom_call_target="tpu_custom_call" | custom-call | flops 1000000000 | tf_op jit(solution)/shard_map/place/pallas_call | solution.py:287
  31.6 0.4 %collective-permute-done.11 = bf16[8,2048]{1,0:T(8,128)(2,1)S(1)} collective-permute-done((bf16[8,2048]{1,0:T(8,128)(2,1)S(1)}, bf16[8,2048]{1,0:T(8,128)(2,1)S(1)}, u32[]{:S(2)}, u32[]{:S(2)}) %collective-permute-start.11) | collective-permute-done | bytes 32800 | tf_op jit(solution)/shard_map/ppermute | solution.py:43
  32.0 0.4 %collective-permute-done.10 = bf16[8,2048]{1,0:T(8,128)(2,1)S(1)} collective-permute-done((bf16[8,2048]{1,0:T(8,128)(2,1)S(1)}, bf16[8,2048]{1,0:T(8,128)(2,1)S(1)}, u32[]{:S(2)}, u32[]{:S(2)}) %collective-permute-start.10) | collective-permute-done | bytes 32800 | tf_op jit(solution)/shard_map/ppermute | solution.py:43
  32.5 0.6 %add_convert_fusion = bf16[2,4,2048]{2,1,0:T(4,128)(2,1)} fusion(f32[2,4,2048]{2,1,0:T(4,128)S(1)} %reshape.11, bf16[2,4,2048]{2,1,0:T(4,128)(2,1)S(1)} %copy-done.2), kind=kLoop, calls=%fused_computation | loop fusion | flops 49152 | bytes 131072 | tf_op jit(solution)/shard_map/convert_element_type | solution.py:525
  (28 shorter events, 0.1 us)
Async XLA Ops:
  0.6 7.2 %copy-start = (bf16[2048,2048]{1,0:T(8,128)(2,1)S(1)}, bf16[2048,2048]{1,0:T(8,128)(2,1)}, u32[]{:S(2)}) copy-start(bf16[2048,2048]{1,0:T(8,128)(2,1)} %wq_ref.1) | copy-start | bytes 25165828
  0.6 7.2 %copy-start.1 = (bf16[2048,2,256]{2,1,0:T(2,128)(2,1)S(1)}, bf16[2048,2,256]{2,1,0:T(2,128)(2,1)}, u32[]{:S(2)}) copy-start(bf16[2048,2,256]{2,1,0:T(2,128)(2,1)} %wkv_ref.1) | copy-start | bytes 6291460
  0.7 7.2 %copy-start.2 = (bf16[2,4,2048]{2,1,0:T(4,128)(2,1)S(1)}, bf16[2,4,2048]{2,1,0:T(4,128)(2,1)}, u32[]{:S(2)}) copy-start(bf16[2,4,2048]{2,1,0:T(4,128)(2,1)} %hidden_ref.1) | copy-start | bytes 98308
  0.7 7.2 %copy-start.3 = (bf16[2048]{0:T(1024)(128)(2,1)S(1)}, bf16[2048]{0:T(1024)(128)(2,1)}, u32[]{:S(2)}) copy-start(bf16[2048]{0:T(1024)(128)(2,1)} %param.12) | copy-start | bytes 12292
  0.7 7.2 %copy-start.4 = (s32[2,8,4]{1,2,0:T(4,128)S(1)}, s32[2,8,4]{1,2,0:T(4,128)}, u32[]{:S(2)}) copy-start(s32[2,8,4]{1,2,0:T(4,128)} %param.10) | copy-start | bytes 772
  2.1 18.3 %copy-start.5 = (f32[8,128]{1,0:T(8,128)S(1)}, f32[8,128]{1,0:T(8,128)}, u32[]{:S(2)}) copy-start(f32[8,128]{1,0:T(8,128)} %constant.5.clone.sin_ref) | copy-start | bytes 12292
  2.1 18.3 %copy-start.6 = (f32[8,128]{1,0:T(8,128)S(1)}, f32[8,128]{1,0:T(8,128)}, u32[]{:S(2)}) copy-start(f32[8,128]{1,0:T(8,128)} %constant.4.clone.cos_ref) | copy-start | bytes 12292
  2.1 12.4 %collective-permute-start = (bf16[256,256]{1,0:T(8,128)(2,1)S(1)}, bf16[256,256]{1,0:T(8,128)(2,1)S(1)}, u32[]{:S(2)}, u32[]{:S(2)}) collective-permute-start(bf16[256,256]{1,0:T(8,128)(2,1)S(1)} %get-tuple-element.22), channel_id=1, source_target_pairs={{0,12},{4,8},{8,4},{12,0},{1,13},{5,9},{9,5},{13,1},{2,14},{6,10},... | collective-permute-start | bytes 393224 | tf_op jit(solution)/shard_map/ppermute | solution.py:43
  7.2 13.2 %collective-permute-start.1 = (bf16[256,256]{1,0:T(8,128)(2,1)S(1)}, bf16[256,256]{1,0:T(8,128)(2,1)S(1)}, u32[]{:S(2)}, u32[]{:S(2)}) collective-permute-start(bf16[256,256]{1,0:T(8,128)(2,1)S(1)} %get-tuple-element.24), channel_id=1, source_target_pairs={{0,8},{4,12},{8,0},{12,4},{1,9},{5,13},{9,1},{13,5},{2,10},{6,14},... | collective-permute-start | bytes 393224 | tf_op jit(solution)/shard_map/ppermute | solution.py:43
  7.2 13.2 %collective-permute-start.2 = (bf16[256,256]{1,0:T(8,128)(2,1)S(1)}, bf16[256,256]{1,0:T(8,128)(2,1)S(1)}, u32[]{:S(2)}, u32[]{:S(2)}) collective-permute-start(bf16[256,256]{1,0:T(8,128)(2,1)S(1)} %get-tuple-element.25), channel_id=1, source_target_pairs={{0,4},{4,0},{8,12},{12,8},{1,5},{5,1},{9,13},{13,9},{2,6},{6,2},{1... | collective-permute-start | bytes 393224 | tf_op jit(solution)/shard_map/ppermute | solution.py:43
  7.9 18.7 %slice-start = ((s8[8388608]{0:T(1024)(128)(4,1)}), s8[4194304]{0:T(1024)(128)(4,1)S(1)}, s32[]{:S(2)}) async-start(s8[8388608]{0:T(1024)(128)(4,1)} %bitcast.2), calls=%async_computation | async-start | bytes 8388608
  10.7 6.9 %collective-permute-start.3 = (f32[48,128]{1,0:T(8,128)S(1)}, f32[48,128]{1,0:T(8,128)S(1)}, u32[]{:S(2)}, u32[]{:S(2)}) collective-permute-start(f32[48,128]{1,0:T(8,128)S(1)} %get-tuple-element.26), channel_id=1, source_target_pairs={{0,12},{4,8},{8,4},{12,0},{1,13},{5,9},{9,5},{13,1},{2,14},{6,10},... | collective-permute-start | bytes 73736 | tf_op jit(solution)/shard_map/ppermute | solution.py:43
  14.5 5.9 %collective-permute-start.4 = (f32[48,128]{1,0:T(8,128)S(1)}, f32[48,128]{1,0:T(8,128)S(1)}, u32[]{:S(2)}, u32[]{:S(2)}) collective-permute-start(f32[48,128]{1,0:T(8,128)S(1)} %get-tuple-element.27), channel_id=1, source_target_pairs={{0,8},{4,12},{8,0},{12,4},{1,9},{5,13},{9,1},{13,5},{2,10},{6,14},... | collective-permute-start | bytes 73736 | tf_op jit(solution)/shard_map/ppermute | solution.py:43
  14.5 5.9 %collective-permute-start.5 = (f32[48,128]{1,0:T(8,128)S(1)}, f32[48,128]{1,0:T(8,128)S(1)}, u32[]{:S(2)}, u32[]{:S(2)}) collective-permute-start(f32[48,128]{1,0:T(8,128)S(1)} %get-tuple-element.28), channel_id=1, source_target_pairs={{0,4},{4,0},{8,12},{12,8},{1,5},{5,1},{9,13},{13,9},{2,6},{6,2},{1... | collective-permute-start | bytes 73736 | tf_op jit(solution)/shard_map/ppermute | solution.py:43
  20.4 6.1 %slice-start.1 = ((s8[8388608]{0:T(1024)(128)(4,1)}), s8[4194304]{0:T(1024)(128)(4,1)S(1)}, s32[]{:S(2)}) async-start(s8[8388608]{0:T(1024)(128)(4,1)} %bitcast.2), calls=%async_computation.1 | async-start | bytes 8388608
  21.0 5.5 %collective-permute-start.8 = (bf16[32,128]{1,0:T(8,128)(2,1)S(1)}, bf16[32,128]{1,0:T(8,128)(2,1)S(1)}, u32[]{:S(2)}, u32[]{:S(2)}) collective-permute-start(bf16[32,128]{1,0:T(8,128)(2,1)S(1)} %attend.1.own_ref.after_ref), channel_id=1, source_target_pairs={{0,4},{4,8},{8,12},{12,0},{1,5},{5,9},{9,13},{13,1},{2,6},{6,10},{... | collective-permute-start | bytes 24584 | tf_op jit(solution)/shard_map/ppermute | solution.py:48
  22.0 4.6 %collective-permute-start.7 = (bf16[32,128]{1,0:T(8,128)(2,1)S(1)}, bf16[32,128]{1,0:T(8,128)(2,1)S(1)}, u32[]{:S(2)}, u32[]{:S(2)}) collective-permute-start(bf16[32,128]{1,0:T(8,128)(2,1)S(1)} %attend.1.own_ref.after_ref), channel_id=1, source_target_pairs={{0,8},{4,12},{8,0},{12,4},{1,9},{5,13},{9,1},{13,5},{2,10},{6,14},... | collective-permute-start | bytes 24584 | tf_op jit(solution)/shard_map/ppermute | solution.py:48
  24.1 3.7 %collective-permute-start.6 = (bf16[32,128]{1,0:T(8,128)(2,1)S(1)}, bf16[32,128]{1,0:T(8,128)(2,1)S(1)}, u32[]{:S(2)}, u32[]{:S(2)}) collective-permute-start(bf16[32,128]{1,0:T(8,128)(2,1)S(1)} %attend.1.own_ref.after_ref), channel_id=1, source_target_pairs={{0,12},{4,0},{8,4},{12,8},{1,13},{5,1},{9,5},{13,9},{2,14},{6,2},{... | collective-permute-start | bytes 24584 | tf_op jit(solution)/shard_map/ppermute | solution.py:48
  28.4 3.7 %collective-permute-start.11 = (bf16[8,2048]{1,0:T(8,128)(2,1)S(1)}, bf16[8,2048]{1,0:T(8,128)(2,1)S(1)}, u32[]{:S(2)}, u32[]{:S(2)}) collective-permute-start(bf16[8,2048]{1,0:T(8,128)(2,1)S(1)} %output_half.3), channel_id=1, source_target_pairs={{0,3},{1,2},{2,1},{3,0},{4,7},{5,6},{6,5},{7,4},{8,11},{9,10},{10,... | collective-permute-start | bytes 98312 | tf_op jit(solution)/shard_map/ppermute | solution.py:43
  28.4 4.1 %collective-permute-start.10 = (bf16[8,2048]{1,0:T(8,128)(2,1)S(1)}, bf16[8,2048]{1,0:T(8,128)(2,1)S(1)}, u32[]{:S(2)}, u32[]{:S(2)}) collective-permute-start(bf16[8,2048]{1,0:T(8,128)(2,1)S(1)} %output_half.3), channel_id=1, source_target_pairs={{0,2},{1,3},{2,0},{3,1},{4,6},{5,7},{6,4},{7,5},{8,10},{9,11},{10,... | collective-permute-start | bytes 98312 | tf_op jit(solution)/shard_map/ppermute | solution.py:43
  29.9 2.5 %collective-permute-start.9 = (bf16[8,2048]{1,0:T(8,128)(2,1)S(1)}, bf16[8,2048]{1,0:T(8,128)(2,1)S(1)}, u32[]{:S(2)}, u32[]{:S(2)}) collective-permute-start(bf16[8,2048]{1,0:T(8,128)(2,1)S(1)} %output_half.3), channel_id=1, source_target_pairs={{0,1},{1,0},{2,3},{3,2},{4,5},{5,4},{6,7},{7,6},{8,9},{9,8},{10,11... | collective-permute-start | bytes 98312 | tf_op jit(solution)/shard_map/ppermute | solution.py:43

commit v18 on v17

--- a/solution.py
+++ b/solution.py
@@ -173,21 +173,14 @@
 def project_kernel(direct, source_blocks, after_ref, hidden_ref, gain_ref, wq_ref, wkv_ref, *refs):
     del after_ref
     outs = refs
+    if direct:
+        kept_hbm_ref, *outs, mask_ref, kept_ref, sem = refs
+        kept_copy = pltpu.make_async_copy(kept_hbm_ref, kept_ref, sem)
+        kept_copy.start()
     requests, step_count, width = hidden_ref.shape
     heads_local = wkv_ref.shape[1]
     row_count = requests * step_count
     me = lax.axis_index("seq")
-    if direct:
-        kept_ref, *outs, mask_ref = refs
-        request = lax.div(me, heads_local)
-        head = lax.axis_index("head") * heads_local + lax.rem(me, heads_local)
-        column = lax.broadcasted_iota(jnp.int32, mask_ref.shape[1:], 1)
-        for offset in range(mask_ref.shape[0]):
-            filled = jnp.int32(0)
-            for k in range(kept_ref.shape[1]):
-                source = lax.div(kept_ref[request, k, head], source_blocks)
-                filled += (source == jnp.bitwise_xor(me, offset)).astype(jnp.int32)
-            mask_ref[offset] = jnp.where(column < filled * BLK, 0.0, -jnp.inf)
     hidden = jnp.concatenate(
         [hidden_ref[r].astype(jnp.float32) for r in range(requests)], axis=0
     )
@@ -224,6 +217,17 @@
                 pl.when(jnp.bitwise_xor(me, offset) == pair)(
                     functools.partial(write_pair, out_ref, pieces)
                 )
+    if direct:
+        kept_copy.wait()
+        request = lax.div(me, heads_local)
+        head = lax.axis_index("head") * heads_local + lax.rem(me, heads_local)
+        column = lax.broadcasted_iota(jnp.int32, mask_ref.shape[1:], 1)
+        for offset in range(mask_ref.shape[0]):
+            filled = jnp.int32(0)
+            for k in range(kept_ref.shape[1]):
+                source = lax.div(kept_ref[request, k, head], source_blocks)
+                filled += (source == jnp.bitwise_xor(me, offset)).astype(jnp.int32)
+            mask_ref[offset] = jnp.where(column < filled * BLK, 0.0, -jnp.inf)
 
 
 def project(after, new_hidden, norm_gain, w_query, w_keyval, kept_blocks, source_blocks, direct):
@@ -242,8 +246,11 @@
         out_shape=shapes,
         in_specs=[pl.BlockSpec(memory_space=pl.ANY)]
         + [vmem] * 4
-        + [pl.BlockSpec(memory_space=pltpu.SMEM)] * direct,
+        + [pl.BlockSpec(memory_space=pl.ANY)] * direct,
         out_specs=[vmem] * len(shapes),
+        scratch_shapes=[pltpu.SMEM(kept_blocks.shape, jnp.int32), pltpu.SemaphoreType.DMA]
+        if direct
+        else [],
         compiler_params=pltpu.CompilerParams(vmem_limit_bytes=8 * 1024 * 1024),
         cost_estimate=pl.CostEstimate(
             flops=2 * requests * step_count * weights,
@@ -257,7 +264,7 @@
         norm_gain.reshape(width // HD, HD),
         pltpu.with_memory_space_constraint(w_query, pltpu.VMEM),
         pltpu.with_memory_space_constraint(w_keyval, pltpu.VMEM),
-        *([kept_blocks] if direct else []),
+        *([pltpu.with_memory_space_constraint(kept_blocks, pltpu.HBM)] if direct else []),
     )
 
 

time: 33.3 us -> 33.3 us (level)
  no operation moved by 1% of the time
where the time goes in v18:
time: 33.3 us; the launch traced here: 33.1 us
  starting transfers between devices  19.4 us (58%)
  Pallas kernels  7.33 us (22%)
  waiting for transfers between devices  4.93 us (15%)
  between operations  0.78 us (2%)
  other arithmetic  0.65 us (2%)
    ppermute x9, starting transfers between devices, swap(): return lax.ppermute(outgoing, axis, [(i, i ^ offset) for i in range(count)])  14.5 us
    ppermute x3, starting transfers between devices, shift(): lax.ppermute(outgoing, axis, [(i, (i + step) % count) for i in range(coun...  4.87 us
    ppermute x9, waiting for transfers between devices, swap(): return lax.ppermute(outgoing, axis, [(i, i ^ offset) for i in range(count)])  3.71 us
    pallas_call x1, Pallas kernels, project(): pl.pallas_call(functools.partial(project_kernel, direct, source_blocks),...  2.77 us
    pallas_call x1, Pallas kernels, pick(): pl.pallas_call(pick_near_kernel if direct else pick_all_kernel, out_shape...  1.41 us
    pallas_call x1, Pallas kernels, place(): pl.pallas_call(functools.partial(place_kernel, source_blocks, heads_local...  1.32 us
    pallas_call x2, Pallas kernels, output_half(): pl.pallas_call(kernel, out_shape=jax.ShapeDtypeStruct((rows, w_out.shape[...  1.3 us
    ppermute x3, waiting for transfers between devices, shift(): lax.ppermute(outgoing, axis, [(i, (i + step) % count) for i in range(coun...  1.22 us
  transfers between devices with their start and end apart: 12, of which 6 were waited for; matrix products, arithmetic and copies ran while one was open for 0% of the time, Pallas kernels for 14%

profile of v18, /device:TPU:0, one launch (start us, length us, event | category | flops | bytes accessed | tf_op | source)
XLA Modules:
  0.0 33.1 jit_solution(893310951346162436)
XLA Ops:
  0.7 1.4 %pick_blocks.1 = (bf16[256,256]{1,0:T(8,128)(2,1)S(1)}, bf16[256,256]{1,0:T(8,128)(2,1)S(1)}, bf16[256,256]{1,0:T(8,128)(2,1)S(1)}, bf16[256,256]{1,0:T(8,128)(2,1)S(1)}) custom-call(s32[2,4,8]{2,1,0:T(4,128)} %bitcast.5, bf16[2,2,512,256]{3,2,1,0:T(8,128)(2,1)} %cache_ref.1), custom_call_target="tpu_custom_call" | custom-call | flops 10000000000 | tf_op jit(solution)/shard_map/pick_blocks/pallas_call | solution.py:135
  2.1 5.1 %collective-permute-start = (bf16[256,256]{1,0:T(8,128)(2,1)S(1)}, bf16[256,256]{1,0:T(8,128)(2,1)S(1)}, u32[]{:S(2)}, u32[]{:S(2)}) collective-permute-start(bf16[256,256]{1,0:T(8,128)(2,1)S(1)} %get-tuple-element.22), channel_id=1, source_target_pairs={{0,12},{4,8},{8,4},{12,0},{1,13},{5,9},{9,5},{13,1},{2,14},{6,10},... | collective-permute-start | bytes 393224 | tf_op jit(solution)/shard_map/ppermute | solution.py:43
  7.2 0.6 %collective-permute-start.2 = (bf16[256,256]{1,0:T(8,128)(2,1)S(1)}, bf16[256,256]{1,0:T(8,128)(2,1)S(1)}, u32[]{:S(2)}, u32[]{:S(2)}) collective-permute-start(bf16[256,256]{1,0:T(8,128)(2,1)S(1)} %get-tuple-element.25), channel_id=1, source_target_pairs={{0,4},{4,0},{8,12},{12,8},{1,5},{5,1},{9,13},{13,9},{2,6},{6,2},{1... | collective-permute-start | bytes 393224 | tf_op jit(solution)/shard_map/ppermute | solution.py:43
  7.9 0.0 slice-start
  7.9 2.8 %project.1 = (f32[48,128]{1,0:T(8,128)S(1)}, f32[48,128]{1,0:T(8,128)S(1)}, f32[48,128]{1,0:T(8,128)S(1)}, f32[48,128]{1,0:T(8,128)S(1)}, f32[4,8,256]{2,1,0:T(8,128)S(1)}) custom-call(bf16[256,256]{1,0:T(8,128)(2,1)S(1)} %get-tuple-element.19.after_ref.refs_3_.refs_0_, bf16[2,4,2048]{2,1,0:T(4,128)(2,1)S(1)} %copy-done.2, bf16[16,128]{1,0:T(8,128)(2,1)S(1)} %bitcast.4, ...), custom_call_target="tpu_custom_call" | custom-call | flops 83886080 | bytes 10485760 | tf_op jit(solution)/shard_map/project/pallas_call | solution.py:244
  10.7 3.8 %collective-permute-start.3 = (f32[48,128]{1,0:T(8,128)S(1)}, f32[48,128]{1,0:T(8,128)S(1)}, u32[]{:S(2)}, u32[]{:S(2)}) collective-permute-start(f32[48,128]{1,0:T(8,128)S(1)} %get-tuple-element.26), channel_id=1, source_target_pairs={{0,12},{4,8},{8,4},{12,0},{1,13},{5,9},{9,5},{13,1},{2,14},{6,10},... | collective-permute-start | bytes 73736 | tf_op jit(solution)/shard_map/ppermute | solution.py:43
  14.5 3.1 %collective-permute-start.5 = (f32[48,128]{1,0:T(8,128)S(1)}, f32[48,128]{1,0:T(8,128)S(1)}, u32[]{:S(2)}, u32[]{:S(2)}) collective-permute-start(f32[48,128]{1,0:T(8,128)S(1)} %get-tuple-element.28), channel_id=1, source_target_pairs={{0,4},{4,0},{8,12},{12,8},{1,5},{5,1},{9,13},{13,9},{2,6},{6,2},{1... | collective-permute-start | bytes 73736 | tf_op jit(solution)/shard_map/ppermute | solution.py:43
  17.6 2.8 %collective-permute-done.4.refs_5_ = f32[48,128]{1,0:T(8,128)S(1)} collective-permute-done((f32[48,128]{1,0:T(8,128)S(1)}, f32[48,128]{1,0:T(8,128)S(1)}, u32[]{:S(2)}, u32[]{:S(2)}) %collective-permute-start.4) | collective-permute-done | bytes 24608 | tf_op jit(solution)/shard_map/ppermute | solution.py:43
  20.4 0.0 slice-start.1
  20.5 0.5 %attend.1.own_ref.after_ref = bf16[32,128]{1,0:T(8,128)(2,1)S(1)} custom-call(f32[4,8,256]{2,1,0:T(8,128)S(1)} %get-tuple-element.20.which_ref, f32[8,128]{1,0:T(8,128)S(1)} %copy-done.6, f32[8,128]{1,0:T(8,128)S(1)} %copy-done.5, bf16[256,256]{1,0:T(8,128)(2,1)S(1)} %collective-permute-done.refs_0_.refs_3_, ...), custom_call_target="tpu_custom_call" | custom-call | flops 10000000000 | tf_op jit(solution)/shard_map/attend/pallas_call | solution.py:396
  21.0 1.0 %collective-permute-start.8 = (bf16[32,128]{1,0:T(8,128)(2,1)S(1)}, bf16[32,128]{1,0:T(8,128)(2,1)S(1)}, u32[]{:S(2)}, u32[]{:S(2)}) collective-permute-start(bf16[32,128]{1,0:T(8,128)(2,1)S(1)} %attend.1.own_ref.after_ref), channel_id=1, source_target_pairs={{0,4},{4,8},{8,12},{12,0},{1,5},{5,9},{9,13},{13,1},{2,6},{6,10},{... | collective-permute-start | bytes 24584 | tf_op jit(solution)/shard_map/ppermute | solution.py:48
  22.0 2.1 %collective-permute-start.7 = (bf16[32,128]{1,0:T(8,128)(2,1)S(1)}, bf16[32,128]{1,0:T(8,128)(2,1)S(1)}, u32[]{:S(2)}, u32[]{:S(2)}) collective-permute-start(bf16[32,128]{1,0:T(8,128)(2,1)S(1)} %attend.1.own_ref.after_ref), channel_id=1, source_target_pairs={{0,8},{4,12},{8,0},{12,4},{1,9},{5,13},{9,1},{13,5},{2,10},{6,14},... | collective-permute-start | bytes 24584 | tf_op jit(solution)/shard_map/ppermute | solution.py:48
  24.1 1.8 %collective-permute-start.6 = (bf16[32,128]{1,0:T(8,128)(2,1)S(1)}, bf16[32,128]{1,0:T(8,128)(2,1)S(1)}, u32[]{:S(2)}, u32[]{:S(2)}) collective-permute-start(bf16[32,128]{1,0:T(8,128)(2,1)S(1)} %attend.1.own_ref.after_ref), channel_id=1, source_target_pairs={{0,12},{4,0},{8,4},{12,8},{1,13},{5,1},{9,5},{13,9},{2,14},{6,2},{... | collective-permute-start | bytes 24584 | tf_op jit(solution)/shard_map/ppermute | solution.py:48
  25.9 0.6 %collective-permute-done.8.below_ref = bf16[32,128]{1,0:T(8,128)(2,1)S(1)} collective-permute-done((bf16[32,128]{1,0:T(8,128)(2,1)S(1)}, bf16[32,128]{1,0:T(8,128)(2,1)S(1)}, u32[]{:S(2)}, u32[]{:S(2)}) %collective-permute-start.8) | collective-permute-done | bytes 8224 | tf_op jit(solution)/shard_map/ppermute | solution.py:48
  26.5 0.1 collective-permute-done.7.second_ref
  26.6 0.7 %output_half.2.addend_ref = f32[8,2048]{1,0:T(8,128)S(1)} custom-call(bf16[2048,2048]{1,0:T(8,128)(2,1)S(1)} %bitcast.3, bf16[32,128]{1,0:T(8,128)(2,1)S(1)} %attend.1.own_ref.after_ref, bf16[32,128]{1,0:T(8,128)(2,1)S(1)} %collective-permute-done.7.second_ref), custom_call_target="tpu_custom_call" | custom-call | flops 1000000000 | tf_op jit(solution)/shard_map/output_half/pallas_call | solution.py:448
  27.2 0.5 %collective-permute-done.6.above_ref = bf16[32,128]{1,0:T(8,128)(2,1)S(1)} collective-permute-done((bf16[32,128]{1,0:T(8,128)(2,1)S(1)}, bf16[32,128]{1,0:T(8,128)(2,1)S(1)}, u32[]{:S(2)}, u32[]{:S(2)}) %collective-permute-start.6) | collective-permute-done | bytes 8224 | tf_op jit(solution)/shard_map/ppermute | solution.py:48
  27.7 0.7 %output_half.3 = bf16[8,2048]{1,0:T(8,128)(2,1)S(1)} custom-call(bf16[2048,2048]{1,0:T(8,128)(2,1)S(1)} %bitcast.3, bf16[32,128]{1,0:T(8,128)(2,1)S(1)} %collective-permute-done.6.above_ref, bf16[32,128]{1,0:T(8,128)(2,1)S(1)} %collective-permute-done.8.below_ref, f32[8,2048]{1,0:T(8,128)S(1)} %output_half.2.addend_ref), custom_call_target="tpu_custom_call" | custom-call | flops 1000000000 | tf_op jit(solution)/shard_map/output_half/pallas_call | solution.py:448
  28.4 1.5 %collective-permute-start.10 = (bf16[8,2048]{1,0:T(8,128)(2,1)S(1)}, bf16[8,2048]{1,0:T(8,128)(2,1)S(1)}, u32[]{:S(2)}, u32[]{:S(2)}) collective-permute-start(bf16[8,2048]{1,0:T(8,128)(2,1)S(1)} %output_half.3), channel_id=1, source_target_pairs={{0,2},{1,3},{2,0},{3,1},{4,6},{5,7},{6,4},{7,5},{8,10},{9,11},{10,... | collective-permute-start | bytes 98312 | tf_op jit(solution)/shard_map/ppermute | solution.py:43
  29.9 0.3 collective-permute-start.9
  30.3 1.3 %place.1 = bf16[1,1,512,256]{3,2,1,0:T(8,128)(2,1)} custom-call(s32[2,4,8]{2,1,0:T(4,128)S(1)} %bitcast.7, bf16[32,128]{1,0:T(8,128)(2,1)S(1)} %attend.1.own_ref.after_ref, bf16[256,256]{1,0:T(8,128)(2,1)S(1)} %get-tuple-element.19.after_ref.refs_3_.refs_0_, bf16[256,256]{1,0:T(8,128)(2,1)S(1)} %collective-permute-done.2.refs_2_.refs_1_, ...), custom_call_target="tpu_custom_call" | custom-call | flops 1000000000 | tf_op jit(solution)/shard_map/place/pallas_call | solution.py:294
  31.6 0.4 %collective-permute-done.11 = bf16[8,2048]{1,0:T(8,128)(2,1)S(1)} collective-permute-done((bf16[8,2048]{1,0:T(8,128)(2,1)S(1)}, bf16[8,2048]{1,0:T(8,128)(2,1)S(1)}, u32[]{:S(2)}, u32[]{:S(2)}) %collective-permute-start.11) | collective-permute-done | bytes 32800 | tf_op jit(solution)/shard_map/ppermute | solution.py:43
  32.1 0.4 %collective-permute-done.10 = bf16[8,2048]{1,0:T(8,128)(2,1)S(1)} collective-permute-done((bf16[8,2048]{1,0:T(8,128)(2,1)S(1)}, bf16[8,2048]{1,0:T(8,128)(2,1)S(1)}, u32[]{:S(2)}, u32[]{:S(2)}) %collective-permute-start.10) | collective-permute-done | bytes 32800 | tf_op jit(solution)/shard_map/ppermute | solution.py:43
  32.5 0.6 %add_convert_fusion = bf16[2,4,2048]{2,1,0:T(4,128)(2,1)} fusion(f32[2,4,2048]{2,1,0:T(4,128)S(1)} %reshape.11, bf16[2,4,2048]{2,1,0:T(4,128)(2,1)S(1)} %copy-done.2), kind=kLoop, calls=%fused_computation | loop fusion | flops 49152 | bytes 131072 | tf_op jit(solution)/shard_map/convert_element_type | solution.py:532
  (28 shorter events, 0.1 us)
Async XLA Ops:
  0.6 7.2 %copy-start = (bf16[2048,2048]{1,0:T(8,128)(2,1)S(1)}, bf16[2048,2048]{1,0:T(8,128)(2,1)}, u32[]{:S(2)}) copy-start(bf16[2048,2048]{1,0:T(8,128)(2,1)} %wq_ref.1) | copy-start | bytes 25165828
  0.6 7.2 %copy-start.1 = (bf16[2048,2,256]{2,1,0:T(2,128)(2,1)S(1)}, bf16[2048,2,256]{2,1,0:T(2,128)(2,1)}, u32[]{:S(2)}) copy-start(bf16[2048,2,256]{2,1,0:T(2,128)(2,1)} %wkv_ref.1) | copy-start | bytes 6291460
  0.7 7.2 %copy-start.2 = (bf16[2,4,2048]{2,1,0:T(4,128)(2,1)S(1)}, bf16[2,4,2048]{2,1,0:T(4,128)(2,1)}, u32[]{:S(2)}) copy-start(bf16[2,4,2048]{2,1,0:T(4,128)(2,1)} %hidden_ref.1) | copy-start | bytes 98308
  0.7 7.2 %copy-start.3 = (bf16[2048]{0:T(1024)(128)(2,1)S(1)}, bf16[2048]{0:T(1024)(128)(2,1)}, u32[]{:S(2)}) copy-start(bf16[2048]{0:T(1024)(128)(2,1)} %param.12) | copy-start | bytes 12292
  2.1 18.3 %copy-start.5 = (f32[8,128]{1,0:T(8,128)S(1)}, f32[8,128]{1,0:T(8,128)}, u32[]{:S(2)}) copy-start(f32[8,128]{1,0:T(8,128)} %constant.5.clone.sin_ref) | copy-start | bytes 12292
  2.1 18.3 %copy-start.6 = (f32[8,128]{1,0:T(8,128)S(1)}, f32[8,128]{1,0:T(8,128)}, u32[]{:S(2)}) copy-start(f32[8,128]{1,0:T(8,128)} %constant.4.clone.cos_ref) | copy-start | bytes 12292
  2.1 12.4 %collective-permute-start = (bf16[256,256]{1,0:T(8,128)(2,1)S(1)}, bf16[256,256]{1,0:T(8,128)(2,1)S(1)}, u32[]{:S(2)}, u32[]{:S(2)}) collective-permute-start(bf16[256,256]{1,0:T(8,128)(2,1)S(1)} %get-tuple-element.22), channel_id=1, source_target_pairs={{0,12},{4,8},{8,4},{12,0},{1,13},{5,9},{9,5},{13,1},{2,14},{6,10},... | collective-permute-start | bytes 393224 | tf_op jit(solution)/shard_map/ppermute | solution.py:43
  7.2 13.2 %collective-permute-start.1 = (bf16[256,256]{1,0:T(8,128)(2,1)S(1)}, bf16[256,256]{1,0:T(8,128)(2,1)S(1)}, u32[]{:S(2)}, u32[]{:S(2)}) collective-permute-start(bf16[256,256]{1,0:T(8,128)(2,1)S(1)} %get-tuple-element.24), channel_id=1, source_target_pairs={{0,8},{4,12},{8,0},{12,4},{1,9},{5,13},{9,1},{13,5},{2,10},{6,14},... | collective-permute-start | bytes 393224 | tf_op jit(solution)/shard_map/ppermute | solution.py:43
  7.2 13.2 %collective-permute-start.2 = (bf16[256,256]{1,0:T(8,128)(2,1)S(1)}, bf16[256,256]{1,0:T(8,128)(2,1)S(1)}, u32[]{:S(2)}, u32[]{:S(2)}) collective-permute-start(bf16[256,256]{1,0:T(8,128)(2,1)S(1)} %get-tuple-element.25), channel_id=1, source_target_pairs={{0,4},{4,0},{8,12},{12,8},{1,5},{5,1},{9,13},{13,9},{2,6},{6,2},{1... | collective-permute-start | bytes 393224 | tf_op jit(solution)/shard_map/ppermute | solution.py:43
  7.9 18.7 %slice-start = ((s8[8388608]{0:T(1024)(128)(4,1)}), s8[4194304]{0:T(1024)(128)(4,1)S(1)}, s32[]{:S(2)}) async-start(s8[8388608]{0:T(1024)(128)(4,1)} %bitcast.2), calls=%async_computation | async-start | bytes 8388608
  10.7 6.9 %collective-permute-start.3 = (f32[48,128]{1,0:T(8,128)S(1)}, f32[48,128]{1,0:T(8,128)S(1)}, u32[]{:S(2)}, u32[]{:S(2)}) collective-permute-start(f32[48,128]{1,0:T(8,128)S(1)} %get-tuple-element.26), channel_id=1, source_target_pairs={{0,12},{4,8},{8,4},{12,0},{1,13},{5,9},{9,5},{13,1},{2,14},{6,10},... | collective-permute-start | bytes 73736 | tf_op jit(solution)/shard_map/ppermute | solution.py:43
  14.5 5.9 %collective-permute-start.4 = (f32[48,128]{1,0:T(8,128)S(1)}, f32[48,128]{1,0:T(8,128)S(1)}, u32[]{:S(2)}, u32[]{:S(2)}) collective-permute-start(f32[48,128]{1,0:T(8,128)S(1)} %get-tuple-element.27), channel_id=1, source_target_pairs={{0,8},{4,12},{8,0},{12,4},{1,9},{5,13},{9,1},{13,5},{2,10},{6,14},... | collective-permute-start | bytes 73736 | tf_op jit(solution)/shard_map/ppermute | solution.py:43
  14.5 5.9 %collective-permute-start.5 = (f32[48,128]{1,0:T(8,128)S(1)}, f32[48,128]{1,0:T(8,128)S(1)}, u32[]{:S(2)}, u32[]{:S(2)}) collective-permute-start(f32[48,128]{1,0:T(8,128)S(1)} %get-tuple-element.28), channel_id=1, source_target_pairs={{0,4},{4,0},{8,12},{12,8},{1,5},{5,1},{9,13},{13,9},{2,6},{6,2},{1... | collective-permute-start | bytes 73736 | tf_op jit(solution)/shard_map/ppermute | solution.py:43
  20.4 6.2 %slice-start.1 = ((s8[8388608]{0:T(1024)(128)(4,1)}), s8[4194304]{0:T(1024)(128)(4,1)S(1)}, s32[]{:S(2)}) async-start(s8[8388608]{0:T(1024)(128)(4,1)} %bitcast.2), calls=%async_computation.1 | async-start | bytes 8388608
  21.0 9.3 %copy-start.4 = (s32[2,8,4]{1,2,0:T(4,128)S(1)}, s32[2,8,4]{1,2,0:T(4,128)}, u32[]{:S(2)}) copy-start(s32[2,8,4]{1,2,0:T(4,128)} %param.10) | copy-start | bytes 772
  21.0 5.5 %collective-permute-start.8 = (bf16[32,128]{1,0:T(8,128)(2,1)S(1)}, bf16[32,128]{1,0:T(8,128)(2,1)S(1)}, u32[]{:S(2)}, u32[]{:S(2)}) collective-permute-start(bf16[32,128]{1,0:T(8,128)(2,1)S(1)} %attend.1.own_ref.after_ref), channel_id=1, source_target_pairs={{0,4},{4,8},{8,12},{12,0},{1,5},{5,9},{9,13},{13,1},{2,6},{6,10},{... | collective-permute-start | bytes 24584 | tf_op jit(solution)/shard_map/ppermute | solution.py:48
  22.0 4.6 %collective-permute-start.7 = (bf16[32,128]{1,0:T(8,128)(2,1)S(1)}, bf16[32,128]{1,0:T(8,128)(2,1)S(1)}, u32[]{:S(2)}, u32[]{:S(2)}) collective-permute-start(bf16[32,128]{1,0:T(8,128)(2,1)S(1)} %attend.1.own_ref.after_ref), channel_id=1, source_target_pairs={{0,8},{4,12},{8,0},{12,4},{1,9},{5,13},{9,1},{13,5},{2,10},{6,14},... | collective-permute-start | bytes 24584 | tf_op jit(solution)/shard_map/ppermute | solution.py:48
  24.1 3.7 %collective-permute-start.6 = (bf16[32,128]{1,0:T(8,128)(2,1)S(1)}, bf16[32,128]{1,0:T(8,128)(2,1)S(1)}, u32[]{:S(2)}, u32[]{:S(2)}) collective-permute-start(bf16[32,128]{1,0:T(8,128)(2,1)S(1)} %attend.1.own_ref.after_ref), channel_id=1, source_target_pairs={{0,12},{4,0},{8,4},{12,8},{1,13},{5,1},{9,5},{13,9},{2,14},{6,2},{... | collective-permute-start | bytes 24584 | tf_op jit(solution)/shard_map/ppermute | solution.py:48
  28.4 3.7 %collective-permute-start.11 = (bf16[8,2048]{1,0:T(8,128)(2,1)S(1)}, bf16[8,2048]{1,0:T(8,128)(2,1)S(1)}, u32[]{:S(2)}, u32[]{:S(2)}) collective-permute-start(bf16[8,2048]{1,0:T(8,128)(2,1)S(1)} %output_half.3), channel_id=1, source_target_pairs={{0,3},{1,2},{2,1},{3,0},{4,7},{5,6},{6,5},{7,4},{8,11},{9,10},{10,... | collective-permute-start | bytes 98312 | tf_op jit(solution)/shard_map/ppermute | solution.py:43
  28.4 4.1 %collective-permute-start.10 = (bf16[8,2048]{1,0:T(8,128)(2,1)S(1)}, bf16[8,2048]{1,0:T(8,128)(2,1)S(1)}, u32[]{:S(2)}, u32[]{:S(2)}) collective-permute-start(bf16[8,2048]{1,0:T(8,128)(2,1)S(1)} %output_half.3), channel_id=1, source_target_pairs={{0,2},{1,3},{2,0},{3,1},{4,6},{5,7},{6,4},{7,5},{8,10},{9,11},{10,... | collective-permute-start | bytes 98312 | tf_op jit(solution)/shard_map/ppermute | solution.py:43
  29.9 2.5 %collective-permute-start.9 = (bf16[8,2048]{1,0:T(8,128)(2,1)S(1)}, bf16[8,2048]{1,0:T(8,128)(2,1)S(1)}, u32[]{:S(2)}, u32[]{:S(2)}) collective-permute-start(bf16[8,2048]{1,0:T(8,128)(2,1)S(1)} %output_half.3), channel_id=1, source_target_pairs={{0,1},{1,0},{2,3},{3,2},{4,5},{5,4},{6,7},{7,6},{8,9},{9,8},{10,11... | collective-permute-start | bytes 98312 | tf_op jit(solution)/shard_map/ppermute | solution.py:43

commit v19 on v18

--- a/solution.py
+++ b/solution.py
@@ -52,63 +52,63 @@
     return lax.all_to_all(outgoing, axis, split_axis=0, concat_axis=0, tiled=True)
 
 
-def picked_rows(kept_ref, cache_shape, pair, slot):
+def split_index(index, size):
+    if size & (size - 1):
+        return lax.div(index, size), lax.rem(index, size)
+    shift = jnp.full_like(index, size.bit_length() - 1)
+    return lax.shift_right_logical(index, shift), jnp.bitwise_and(index, size - 1)
+
+
+def picked_rows(kept_ref, cache_shape, pair):
     _, heads_local, source_tokens, _ = cache_shape
     source_blocks = source_tokens // BLK
     kept_count = kept_ref.shape[1]
     first_block = lax.axis_index("seq") * source_blocks
-    request = lax.div(pair, heads_local)
-    local = lax.rem(pair, heads_local)
+    request, local = split_index(pair, heads_local)
     head = lax.axis_index("head") * heads_local + local
 
     def count(k, total):
         return total + (kept_ref[request, k, head] < first_block).astype(jnp.int32)
 
     start = lax.fori_loop(0, kept_count, count, jnp.int32(0), unroll=kept_count <= 8)
-    rank = jnp.minimum(start + slot, kept_count - 1)
-    block = jnp.clip(kept_ref[request, rank, head] - first_block, 0, source_blocks - 1)
-    return request, local, pl.ds(pl.multiple_of(block * BLK, BLK), BLK)
+    places = []
+    for slot in range(MOST):
+        rank = jnp.minimum(start + slot, kept_count - 1)
+        block = jnp.clip(kept_ref[request, rank, head] - first_block, 0, source_blocks - 1)
+        places.append((request, local, pl.ds(pl.multiple_of(block * BLK, BLK), BLK)))
+    return places
 
 
 def pick_near_kernel(kept_hbm_ref, cache_ref, *refs):
     *outs, kept_ref, cache, kept_sem, sem = refs
     heads_local = cache.shape[1]
     me = lax.axis_index("seq")
-
-    def pair_copy(pair):
-        place = (lax.div(pair, heads_local), lax.rem(pair, heads_local))
-        return pltpu.make_async_copy(cache_ref.at[place], cache.at[place], sem.at[pair])
-
     kept_copy = pltpu.make_async_copy(kept_hbm_ref, kept_ref, kept_sem)
     kept_copy.start()
+
+    def pair_copy(pair):
+        place = split_index(pair, heads_local)
+        return pltpu.make_async_copy(cache_ref.at[place], cache.at[place], sem.at[pair])
+
     offsets = list(reversed(range(len(outs))))
+    copies = {offset: pair_copy(jnp.bitwise_xor(me, offset)) for offset in offsets}
     for offset in offsets:
-        pair_copy(jnp.bitwise_xor(me, offset)).start()
+        copies[offset].start()
     kept_copy.wait()
-    places = {
-        offset: [
-            picked_rows(kept_ref, cache.shape, jnp.bitwise_xor(me, offset), slot)
-            for slot in range(MOST)
-        ]
-        for offset in offsets
-    }
     for offset in offsets:
-        pair_copy(jnp.bitwise_xor(me, offset)).wait()
-        for slot, (request, local, rows) in enumerate(places[offset]):
-            out = outs[offset]
-            out[slot * BLK : (slot + 1) * BLK, :] = cache[request, local, rows, :]
+        places = picked_rows(kept_ref, cache.shape, jnp.bitwise_xor(me, offset))
+        copies[offset].wait()
+        for slot, (request, local, rows) in enumerate(places):
+            outs[offset][slot * BLK : (slot + 1) * BLK, :] = cache[request, local, rows, :]
 
 
 def pick_all_kernel(kept_hbm_ref, cache_ref, out_ref, kept_ref, sem):
     pltpu.sync_copy(kept_hbm_ref, kept_ref)
 
     def pair_body(pair, carry):
-        for slot in range(MOST):
-            request, local, rows = picked_rows(kept_ref, cache_ref.shape, pair, slot)
+        for slot, place in enumerate(picked_rows(kept_ref, cache_ref.shape, pair)):
             pltpu.make_async_copy(
-                cache_ref.at[request, local, rows],
-                out_ref.at[pair, pl.ds(slot * BLK, BLK)],
-                sem,
+                cache_ref.at[place], out_ref.at[pair, pl.ds(slot * BLK, BLK)], sem
             ).start()
         return carry
 
@@ -219,14 +219,16 @@
                 )
     if direct:
         kept_copy.wait()
-        request = lax.div(me, heads_local)
-        head = lax.axis_index("head") * heads_local + lax.rem(me, heads_local)
+        request, local = split_index(me, heads_local)
+        head = lax.axis_index("head") * heads_local + local
+        kept = [kept_ref[request, k, head] for k in range(kept_ref.shape[1])]
         column = lax.broadcasted_iota(jnp.int32, mask_ref.shape[1:], 1)
         for offset in range(mask_ref.shape[0]):
+            first_block = jnp.bitwise_xor(me, offset) * source_blocks
             filled = jnp.int32(0)
-            for k in range(kept_ref.shape[1]):
-                source = lax.div(kept_ref[request, k, head], source_blocks)
-                filled += (source == jnp.bitwise_xor(me, offset)).astype(jnp.int32)
+            for block in kept:
+                here = (block >= first_block) & (block < first_block + source_blocks)
+                filled += here.astype(jnp.int32)
             mask_ref[offset] = jnp.where(column < filled * BLK, 0.0, -jnp.inf)
 
 
@@ -272,11 +274,11 @@
     del after_ref
     *by_offset, cache_ref, sem = refs
     me = lax.axis_index("seq")
-    request = lax.div(me, heads_local)
-    head = lax.axis_index("head") * heads_local + lax.rem(me, heads_local)
+    request, local = split_index(me, heads_local)
+    head = lax.axis_index("head") * heads_local + local
     previous, slot = jnp.int32(-1), jnp.int32(0)
     for k in range(kept_ref.shape[1]):
-        source = lax.div(kept_ref[request, k, head], source_blocks)
+        source, _ = split_index(kept_ref[request, k, head], source_blocks)
         slot = jnp.where(source == previous, jnp.minimum(slot + 1, MOST - 1), 0)
         previous = source
         rows = pl.ds(pl.multiple_of(slot * BLK, BLK), BLK)
@@ -312,12 +314,12 @@
         parts_ref, blocks_ref, attended_ref, cache_ref, sem, kept = refs
         kept_count = which_ref.shape[1]
         me = lax.axis_index("seq")
-        request = lax.div(me, heads_local)
-        head = lax.axis_index("head") * heads_local + lax.rem(me, heads_local)
+        request, local = split_index(me, heads_local)
+        head = lax.axis_index("head") * heads_local + local
 
         def start_copy(k, carry):
             previous, slot = carry
-            source = lax.div(which_ref[request, k, head], source_blocks)
+            source, _ = split_index(which_ref[request, k, head], source_blocks)
             slot = jnp.where(source == previous, jnp.minimum(slot + 1, MOST - 1), 0)
             target = kept.at[pl.ds(pl.multiple_of(k * BLK, BLK), BLK)]
             rows = pl.ds(pl.multiple_of(slot * BLK, BLK), BLK)
@@ -341,7 +343,7 @@
     score = lax.dot_general(query, new_key, CONTRACT_LAST, preferred_element_type=jnp.float32)
     row = lax.broadcasted_iota(jnp.int32, score.shape, 0)
     column = lax.broadcasted_iota(jnp.int32, score.shape, 1)
-    scores = [jnp.where(column <= lax.rem(row, step_count), score * scale, -jnp.inf)]
+    scores = [jnp.where(column <= split_index(row, step_count)[1], score * scale, -jnp.inf)]
     values = [new_value]
 
     def add_block(block):

time: 33.3 us -> 33.3 us (level)
  no operation moved by 1% of the time
where the time goes in v19:
time: 33.3 us; the launch traced here: 33.1 us
  starting transfers between devices  19.4 us (58%)
  Pallas kernels  7.3 us (22%)
  waiting for transfers between devices  4.93 us (15%)
  between operations  0.78 us (2%)
  other arithmetic  0.65 us (2%)
    ppermute x9, starting transfers between devices, swap(): return lax.ppermute(outgoing, axis, [(i, i ^ offset) for i in range(count)])  14.5 us
    ppermute x3, starting transfers between devices, shift(): lax.ppermute(outgoing, axis, [(i, (i + step) % count) for i in range(coun...  4.87 us
    ppermute x9, waiting for transfers between devices, swap(): return lax.ppermute(outgoing, axis, [(i, i ^ offset) for i in range(count)])  3.72 us
    pallas_call x1, Pallas kernels, project(): pl.pallas_call(functools.partial(project_kernel, direct, source_blocks),...  2.75 us
    pallas_call x1, Pallas kernels, pick(): pl.pallas_call(pick_near_kernel if direct else pick_all_kernel, out_shape...  1.4 us
    pallas_call x1, Pallas kernels, place(): pl.pallas_call(functools.partial(place_kernel, source_blocks, heads_local...  1.32 us
    pallas_call x2, Pallas kernels, output_half(): pl.pallas_call(kernel, out_shape=jax.ShapeDtypeStruct((rows, w_out.shape[...  1.3 us
    ppermute x3, waiting for transfers between devices, shift(): lax.ppermute(outgoing, axis, [(i, (i + step) % count) for i in range(coun...  1.22 us
  transfers between devices with their start and end apart: 12, of which 6 were waited for; matrix products, arithmetic and copies ran while one was open for 0% of the time, Pallas kernels for 14%

profile of v19, /device:TPU:0, one launch (start us, length us, event | category | flops | bytes accessed | tf_op | source)
XLA Modules:
  0.0 33.1 jit_solution(8964200473010744983)
XLA Ops:
  0.7 1.4 %pick_blocks.1 = (bf16[256,256]{1,0:T(8,128)(2,1)S(1)}, bf16[256,256]{1,0:T(8,128)(2,1)S(1)}, bf16[256,256]{1,0:T(8,128)(2,1)S(1)}, bf16[256,256]{1,0:T(8,128)(2,1)S(1)}) custom-call(s32[2,4,8]{2,1,0:T(4,128)} %bitcast.5, bf16[2,2,512,256]{3,2,1,0:T(8,128)(2,1)} %cache_ref.1), custom_call_target="tpu_custom_call" | custom-call | flops 10000000000 | tf_op jit(solution)/shard_map/pick_blocks/pallas_call | solution.py:135
  2.1 5.1 %collective-permute-start = (bf16[256,256]{1,0:T(8,128)(2,1)S(1)}, bf16[256,256]{1,0:T(8,128)(2,1)S(1)}, u32[]{:S(2)}, u32[]{:S(2)}) collective-permute-start(bf16[256,256]{1,0:T(8,128)(2,1)S(1)} %get-tuple-element.22), channel_id=1, source_target_pairs={{0,12},{4,8},{8,4},{12,0},{1,13},{5,9},{9,5},{13,1},{2,14},{6,10},... | collective-permute-start | bytes 393224 | tf_op jit(solution)/shard_map/ppermute | solution.py:43
  7.2 0.6 %collective-permute-start.2 = (bf16[256,256]{1,0:T(8,128)(2,1)S(1)}, bf16[256,256]{1,0:T(8,128)(2,1)S(1)}, u32[]{:S(2)}, u32[]{:S(2)}) collective-permute-start(bf16[256,256]{1,0:T(8,128)(2,1)S(1)} %get-tuple-element.25), channel_id=1, source_target_pairs={{0,4},{4,0},{8,12},{12,8},{1,5},{5,1},{9,13},{13,9},{2,6},{6,2},{1... | collective-permute-start | bytes 393224 | tf_op jit(solution)/shard_map/ppermute | solution.py:43
  7.9 0.0 slice-start
  7.9 2.8 %project.1 = (f32[48,128]{1,0:T(8,128)S(1)}, f32[48,128]{1,0:T(8,128)S(1)}, f32[48,128]{1,0:T(8,128)S(1)}, f32[48,128]{1,0:T(8,128)S(1)}, f32[4,8,256]{2,1,0:T(8,128)S(1)}) custom-call(bf16[256,256]{1,0:T(8,128)(2,1)S(1)} %get-tuple-element.19.after_ref.refs_3_.refs_0_, bf16[2,4,2048]{2,1,0:T(4,128)(2,1)S(1)} %copy-done.2, bf16[16,128]{1,0:T(8,128)(2,1)S(1)} %bitcast.4, ...), custom_call_target="tpu_custom_call" | custom-call | flops 83886080 | bytes 10485760 | tf_op jit(solution)/shard_map/project/pallas_call | solution.py:246
  10.7 3.8 %collective-permute-start.3 = (f32[48,128]{1,0:T(8,128)S(1)}, f32[48,128]{1,0:T(8,128)S(1)}, u32[]{:S(2)}, u32[]{:S(2)}) collective-permute-start(f32[48,128]{1,0:T(8,128)S(1)} %get-tuple-element.26), channel_id=1, source_target_pairs={{0,12},{4,8},{8,4},{12,0},{1,13},{5,9},{9,5},{13,1},{2,14},{6,10},... | collective-permute-start | bytes 73736 | tf_op jit(solution)/shard_map/ppermute | solution.py:43
  14.5 3.1 %collective-permute-start.5 = (f32[48,128]{1,0:T(8,128)S(1)}, f32[48,128]{1,0:T(8,128)S(1)}, u32[]{:S(2)}, u32[]{:S(2)}) collective-permute-start(f32[48,128]{1,0:T(8,128)S(1)} %get-tuple-element.28), channel_id=1, source_target_pairs={{0,4},{4,0},{8,12},{12,8},{1,5},{5,1},{9,13},{13,9},{2,6},{6,2},{1... | collective-permute-start | bytes 73736 | tf_op jit(solution)/shard_map/ppermute | solution.py:43
  17.6 2.8 %collective-permute-done.4.refs_5_ = f32[48,128]{1,0:T(8,128)S(1)} collective-permute-done((f32[48,128]{1,0:T(8,128)S(1)}, f32[48,128]{1,0:T(8,128)S(1)}, u32[]{:S(2)}, u32[]{:S(2)}) %collective-permute-start.4) | collective-permute-done | bytes 24608 | tf_op jit(solution)/shard_map/ppermute | solution.py:43
  20.4 0.0 slice-start.1
  20.4 0.5 %attend.1.own_ref.after_ref = bf16[32,128]{1,0:T(8,128)(2,1)S(1)} custom-call(f32[4,8,256]{2,1,0:T(8,128)S(1)} %get-tuple-element.20.which_ref, f32[8,128]{1,0:T(8,128)S(1)} %copy-done.6, f32[8,128]{1,0:T(8,128)S(1)} %copy-done.5, bf16[256,256]{1,0:T(8,128)(2,1)S(1)} %collective-permute-done.refs_0_.refs_3_, ...), custom_call_target="tpu_custom_call" | custom-call | flops 10000000000 | tf_op jit(solution)/shard_map/attend/pallas_call | solution.py:398
  21.0 1.0 %collective-permute-start.8 = (bf16[32,128]{1,0:T(8,128)(2,1)S(1)}, bf16[32,128]{1,0:T(8,128)(2,1)S(1)}, u32[]{:S(2)}, u32[]{:S(2)}) collective-permute-start(bf16[32,128]{1,0:T(8,128)(2,1)S(1)} %attend.1.own_ref.after_ref), channel_id=1, source_target_pairs={{0,4},{4,8},{8,12},{12,0},{1,5},{5,9},{9,13},{13,1},{2,6},{6,10},{... | collective-permute-start | bytes 24584 | tf_op jit(solution)/shard_map/ppermute | solution.py:48
  22.0 2.1 %collective-permute-start.7 = (bf16[32,128]{1,0:T(8,128)(2,1)S(1)}, bf16[32,128]{1,0:T(8,128)(2,1)S(1)}, u32[]{:S(2)}, u32[]{:S(2)}) collective-permute-start(bf16[32,128]{1,0:T(8,128)(2,1)S(1)} %attend.1.own_ref.after_ref), channel_id=1, source_target_pairs={{0,8},{4,12},{8,0},{12,4},{1,9},{5,13},{9,1},{13,5},{2,10},{6,14},... | collective-permute-start | bytes 24584 | tf_op jit(solution)/shard_map/ppermute | solution.py:48
  24.1 1.8 %collective-permute-start.6 = (bf16[32,128]{1,0:T(8,128)(2,1)S(1)}, bf16[32,128]{1,0:T(8,128)(2,1)S(1)}, u32[]{:S(2)}, u32[]{:S(2)}) collective-permute-start(bf16[32,128]{1,0:T(8,128)(2,1)S(1)} %attend.1.own_ref.after_ref), channel_id=1, source_target_pairs={{0,12},{4,0},{8,4},{12,8},{1,13},{5,1},{9,5},{13,9},{2,14},{6,2},{... | collective-permute-start | bytes 24584 | tf_op jit(solution)/shard_map/ppermute | solution.py:48
  25.9 0.6 %collective-permute-done.8.below_ref = bf16[32,128]{1,0:T(8,128)(2,1)S(1)} collective-permute-done((bf16[32,128]{1,0:T(8,128)(2,1)S(1)}, bf16[32,128]{1,0:T(8,128)(2,1)S(1)}, u32[]{:S(2)}, u32[]{:S(2)}) %collective-permute-start.8) | collective-permute-done | bytes 8224 | tf_op jit(solution)/shard_map/ppermute | solution.py:48
  26.5 0.1 collective-permute-done.7.second_ref
  26.6 0.7 %output_half.2.addend_ref = f32[8,2048]{1,0:T(8,128)S(1)} custom-call(bf16[2048,2048]{1,0:T(8,128)(2,1)S(1)} %bitcast.3, bf16[32,128]{1,0:T(8,128)(2,1)S(1)} %attend.1.own_ref.after_ref, bf16[32,128]{1,0:T(8,128)(2,1)S(1)} %collective-permute-done.7.second_ref), custom_call_target="tpu_custom_call" | custom-call | flops 1000000000 | tf_op jit(solution)/shard_map/output_half/pallas_call | solution.py:450
  27.2 0.5 %collective-permute-done.6.above_ref = bf16[32,128]{1,0:T(8,128)(2,1)S(1)} collective-permute-done((bf16[32,128]{1,0:T(8,128)(2,1)S(1)}, bf16[32,128]{1,0:T(8,128)(2,1)S(1)}, u32[]{:S(2)}, u32[]{:S(2)}) %collective-permute-start.6) | collective-permute-done | bytes 8224 | tf_op jit(solution)/shard_map/ppermute | solution.py:48
  27.7 0.7 %output_half.3 = bf16[8,2048]{1,0:T(8,128)(2,1)S(1)} custom-call(bf16[2048,2048]{1,0:T(8,128)(2,1)S(1)} %bitcast.3, bf16[32,128]{1,0:T(8,128)(2,1)S(1)} %collective-permute-done.6.above_ref, bf16[32,128]{1,0:T(8,128)(2,1)S(1)} %collective-permute-done.8.below_ref, f32[8,2048]{1,0:T(8,128)S(1)} %output_half.2.addend_ref), custom_call_target="tpu_custom_call" | custom-call | flops 1000000000 | tf_op jit(solution)/shard_map/output_half/pallas_call | solution.py:450
  28.4 1.5 %collective-permute-start.10 = (bf16[8,2048]{1,0:T(8,128)(2,1)S(1)}, bf16[8,2048]{1,0:T(8,128)(2,1)S(1)}, u32[]{:S(2)}, u32[]{:S(2)}) collective-permute-start(bf16[8,2048]{1,0:T(8,128)(2,1)S(1)} %output_half.3), channel_id=1, source_target_pairs={{0,2},{1,3},{2,0},{3,1},{4,6},{5,7},{6,4},{7,5},{8,10},{9,11},{10,... | collective-permute-start | bytes 98312 | tf_op jit(solution)/shard_map/ppermute | solution.py:43
  29.9 0.3 collective-permute-start.9
  30.3 1.3 %place.1 = bf16[1,1,512,256]{3,2,1,0:T(8,128)(2,1)} custom-call(s32[2,4,8]{2,1,0:T(4,128)S(1)} %bitcast.7, bf16[32,128]{1,0:T(8,128)(2,1)S(1)} %attend.1.own_ref.after_ref, bf16[256,256]{1,0:T(8,128)(2,1)S(1)} %get-tuple-element.19.after_ref.refs_3_.refs_0_, bf16[256,256]{1,0:T(8,128)(2,1)S(1)} %collective-permute-done.2.refs_2_.refs_1_, ...), custom_call_target="tpu_custom_call" | custom-call | flops 1000000000 | tf_op jit(solution)/shard_map/place/pallas_call | solution.py:296
  31.6 0.5 %collective-permute-done.11 = bf16[8,2048]{1,0:T(8,128)(2,1)S(1)} collective-permute-done((bf16[8,2048]{1,0:T(8,128)(2,1)S(1)}, bf16[8,2048]{1,0:T(8,128)(2,1)S(1)}, u32[]{:S(2)}, u32[]{:S(2)}) %collective-permute-start.11) | collective-permute-done | bytes 32800 | tf_op jit(solution)/shard_map/ppermute | solution.py:43
  32.1 0.4 %collective-permute-done.10 = bf16[8,2048]{1,0:T(8,128)(2,1)S(1)} collective-permute-done((bf16[8,2048]{1,0:T(8,128)(2,1)S(1)}, bf16[8,2048]{1,0:T(8,128)(2,1)S(1)}, u32[]{:S(2)}, u32[]{:S(2)}) %collective-permute-start.10) | collective-permute-done | bytes 32800 | tf_op jit(solution)/shard_map/ppermute | solution.py:43
  32.5 0.6 %add_convert_fusion = bf16[2,4,2048]{2,1,0:T(4,128)(2,1)} fusion(f32[2,4,2048]{2,1,0:T(4,128)S(1)} %reshape.11, bf16[2,4,2048]{2,1,0:T(4,128)(2,1)S(1)} %copy-done.2), kind=kLoop, calls=%fused_computation | loop fusion | flops 49152 | bytes 131072 | tf_op jit(solution)/shard_map/convert_element_type | solution.py:534
  (28 shorter events, 0.1 us)
Async XLA Ops:
  0.6 7.2 %copy-start = (bf16[2048,2048]{1,0:T(8,128)(2,1)S(1)}, bf16[2048,2048]{1,0:T(8,128)(2,1)}, u32[]{:S(2)}) copy-start(bf16[2048,2048]{1,0:T(8,128)(2,1)} %wq_ref.1) | copy-start | bytes 25165828
  0.6 7.2 %copy-start.1 = (bf16[2048,2,256]{2,1,0:T(2,128)(2,1)S(1)}, bf16[2048,2,256]{2,1,0:T(2,128)(2,1)}, u32[]{:S(2)}) copy-start(bf16[2048,2,256]{2,1,0:T(2,128)(2,1)} %wkv_ref.1) | copy-start | bytes 6291460
  0.7 7.2 %copy-start.2 = (bf16[2,4,2048]{2,1,0:T(4,128)(2,1)S(1)}, bf16[2,4,2048]{2,1,0:T(4,128)(2,1)}, u32[]{:S(2)}) copy-start(bf16[2,4,2048]{2,1,0:T(4,128)(2,1)} %hidden_ref.1) | copy-start | bytes 98308
  0.7 7.2 %copy-start.3 = (bf16[2048]{0:T(1024)(128)(2,1)S(1)}, bf16[2048]{0:T(1024)(128)(2,1)}, u32[]{:S(2)}) copy-start(bf16[2048]{0:T(1024)(128)(2,1)} %param.12) | copy-start | bytes 12292
  2.1 18.3 %copy-start.5 = (f32[8,128]{1,0:T(8,128)S(1)}, f32[8,128]{1,0:T(8,128)}, u32[]{:S(2)}) copy-start(f32[8,128]{1,0:T(8,128)} %constant.5.clone.sin_ref) | copy-start | bytes 12292
  2.1 18.3 %copy-start.6 = (f32[8,128]{1,0:T(8,128)S(1)}, f32[8,128]{1,0:T(8,128)}, u32[]{:S(2)}) copy-start(f32[8,128]{1,0:T(8,128)} %constant.4.clone.cos_ref) | copy-start | bytes 12292
  2.1 12.4 %collective-permute-start = (bf16[256,256]{1,0:T(8,128)(2,1)S(1)}, bf16[256,256]{1,0:T(8,128)(2,1)S(1)}, u32[]{:S(2)}, u32[]{:S(2)}) collective-permute-start(bf16[256,256]{1,0:T(8,128)(2,1)S(1)} %get-tuple-element.22), channel_id=1, source_target_pairs={{0,12},{4,8},{8,4},{12,0},{1,13},{5,9},{9,5},{13,1},{2,14},{6,10},... | collective-permute-start | bytes 393224 | tf_op jit(solution)/shard_map/ppermute | solution.py:43
  7.2 13.2 %collective-permute-start.1 = (bf16[256,256]{1,0:T(8,128)(2,1)S(1)}, bf16[256,256]{1,0:T(8,128)(2,1)S(1)}, u32[]{:S(2)}, u32[]{:S(2)}) collective-permute-start(bf16[256,256]{1,0:T(8,128)(2,1)S(1)} %get-tuple-element.24), channel_id=1, source_target_pairs={{0,8},{4,12},{8,0},{12,4},{1,9},{5,13},{9,1},{13,5},{2,10},{6,14},... | collective-permute-start | bytes 393224 | tf_op jit(solution)/shard_map/ppermute | solution.py:43
  7.2 13.2 %collective-permute-start.2 = (bf16[256,256]{1,0:T(8,128)(2,1)S(1)}, bf16[256,256]{1,0:T(8,128)(2,1)S(1)}, u32[]{:S(2)}, u32[]{:S(2)}) collective-permute-start(bf16[256,256]{1,0:T(8,128)(2,1)S(1)} %get-tuple-element.25), channel_id=1, source_target_pairs={{0,4},{4,0},{8,12},{12,8},{1,5},{5,1},{9,13},{13,9},{2,6},{6,2},{1... | collective-permute-start | bytes 393224 | tf_op jit(solution)/shard_map/ppermute | solution.py:43
  7.9 18.7 %slice-start = ((s8[8388608]{0:T(1024)(128)(4,1)}), s8[4194304]{0:T(1024)(128)(4,1)S(1)}, s32[]{:S(2)}) async-start(s8[8388608]{0:T(1024)(128)(4,1)} %bitcast.2), calls=%async_computation | async-start | bytes 8388608
  10.7 6.9 %collective-permute-start.3 = (f32[48,128]{1,0:T(8,128)S(1)}, f32[48,128]{1,0:T(8,128)S(1)}, u32[]{:S(2)}, u32[]{:S(2)}) collective-permute-start(f32[48,128]{1,0:T(8,128)S(1)} %get-tuple-element.26), channel_id=1, source_target_pairs={{0,12},{4,8},{8,4},{12,0},{1,13},{5,9},{9,5},{13,1},{2,14},{6,10},... | collective-permute-start | bytes 73736 | tf_op jit(solution)/shard_map/ppermute | solution.py:43
  14.5 5.9 %collective-permute-start.4 = (f32[48,128]{1,0:T(8,128)S(1)}, f32[48,128]{1,0:T(8,128)S(1)}, u32[]{:S(2)}, u32[]{:S(2)}) collective-permute-start(f32[48,128]{1,0:T(8,128)S(1)} %get-tuple-element.27), channel_id=1, source_target_pairs={{0,8},{4,12},{8,0},{12,4},{1,9},{5,13},{9,1},{13,5},{2,10},{6,14},... | collective-permute-start | bytes 73736 | tf_op jit(solution)/shard_map/ppermute | solution.py:43
  14.5 5.9 %collective-permute-start.5 = (f32[48,128]{1,0:T(8,128)S(1)}, f32[48,128]{1,0:T(8,128)S(1)}, u32[]{:S(2)}, u32[]{:S(2)}) collective-permute-start(f32[48,128]{1,0:T(8,128)S(1)} %get-tuple-element.28), channel_id=1, source_target_pairs={{0,4},{4,0},{8,12},{12,8},{1,5},{5,1},{9,13},{13,9},{2,6},{6,2},{1... | collective-permute-start | bytes 73736 | tf_op jit(solution)/shard_map/ppermute | solution.py:43
  20.4 6.2 %slice-start.1 = ((s8[8388608]{0:T(1024)(128)(4,1)}), s8[4194304]{0:T(1024)(128)(4,1)S(1)}, s32[]{:S(2)}) async-start(s8[8388608]{0:T(1024)(128)(4,1)} %bitcast.2), calls=%async_computation.1 | async-start | bytes 8388608
  21.0 9.3 %copy-start.4 = (s32[2,8,4]{1,2,0:T(4,128)S(1)}, s32[2,8,4]{1,2,0:T(4,128)}, u32[]{:S(2)}) copy-start(s32[2,8,4]{1,2,0:T(4,128)} %param.10) | copy-start | bytes 772
  21.0 5.5 %collective-permute-start.8 = (bf16[32,128]{1,0:T(8,128)(2,1)S(1)}, bf16[32,128]{1,0:T(8,128)(2,1)S(1)}, u32[]{:S(2)}, u32[]{:S(2)}) collective-permute-start(bf16[32,128]{1,0:T(8,128)(2,1)S(1)} %attend.1.own_ref.after_ref), channel_id=1, source_target_pairs={{0,4},{4,8},{8,12},{12,0},{1,5},{5,9},{9,13},{13,1},{2,6},{6,10},{... | collective-permute-start | bytes 24584 | tf_op jit(solution)/shard_map/ppermute | solution.py:48
  22.0 4.6 %collective-permute-start.7 = (bf16[32,128]{1,0:T(8,128)(2,1)S(1)}, bf16[32,128]{1,0:T(8,128)(2,1)S(1)}, u32[]{:S(2)}, u32[]{:S(2)}) collective-permute-start(bf16[32,128]{1,0:T(8,128)(2,1)S(1)} %attend.1.own_ref.after_ref), channel_id=1, source_target_pairs={{0,8},{4,12},{8,0},{12,4},{1,9},{5,13},{9,1},{13,5},{2,10},{6,14},... | collective-permute-start | bytes 24584 | tf_op jit(solution)/shard_map/ppermute | solution.py:48
  24.1 3.7 %collective-permute-start.6 = (bf16[32,128]{1,0:T(8,128)(2,1)S(1)}, bf16[32,128]{1,0:T(8,128)(2,1)S(1)}, u32[]{:S(2)}, u32[]{:S(2)}) collective-permute-start(bf16[32,128]{1,0:T(8,128)(2,1)S(1)} %attend.1.own_ref.after_ref), channel_id=1, source_target_pairs={{0,12},{4,0},{8,4},{12,8},{1,13},{5,1},{9,5},{13,9},{2,14},{6,2},{... | collective-permute-start | bytes 24584 | tf_op jit(solution)/shard_map/ppermute | solution.py:48
  28.4 3.7 %collective-permute-start.11 = (bf16[8,2048]{1,0:T(8,128)(2,1)S(1)}, bf16[8,2048]{1,0:T(8,128)(2,1)S(1)}, u32[]{:S(2)}, u32[]{:S(2)}) collective-permute-start(bf16[8,2048]{1,0:T(8,128)(2,1)S(1)} %output_half.3), channel_id=1, source_target_pairs={{0,3},{1,2},{2,1},{3,0},{4,7},{5,6},{6,5},{7,4},{8,11},{9,10},{10,... | collective-permute-start | bytes 98312 | tf_op jit(solution)/shard_map/ppermute | solution.py:43
  28.4 4.1 %collective-permute-start.10 = (bf16[8,2048]{1,0:T(8,128)(2,1)S(1)}, bf16[8,2048]{1,0:T(8,128)(2,1)S(1)}, u32[]{:S(2)}, u32[]{:S(2)}) collective-permute-start(bf16[8,2048]{1,0:T(8,128)(2,1)S(1)} %output_half.3), channel_id=1, source_target_pairs={{0,2},{1,3},{2,0},{3,1},{4,6},{5,7},{6,4},{7,5},{8,10},{9,11},{10,... | collective-permute-start | bytes 98312 | tf_op jit(solution)/shard_map/ppermute | solution.py:43
  29.9 2.5 %collective-permute-start.9 = (bf16[8,2048]{1,0:T(8,128)(2,1)S(1)}, bf16[8,2048]{1,0:T(8,128)(2,1)S(1)}, u32[]{:S(2)}, u32[]{:S(2)}) collective-permute-start(bf16[8,2048]{1,0:T(8,128)(2,1)S(1)} %output_half.3), channel_id=1, source_target_pairs={{0,1},{1,0},{2,3},{3,2},{4,5},{5,4},{6,7},{7,6},{8,9},{9,8},{10,11... | collective-permute-start | bytes 98312 | tf_op jit(solution)/shard_map/ppermute | solution.py:43

commit v20 on v19

--- a/solution.py
+++ b/solution.py
@@ -174,9 +174,7 @@
     del after_ref
     outs = refs
     if direct:
-        kept_hbm_ref, *outs, mask_ref, kept_ref, sem = refs
-        kept_copy = pltpu.make_async_copy(kept_hbm_ref, kept_ref, sem)
-        kept_copy.start()
+        kept_ref, *outs, mask_ref = refs
     requests, step_count, width = hidden_ref.shape
     heads_local = wkv_ref.shape[1]
     row_count = requests * step_count
@@ -218,18 +216,17 @@
                     functools.partial(write_pair, out_ref, pieces)
                 )
     if direct:
-        kept_copy.wait()
         request, local = split_index(me, heads_local)
         head = lax.axis_index("head") * heads_local + local
-        kept = [kept_ref[request, k, head] for k in range(kept_ref.shape[1])]
-        column = lax.broadcasted_iota(jnp.int32, mask_ref.shape[1:], 1)
+        kept = jnp.where(request == 0, kept_ref[0], kept_ref[1]).astype(jnp.float32)
+        lane = lax.broadcasted_iota(jnp.int32, kept.shape, 1)
+        kept = jnp.sum(jnp.where(lane == head, kept, 0.0), axis=1, keepdims=True)
+        column = lax.broadcasted_iota(jnp.int32, mask_ref.shape[1:], 1).astype(jnp.float32)
         for offset in range(mask_ref.shape[0]):
-            first_block = jnp.bitwise_xor(me, offset) * source_blocks
-            filled = jnp.int32(0)
-            for block in kept:
-                here = (block >= first_block) & (block < first_block + source_blocks)
-                filled += here.astype(jnp.int32)
-            mask_ref[offset] = jnp.where(column < filled * BLK, 0.0, -jnp.inf)
+            first_block = (jnp.bitwise_xor(me, offset) * source_blocks).astype(jnp.float32)
+            here = (kept >= first_block) & (kept < first_block + source_blocks)
+            filled = jnp.sum(jnp.where(here, float(BLK), 0.0), axis=0, keepdims=True)
+            mask_ref[offset] = jnp.where(column < filled, 0.0, -jnp.inf)
 
 
 def project(after, new_hidden, norm_gain, w_query, w_keyval, kept_blocks, source_blocks, direct):
@@ -246,13 +243,8 @@
     return pl.pallas_call(
         functools.partial(project_kernel, direct, source_blocks),
         out_shape=shapes,
-        in_specs=[pl.BlockSpec(memory_space=pl.ANY)]
-        + [vmem] * 4
-        + [pl.BlockSpec(memory_space=pl.ANY)] * direct,
+        in_specs=[pl.BlockSpec(memory_space=pl.ANY)] + [vmem] * (4 + direct),
         out_specs=[vmem] * len(shapes),
-        scratch_shapes=[pltpu.SMEM(kept_blocks.shape, jnp.int32), pltpu.SemaphoreType.DMA]
-        if direct
-        else [],
         compiler_params=pltpu.CompilerParams(vmem_limit_bytes=8 * 1024 * 1024),
         cost_estimate=pl.CostEstimate(
             flops=2 * requests * step_count * weights,
@@ -266,7 +258,7 @@
         norm_gain.reshape(width // HD, HD),
         pltpu.with_memory_space_constraint(w_query, pltpu.VMEM),
         pltpu.with_memory_space_constraint(w_keyval, pltpu.VMEM),
-        *([pltpu.with_memory_space_constraint(kept_blocks, pltpu.HBM)] if direct else []),
+        *([kept_blocks] if direct else []),
     )
 
 
@@ -499,7 +491,7 @@
 
     kept_blocks = kept_blocks.transpose(0, 2, 1)
     source_blocks = source_tokens // BLK
-    direct = is_direct(seq_count) and heads_local == 2
+    direct = is_direct(seq_count) and heads_local == 2 and requests == 2
     weights = (new_hidden, norm_gain, w_query, w_keyval)
     w_out = pltpu.with_memory_space_constraint(w_out, pltpu.VMEM)
     shape = (source_blocks, heads_local, step_count, seq_count, direct)

time: 33.3 us -> 33.3 us (level)
  Pallas kernels: 7.3 us -> 6.78 us
  starting transfers between devices: 19.4 us -> 19.9 us
    pallas_call x1, Pallas kernels: 2.75 us -> 2.23 us  [project(): pl.pallas_call(functools.partial(project_kernel, direct, source_blocks),...]
    ppermute x9, starting transfers between devices: 14.5 us -> 15 us  [swap(): return lax.ppermute(outgoing, axis, [(i, i ^ offset) for i in range(count)])]
  transfers between devices with their start and end apart: 12 -> 12, of which waited for: 6 -> 6; matrix products, arithmetic and copies ran while one was open for 0% -> 0% of each run, Pallas kernels for 14% -> 13%
where the time goes in v20:
time: 33.3 us; the launch traced here: 33.1 us
  starting transfers between devices  19.9 us (60%)
  Pallas kernels  6.78 us (20%)
  waiting for transfers between devices  4.94 us (15%)
  between operations  0.78 us (2%)
  other arithmetic  0.65 us (2%)
    ppermute x9, starting transfers between devices, swap(): return lax.ppermute(outgoing, axis, [(i, i ^ offset) for i in range(count)])  15 us
    ppermute x3, starting transfers between devices, shift(): lax.ppermute(outgoing, axis, [(i, (i + step) % count) for i in range(coun...  4.87 us
    ppermute x9, waiting for transfers between devices, swap(): return lax.ppermute(outgoing, axis, [(i, i ^ offset) for i in range(count)])  3.72 us
    pallas_call x1, Pallas kernels, project(): pl.pallas_call(functools.partial(project_kernel, direct, source_blocks),...  2.23 us
    pallas_call x1, Pallas kernels, pick(): pl.pallas_call(pick_near_kernel if direct else pick_all_kernel, out_shape...  1.4 us
    pallas_call x1, Pallas kernels, place(): pl.pallas_call(functools.partial(place_kernel, source_blocks, heads_local...  1.32 us
    pallas_call x2, Pallas kernels, output_half(): pl.pallas_call(kernel, out_shape=jax.ShapeDtypeStruct((rows, w_out.shape[...  1.3 us
    ppermute x3, waiting for transfers between devices, shift(): lax.ppermute(outgoing, axis, [(i, (i + step) % count) for i in range(coun...  1.22 us
  transfers between devices with their start and end apart: 12, of which 6 were waited for; matrix products, arithmetic and copies ran while one was open for 0% of the time, Pallas kernels for 13%

profile of v20, /device:TPU:0, one launch (start us, length us, event | category | flops | bytes accessed | tf_op | source)
XLA Modules:
  0.0 33.1 jit_solution(12712281538496718778)
XLA Ops:
  0.7 1.4 %pick_blocks.1 = (bf16[256,256]{1,0:T(8,128)(2,1)S(1)}, bf16[256,256]{1,0:T(8,128)(2,1)S(1)}, bf16[256,256]{1,0:T(8,128)(2,1)S(1)}, bf16[256,256]{1,0:T(8,128)(2,1)S(1)}) custom-call(s32[2,4,8]{2,1,0:T(4,128)} %bitcast.5, bf16[2,2,512,256]{3,2,1,0:T(8,128)(2,1)} %cache_ref.1), custom_call_target="tpu_custom_call" | custom-call | flops 10000000000 | tf_op jit(solution)/shard_map/pick_blocks/pallas_call | solution.py:135
  2.1 5.1 %collective-permute-start = (bf16[256,256]{1,0:T(8,128)(2,1)S(1)}, bf16[256,256]{1,0:T(8,128)(2,1)S(1)}, u32[]{:S(2)}, u32[]{:S(2)}) collective-permute-start(bf16[256,256]{1,0:T(8,128)(2,1)S(1)} %get-tuple-element.22), channel_id=1, source_target_pairs={{0,12},{4,8},{8,4},{12,0},{1,13},{5,9},{9,5},{13,1},{2,14},{6,10},... | collective-permute-start | bytes 393224 | tf_op jit(solution)/shard_map/ppermute | solution.py:43
  7.2 0.6 %collective-permute-start.2 = (bf16[256,256]{1,0:T(8,128)(2,1)S(1)}, bf16[256,256]{1,0:T(8,128)(2,1)S(1)}, u32[]{:S(2)}, u32[]{:S(2)}) collective-permute-start(bf16[256,256]{1,0:T(8,128)(2,1)S(1)} %get-tuple-element.25), channel_id=1, source_target_pairs={{0,4},{4,0},{8,12},{12,8},{1,5},{5,1},{9,13},{13,9},{2,6},{6,2},{1... | collective-permute-start | bytes 393224 | tf_op jit(solution)/shard_map/ppermute | solution.py:43
  7.9 0.0 slice-start
  7.9 2.2 %project.1 = (f32[48,128]{1,0:T(8,128)S(1)}, f32[48,128]{1,0:T(8,128)S(1)}, f32[48,128]{1,0:T(8,128)S(1)}, f32[48,128]{1,0:T(8,128)S(1)}, f32[4,8,256]{2,1,0:T(8,128)S(1)}) custom-call(bf16[256,256]{1,0:T(8,128)(2,1)S(1)} %get-tuple-element.19.after_ref.refs_3_.refs_0_, bf16[2,4,2048]{2,1,0:T(4,128)(2,1)S(1)} %copy-done.2, bf16[16,128]{1,0:T(8,128)(2,1)S(1)} %bitcast.4, ...), custom_call_target="tpu_custom_call" | custom-call | flops 83886080 | bytes 10485760 | tf_op jit(solution)/shard_map/project/pallas_call | solution.py:243
  10.1 3.8 %collective-permute-start.3 = (f32[48,128]{1,0:T(8,128)S(1)}, f32[48,128]{1,0:T(8,128)S(1)}, u32[]{:S(2)}, u32[]{:S(2)}) collective-permute-start(f32[48,128]{1,0:T(8,128)S(1)} %get-tuple-element.26), channel_id=1, source_target_pairs={{0,12},{4,8},{8,4},{12,0},{1,13},{5,9},{9,5},{13,1},{2,14},{6,10},... | collective-permute-start | bytes 73736 | tf_op jit(solution)/shard_map/ppermute | solution.py:43
  14.0 3.6 %collective-permute-start.5 = (f32[48,128]{1,0:T(8,128)S(1)}, f32[48,128]{1,0:T(8,128)S(1)}, u32[]{:S(2)}, u32[]{:S(2)}) collective-permute-start(f32[48,128]{1,0:T(8,128)S(1)} %get-tuple-element.28), channel_id=1, source_target_pairs={{0,4},{4,0},{8,12},{12,8},{1,5},{5,1},{9,13},{13,9},{2,6},{6,2},{1... | collective-permute-start | bytes 73736 | tf_op jit(solution)/shard_map/ppermute | solution.py:43
  17.6 2.8 %collective-permute-done.4.refs_5_ = f32[48,128]{1,0:T(8,128)S(1)} collective-permute-done((f32[48,128]{1,0:T(8,128)S(1)}, f32[48,128]{1,0:T(8,128)S(1)}, u32[]{:S(2)}, u32[]{:S(2)}) %collective-permute-start.4) | collective-permute-done | bytes 24608 | tf_op jit(solution)/shard_map/ppermute | solution.py:43
  20.4 0.0 slice-start.1
  20.5 0.5 %attend.1.own_ref.after_ref = bf16[32,128]{1,0:T(8,128)(2,1)S(1)} custom-call(f32[4,8,256]{2,1,0:T(8,128)S(1)} %get-tuple-element.20.which_ref, f32[8,128]{1,0:T(8,128)S(1)} %copy-done.6, f32[8,128]{1,0:T(8,128)S(1)} %copy-done.5, bf16[256,256]{1,0:T(8,128)(2,1)S(1)} %collective-permute-done.refs_0_.refs_3_, ...), custom_call_target="tpu_custom_call" | custom-call | flops 10000000000 | tf_op jit(solution)/shard_map/attend/pallas_call | solution.py:390
  21.0 1.0 %collective-permute-start.8 = (bf16[32,128]{1,0:T(8,128)(2,1)S(1)}, bf16[32,128]{1,0:T(8,128)(2,1)S(1)}, u32[]{:S(2)}, u32[]{:S(2)}) collective-permute-start(bf16[32,128]{1,0:T(8,128)(2,1)S(1)} %attend.1.own_ref.after_ref), channel_id=1, source_target_pairs={{0,4},{4,8},{8,12},{12,0},{1,5},{5,9},{9,13},{13,1},{2,6},{6,10},{... | collective-permute-start | bytes 24584 | tf_op jit(solution)/shard_map/ppermute | solution.py:48
  22.0 2.1 %collective-permute-start.7 = (bf16[32,128]{1,0:T(8,128)(2,1)S(1)}, bf16[32,128]{1,0:T(8,128)(2,1)S(1)}, u32[]{:S(2)}, u32[]{:S(2)}) collective-permute-start(bf16[32,128]{1,0:T(8,128)(2,1)S(1)} %attend.1.own_ref.after_ref), channel_id=1, source_target_pairs={{0,8},{4,12},{8,0},{12,4},{1,9},{5,13},{9,1},{13,5},{2,10},{6,14},... | collective-permute-start | bytes 24584 | tf_op jit(solution)/shard_map/ppermute | solution.py:48
  24.1 1.8 %collective-permute-start.6 = (bf16[32,128]{1,0:T(8,128)(2,1)S(1)}, bf16[32,128]{1,0:T(8,128)(2,1)S(1)}, u32[]{:S(2)}, u32[]{:S(2)}) collective-permute-start(bf16[32,128]{1,0:T(8,128)(2,1)S(1)} %attend.1.own_ref.after_ref), channel_id=1, source_target_pairs={{0,12},{4,0},{8,4},{12,8},{1,13},{5,1},{9,5},{13,9},{2,14},{6,2},{... | collective-permute-start | bytes 24584 | tf_op jit(solution)/shard_map/ppermute | solution.py:48
  25.9 0.6 %collective-permute-done.8.below_ref = bf16[32,128]{1,0:T(8,128)(2,1)S(1)} collective-permute-done((bf16[32,128]{1,0:T(8,128)(2,1)S(1)}, bf16[32,128]{1,0:T(8,128)(2,1)S(1)}, u32[]{:S(2)}, u32[]{:S(2)}) %collective-permute-start.8) | collective-permute-done | bytes 8224 | tf_op jit(solution)/shard_map/ppermute | solution.py:48
  26.5 0.1 collective-permute-done.7.second_ref
  26.6 0.7 %output_half.2.addend_ref = f32[8,2048]{1,0:T(8,128)S(1)} custom-call(bf16[2048,2048]{1,0:T(8,128)(2,1)S(1)} %bitcast.3, bf16[32,128]{1,0:T(8,128)(2,1)S(1)} %attend.1.own_ref.after_ref, bf16[32,128]{1,0:T(8,128)(2,1)S(1)} %collective-permute-done.7.second_ref), custom_call_target="tpu_custom_call" | custom-call | flops 1000000000 | tf_op jit(solution)/shard_map/output_half/pallas_call | solution.py:442
  27.2 0.5 %collective-permute-done.6.above_ref = bf16[32,128]{1,0:T(8,128)(2,1)S(1)} collective-permute-done((bf16[32,128]{1,0:T(8,128)(2,1)S(1)}, bf16[32,128]{1,0:T(8,128)(2,1)S(1)}, u32[]{:S(2)}, u32[]{:S(2)}) %collective-permute-start.6) | collective-permute-done | bytes 8224 | tf_op jit(solution)/shard_map/ppermute | solution.py:48
  27.7 0.7 %output_half.3 = bf16[8,2048]{1,0:T(8,128)(2,1)S(1)} custom-call(bf16[2048,2048]{1,0:T(8,128)(2,1)S(1)} %bitcast.3, bf16[32,128]{1,0:T(8,128)(2,1)S(1)} %collective-permute-done.6.above_ref, bf16[32,128]{1,0:T(8,128)(2,1)S(1)} %collective-permute-done.8.below_ref, f32[8,2048]{1,0:T(8,128)S(1)} %output_half.2.addend_ref), custom_call_target="tpu_custom_call" | custom-call | flops 1000000000 | tf_op jit(solution)/shard_map/output_half/pallas_call | solution.py:442
  28.4 1.5 %collective-permute-start.10 = (bf16[8,2048]{1,0:T(8,128)(2,1)S(1)}, bf16[8,2048]{1,0:T(8,128)(2,1)S(1)}, u32[]{:S(2)}, u32[]{:S(2)}) collective-permute-start(bf16[8,2048]{1,0:T(8,128)(2,1)S(1)} %output_half.3), channel_id=1, source_target_pairs={{0,2},{1,3},{2,0},{3,1},{4,6},{5,7},{6,4},{7,5},{8,10},{9,11},{10,... | collective-permute-start | bytes 98312 | tf_op jit(solution)/shard_map/ppermute | solution.py:43
  29.9 0.3 collective-permute-start.9
  30.3 1.3 %place.1 = bf16[1,1,512,256]{3,2,1,0:T(8,128)(2,1)} custom-call(s32[2,4,8]{2,1,0:T(4,128)S(1)} %bitcast.7, bf16[32,128]{1,0:T(8,128)(2,1)S(1)} %attend.1.own_ref.after_ref, bf16[256,256]{1,0:T(8,128)(2,1)S(1)} %get-tuple-element.19.after_ref.refs_3_.refs_0_, bf16[256,256]{1,0:T(8,128)(2,1)S(1)} %collective-permute-done.2.refs_2_.refs_1_, ...), custom_call_target="tpu_custom_call" | custom-call | flops 1000000000 | tf_op jit(solution)/shard_map/place/pallas_call | solution.py:288
  31.6 0.5 %collective-permute-done.11 = bf16[8,2048]{1,0:T(8,128)(2,1)S(1)} collective-permute-done((bf16[8,2048]{1,0:T(8,128)(2,1)S(1)}, bf16[8,2048]{1,0:T(8,128)(2,1)S(1)}, u32[]{:S(2)}, u32[]{:S(2)}) %collective-permute-start.11) | collective-permute-done | bytes 32800 | tf_op jit(solution)/shard_map/ppermute | solution.py:43
  32.1 0.4 %collective-permute-done.10 = bf16[8,2048]{1,0:T(8,128)(2,1)S(1)} collective-permute-done((bf16[8,2048]{1,0:T(8,128)(2,1)S(1)}, bf16[8,2048]{1,0:T(8,128)(2,1)S(1)}, u32[]{:S(2)}, u32[]{:S(2)}) %collective-permute-start.10) | collective-permute-done | bytes 32800 | tf_op jit(solution)/shard_map/ppermute | solution.py:43
  32.5 0.6 %add_convert_fusion = bf16[2,4,2048]{2,1,0:T(4,128)(2,1)} fusion(f32[2,4,2048]{2,1,0:T(4,128)S(1)} %reshape.11, bf16[2,4,2048]{2,1,0:T(4,128)(2,1)S(1)} %copy-done.2), kind=kLoop, calls=%fused_computation | loop fusion | flops 49152 | bytes 131072 | tf_op jit(solution)/shard_map/convert_element_type | solution.py:526
  (28 shorter events, 0.1 us)
Async XLA Ops:
  0.6 7.2 %copy-start = (bf16[2048,2048]{1,0:T(8,128)(2,1)S(1)}, bf16[2048,2048]{1,0:T(8,128)(2,1)}, u32[]{:S(2)}) copy-start(bf16[2048,2048]{1,0:T(8,128)(2,1)} %wq_ref.1) | copy-start | bytes 25165828
  0.6 7.2 %copy-start.1 = (bf16[2048,2,256]{2,1,0:T(2,128)(2,1)S(1)}, bf16[2048,2,256]{2,1,0:T(2,128)(2,1)}, u32[]{:S(2)}) copy-start(bf16[2048,2,256]{2,1,0:T(2,128)(2,1)} %wkv_ref.1) | copy-start | bytes 6291460
  0.7 7.2 %copy-start.2 = (bf16[2,4,2048]{2,1,0:T(4,128)(2,1)S(1)}, bf16[2,4,2048]{2,1,0:T(4,128)(2,1)}, u32[]{:S(2)}) copy-start(bf16[2,4,2048]{2,1,0:T(4,128)(2,1)} %hidden_ref.1) | copy-start | bytes 98308
  0.7 7.2 %copy-start.3 = (bf16[2048]{0:T(1024)(128)(2,1)S(1)}, bf16[2048]{0:T(1024)(128)(2,1)}, u32[]{:S(2)}) copy-start(bf16[2048]{0:T(1024)(128)(2,1)} %param.12) | copy-start | bytes 12292
  0.7 7.2 %copy-start.4 = (s32[2,8,4]{1,2,0:T(4,128)S(1)}, s32[2,8,4]{1,2,0:T(4,128)}, u32[]{:S(2)}) copy-start(s32[2,8,4]{1,2,0:T(4,128)} %param.10) | copy-start | bytes 772
  2.1 18.3 %copy-start.5 = (f32[8,128]{1,0:T(8,128)S(1)}, f32[8,128]{1,0:T(8,128)}, u32[]{:S(2)}) copy-start(f32[8,128]{1,0:T(8,128)} %constant.5.clone.sin_ref) | copy-start | bytes 12292
  2.1 18.3 %copy-start.6 = (f32[8,128]{1,0:T(8,128)S(1)}, f32[8,128]{1,0:T(8,128)}, u32[]{:S(2)}) copy-start(f32[8,128]{1,0:T(8,128)} %constant.4.clone.cos_ref) | copy-start | bytes 12292
  2.1 11.9 %collective-permute-start = (bf16[256,256]{1,0:T(8,128)(2,1)S(1)}, bf16[256,256]{1,0:T(8,128)(2,1)S(1)}, u32[]{:S(2)}, u32[]{:S(2)}) collective-permute-start(bf16[256,256]{1,0:T(8,128)(2,1)S(1)} %get-tuple-element.22), channel_id=1, source_target_pairs={{0,12},{4,8},{8,4},{12,0},{1,13},{5,9},{9,5},{13,1},{2,14},{6,10},... | collective-permute-start | bytes 393224 | tf_op jit(solution)/shard_map/ppermute | solution.py:43
  7.2 13.2 %collective-permute-start.1 = (bf16[256,256]{1,0:T(8,128)(2,1)S(1)}, bf16[256,256]{1,0:T(8,128)(2,1)S(1)}, u32[]{:S(2)}, u32[]{:S(2)}) collective-permute-start(bf16[256,256]{1,0:T(8,128)(2,1)S(1)} %get-tuple-element.24), channel_id=1, source_target_pairs={{0,8},{4,12},{8,0},{12,4},{1,9},{5,13},{9,1},{13,5},{2,10},{6,14},... | collective-permute-start | bytes 393224 | tf_op jit(solution)/shard_map/ppermute | solution.py:43
  7.2 13.2 %collective-permute-start.2 = (bf16[256,256]{1,0:T(8,128)(2,1)S(1)}, bf16[256,256]{1,0:T(8,128)(2,1)S(1)}, u32[]{:S(2)}, u32[]{:S(2)}) collective-permute-start(bf16[256,256]{1,0:T(8,128)(2,1)S(1)} %get-tuple-element.25), channel_id=1, source_target_pairs={{0,4},{4,0},{8,12},{12,8},{1,5},{5,1},{9,13},{13,9},{2,6},{6,2},{1... | collective-permute-start | bytes 393224 | tf_op jit(solution)/shard_map/ppermute | solution.py:43
  7.9 18.7 %slice-start = ((s8[8388608]{0:T(1024)(128)(4,1)}), s8[4194304]{0:T(1024)(128)(4,1)S(1)}, s32[]{:S(2)}) async-start(s8[8388608]{0:T(1024)(128)(4,1)} %bitcast.2), calls=%async_computation | async-start | bytes 8388608
  10.1 7.4 %collective-permute-start.3 = (f32[48,128]{1,0:T(8,128)S(1)}, f32[48,128]{1,0:T(8,128)S(1)}, u32[]{:S(2)}, u32[]{:S(2)}) collective-permute-start(f32[48,128]{1,0:T(8,128)S(1)} %get-tuple-element.26), channel_id=1, source_target_pairs={{0,12},{4,8},{8,4},{12,0},{1,13},{5,9},{9,5},{13,1},{2,14},{6,10},... | collective-permute-start | bytes 73736 | tf_op jit(solution)/shard_map/ppermute | solution.py:43
  14.0 6.4 %collective-permute-start.4 = (f32[48,128]{1,0:T(8,128)S(1)}, f32[48,128]{1,0:T(8,128)S(1)}, u32[]{:S(2)}, u32[]{:S(2)}) collective-permute-start(f32[48,128]{1,0:T(8,128)S(1)} %get-tuple-element.27), channel_id=1, source_target_pairs={{0,8},{4,12},{8,0},{12,4},{1,9},{5,13},{9,1},{13,5},{2,10},{6,14},... | collective-permute-start | bytes 73736 | tf_op jit(solution)/shard_map/ppermute | solution.py:43
  14.0 6.4 %collective-permute-start.5 = (f32[48,128]{1,0:T(8,128)S(1)}, f32[48,128]{1,0:T(8,128)S(1)}, u32[]{:S(2)}, u32[]{:S(2)}) collective-permute-start(f32[48,128]{1,0:T(8,128)S(1)} %get-tuple-element.28), channel_id=1, source_target_pairs={{0,4},{4,0},{8,12},{12,8},{1,5},{5,1},{9,13},{13,9},{2,6},{6,2},{1... | collective-permute-start | bytes 73736 | tf_op jit(solution)/shard_map/ppermute | solution.py:43
  20.4 6.1 %slice-start.1 = ((s8[8388608]{0:T(1024)(128)(4,1)}), s8[4194304]{0:T(1024)(128)(4,1)S(1)}, s32[]{:S(2)}) async-start(s8[8388608]{0:T(1024)(128)(4,1)} %bitcast.2), calls=%async_computation.1 | async-start | bytes 8388608
  21.0 5.5 %collective-permute-start.8 = (bf16[32,128]{1,0:T(8,128)(2,1)S(1)}, bf16[32,128]{1,0:T(8,128)(2,1)S(1)}, u32[]{:S(2)}, u32[]{:S(2)}) collective-permute-start(bf16[32,128]{1,0:T(8,128)(2,1)S(1)} %attend.1.own_ref.after_ref), channel_id=1, source_target_pairs={{0,4},{4,8},{8,12},{12,0},{1,5},{5,9},{9,13},{13,1},{2,6},{6,10},{... | collective-permute-start | bytes 24584 | tf_op jit(solution)/shard_map/ppermute | solution.py:48
  22.0 4.6 %collective-permute-start.7 = (bf16[32,128]{1,0:T(8,128)(2,1)S(1)}, bf16[32,128]{1,0:T(8,128)(2,1)S(1)}, u32[]{:S(2)}, u32[]{:S(2)}) collective-permute-start(bf16[32,128]{1,0:T(8,128)(2,1)S(1)} %attend.1.own_ref.after_ref), channel_id=1, source_target_pairs={{0,8},{4,12},{8,0},{12,4},{1,9},{5,13},{9,1},{13,5},{2,10},{6,14},... | collective-permute-start | bytes 24584 | tf_op jit(solution)/shard_map/ppermute | solution.py:48
  24.1 3.7 %collective-permute-start.6 = (bf16[32,128]{1,0:T(8,128)(2,1)S(1)}, bf16[32,128]{1,0:T(8,128)(2,1)S(1)}, u32[]{:S(2)}, u32[]{:S(2)}) collective-permute-start(bf16[32,128]{1,0:T(8,128)(2,1)S(1)} %attend.1.own_ref.after_ref), channel_id=1, source_target_pairs={{0,12},{4,0},{8,4},{12,8},{1,13},{5,1},{9,5},{13,9},{2,14},{6,2},{... | collective-permute-start | bytes 24584 | tf_op jit(solution)/shard_map/ppermute | solution.py:48
  28.4 3.7 %collective-permute-start.11 = (bf16[8,2048]{1,0:T(8,128)(2,1)S(1)}, bf16[8,2048]{1,0:T(8,128)(2,1)S(1)}, u32[]{:S(2)}, u32[]{:S(2)}) collective-permute-start(bf16[8,2048]{1,0:T(8,128)(2,1)S(1)} %output_half.3), channel_id=1, source_target_pairs={{0,3},{1,2},{2,1},{3,0},{4,7},{5,6},{6,5},{7,4},{8,11},{9,10},{10,... | collective-permute-start | bytes 98312 | tf_op jit(solution)/shard_map/ppermute | solution.py:43
  28.4 4.1 %collective-permute-start.10 = (bf16[8,2048]{1,0:T(8,128)(2,1)S(1)}, bf16[8,2048]{1,0:T(8,128)(2,1)S(1)}, u32[]{:S(2)}, u32[]{:S(2)}) collective-permute-start(bf16[8,2048]{1,0:T(8,128)(2,1)S(1)} %output_half.3), channel_id=1, source_target_pairs={{0,2},{1,3},{2,0},{3,1},{4,6},{5,7},{6,4},{7,5},{8,10},{9,11},{10,... | collective-permute-start | bytes 98312 | tf_op jit(solution)/shard_map/ppermute | solution.py:43
  29.9 2.5 %collective-permute-start.9 = (bf16[8,2048]{1,0:T(8,128)(2,1)S(1)}, bf16[8,2048]{1,0:T(8,128)(2,1)S(1)}, u32[]{:S(2)}, u32[]{:S(2)}) collective-permute-start(bf16[8,2048]{1,0:T(8,128)(2,1)S(1)} %output_half.3), channel_id=1, source_target_pairs={{0,1},{1,0},{2,3},{3,2},{4,5},{5,4},{6,7},{7,6},{8,9},{9,8},{10,11... | collective-permute-start | bytes 98312 | tf_op jit(solution)/shard_map/ppermute | solution.py:43

commit v21 on v20

--- a/solution.py
+++ b/solution.py
@@ -81,8 +81,10 @@
 
 def pick_near_kernel(kept_hbm_ref, cache_ref, *refs):
     *outs, kept_ref, cache, kept_sem, sem = refs
-    heads_local = cache.shape[1]
+    heads_local, source_tokens = cache.shape[1:3]
+    source_blocks = source_tokens // BLK
     me = lax.axis_index("seq")
+    first_head = lax.axis_index("head") * heads_local
     kept_copy = pltpu.make_async_copy(kept_hbm_ref, kept_ref, kept_sem)
     kept_copy.start()
 
@@ -95,10 +97,26 @@
     for offset in offsets:
         copies[offset].start()
     kept_copy.wait()
+    past = float(2**30)
+    first_block = me * source_blocks
+    by_request = [kept_ref[r].astype(jnp.float32) for r in range(kept_ref.shape[0])]
+    lane = lax.broadcasted_iota(jnp.int32, by_request[0].shape, 1)
+    places = {}
     for offset in offsets:
-        places = picked_rows(kept_ref, cache.shape, jnp.bitwise_xor(me, offset))
+        request, local = split_index(jnp.bitwise_xor(me, offset), heads_local)
+        row = jnp.where(request == 0, by_request[0], by_request[1])
+        row = jnp.where(lane == first_head + local, row, past)
+        least = first_block.astype(jnp.float32)
+        places[offset] = []
+        for _ in range(MOST):
+            found = jnp.min(jnp.where(row >= least, row, past))
+            least = found + 1.0
+            block = jnp.clip(found.astype(jnp.int32) - first_block, 0, source_blocks - 1)
+            rows = pl.ds(pl.multiple_of(block * BLK, BLK), BLK)
+            places[offset].append((request, local, rows))
+    for offset in offsets:
         copies[offset].wait()
-        for slot, (request, local, rows) in enumerate(places):
+        for slot, (request, local, rows) in enumerate(places[offset]):
             outs[offset][slot * BLK : (slot + 1) * BLK, :] = cache[request, local, rows, :]
 
 
@@ -120,18 +138,17 @@
     requests, heads_local, _, row_width = source_cache.shape
     pair_count = requests * heads_local
     block = (MOST * BLK, row_width)
-    kept_scratch = pltpu.SMEM(kept_blocks.shape, jnp.int32)
     if direct:
         shapes = [jax.ShapeDtypeStruct(block, jnp.bfloat16)] * pair_count
         scratch = [
-            kept_scratch,
+            pltpu.VMEM(kept_blocks.shape, jnp.int32),
             pltpu.VMEM(source_cache.shape, jnp.bfloat16),
             pltpu.SemaphoreType.DMA,
             pltpu.SemaphoreType.DMA((pair_count,)),
         ]
     else:
         shapes = [jax.ShapeDtypeStruct((pair_count,) + block, jnp.bfloat16)]
-        scratch = [kept_scratch, pltpu.SemaphoreType.DMA]
+        scratch = [pltpu.SMEM(kept_blocks.shape, jnp.int32), pltpu.SemaphoreType.DMA]
     return pl.pallas_call(
         pick_near_kernel if direct else pick_all_kernel,
         out_shape=shapes,

time: 33.3 us -> 33.4 us (level)
  no operation moved by 1% of the time
where the time goes in v21:
time: 33.4 us; the launch traced here: 33.3 us
  starting transfers between devices  19.9 us (60%)
  Pallas kernels  6.92 us (21%)
  waiting for transfers between devices  4.94 us (15%)
  between operations  0.78 us (2%)
  other arithmetic  0.65 us (2%)
    ppermute x9, starting transfers between devices, swap(): return lax.ppermute(outgoing, axis, [(i, i ^ offset) for i in range(count)])  15 us
    ppermute x3, starting transfers between devices, shift(): lax.ppermute(outgoing, axis, [(i, (i + step) % count) for i in range(coun...  4.87 us
    ppermute x9, waiting for transfers between devices, swap(): return lax.ppermute(outgoing, axis, [(i, i ^ offset) for i in range(count)])  3.72 us
    pallas_call x1, Pallas kernels, project(): pl.pallas_call(functools.partial(project_kernel, direct, source_blocks),...  2.23 us
    pallas_call x1, Pallas kernels, pick(): pl.pallas_call(pick_near_kernel if direct else pick_all_kernel, out_shape...  1.54 us
    pallas_call x1, Pallas kernels, place(): pl.pallas_call(functools.partial(place_kernel, source_blocks, heads_local...  1.32 us
    pallas_call x2, Pallas kernels, output_half(): pl.pallas_call(kernel, out_shape=jax.ShapeDtypeStruct((rows, w_out.shape[...  1.3 us
    ppermute x3, waiting for transfers between devices, shift(): lax.ppermute(outgoing, axis, [(i, (i + step) % count) for i in range(coun...  1.22 us
  transfers between devices with their start and end apart: 12, of which 6 were waited for; matrix products, arithmetic and copies ran while one was open for 0% of the time, Pallas kernels for 13%

profile of v21, /device:TPU:0, one launch (start us, length us, event | category | flops | bytes accessed | tf_op | source)
XLA Modules:
  0.0 33.3 jit_solution(4342002811934072349)
XLA Ops:
  0.7 1.5 %pick_blocks.1 = (bf16[256,256]{1,0:T(8,128)(2,1)S(1)}, bf16[256,256]{1,0:T(8,128)(2,1)S(1)}, bf16[256,256]{1,0:T(8,128)(2,1)S(1)}, bf16[256,256]{1,0:T(8,128)(2,1)S(1)}) custom-call(s32[2,4,8]{2,1,0:T(4,128)} %bitcast.5, bf16[2,2,512,256]{3,2,1,0:T(8,128)(2,1)} %cache_ref.1), custom_call_target="tpu_custom_call" | custom-call | flops 10000000000 | tf_op jit(solution)/shard_map/pick_blocks/pallas_call | solution.py:152
  2.3 5.1 %collective-permute-start = (bf16[256,256]{1,0:T(8,128)(2,1)S(1)}, bf16[256,256]{1,0:T(8,128)(2,1)S(1)}, u32[]{:S(2)}, u32[]{:S(2)}) collective-permute-start(bf16[256,256]{1,0:T(8,128)(2,1)S(1)} %get-tuple-element.22), channel_id=1, source_target_pairs={{0,12},{4,8},{8,4},{12,0},{1,13},{5,9},{9,5},{13,1},{2,14},{6,10},... | collective-permute-start | bytes 393224 | tf_op jit(solution)/shard_map/ppermute | solution.py:43
  7.4 0.6 %collective-permute-start.2 = (bf16[256,256]{1,0:T(8,128)(2,1)S(1)}, bf16[256,256]{1,0:T(8,128)(2,1)S(1)}, u32[]{:S(2)}, u32[]{:S(2)}) collective-permute-start(bf16[256,256]{1,0:T(8,128)(2,1)S(1)} %get-tuple-element.25), channel_id=1, source_target_pairs={{0,4},{4,0},{8,12},{12,8},{1,5},{5,1},{9,13},{13,9},{2,6},{6,2},{1... | collective-permute-start | bytes 393224 | tf_op jit(solution)/shard_map/ppermute | solution.py:43
  8.0 0.0 slice-start
  8.0 2.2 %project.1 = (f32[48,128]{1,0:T(8,128)S(1)}, f32[48,128]{1,0:T(8,128)S(1)}, f32[48,128]{1,0:T(8,128)S(1)}, f32[48,128]{1,0:T(8,128)S(1)}, f32[4,8,256]{2,1,0:T(8,128)S(1)}) custom-call(bf16[256,256]{1,0:T(8,128)(2,1)S(1)} %get-tuple-element.19.after_ref.refs_3_.refs_0_, bf16[2,4,2048]{2,1,0:T(4,128)(2,1)S(1)} %copy-done.2, bf16[16,128]{1,0:T(8,128)(2,1)S(1)} %bitcast.4, ...), custom_call_target="tpu_custom_call" | custom-call | flops 83886080 | bytes 10485760 | tf_op jit(solution)/shard_map/project/pallas_call | solution.py:260
  10.3 3.8 %collective-permute-start.3 = (f32[48,128]{1,0:T(8,128)S(1)}, f32[48,128]{1,0:T(8,128)S(1)}, u32[]{:S(2)}, u32[]{:S(2)}) collective-permute-start(f32[48,128]{1,0:T(8,128)S(1)} %get-tuple-element.26), channel_id=1, source_target_pairs={{0,12},{4,8},{8,4},{12,0},{1,13},{5,9},{9,5},{13,1},{2,14},{6,10},... | collective-permute-start | bytes 73736 | tf_op jit(solution)/shard_map/ppermute | solution.py:43
  14.1 3.6 %collective-permute-start.5 = (f32[48,128]{1,0:T(8,128)S(1)}, f32[48,128]{1,0:T(8,128)S(1)}, u32[]{:S(2)}, u32[]{:S(2)}) collective-permute-start(f32[48,128]{1,0:T(8,128)S(1)} %get-tuple-element.28), channel_id=1, source_target_pairs={{0,4},{4,0},{8,12},{12,8},{1,5},{5,1},{9,13},{13,9},{2,6},{6,2},{1... | collective-permute-start | bytes 73736 | tf_op jit(solution)/shard_map/ppermute | solution.py:43
  17.7 2.8 %collective-permute-done.4.refs_5_ = f32[48,128]{1,0:T(8,128)S(1)} collective-permute-done((f32[48,128]{1,0:T(8,128)S(1)}, f32[48,128]{1,0:T(8,128)S(1)}, u32[]{:S(2)}, u32[]{:S(2)}) %collective-permute-start.4) | collective-permute-done | bytes 24608 | tf_op jit(solution)/shard_map/ppermute | solution.py:43
  20.6 0.0 slice-start.1
  20.6 0.5 %attend.1.own_ref.after_ref = bf16[32,128]{1,0:T(8,128)(2,1)S(1)} custom-call(f32[4,8,256]{2,1,0:T(8,128)S(1)} %get-tuple-element.20.which_ref, f32[8,128]{1,0:T(8,128)S(1)} %copy-done.6, f32[8,128]{1,0:T(8,128)S(1)} %copy-done.5, bf16[256,256]{1,0:T(8,128)(2,1)S(1)} %collective-permute-done.refs_0_.refs_3_, ...), custom_call_target="tpu_custom_call" | custom-call | flops 10000000000 | tf_op jit(solution)/shard_map/attend/pallas_call | solution.py:407
  21.1 1.0 %collective-permute-start.8 = (bf16[32,128]{1,0:T(8,128)(2,1)S(1)}, bf16[32,128]{1,0:T(8,128)(2,1)S(1)}, u32[]{:S(2)}, u32[]{:S(2)}) collective-permute-start(bf16[32,128]{1,0:T(8,128)(2,1)S(1)} %attend.1.own_ref.after_ref), channel_id=1, source_target_pairs={{0,4},{4,8},{8,12},{12,0},{1,5},{5,9},{9,13},{13,1},{2,6},{6,10},{... | collective-permute-start | bytes 24584 | tf_op jit(solution)/shard_map/ppermute | solution.py:48
  22.1 2.1 %collective-permute-start.7 = (bf16[32,128]{1,0:T(8,128)(2,1)S(1)}, bf16[32,128]{1,0:T(8,128)(2,1)S(1)}, u32[]{:S(2)}, u32[]{:S(2)}) collective-permute-start(bf16[32,128]{1,0:T(8,128)(2,1)S(1)} %attend.1.own_ref.after_ref), channel_id=1, source_target_pairs={{0,8},{4,12},{8,0},{12,4},{1,9},{5,13},{9,1},{13,5},{2,10},{6,14},... | collective-permute-start | bytes 24584 | tf_op jit(solution)/shard_map/ppermute | solution.py:48
  24.2 1.8 %collective-permute-start.6 = (bf16[32,128]{1,0:T(8,128)(2,1)S(1)}, bf16[32,128]{1,0:T(8,128)(2,1)S(1)}, u32[]{:S(2)}, u32[]{:S(2)}) collective-permute-start(bf16[32,128]{1,0:T(8,128)(2,1)S(1)} %attend.1.own_ref.after_ref), channel_id=1, source_target_pairs={{0,12},{4,0},{8,4},{12,8},{1,13},{5,1},{9,5},{13,9},{2,14},{6,2},{... | collective-permute-start | bytes 24584 | tf_op jit(solution)/shard_map/ppermute | solution.py:48
  26.0 0.6 %collective-permute-done.8.below_ref = bf16[32,128]{1,0:T(8,128)(2,1)S(1)} collective-permute-done((bf16[32,128]{1,0:T(8,128)(2,1)S(1)}, bf16[32,128]{1,0:T(8,128)(2,1)S(1)}, u32[]{:S(2)}, u32[]{:S(2)}) %collective-permute-start.8) | collective-permute-done | bytes 8224 | tf_op jit(solution)/shard_map/ppermute | solution.py:48
  26.6 0.1 collective-permute-done.7.second_ref
  26.7 0.7 %output_half.2.addend_ref = f32[8,2048]{1,0:T(8,128)S(1)} custom-call(bf16[2048,2048]{1,0:T(8,128)(2,1)S(1)} %bitcast.3, bf16[32,128]{1,0:T(8,128)(2,1)S(1)} %attend.1.own_ref.after_ref, bf16[32,128]{1,0:T(8,128)(2,1)S(1)} %collective-permute-done.7.second_ref), custom_call_target="tpu_custom_call" | custom-call | flops 1000000000 | tf_op jit(solution)/shard_map/output_half/pallas_call | solution.py:459
  27.4 0.5 %collective-permute-done.6.above_ref = bf16[32,128]{1,0:T(8,128)(2,1)S(1)} collective-permute-done((bf16[32,128]{1,0:T(8,128)(2,1)S(1)}, bf16[32,128]{1,0:T(8,128)(2,1)S(1)}, u32[]{:S(2)}, u32[]{:S(2)}) %collective-permute-start.6) | collective-permute-done | bytes 8224 | tf_op jit(solution)/shard_map/ppermute | solution.py:48
  27.9 0.7 %output_half.3 = bf16[8,2048]{1,0:T(8,128)(2,1)S(1)} custom-call(bf16[2048,2048]{1,0:T(8,128)(2,1)S(1)} %bitcast.3, bf16[32,128]{1,0:T(8,128)(2,1)S(1)} %collective-permute-done.6.above_ref, bf16[32,128]{1,0:T(8,128)(2,1)S(1)} %collective-permute-done.8.below_ref, f32[8,2048]{1,0:T(8,128)S(1)} %output_half.2.addend_ref), custom_call_target="tpu_custom_call" | custom-call | flops 1000000000 | tf_op jit(solution)/shard_map/output_half/pallas_call | solution.py:459
  28.5 1.5 %collective-permute-start.10 = (bf16[8,2048]{1,0:T(8,128)(2,1)S(1)}, bf16[8,2048]{1,0:T(8,128)(2,1)S(1)}, u32[]{:S(2)}, u32[]{:S(2)}) collective-permute-start(bf16[8,2048]{1,0:T(8,128)(2,1)S(1)} %output_half.3), channel_id=1, source_target_pairs={{0,2},{1,3},{2,0},{3,1},{4,6},{5,7},{6,4},{7,5},{8,10},{9,11},{10,... | collective-permute-start | bytes 98312 | tf_op jit(solution)/shard_map/ppermute | solution.py:43
  30.1 0.3 collective-permute-start.9
  30.4 1.3 %place.1 = bf16[1,1,512,256]{3,2,1,0:T(8,128)(2,1)} custom-call(s32[2,4,8]{2,1,0:T(4,128)S(1)} %bitcast.7, bf16[32,128]{1,0:T(8,128)(2,1)S(1)} %attend.1.own_ref.after_ref, bf16[256,256]{1,0:T(8,128)(2,1)S(1)} %get-tuple-element.19.after_ref.refs_3_.refs_0_, bf16[256,256]{1,0:T(8,128)(2,1)S(1)} %collective-permute-done.2.refs_2_.refs_1_, ...), custom_call_target="tpu_custom_call" | custom-call | flops 1000000000 | tf_op jit(solution)/shard_map/place/pallas_call | solution.py:305
  31.7 0.5 %collective-permute-done.11 = bf16[8,2048]{1,0:T(8,128)(2,1)S(1)} collective-permute-done((bf16[8,2048]{1,0:T(8,128)(2,1)S(1)}, bf16[8,2048]{1,0:T(8,128)(2,1)S(1)}, u32[]{:S(2)}, u32[]{:S(2)}) %collective-permute-start.11) | collective-permute-done | bytes 32800 | tf_op jit(solution)/shard_map/ppermute | solution.py:43
  32.2 0.4 %collective-permute-done.10 = bf16[8,2048]{1,0:T(8,128)(2,1)S(1)} collective-permute-done((bf16[8,2048]{1,0:T(8,128)(2,1)S(1)}, bf16[8,2048]{1,0:T(8,128)(2,1)S(1)}, u32[]{:S(2)}, u32[]{:S(2)}) %collective-permute-start.10) | collective-permute-done | bytes 32800 | tf_op jit(solution)/shard_map/ppermute | solution.py:43
  32.6 0.6 %add_convert_fusion = bf16[2,4,2048]{2,1,0:T(4,128)(2,1)} fusion(f32[2,4,2048]{2,1,0:T(4,128)S(1)} %reshape.11, bf16[2,4,2048]{2,1,0:T(4,128)(2,1)S(1)} %copy-done.2), kind=kLoop, calls=%fused_computation | loop fusion | flops 49152 | bytes 131072 | tf_op jit(solution)/shard_map/convert_element_type | solution.py:543
  (28 shorter events, 0.1 us)
Async XLA Ops:
  0.6 7.4 %copy-start = (bf16[2048,2048]{1,0:T(8,128)(2,1)S(1)}, bf16[2048,2048]{1,0:T(8,128)(2,1)}, u32[]{:S(2)}) copy-start(bf16[2048,2048]{1,0:T(8,128)(2,1)} %wq_ref.1) | copy-start | bytes 25165828
  0.6 7.4 %copy-start.1 = (bf16[2048,2,256]{2,1,0:T(2,128)(2,1)S(1)}, bf16[2048,2,256]{2,1,0:T(2,128)(2,1)}, u32[]{:S(2)}) copy-start(bf16[2048,2,256]{2,1,0:T(2,128)(2,1)} %wkv_ref.1) | copy-start | bytes 6291460
  0.7 7.4 %copy-start.2 = (bf16[2,4,2048]{2,1,0:T(4,128)(2,1)S(1)}, bf16[2,4,2048]{2,1,0:T(4,128)(2,1)}, u32[]{:S(2)}) copy-start(bf16[2,4,2048]{2,1,0:T(4,128)(2,1)} %hidden_ref.1) | copy-start | bytes 98308
  0.7 7.4 %copy-start.3 = (bf16[2048]{0:T(1024)(128)(2,1)S(1)}, bf16[2048]{0:T(1024)(128)(2,1)}, u32[]{:S(2)}) copy-start(bf16[2048]{0:T(1024)(128)(2,1)} %param.12) | copy-start | bytes 12292
  0.7 7.4 %copy-start.4 = (s32[2,8,4]{1,2,0:T(4,128)S(1)}, s32[2,8,4]{1,2,0:T(4,128)}, u32[]{:S(2)}) copy-start(s32[2,8,4]{1,2,0:T(4,128)} %param.10) | copy-start | bytes 772
  2.2 18.3 %copy-start.5 = (f32[8,128]{1,0:T(8,128)S(1)}, f32[8,128]{1,0:T(8,128)}, u32[]{:S(2)}) copy-start(f32[8,128]{1,0:T(8,128)} %constant.5.clone.sin_ref) | copy-start | bytes 12292
  2.2 18.3 %copy-start.6 = (f32[8,128]{1,0:T(8,128)S(1)}, f32[8,128]{1,0:T(8,128)}, u32[]{:S(2)}) copy-start(f32[8,128]{1,0:T(8,128)} %constant.4.clone.cos_ref) | copy-start | bytes 12292
  2.3 11.9 %collective-permute-start = (bf16[256,256]{1,0:T(8,128)(2,1)S(1)}, bf16[256,256]{1,0:T(8,128)(2,1)S(1)}, u32[]{:S(2)}, u32[]{:S(2)}) collective-permute-start(bf16[256,256]{1,0:T(8,128)(2,1)S(1)} %get-tuple-element.22), channel_id=1, source_target_pairs={{0,12},{4,8},{8,4},{12,0},{1,13},{5,9},{9,5},{13,1},{2,14},{6,10},... | collective-permute-start | bytes 393224 | tf_op jit(solution)/shard_map/ppermute | solution.py:43
  7.4 13.2 %collective-permute-start.1 = (bf16[256,256]{1,0:T(8,128)(2,1)S(1)}, bf16[256,256]{1,0:T(8,128)(2,1)S(1)}, u32[]{:S(2)}, u32[]{:S(2)}) collective-permute-start(bf16[256,256]{1,0:T(8,128)(2,1)S(1)} %get-tuple-element.24), channel_id=1, source_target_pairs={{0,8},{4,12},{8,0},{12,4},{1,9},{5,13},{9,1},{13,5},{2,10},{6,14},... | collective-permute-start | bytes 393224 | tf_op jit(solution)/shard_map/ppermute | solution.py:43
  7.4 13.2 %collective-permute-start.2 = (bf16[256,256]{1,0:T(8,128)(2,1)S(1)}, bf16[256,256]{1,0:T(8,128)(2,1)S(1)}, u32[]{:S(2)}, u32[]{:S(2)}) collective-permute-start(bf16[256,256]{1,0:T(8,128)(2,1)S(1)} %get-tuple-element.25), channel_id=1, source_target_pairs={{0,4},{4,0},{8,12},{12,8},{1,5},{5,1},{9,13},{13,9},{2,6},{6,2},{1... | collective-permute-start | bytes 393224 | tf_op jit(solution)/shard_map/ppermute | solution.py:43
  8.0 18.7 %slice-start = ((s8[8388608]{0:T(1024)(128)(4,1)}), s8[4194304]{0:T(1024)(128)(4,1)S(1)}, s32[]{:S(2)}) async-start(s8[8388608]{0:T(1024)(128)(4,1)} %bitcast.2), calls=%async_computation | async-start | bytes 8388608
  10.3 7.4 %collective-permute-start.3 = (f32[48,128]{1,0:T(8,128)S(1)}, f32[48,128]{1,0:T(8,128)S(1)}, u32[]{:S(2)}, u32[]{:S(2)}) collective-permute-start(f32[48,128]{1,0:T(8,128)S(1)} %get-tuple-element.26), channel_id=1, source_target_pairs={{0,12},{4,8},{8,4},{12,0},{1,13},{5,9},{9,5},{13,1},{2,14},{6,10},... | collective-permute-start | bytes 73736 | tf_op jit(solution)/shard_map/ppermute | solution.py:43
  14.1 6.4 %collective-permute-start.4 = (f32[48,128]{1,0:T(8,128)S(1)}, f32[48,128]{1,0:T(8,128)S(1)}, u32[]{:S(2)}, u32[]{:S(2)}) collective-permute-start(f32[48,128]{1,0:T(8,128)S(1)} %get-tuple-element.27), channel_id=1, source_target_pairs={{0,8},{4,12},{8,0},{12,4},{1,9},{5,13},{9,1},{13,5},{2,10},{6,14},... | collective-permute-start | bytes 73736 | tf_op jit(solution)/shard_map/ppermute | solution.py:43
  14.1 6.4 %collective-permute-start.5 = (f32[48,128]{1,0:T(8,128)S(1)}, f32[48,128]{1,0:T(8,128)S(1)}, u32[]{:S(2)}, u32[]{:S(2)}) collective-permute-start(f32[48,128]{1,0:T(8,128)S(1)} %get-tuple-element.28), channel_id=1, source_target_pairs={{0,4},{4,0},{8,12},{12,8},{1,5},{5,1},{9,13},{13,9},{2,6},{6,2},{1... | collective-permute-start | bytes 73736 | tf_op jit(solution)/shard_map/ppermute | solution.py:43
  20.6 6.1 %slice-start.1 = ((s8[8388608]{0:T(1024)(128)(4,1)}), s8[4194304]{0:T(1024)(128)(4,1)S(1)}, s32[]{:S(2)}) async-start(s8[8388608]{0:T(1024)(128)(4,1)} %bitcast.2), calls=%async_computation.1 | async-start | bytes 8388608
  21.1 5.5 %collective-permute-start.8 = (bf16[32,128]{1,0:T(8,128)(2,1)S(1)}, bf16[32,128]{1,0:T(8,128)(2,1)S(1)}, u32[]{:S(2)}, u32[]{:S(2)}) collective-permute-start(bf16[32,128]{1,0:T(8,128)(2,1)S(1)} %attend.1.own_ref.after_ref), channel_id=1, source_target_pairs={{0,4},{4,8},{8,12},{12,0},{1,5},{5,9},{9,13},{13,1},{2,6},{6,10},{... | collective-permute-start | bytes 24584 | tf_op jit(solution)/shard_map/ppermute | solution.py:48
  22.1 4.6 %collective-permute-start.7 = (bf16[32,128]{1,0:T(8,128)(2,1)S(1)}, bf16[32,128]{1,0:T(8,128)(2,1)S(1)}, u32[]{:S(2)}, u32[]{:S(2)}) collective-permute-start(bf16[32,128]{1,0:T(8,128)(2,1)S(1)} %attend.1.own_ref.after_ref), channel_id=1, source_target_pairs={{0,8},{4,12},{8,0},{12,4},{1,9},{5,13},{9,1},{13,5},{2,10},{6,14},... | collective-permute-start | bytes 24584 | tf_op jit(solution)/shard_map/ppermute | solution.py:48
  24.2 3.7 %collective-permute-start.6 = (bf16[32,128]{1,0:T(8,128)(2,1)S(1)}, bf16[32,128]{1,0:T(8,128)(2,1)S(1)}, u32[]{:S(2)}, u32[]{:S(2)}) collective-permute-start(bf16[32,128]{1,0:T(8,128)(2,1)S(1)} %attend.1.own_ref.after_ref), channel_id=1, source_target_pairs={{0,12},{4,0},{8,4},{12,8},{1,13},{5,1},{9,5},{13,9},{2,14},{6,2},{... | collective-permute-start | bytes 24584 | tf_op jit(solution)/shard_map/ppermute | solution.py:48
  28.5 3.7 %collective-permute-start.11 = (bf16[8,2048]{1,0:T(8,128)(2,1)S(1)}, bf16[8,2048]{1,0:T(8,128)(2,1)S(1)}, u32[]{:S(2)}, u32[]{:S(2)}) collective-permute-start(bf16[8,2048]{1,0:T(8,128)(2,1)S(1)} %output_half.3), channel_id=1, source_target_pairs={{0,3},{1,2},{2,1},{3,0},{4,7},{5,6},{6,5},{7,4},{8,11},{9,10},{10,... | collective-permute-start | bytes 98312 | tf_op jit(solution)/shard_map/ppermute | solution.py:43
  28.5 4.1 %collective-permute-start.10 = (bf16[8,2048]{1,0:T(8,128)(2,1)S(1)}, bf16[8,2048]{1,0:T(8,128)(2,1)S(1)}, u32[]{:S(2)}, u32[]{:S(2)}) collective-permute-start(bf16[8,2048]{1,0:T(8,128)(2,1)S(1)} %output_half.3), channel_id=1, source_target_pairs={{0,2},{1,3},{2,0},{3,1},{4,6},{5,7},{6,4},{7,5},{8,10},{9,11},{10,... | collective-permute-start | bytes 98312 | tf_op jit(solution)/shard_map/ppermute | solution.py:43
  30.1 2.5 %collective-permute-start.9 = (bf16[8,2048]{1,0:T(8,128)(2,1)S(1)}, bf16[8,2048]{1,0:T(8,128)(2,1)S(1)}, u32[]{:S(2)}, u32[]{:S(2)}) collective-permute-start(bf16[8,2048]{1,0:T(8,128)(2,1)S(1)} %output_half.3), channel_id=1, source_target_pairs={{0,1},{1,0},{2,3},{3,2},{4,5},{5,4},{6,7},{7,6},{8,9},{9,8},{10,11... | collective-permute-start | bytes 98312 | tf_op jit(solution)/shard_map/ppermute | solution.py:43

commit v22 on v20

--- a/solution.py
+++ b/solution.py
@@ -15,6 +15,7 @@
 BLK = 128
 MOST = 2
 ROPE_BASE = 500000.0
+TERM_ORDER = (2, 3, 1, 0)
 EPS = 1e-05
 
 CONTRACT_LAST = (((1,), (1,)), ((), ()))
@@ -502,7 +503,8 @@
         blocks = [blocks[0]] + [swap(blocks[k], "seq", k) for k in partners]
         parts[1], blocks[3] = lax.optimization_barrier((parts[1], blocks[3]))
         parts = [parts[0]] + [swap(parts[k], "seq", k) for k in partners]
-        (attended,) = attend(mask, blocks[::-1] + parts[::-1], *shape)
+        arrivals = blocks[::-1] + [parts[k] for k in TERM_ORDER]
+        (attended,) = attend(mask, arrivals, *shape)
         kept_cache = place(kept_blocks, attended, blocks, source_blocks, heads_local)
         below, second, above = [shift(attended, "seq", step) for step in (1, 2, -1)]
         second, below = lax.optimization_barrier((second, below))

time: 33.3 us -> 33.1 us (level)
  no operation moved by 1% of the time
where the time goes in v22:
time: 33.1 us; the launch traced here: 33 us
  starting transfers between devices  20.1 us (61%)
  Pallas kernels  6.78 us (20%)
  waiting for transfers between devices  4.61 us (14%)
  between operations  0.78 us (2%)
  other arithmetic  0.65 us (2%)
    ppermute x9, starting transfers between devices, swap(): return lax.ppermute(outgoing, axis, [(i, i ^ offset) for i in range(count)])  15 us
    ppermute x3, starting transfers between devices, shift(): lax.ppermute(outgoing, axis, [(i, (i + step) % count) for i in range(coun...  5.06 us
    ppermute x9, waiting for transfers between devices, swap(): return lax.ppermute(outgoing, axis, [(i, i ^ offset) for i in range(count)])  3.54 us
    pallas_call x1, Pallas kernels, project(): pl.pallas_call(functools.partial(project_kernel, direct, source_blocks),...  2.23 us
    pallas_call x1, Pallas kernels, pick(): pl.pallas_call(pick_near_kernel if direct else pick_all_kernel, out_shape...  1.4 us
    pallas_call x1, Pallas kernels, place(): pl.pallas_call(functools.partial(place_kernel, source_blocks, heads_local...  1.32 us
    pallas_call x2, Pallas kernels, output_half(): pl.pallas_call(kernel, out_shape=jax.ShapeDtypeStruct((rows, w_out.shape[...  1.3 us
    ppermute x3, waiting for transfers between devices, shift(): lax.ppermute(outgoing, axis, [(i, (i + step) % count) for i in range(coun...  1.07 us
  transfers between devices with their start and end apart: 12, of which 6 were waited for; matrix products, arithmetic and copies ran while one was open for 0% of the time, Pallas kernels for 13%

profile of v22, /device:TPU:0, one launch (start us, length us, event | category | flops | bytes accessed | tf_op | source)
XLA Modules:
  0.0 33.0 jit_solution(1604462513169249583)
XLA Ops:
  0.7 1.4 %pick_blocks.1 = (bf16[256,256]{1,0:T(8,128)(2,1)S(1)}, bf16[256,256]{1,0:T(8,128)(2,1)S(1)}, bf16[256,256]{1,0:T(8,128)(2,1)S(1)}, bf16[256,256]{1,0:T(8,128)(2,1)S(1)}) custom-call(s32[2,4,8]{2,1,0:T(4,128)} %bitcast.5, bf16[2,2,512,256]{3,2,1,0:T(8,128)(2,1)} %cache_ref.1), custom_call_target="tpu_custom_call" | custom-call | flops 10000000000 | tf_op jit(solution)/shard_map/pick_blocks/pallas_call | solution.py:136
  2.1 5.1 %collective-permute-start = (bf16[256,256]{1,0:T(8,128)(2,1)S(1)}, bf16[256,256]{1,0:T(8,128)(2,1)S(1)}, u32[]{:S(2)}, u32[]{:S(2)}) collective-permute-start(bf16[256,256]{1,0:T(8,128)(2,1)S(1)} %get-tuple-element.22), channel_id=1, source_target_pairs={{0,12},{4,8},{8,4},{12,0},{1,13},{5,9},{9,5},{13,1},{2,14},{6,10},... | collective-permute-start | bytes 393224 | tf_op jit(solution)/shard_map/ppermute | solution.py:44
  7.2 0.6 %collective-permute-start.2 = (bf16[256,256]{1,0:T(8,128)(2,1)S(1)}, bf16[256,256]{1,0:T(8,128)(2,1)S(1)}, u32[]{:S(2)}, u32[]{:S(2)}) collective-permute-start(bf16[256,256]{1,0:T(8,128)(2,1)S(1)} %get-tuple-element.25), channel_id=1, source_target_pairs={{0,4},{4,0},{8,12},{12,8},{1,5},{5,1},{9,13},{13,9},{2,6},{6,2},{1... | collective-permute-start | bytes 393224 | tf_op jit(solution)/shard_map/ppermute | solution.py:44
  7.9 2.2 %project.1 = (f32[48,128]{1,0:T(8,128)S(1)}, f32[48,128]{1,0:T(8,128)S(1)}, f32[48,128]{1,0:T(8,128)S(1)}, f32[48,128]{1,0:T(8,128)S(1)}, f32[4,8,256]{2,1,0:T(8,128)S(1)}) custom-call(bf16[256,256]{1,0:T(8,128)(2,1)S(1)} %get-tuple-element.19.after_ref.refs_3_.refs_0_, bf16[2,4,2048]{2,1,0:T(4,128)(2,1)S(1)} %copy-done.2, bf16[16,128]{1,0:T(8,128)(2,1)S(1)} %bitcast.4, ...), custom_call_target="tpu_custom_call" | custom-call | flops 83886080 | bytes 10485760 | tf_op jit(solution)/shard_map/project/pallas_call | solution.py:244
  10.1 2.4 %collective-permute-start.3 = (f32[48,128]{1,0:T(8,128)S(1)}, f32[48,128]{1,0:T(8,128)S(1)}, u32[]{:S(2)}, u32[]{:S(2)}) collective-permute-start(f32[48,128]{1,0:T(8,128)S(1)} %get-tuple-element.26), channel_id=1, source_target_pairs={{0,8},{4,12},{8,0},{12,4},{1,9},{5,13},{9,1},{13,5},{2,10},{6,14},... | collective-permute-start | bytes 73736 | tf_op jit(solution)/shard_map/ppermute | solution.py:44
  12.5 1.5 %collective-permute-start.4 = (f32[48,128]{1,0:T(8,128)S(1)}, f32[48,128]{1,0:T(8,128)S(1)}, u32[]{:S(2)}, u32[]{:S(2)}) collective-permute-start(f32[48,128]{1,0:T(8,128)S(1)} %get-tuple-element.27), channel_id=1, source_target_pairs={{0,12},{4,8},{8,4},{12,0},{1,13},{5,9},{9,5},{13,1},{2,14},{6,10},... | collective-permute-start | bytes 73736 | tf_op jit(solution)/shard_map/ppermute | solution.py:44
  14.1 3.5 %collective-permute-start.5 = (f32[48,128]{1,0:T(8,128)S(1)}, f32[48,128]{1,0:T(8,128)S(1)}, u32[]{:S(2)}, u32[]{:S(2)}) collective-permute-start(f32[48,128]{1,0:T(8,128)S(1)} %get-tuple-element.28), channel_id=1, source_target_pairs={{0,4},{4,0},{8,12},{12,8},{1,5},{5,1},{9,13},{13,9},{2,6},{6,2},{1... | collective-permute-start | bytes 73736 | tf_op jit(solution)/shard_map/ppermute | solution.py:44
  17.5 2.7 %collective-permute-done.3.refs_4_ = f32[48,128]{1,0:T(8,128)S(1)} collective-permute-done((f32[48,128]{1,0:T(8,128)S(1)}, f32[48,128]{1,0:T(8,128)S(1)}, u32[]{:S(2)}, u32[]{:S(2)}) %collective-permute-start.3) | collective-permute-done | bytes 24608 | tf_op jit(solution)/shard_map/ppermute | solution.py:44
  20.2 0.0 collective-permute-done.5.refs_6_
  20.3 0.5 %attend.1.own_ref.after_ref = bf16[32,128]{1,0:T(8,128)(2,1)S(1)} custom-call(f32[4,8,256]{2,1,0:T(8,128)S(1)} %get-tuple-element.20.which_ref, f32[8,128]{1,0:T(8,128)S(1)} %copy-done.6, f32[8,128]{1,0:T(8,128)S(1)} %copy-done.5, bf16[256,256]{1,0:T(8,128)(2,1)S(1)} %collective-permute-done.refs_0_.refs_3_, ...), custom_call_target="tpu_custom_call" | custom-call | flops 10000000000 | tf_op jit(solution)/shard_map/attend/pallas_call | solution.py:391
  20.8 1.2 %collective-permute-start.8 = (bf16[32,128]{1,0:T(8,128)(2,1)S(1)}, bf16[32,128]{1,0:T(8,128)(2,1)S(1)}, u32[]{:S(2)}, u32[]{:S(2)}) collective-permute-start(bf16[32,128]{1,0:T(8,128)(2,1)S(1)} %attend.1.own_ref.after_ref), channel_id=1, source_target_pairs={{0,4},{4,8},{8,12},{12,0},{1,5},{5,9},{9,13},{13,1},{2,6},{6,10},{... | collective-permute-start | bytes 24584 | tf_op jit(solution)/shard_map/ppermute | solution.py:49
  22.0 2.0 %collective-permute-start.7 = (bf16[32,128]{1,0:T(8,128)(2,1)S(1)}, bf16[32,128]{1,0:T(8,128)(2,1)S(1)}, u32[]{:S(2)}, u32[]{:S(2)}) collective-permute-start(bf16[32,128]{1,0:T(8,128)(2,1)S(1)} %attend.1.own_ref.after_ref), channel_id=1, source_target_pairs={{0,8},{4,12},{8,0},{12,4},{1,9},{5,13},{9,1},{13,5},{2,10},{6,14},... | collective-permute-start | bytes 24584 | tf_op jit(solution)/shard_map/ppermute | solution.py:49
  23.9 1.9 %collective-permute-start.6 = (bf16[32,128]{1,0:T(8,128)(2,1)S(1)}, bf16[32,128]{1,0:T(8,128)(2,1)S(1)}, u32[]{:S(2)}, u32[]{:S(2)}) collective-permute-start(bf16[32,128]{1,0:T(8,128)(2,1)S(1)} %attend.1.own_ref.after_ref), channel_id=1, source_target_pairs={{0,12},{4,0},{8,4},{12,8},{1,13},{5,1},{9,5},{13,9},{2,14},{6,2},{... | collective-permute-start | bytes 24584 | tf_op jit(solution)/shard_map/ppermute | solution.py:49
  25.9 0.4 %collective-permute-done.8.below_ref = bf16[32,128]{1,0:T(8,128)(2,1)S(1)} collective-permute-done((bf16[32,128]{1,0:T(8,128)(2,1)S(1)}, bf16[32,128]{1,0:T(8,128)(2,1)S(1)}, u32[]{:S(2)}, u32[]{:S(2)}) %collective-permute-start.8) | collective-permute-done | bytes 8224 | tf_op jit(solution)/shard_map/ppermute | solution.py:49
  26.3 0.2 collective-permute-done.7.second_ref
  26.5 0.7 %output_half.2.addend_ref = f32[8,2048]{1,0:T(8,128)S(1)} custom-call(bf16[2048,2048]{1,0:T(8,128)(2,1)S(1)} %bitcast.3, bf16[32,128]{1,0:T(8,128)(2,1)S(1)} %attend.1.own_ref.after_ref, bf16[32,128]{1,0:T(8,128)(2,1)S(1)} %collective-permute-done.7.second_ref), custom_call_target="tpu_custom_call" | custom-call | flops 1000000000 | tf_op jit(solution)/shard_map/output_half/pallas_call | solution.py:443
  27.2 0.4 %collective-permute-done.6.above_ref = bf16[32,128]{1,0:T(8,128)(2,1)S(1)} collective-permute-done((bf16[32,128]{1,0:T(8,128)(2,1)S(1)}, bf16[32,128]{1,0:T(8,128)(2,1)S(1)}, u32[]{:S(2)}, u32[]{:S(2)}) %collective-permute-start.6) | collective-permute-done | bytes 8224 | tf_op jit(solution)/shard_map/ppermute | solution.py:49
  27.6 0.7 %output_half.3 = bf16[8,2048]{1,0:T(8,128)(2,1)S(1)} custom-call(bf16[2048,2048]{1,0:T(8,128)(2,1)S(1)} %bitcast.3, bf16[32,128]{1,0:T(8,128)(2,1)S(1)} %collective-permute-done.6.above_ref, bf16[32,128]{1,0:T(8,128)(2,1)S(1)} %collective-permute-done.8.below_ref, f32[8,2048]{1,0:T(8,128)S(1)} %output_half.2.addend_ref), custom_call_target="tpu_custom_call" | custom-call | flops 1000000000 | tf_op jit(solution)/shard_map/output_half/pallas_call | solution.py:443
  28.2 1.5 %collective-permute-start.10 = (bf16[8,2048]{1,0:T(8,128)(2,1)S(1)}, bf16[8,2048]{1,0:T(8,128)(2,1)S(1)}, u32[]{:S(2)}, u32[]{:S(2)}) collective-permute-start(bf16[8,2048]{1,0:T(8,128)(2,1)S(1)} %output_half.3), channel_id=1, source_target_pairs={{0,2},{1,3},{2,0},{3,1},{4,6},{5,7},{6,4},{7,5},{8,10},{9,11},{10,... | collective-permute-start | bytes 98312 | tf_op jit(solution)/shard_map/ppermute | solution.py:44
  29.8 0.3 collective-permute-start.9
  30.1 1.3 %place.1 = bf16[1,1,512,256]{3,2,1,0:T(8,128)(2,1)} custom-call(s32[2,4,8]{2,1,0:T(4,128)S(1)} %bitcast.7, bf16[32,128]{1,0:T(8,128)(2,1)S(1)} %attend.1.own_ref.after_ref, bf16[256,256]{1,0:T(8,128)(2,1)S(1)} %get-tuple-element.19.after_ref.refs_3_.refs_0_, bf16[256,256]{1,0:T(8,128)(2,1)S(1)} %collective-permute-done.2.refs_2_.refs_1_, ...), custom_call_target="tpu_custom_call" | custom-call | flops 1000000000 | tf_op jit(solution)/shard_map/place/pallas_call | solution.py:289
  31.4 0.5 %collective-permute-done.11 = bf16[8,2048]{1,0:T(8,128)(2,1)S(1)} collective-permute-done((bf16[8,2048]{1,0:T(8,128)(2,1)S(1)}, bf16[8,2048]{1,0:T(8,128)(2,1)S(1)}, u32[]{:S(2)}, u32[]{:S(2)}) %collective-permute-start.11) | collective-permute-done | bytes 32800 | tf_op jit(solution)/shard_map/ppermute | solution.py:44
  31.9 0.4 %collective-permute-done.10 = bf16[8,2048]{1,0:T(8,128)(2,1)S(1)} collective-permute-done((bf16[8,2048]{1,0:T(8,128)(2,1)S(1)}, bf16[8,2048]{1,0:T(8,128)(2,1)S(1)}, u32[]{:S(2)}, u32[]{:S(2)}) %collective-permute-start.10) | collective-permute-done | bytes 32800 | tf_op jit(solution)/shard_map/ppermute | solution.py:44
  32.4 0.6 %add_convert_fusion = bf16[2,4,2048]{2,1,0:T(4,128)(2,1)} fusion(f32[2,4,2048]{2,1,0:T(4,128)S(1)} %reshape.11, bf16[2,4,2048]{2,1,0:T(4,128)(2,1)S(1)} %copy-done.2), kind=kLoop, calls=%fused_computation | loop fusion | flops 49152 | bytes 131072 | tf_op jit(solution)/shard_map/convert_element_type | solution.py:528
  (28 shorter events, 0.1 us)
Async XLA Ops:
  0.6 7.2 %copy-start = (bf16[2048,2048]{1,0:T(8,128)(2,1)S(1)}, bf16[2048,2048]{1,0:T(8,128)(2,1)}, u32[]{:S(2)}) copy-start(bf16[2048,2048]{1,0:T(8,128)(2,1)} %wq_ref.1) | copy-start | bytes 25165828
  0.6 7.2 %copy-start.1 = (bf16[2048,2,256]{2,1,0:T(2,128)(2,1)S(1)}, bf16[2048,2,256]{2,1,0:T(2,128)(2,1)}, u32[]{:S(2)}) copy-start(bf16[2048,2,256]{2,1,0:T(2,128)(2,1)} %wkv_ref.1) | copy-start | bytes 6291460
  0.7 7.2 %copy-start.2 = (bf16[2,4,2048]{2,1,0:T(4,128)(2,1)S(1)}, bf16[2,4,2048]{2,1,0:T(4,128)(2,1)}, u32[]{:S(2)}) copy-start(bf16[2,4,2048]{2,1,0:T(4,128)(2,1)} %hidden_ref.1) | copy-start | bytes 98308
  0.7 7.2 %copy-start.3 = (bf16[2048]{0:T(1024)(128)(2,1)S(1)}, bf16[2048]{0:T(1024)(128)(2,1)}, u32[]{:S(2)}) copy-start(bf16[2048]{0:T(1024)(128)(2,1)} %param.12) | copy-start | bytes 12292
  0.7 7.2 %copy-start.4 = (s32[2,8,4]{1,2,0:T(4,128)S(1)}, s32[2,8,4]{1,2,0:T(4,128)}, u32[]{:S(2)}) copy-start(s32[2,8,4]{1,2,0:T(4,128)} %param.10) | copy-start | bytes 772
  2.1 18.1 %copy-start.5 = (f32[8,128]{1,0:T(8,128)S(1)}, f32[8,128]{1,0:T(8,128)}, u32[]{:S(2)}) copy-start(f32[8,128]{1,0:T(8,128)} %constant.5.clone.sin_ref) | copy-start | bytes 12292
  2.1 18.1 %copy-start.6 = (f32[8,128]{1,0:T(8,128)S(1)}, f32[8,128]{1,0:T(8,128)}, u32[]{:S(2)}) copy-start(f32[8,128]{1,0:T(8,128)} %constant.4.clone.cos_ref) | copy-start | bytes 12292
  2.1 11.9 %collective-permute-start = (bf16[256,256]{1,0:T(8,128)(2,1)S(1)}, bf16[256,256]{1,0:T(8,128)(2,1)S(1)}, u32[]{:S(2)}, u32[]{:S(2)}) collective-permute-start(bf16[256,256]{1,0:T(8,128)(2,1)S(1)} %get-tuple-element.22), channel_id=1, source_target_pairs={{0,12},{4,8},{8,4},{12,0},{1,13},{5,9},{9,5},{13,1},{2,14},{6,10},... | collective-permute-start | bytes 393224 | tf_op jit(solution)/shard_map/ppermute | solution.py:44
  7.2 13.0 %collective-permute-start.1 = (bf16[256,256]{1,0:T(8,128)(2,1)S(1)}, bf16[256,256]{1,0:T(8,128)(2,1)S(1)}, u32[]{:S(2)}, u32[]{:S(2)}) collective-permute-start(bf16[256,256]{1,0:T(8,128)(2,1)S(1)} %get-tuple-element.24), channel_id=1, source_target_pairs={{0,8},{4,12},{8,0},{12,4},{1,9},{5,13},{9,1},{13,5},{2,10},{6,14},... | collective-permute-start | bytes 393224 | tf_op jit(solution)/shard_map/ppermute | solution.py:44
  7.2 13.0 %collective-permute-start.2 = (bf16[256,256]{1,0:T(8,128)(2,1)S(1)}, bf16[256,256]{1,0:T(8,128)(2,1)S(1)}, u32[]{:S(2)}, u32[]{:S(2)}) collective-permute-start(bf16[256,256]{1,0:T(8,128)(2,1)S(1)} %get-tuple-element.25), channel_id=1, source_target_pairs={{0,4},{4,0},{8,12},{12,8},{1,5},{5,1},{9,13},{13,9},{2,6},{6,2},{1... | collective-permute-start | bytes 393224 | tf_op jit(solution)/shard_map/ppermute | solution.py:44
  7.9 18.6 %slice-start = ((s8[8388608]{0:T(1024)(128)(4,1)}), s8[4194304]{0:T(1024)(128)(4,1)S(1)}, s32[]{:S(2)}) async-start(s8[8388608]{0:T(1024)(128)(4,1)} %bitcast.2), calls=%async_computation | async-start | bytes 8388608
  10.1 10.1 %collective-permute-start.3 = (f32[48,128]{1,0:T(8,128)S(1)}, f32[48,128]{1,0:T(8,128)S(1)}, u32[]{:S(2)}, u32[]{:S(2)}) collective-permute-start(f32[48,128]{1,0:T(8,128)S(1)} %get-tuple-element.26), channel_id=1, source_target_pairs={{0,8},{4,12},{8,0},{12,4},{1,9},{5,13},{9,1},{13,5},{2,10},{6,14},... | collective-permute-start | bytes 73736 | tf_op jit(solution)/shard_map/ppermute | solution.py:44
  12.5 7.7 %collective-permute-start.4 = (f32[48,128]{1,0:T(8,128)S(1)}, f32[48,128]{1,0:T(8,128)S(1)}, u32[]{:S(2)}, u32[]{:S(2)}) collective-permute-start(f32[48,128]{1,0:T(8,128)S(1)} %get-tuple-element.27), channel_id=1, source_target_pairs={{0,12},{4,8},{8,4},{12,0},{1,13},{5,9},{9,5},{13,1},{2,14},{6,10},... | collective-permute-start | bytes 73736 | tf_op jit(solution)/shard_map/ppermute | solution.py:44
  14.1 6.2 %collective-permute-start.5 = (f32[48,128]{1,0:T(8,128)S(1)}, f32[48,128]{1,0:T(8,128)S(1)}, u32[]{:S(2)}, u32[]{:S(2)}) collective-permute-start(f32[48,128]{1,0:T(8,128)S(1)} %get-tuple-element.28), channel_id=1, source_target_pairs={{0,4},{4,0},{8,12},{12,8},{1,5},{5,1},{9,13},{13,9},{2,6},{6,2},{1... | collective-permute-start | bytes 73736 | tf_op jit(solution)/shard_map/ppermute | solution.py:44
  20.3 6.3 %slice-start.1 = ((s8[8388608]{0:T(1024)(128)(4,1)}), s8[4194304]{0:T(1024)(128)(4,1)S(1)}, s32[]{:S(2)}) async-start(s8[8388608]{0:T(1024)(128)(4,1)} %bitcast.2), calls=%async_computation.1 | async-start | bytes 8388608
  20.8 5.5 %collective-permute-start.8 = (bf16[32,128]{1,0:T(8,128)(2,1)S(1)}, bf16[32,128]{1,0:T(8,128)(2,1)S(1)}, u32[]{:S(2)}, u32[]{:S(2)}) collective-permute-start(bf16[32,128]{1,0:T(8,128)(2,1)S(1)} %attend.1.own_ref.after_ref), channel_id=1, source_target_pairs={{0,4},{4,8},{8,12},{12,0},{1,5},{5,9},{9,13},{13,1},{2,6},{6,10},{... | collective-permute-start | bytes 24584 | tf_op jit(solution)/shard_map/ppermute | solution.py:49
  22.0 4.5 %collective-permute-start.7 = (bf16[32,128]{1,0:T(8,128)(2,1)S(1)}, bf16[32,128]{1,0:T(8,128)(2,1)S(1)}, u32[]{:S(2)}, u32[]{:S(2)}) collective-permute-start(bf16[32,128]{1,0:T(8,128)(2,1)S(1)} %attend.1.own_ref.after_ref), channel_id=1, source_target_pairs={{0,8},{4,12},{8,0},{12,4},{1,9},{5,13},{9,1},{13,5},{2,10},{6,14},... | collective-permute-start | bytes 24584 | tf_op jit(solution)/shard_map/ppermute | solution.py:49
  23.9 3.7 %collective-permute-start.6 = (bf16[32,128]{1,0:T(8,128)(2,1)S(1)}, bf16[32,128]{1,0:T(8,128)(2,1)S(1)}, u32[]{:S(2)}, u32[]{:S(2)}) collective-permute-start(bf16[32,128]{1,0:T(8,128)(2,1)S(1)} %attend.1.own_ref.after_ref), channel_id=1, source_target_pairs={{0,12},{4,0},{8,4},{12,8},{1,13},{5,1},{9,5},{13,9},{2,14},{6,2},{... | collective-permute-start | bytes 24584 | tf_op jit(solution)/shard_map/ppermute | solution.py:49
  28.2 3.7 %collective-permute-start.11 = (bf16[8,2048]{1,0:T(8,128)(2,1)S(1)}, bf16[8,2048]{1,0:T(8,128)(2,1)S(1)}, u32[]{:S(2)}, u32[]{:S(2)}) collective-permute-start(bf16[8,2048]{1,0:T(8,128)(2,1)S(1)} %output_half.3), channel_id=1, source_target_pairs={{0,3},{1,2},{2,1},{3,0},{4,7},{5,6},{6,5},{7,4},{8,11},{9,10},{10,... | collective-permute-start | bytes 98312 | tf_op jit(solution)/shard_map/ppermute | solution.py:44
  28.2 4.1 %collective-permute-start.10 = (bf16[8,2048]{1,0:T(8,128)(2,1)S(1)}, bf16[8,2048]{1,0:T(8,128)(2,1)S(1)}, u32[]{:S(2)}, u32[]{:S(2)}) collective-permute-start(bf16[8,2048]{1,0:T(8,128)(2,1)S(1)} %output_half.3), channel_id=1, source_target_pairs={{0,2},{1,3},{2,0},{3,1},{4,6},{5,7},{6,4},{7,5},{8,10},{9,11},{10,... | collective-permute-start | bytes 98312 | tf_op jit(solution)/shard_map/ppermute | solution.py:44
  29.8 2.5 %collective-permute-start.9 = (bf16[8,2048]{1,0:T(8,128)(2,1)S(1)}, bf16[8,2048]{1,0:T(8,128)(2,1)S(1)}, u32[]{:S(2)}, u32[]{:S(2)}) collective-permute-start(bf16[8,2048]{1,0:T(8,128)(2,1)S(1)} %output_half.3), channel_id=1, source_target_pairs={{0,1},{1,0},{2,3},{3,2},{4,5},{5,4},{6,7},{7,6},{8,9},{9,8},{10,11... | collective-permute-start | bytes 98312 | tf_op jit(solution)/shard_map/ppermute | solution.py:44

commit v23 on v22

--- a/solution.py
+++ b/solution.py
@@ -15,7 +15,7 @@
 BLK = 128
 MOST = 2
 ROPE_BASE = 500000.0
-TERM_ORDER = (2, 3, 1, 0)
+TERM_ORDER = (2, 1, 3, 0)
 EPS = 1e-05
 
 CONTRACT_LAST = (((1,), (1,)), ((), ()))
@@ -501,7 +501,7 @@
         blocks = list(pick(kept_blocks, source_cache, direct))
         *parts, mask = project(blocks[0], *weights, kept_blocks, source_blocks, direct)
         blocks = [blocks[0]] + [swap(blocks[k], "seq", k) for k in partners]
-        parts[1], blocks[3] = lax.optimization_barrier((parts[1], blocks[3]))
+        parts[3], blocks[3] = lax.optimization_barrier((parts[3], blocks[3]))
         parts = [parts[0]] + [swap(parts[k], "seq", k) for k in partners]
         arrivals = blocks[::-1] + [parts[k] for k in TERM_ORDER]
         (attended,) = attend(mask, arrivals, *shape)

time: 33.1 us -> 33 us (level)
  starting transfers between devices: 20.1 us -> 18.1 us
  waiting for transfers between devices: 4.61 us -> 6.54 us
    ppermute x9, starting transfers between devices: 15 us -> 13 us  [swap(): return lax.ppermute(outgoing, axis, [(i, i ^ offset) for i in range(count)])]
    ppermute x9, waiting for transfers between devices: 3.54 us -> 5.54 us  [swap(): return lax.ppermute(outgoing, axis, [(i, i ^ offset) for i in range(count)])]
  transfers between devices with their start and end apart: 12 -> 12, of which waited for: 6 -> 7; matrix products, arithmetic and copies ran while one was open for 0% -> 0% of each run, Pallas kernels for 13% -> 13%
where the time goes in v23:
time: 33 us; the launch traced here: 32.9 us
  starting transfers between devices  18.1 us (55%)
  Pallas kernels  6.78 us (21%)
  waiting for transfers between devices  6.54 us (20%)
  between operations  0.76 us (2%)
  other arithmetic  0.65 us (2%)
    ppermute x9, starting transfers between devices, swap(): return lax.ppermute(outgoing, axis, [(i, i ^ offset) for i in range(count)])  13 us
    ppermute x9, waiting for transfers between devices, swap(): return lax.ppermute(outgoing, axis, [(i, i ^ offset) for i in range(count)])  5.54 us
    ppermute x3, starting transfers between devices, shift(): lax.ppermute(outgoing, axis, [(i, (i + step) % count) for i in range(coun...  5.12 us
    pallas_call x1, Pallas kernels, project(): pl.pallas_call(functools.partial(project_kernel, direct, source_blocks),...  2.23 us
    pallas_call x1, Pallas kernels, pick(): pl.pallas_call(pick_near_kernel if direct else pick_all_kernel, out_shape...  1.4 us
    pallas_call x1, Pallas kernels, place(): pl.pallas_call(functools.partial(place_kernel, source_blocks, heads_local...  1.32 us
    pallas_call x2, Pallas kernels, output_half(): pl.pallas_call(kernel, out_shape=jax.ShapeDtypeStruct((rows, w_out.shape[...  1.3 us
    ppermute x3, waiting for transfers between devices, shift(): lax.ppermute(outgoing, axis, [(i, (i + step) % count) for i in range(coun...  0.99 us
  transfers between devices with their start and end apart: 12, of which 7 were waited for; matrix products, arithmetic and copies ran while one was open for 0% of the time, Pallas kernels for 13%

profile of v23, /device:TPU:0, one launch (start us, length us, event | category | flops | bytes accessed | tf_op | source)
XLA Modules:
  0.0 32.9 jit_solution(5833834734324080581)
XLA Ops:
  0.7 1.4 %pick_blocks.1 = (bf16[256,256]{1,0:T(8,128)(2,1)S(1)}, bf16[256,256]{1,0:T(8,128)(2,1)S(1)}, bf16[256,256]{1,0:T(8,128)(2,1)S(1)}, bf16[256,256]{1,0:T(8,128)(2,1)S(1)}) custom-call(s32[2,4,8]{2,1,0:T(4,128)} %bitcast.5, bf16[2,2,512,256]{3,2,1,0:T(8,128)(2,1)} %cache_ref.1), custom_call_target="tpu_custom_call" | custom-call | flops 10000000000 | tf_op jit(solution)/shard_map/pick_blocks/pallas_call | solution.py:136
  2.1 5.1 %collective-permute-start = (bf16[256,256]{1,0:T(8,128)(2,1)S(1)}, bf16[256,256]{1,0:T(8,128)(2,1)S(1)}, u32[]{:S(2)}, u32[]{:S(2)}) collective-permute-start(bf16[256,256]{1,0:T(8,128)(2,1)S(1)} %get-tuple-element.22), channel_id=1, source_target_pairs={{0,12},{4,8},{8,4},{12,0},{1,13},{5,9},{9,5},{13,1},{2,14},{6,10},... | collective-permute-start | bytes 393224 | tf_op jit(solution)/shard_map/ppermute | solution.py:44
  7.2 0.6 %collective-permute-start.2 = (bf16[256,256]{1,0:T(8,128)(2,1)S(1)}, bf16[256,256]{1,0:T(8,128)(2,1)S(1)}, u32[]{:S(2)}, u32[]{:S(2)}) collective-permute-start(bf16[256,256]{1,0:T(8,128)(2,1)S(1)} %get-tuple-element.25), channel_id=1, source_target_pairs={{0,4},{4,0},{8,12},{12,8},{1,5},{5,1},{9,13},{13,9},{2,6},{6,2},{1... | collective-permute-start | bytes 393224 | tf_op jit(solution)/shard_map/ppermute | solution.py:44
  7.9 2.2 %project.1 = (f32[48,128]{1,0:T(8,128)S(1)}, f32[48,128]{1,0:T(8,128)S(1)}, f32[48,128]{1,0:T(8,128)S(1)}, f32[48,128]{1,0:T(8,128)S(1)}, f32[4,8,256]{2,1,0:T(8,128)S(1)}) custom-call(bf16[256,256]{1,0:T(8,128)(2,1)S(1)} %get-tuple-element.19.after_ref.refs_3_.refs_0_, bf16[2,4,2048]{2,1,0:T(4,128)(2,1)S(1)} %copy-done.2, bf16[16,128]{1,0:T(8,128)(2,1)S(1)} %bitcast.4, ...), custom_call_target="tpu_custom_call" | custom-call | flops 83886080 | bytes 10485760 | tf_op jit(solution)/shard_map/project/pallas_call | solution.py:244
  10.1 2.4 %collective-permute-start.3 = (f32[48,128]{1,0:T(8,128)S(1)}, f32[48,128]{1,0:T(8,128)S(1)}, u32[]{:S(2)}, u32[]{:S(2)}) collective-permute-start(f32[48,128]{1,0:T(8,128)S(1)} %get-tuple-element.26), channel_id=1, source_target_pairs={{0,8},{4,12},{8,0},{12,4},{1,9},{5,13},{9,1},{13,5},{2,10},{6,14},... | collective-permute-start | bytes 73736 | tf_op jit(solution)/shard_map/ppermute | solution.py:44
  12.5 2.0 %collective-permute-start.4 = (f32[48,128]{1,0:T(8,128)S(1)}, f32[48,128]{1,0:T(8,128)S(1)}, u32[]{:S(2)}, u32[]{:S(2)}) collective-permute-start(f32[48,128]{1,0:T(8,128)S(1)} %get-tuple-element.27), channel_id=1, source_target_pairs={{0,4},{4,0},{8,12},{12,8},{1,5},{5,1},{9,13},{13,9},{2,6},{6,2},{1... | collective-permute-start | bytes 73736 | tf_op jit(solution)/shard_map/ppermute | solution.py:44
  14.5 0.9 %collective-permute-start.5 = (f32[48,128]{1,0:T(8,128)S(1)}, f32[48,128]{1,0:T(8,128)S(1)}, u32[]{:S(2)}, u32[]{:S(2)}) collective-permute-start(f32[48,128]{1,0:T(8,128)S(1)} %get-tuple-element.28), channel_id=1, source_target_pairs={{0,12},{4,8},{8,4},{12,0},{1,13},{5,9},{9,5},{13,1},{2,14},{6,10},... | collective-permute-start | bytes 73736 | tf_op jit(solution)/shard_map/ppermute | solution.py:44
  15.5 4.4 %collective-permute-done.3.refs_4_ = f32[48,128]{1,0:T(8,128)S(1)} collective-permute-done((f32[48,128]{1,0:T(8,128)S(1)}, f32[48,128]{1,0:T(8,128)S(1)}, u32[]{:S(2)}, u32[]{:S(2)}) %collective-permute-start.3) | collective-permute-done | bytes 24608 | tf_op jit(solution)/shard_map/ppermute | solution.py:44
  19.9 0.3 collective-permute-done.5.refs_6_
  20.2 0.5 %attend.1.own_ref.after_ref = bf16[32,128]{1,0:T(8,128)(2,1)S(1)} custom-call(f32[4,8,256]{2,1,0:T(8,128)S(1)} %get-tuple-element.20.which_ref, f32[8,128]{1,0:T(8,128)S(1)} %copy-done.6, f32[8,128]{1,0:T(8,128)S(1)} %copy-done.5, bf16[256,256]{1,0:T(8,128)(2,1)S(1)} %collective-permute-done.refs_0_.refs_3_, ...), custom_call_target="tpu_custom_call" | custom-call | flops 10000000000 | tf_op jit(solution)/shard_map/attend/pallas_call | solution.py:391
  20.7 1.0 %collective-permute-start.8 = (bf16[32,128]{1,0:T(8,128)(2,1)S(1)}, bf16[32,128]{1,0:T(8,128)(2,1)S(1)}, u32[]{:S(2)}, u32[]{:S(2)}) collective-permute-start(bf16[32,128]{1,0:T(8,128)(2,1)S(1)} %attend.1.own_ref.after_ref), channel_id=1, source_target_pairs={{0,4},{4,8},{8,12},{12,0},{1,5},{5,9},{9,13},{13,1},{2,6},{6,10},{... | collective-permute-start | bytes 24584 | tf_op jit(solution)/shard_map/ppermute | solution.py:49
  21.7 2.1 %collective-permute-start.7 = (bf16[32,128]{1,0:T(8,128)(2,1)S(1)}, bf16[32,128]{1,0:T(8,128)(2,1)S(1)}, u32[]{:S(2)}, u32[]{:S(2)}) collective-permute-start(bf16[32,128]{1,0:T(8,128)(2,1)S(1)} %attend.1.own_ref.after_ref), channel_id=1, source_target_pairs={{0,8},{4,12},{8,0},{12,4},{1,9},{5,13},{9,1},{13,5},{2,10},{6,14},... | collective-permute-start | bytes 24584 | tf_op jit(solution)/shard_map/ppermute | solution.py:49
  23.8 2.0 %collective-permute-start.6 = (bf16[32,128]{1,0:T(8,128)(2,1)S(1)}, bf16[32,128]{1,0:T(8,128)(2,1)S(1)}, u32[]{:S(2)}, u32[]{:S(2)}) collective-permute-start(bf16[32,128]{1,0:T(8,128)(2,1)S(1)} %attend.1.own_ref.after_ref), channel_id=1, source_target_pairs={{0,12},{4,0},{8,4},{12,8},{1,13},{5,1},{9,5},{13,9},{2,14},{6,2},{... | collective-permute-start | bytes 24584 | tf_op jit(solution)/shard_map/ppermute | solution.py:49
  25.8 0.4 %collective-permute-done.8.below_ref = bf16[32,128]{1,0:T(8,128)(2,1)S(1)} collective-permute-done((bf16[32,128]{1,0:T(8,128)(2,1)S(1)}, bf16[32,128]{1,0:T(8,128)(2,1)S(1)}, u32[]{:S(2)}, u32[]{:S(2)}) %collective-permute-start.8) | collective-permute-done | bytes 8224 | tf_op jit(solution)/shard_map/ppermute | solution.py:49
  26.2 0.1 collective-permute-done.7.second_ref
  26.3 0.7 %output_half.2.addend_ref = f32[8,2048]{1,0:T(8,128)S(1)} custom-call(bf16[2048,2048]{1,0:T(8,128)(2,1)S(1)} %bitcast.3, bf16[32,128]{1,0:T(8,128)(2,1)S(1)} %attend.1.own_ref.after_ref, bf16[32,128]{1,0:T(8,128)(2,1)S(1)} %collective-permute-done.7.second_ref), custom_call_target="tpu_custom_call" | custom-call | flops 1000000000 | tf_op jit(solution)/shard_map/output_half/pallas_call | solution.py:443
  27.0 0.5 %collective-permute-done.6.above_ref = bf16[32,128]{1,0:T(8,128)(2,1)S(1)} collective-permute-done((bf16[32,128]{1,0:T(8,128)(2,1)S(1)}, bf16[32,128]{1,0:T(8,128)(2,1)S(1)}, u32[]{:S(2)}, u32[]{:S(2)}) %collective-permute-start.6) | collective-permute-done | bytes 8224 | tf_op jit(solution)/shard_map/ppermute | solution.py:49
  27.5 0.7 %output_half.3 = bf16[8,2048]{1,0:T(8,128)(2,1)S(1)} custom-call(bf16[2048,2048]{1,0:T(8,128)(2,1)S(1)} %bitcast.3, bf16[32,128]{1,0:T(8,128)(2,1)S(1)} %collective-permute-done.6.above_ref, bf16[32,128]{1,0:T(8,128)(2,1)S(1)} %collective-permute-done.8.below_ref, f32[8,2048]{1,0:T(8,128)S(1)} %output_half.2.addend_ref), custom_call_target="tpu_custom_call" | custom-call | flops 1000000000 | tf_op jit(solution)/shard_map/output_half/pallas_call | solution.py:443
  28.1 1.5 %collective-permute-start.10 = (bf16[8,2048]{1,0:T(8,128)(2,1)S(1)}, bf16[8,2048]{1,0:T(8,128)(2,1)S(1)}, u32[]{:S(2)}, u32[]{:S(2)}) collective-permute-start(bf16[8,2048]{1,0:T(8,128)(2,1)S(1)} %output_half.3), channel_id=1, source_target_pairs={{0,2},{1,3},{2,0},{3,1},{4,6},{5,7},{6,4},{7,5},{8,10},{9,11},{10,... | collective-permute-start | bytes 98312 | tf_op jit(solution)/shard_map/ppermute | solution.py:44
  29.7 0.3 %collective-permute-start.9 = (bf16[8,2048]{1,0:T(8,128)(2,1)S(1)}, bf16[8,2048]{1,0:T(8,128)(2,1)S(1)}, u32[]{:S(2)}, u32[]{:S(2)}) collective-permute-start(bf16[8,2048]{1,0:T(8,128)(2,1)S(1)} %output_half.3), channel_id=1, source_target_pairs={{0,1},{1,0},{2,3},{3,2},{4,5},{5,4},{6,7},{7,6},{8,9},{9,8},{10,11... | collective-permute-start | bytes 98312 | tf_op jit(solution)/shard_map/ppermute | solution.py:44
  30.0 1.3 %place.1 = bf16[1,1,512,256]{3,2,1,0:T(8,128)(2,1)} custom-call(s32[2,4,8]{2,1,0:T(4,128)S(1)} %bitcast.7, bf16[32,128]{1,0:T(8,128)(2,1)S(1)} %attend.1.own_ref.after_ref, bf16[256,256]{1,0:T(8,128)(2,1)S(1)} %get-tuple-element.19.after_ref.refs_3_.refs_0_, bf16[256,256]{1,0:T(8,128)(2,1)S(1)} %collective-permute-done.2.refs_2_.refs_1_, ...), custom_call_target="tpu_custom_call" | custom-call | flops 1000000000 | tf_op jit(solution)/shard_map/place/pallas_call | solution.py:289
  31.3 0.5 %collective-permute-done.11 = bf16[8,2048]{1,0:T(8,128)(2,1)S(1)} collective-permute-done((bf16[8,2048]{1,0:T(8,128)(2,1)S(1)}, bf16[8,2048]{1,0:T(8,128)(2,1)S(1)}, u32[]{:S(2)}, u32[]{:S(2)}) %collective-permute-start.11) | collective-permute-done | bytes 32800 | tf_op jit(solution)/shard_map/ppermute | solution.py:44
  31.8 0.4 %collective-permute-done.10 = bf16[8,2048]{1,0:T(8,128)(2,1)S(1)} collective-permute-done((bf16[8,2048]{1,0:T(8,128)(2,1)S(1)}, bf16[8,2048]{1,0:T(8,128)(2,1)S(1)}, u32[]{:S(2)}, u32[]{:S(2)}) %collective-permute-start.10) | collective-permute-done | bytes 32800 | tf_op jit(solution)/shard_map/ppermute | solution.py:44
  32.2 0.6 %add_convert_fusion = bf16[2,4,2048]{2,1,0:T(4,128)(2,1)} fusion(f32[2,4,2048]{2,1,0:T(4,128)S(1)} %reshape.11, bf16[2,4,2048]{2,1,0:T(4,128)(2,1)S(1)} %copy-done.2), kind=kLoop, calls=%fused_computation | loop fusion | flops 49152 | bytes 131072 | tf_op jit(solution)/shard_map/convert_element_type | solution.py:528
  (28 shorter events, 0.1 us)
Async XLA Ops:
  0.6 7.2 %copy-start = (bf16[2048,2048]{1,0:T(8,128)(2,1)S(1)}, bf16[2048,2048]{1,0:T(8,128)(2,1)}, u32[]{:S(2)}) copy-start(bf16[2048,2048]{1,0:T(8,128)(2,1)} %wq_ref.1) | copy-start | bytes 25165828
  0.6 7.2 %copy-start.1 = (bf16[2048,2,256]{2,1,0:T(2,128)(2,1)S(1)}, bf16[2048,2,256]{2,1,0:T(2,128)(2,1)}, u32[]{:S(2)}) copy-start(bf16[2048,2,256]{2,1,0:T(2,128)(2,1)} %wkv_ref.1) | copy-start | bytes 6291460
  0.7 7.2 %copy-start.2 = (bf16[2,4,2048]{2,1,0:T(4,128)(2,1)S(1)}, bf16[2,4,2048]{2,1,0:T(4,128)(2,1)}, u32[]{:S(2)}) copy-start(bf16[2,4,2048]{2,1,0:T(4,128)(2,1)} %hidden_ref.1) | copy-start | bytes 98308
  0.7 7.2 %copy-start.3 = (bf16[2048]{0:T(1024)(128)(2,1)S(1)}, bf16[2048]{0:T(1024)(128)(2,1)}, u32[]{:S(2)}) copy-start(bf16[2048]{0:T(1024)(128)(2,1)} %param.12) | copy-start | bytes 12292
  0.7 7.2 %copy-start.4 = (s32[2,8,4]{1,2,0:T(4,128)S(1)}, s32[2,8,4]{1,2,0:T(4,128)}, u32[]{:S(2)}) copy-start(s32[2,8,4]{1,2,0:T(4,128)} %param.10) | copy-start | bytes 772
  2.1 18.1 %copy-start.5 = (f32[8,128]{1,0:T(8,128)S(1)}, f32[8,128]{1,0:T(8,128)}, u32[]{:S(2)}) copy-start(f32[8,128]{1,0:T(8,128)} %constant.5.clone.sin_ref) | copy-start | bytes 12292
  2.1 18.1 %copy-start.6 = (f32[8,128]{1,0:T(8,128)S(1)}, f32[8,128]{1,0:T(8,128)}, u32[]{:S(2)}) copy-start(f32[8,128]{1,0:T(8,128)} %constant.4.clone.cos_ref) | copy-start | bytes 12292
  2.1 12.4 %collective-permute-start = (bf16[256,256]{1,0:T(8,128)(2,1)S(1)}, bf16[256,256]{1,0:T(8,128)(2,1)S(1)}, u32[]{:S(2)}, u32[]{:S(2)}) collective-permute-start(bf16[256,256]{1,0:T(8,128)(2,1)S(1)} %get-tuple-element.22), channel_id=1, source_target_pairs={{0,12},{4,8},{8,4},{12,0},{1,13},{5,9},{9,5},{13,1},{2,14},{6,10},... | collective-permute-start | bytes 393224 | tf_op jit(solution)/shard_map/ppermute | solution.py:44
  7.2 12.7 %collective-permute-start.1 = (bf16[256,256]{1,0:T(8,128)(2,1)S(1)}, bf16[256,256]{1,0:T(8,128)(2,1)S(1)}, u32[]{:S(2)}, u32[]{:S(2)}) collective-permute-start(bf16[256,256]{1,0:T(8,128)(2,1)S(1)} %get-tuple-element.24), channel_id=1, source_target_pairs={{0,8},{4,12},{8,0},{12,4},{1,9},{5,13},{9,1},{13,5},{2,10},{6,14},... | collective-permute-start | bytes 393224 | tf_op jit(solution)/shard_map/ppermute | solution.py:44
  7.2 12.7 %collective-permute-start.2 = (bf16[256,256]{1,0:T(8,128)(2,1)S(1)}, bf16[256,256]{1,0:T(8,128)(2,1)S(1)}, u32[]{:S(2)}, u32[]{:S(2)}) collective-permute-start(bf16[256,256]{1,0:T(8,128)(2,1)S(1)} %get-tuple-element.25), channel_id=1, source_target_pairs={{0,4},{4,0},{8,12},{12,8},{1,5},{5,1},{9,13},{13,9},{2,6},{6,2},{1... | collective-permute-start | bytes 393224 | tf_op jit(solution)/shard_map/ppermute | solution.py:44
  7.9 18.4 %slice-start = ((s8[8388608]{0:T(1024)(128)(4,1)}), s8[4194304]{0:T(1024)(128)(4,1)S(1)}, s32[]{:S(2)}) async-start(s8[8388608]{0:T(1024)(128)(4,1)} %bitcast.2), calls=%async_computation | async-start | bytes 8388608
  10.1 9.7 %collective-permute-start.3 = (f32[48,128]{1,0:T(8,128)S(1)}, f32[48,128]{1,0:T(8,128)S(1)}, u32[]{:S(2)}, u32[]{:S(2)}) collective-permute-start(f32[48,128]{1,0:T(8,128)S(1)} %get-tuple-element.26), channel_id=1, source_target_pairs={{0,8},{4,12},{8,0},{12,4},{1,9},{5,13},{9,1},{13,5},{2,10},{6,14},... | collective-permute-start | bytes 73736 | tf_op jit(solution)/shard_map/ppermute | solution.py:44
  12.5 7.4 %collective-permute-start.4 = (f32[48,128]{1,0:T(8,128)S(1)}, f32[48,128]{1,0:T(8,128)S(1)}, u32[]{:S(2)}, u32[]{:S(2)}) collective-permute-start(f32[48,128]{1,0:T(8,128)S(1)} %get-tuple-element.27), channel_id=1, source_target_pairs={{0,4},{4,0},{8,12},{12,8},{1,5},{5,1},{9,13},{13,9},{2,6},{6,2},{1... | collective-permute-start | bytes 73736 | tf_op jit(solution)/shard_map/ppermute | solution.py:44
  14.5 5.6 %collective-permute-start.5 = (f32[48,128]{1,0:T(8,128)S(1)}, f32[48,128]{1,0:T(8,128)S(1)}, u32[]{:S(2)}, u32[]{:S(2)}) collective-permute-start(f32[48,128]{1,0:T(8,128)S(1)} %get-tuple-element.28), channel_id=1, source_target_pairs={{0,12},{4,8},{8,4},{12,0},{1,13},{5,9},{9,5},{13,1},{2,14},{6,10},... | collective-permute-start | bytes 73736 | tf_op jit(solution)/shard_map/ppermute | solution.py:44
  20.2 6.1 %slice-start.1 = ((s8[8388608]{0:T(1024)(128)(4,1)}), s8[4194304]{0:T(1024)(128)(4,1)S(1)}, s32[]{:S(2)}) async-start(s8[8388608]{0:T(1024)(128)(4,1)} %bitcast.2), calls=%async_computation.1 | async-start | bytes 8388608
  20.7 5.5 %collective-permute-start.8 = (bf16[32,128]{1,0:T(8,128)(2,1)S(1)}, bf16[32,128]{1,0:T(8,128)(2,1)S(1)}, u32[]{:S(2)}, u32[]{:S(2)}) collective-permute-start(bf16[32,128]{1,0:T(8,128)(2,1)S(1)} %attend.1.own_ref.after_ref), channel_id=1, source_target_pairs={{0,4},{4,8},{8,12},{12,0},{1,5},{5,9},{9,13},{13,1},{2,6},{6,10},{... | collective-permute-start | bytes 24584 | tf_op jit(solution)/shard_map/ppermute | solution.py:49
  21.7 4.6 %collective-permute-start.7 = (bf16[32,128]{1,0:T(8,128)(2,1)S(1)}, bf16[32,128]{1,0:T(8,128)(2,1)S(1)}, u32[]{:S(2)}, u32[]{:S(2)}) collective-permute-start(bf16[32,128]{1,0:T(8,128)(2,1)S(1)} %attend.1.own_ref.after_ref), channel_id=1, source_target_pairs={{0,8},{4,12},{8,0},{12,4},{1,9},{5,13},{9,1},{13,5},{2,10},{6,14},... | collective-permute-start | bytes 24584 | tf_op jit(solution)/shard_map/ppermute | solution.py:49
  23.8 3.7 %collective-permute-start.6 = (bf16[32,128]{1,0:T(8,128)(2,1)S(1)}, bf16[32,128]{1,0:T(8,128)(2,1)S(1)}, u32[]{:S(2)}, u32[]{:S(2)}) collective-permute-start(bf16[32,128]{1,0:T(8,128)(2,1)S(1)} %attend.1.own_ref.after_ref), channel_id=1, source_target_pairs={{0,12},{4,0},{8,4},{12,8},{1,13},{5,1},{9,5},{13,9},{2,14},{6,2},{... | collective-permute-start | bytes 24584 | tf_op jit(solution)/shard_map/ppermute | solution.py:49
  28.1 3.7 %collective-permute-start.11 = (bf16[8,2048]{1,0:T(8,128)(2,1)S(1)}, bf16[8,2048]{1,0:T(8,128)(2,1)S(1)}, u32[]{:S(2)}, u32[]{:S(2)}) collective-permute-start(bf16[8,2048]{1,0:T(8,128)(2,1)S(1)} %output_half.3), channel_id=1, source_target_pairs={{0,3},{1,2},{2,1},{3,0},{4,7},{5,6},{6,5},{7,4},{8,11},{9,10},{10,... | collective-permute-start | bytes 98312 | tf_op jit(solution)/shard_map/ppermute | solution.py:44
  28.1 4.1 %collective-permute-start.10 = (bf16[8,2048]{1,0:T(8,128)(2,1)S(1)}, bf16[8,2048]{1,0:T(8,128)(2,1)S(1)}, u32[]{:S(2)}, u32[]{:S(2)}) collective-permute-start(bf16[8,2048]{1,0:T(8,128)(2,1)S(1)} %output_half.3), channel_id=1, source_target_pairs={{0,2},{1,3},{2,0},{3,1},{4,6},{5,7},{6,4},{7,5},{8,10},{9,11},{10,... | collective-permute-start | bytes 98312 | tf_op jit(solution)/shard_map/ppermute | solution.py:44
  29.7 2.5 %collective-permute-start.9 = (bf16[8,2048]{1,0:T(8,128)(2,1)S(1)}, bf16[8,2048]{1,0:T(8,128)(2,1)S(1)}, u32[]{:S(2)}, u32[]{:S(2)}) collective-permute-start(bf16[8,2048]{1,0:T(8,128)(2,1)S(1)} %output_half.3), channel_id=1, source_target_pairs={{0,1},{1,0},{2,3},{3,2},{4,5},{5,4},{6,7},{7,6},{8,9},{9,8},{10,11... | collective-permute-start | bytes 98312 | tf_op jit(solution)/shard_map/ppermute | solution.py:44

commit v24 on v22

--- a/solution.py
+++ b/solution.py
@@ -80,7 +80,7 @@
     return places
 
 
-def pick_near_kernel(kept_hbm_ref, cache_ref, *refs):
+def pick_near_kernel(offsets, kept_hbm_ref, cache_ref, *refs):
     *outs, kept_ref, cache, kept_sem, sem = refs
     heads_local = cache.shape[1]
     me = lax.axis_index("seq")
@@ -91,7 +91,6 @@
         place = split_index(pair, heads_local)
         return pltpu.make_async_copy(cache_ref.at[place], cache.at[place], sem.at[pair])
 
-    offsets = list(reversed(range(len(outs))))
     copies = {offset: pair_copy(jnp.bitwise_xor(me, offset)) for offset in offsets}
     for offset in offsets:
         copies[offset].start()
@@ -100,7 +99,7 @@
         places = picked_rows(kept_ref, cache.shape, jnp.bitwise_xor(me, offset))
         copies[offset].wait()
         for slot, (request, local, rows) in enumerate(places):
-            outs[offset][slot * BLK : (slot + 1) * BLK, :] = cache[request, local, rows, :]
+            outs[offsets.index(offset)][slot * BLK : (slot + 1) * BLK, :] = cache[request, local, rows, :]
 
 
 def pick_all_kernel(kept_hbm_ref, cache_ref, out_ref, kept_ref, sem):
@@ -117,13 +116,13 @@
     pltpu.make_async_copy(out_ref, out_ref, sem).wait()
 
 
-def pick(kept_blocks, source_cache, direct):
+def pick(kept_blocks, source_cache, offsets):
     requests, heads_local, _, row_width = source_cache.shape
     pair_count = requests * heads_local
     block = (MOST * BLK, row_width)
     kept_scratch = pltpu.SMEM(kept_blocks.shape, jnp.int32)
-    if direct:
-        shapes = [jax.ShapeDtypeStruct(block, jnp.bfloat16)] * pair_count
+    if offsets:
+        shapes = [jax.ShapeDtypeStruct(block, jnp.bfloat16)] * len(offsets)
         scratch = [
             kept_scratch,
             pltpu.VMEM(source_cache.shape, jnp.bfloat16),
@@ -134,13 +133,15 @@
         shapes = [jax.ShapeDtypeStruct((pair_count,) + block, jnp.bfloat16)]
         scratch = [kept_scratch, pltpu.SemaphoreType.DMA]
     return pl.pallas_call(
-        pick_near_kernel if direct else pick_all_kernel,
+        functools.partial(pick_near_kernel, offsets) if offsets else pick_all_kernel,
         out_shape=shapes,
         in_specs=[pl.BlockSpec(memory_space=pl.ANY)] * 2,
         out_specs=[pl.BlockSpec(memory_space=pltpu.VMEM)] * len(shapes),
         scratch_shapes=scratch,
         compiler_params=pltpu.CompilerParams(vmem_limit_bytes=8 * 1024 * 1024),
-        cost_estimate=pl.CostEstimate(flops=10**10, bytes_accessed=0, transcendentals=0),
+        cost_estimate=pl.CostEstimate(
+            flops=10**6 if offsets == (0,) else 10**10, bytes_accessed=0, transcendentals=0
+        ),
         name="pick_blocks",
     )(
         pltpu.with_memory_space_constraint(kept_blocks, pltpu.HBM),
@@ -498,8 +499,11 @@
     shape = (source_blocks, heads_local, step_count, seq_count, direct)
     if direct:
         partners = range(1, seq_count)
-        blocks = list(pick(kept_blocks, source_cache, direct))
-        *parts, mask = project(blocks[0], *weights, kept_blocks, source_blocks, direct)
+        third, second, first = pick(kept_blocks, source_cache, (3, 2, 1))
+        *parts, mask = project(first, *weights, kept_blocks, source_blocks, direct)
+        later, parts[0] = lax.optimization_barrier((kept_blocks, parts[0]))
+        (own,) = pick(later, source_cache, (0,))
+        blocks = [own, first, second, third]
         blocks = [blocks[0]] + [swap(blocks[k], "seq", k) for k in partners]
         parts[1], blocks[3] = lax.optimization_barrier((parts[1], blocks[3]))
         parts = [parts[0]] + [swap(parts[k], "seq", k) for k in partners]
@@ -511,7 +515,7 @@
         terms = output_half(output_same_kernel, jnp.float32, w_out, attended, second)
         terms = output_half(output_other_kernel, jnp.bfloat16, w_out, above, below, terms)
     else:
-        (blocks,) = pick(kept_blocks, source_cache, direct)
+        (blocks,) = pick(kept_blocks, source_cache, ())
         (parts,) = project(blocks, *weights, kept_blocks, source_blocks, direct)
         arrivals = [all_to_all(parts, "seq"), all_to_all(blocks, "seq")]
         attended, kept_cache = attend(kept_blocks, arrivals, *shape)

time: 33.1 us -> 33.1 us (level)
  waiting for transfers between devices: 4.61 us -> 3.44 us
  Pallas kernels: 6.78 us -> 7.84 us
    ppermute x9, waiting for transfers between devices: 3.54 us -> 2.37 us  [swap(): return lax.ppermute(outgoing, axis, [(i, i ^ offset) for i in range(count)])]
    pallas_call x1 -> x2, Pallas kernels: 1.4 us -> 2.48 us  [pick(): pl.pallas_call(functools.partial(pick_near_kernel, offsets) if offsets el...]
  transfers between devices with their start and end apart: 12 -> 12, of which waited for: 6 -> 6; matrix products, arithmetic and copies ran while one was open for 0% -> 0% of each run, Pallas kernels for 13% -> 16%
where the time goes in v24:
time: 33.1 us; the launch traced here: 32.9 us
  starting transfers between devices  20.1 us (61%)
  Pallas kernels  7.84 us (24%)
  waiting for transfers between devices  3.44 us (10%)
  between operations  0.79 us (2%)
  other arithmetic  0.65 us (2%)
    ppermute x9, starting transfers between devices, swap(): return lax.ppermute(outgoing, axis, [(i, i ^ offset) for i in range(count)])  15.1 us
    ppermute x3, starting transfers between devices, shift(): lax.ppermute(outgoing, axis, [(i, (i + step) % count) for i in range(coun...  5.06 us
    pallas_call x2, Pallas kernels, pick(): pl.pallas_call(functools.partial(pick_near_kernel, offsets) if offsets el...  2.48 us
    ppermute x9, waiting for transfers between devices, swap(): return lax.ppermute(outgoing, axis, [(i, i ^ offset) for i in range(count)])  2.37 us
    pallas_call x1, Pallas kernels, project(): pl.pallas_call(functools.partial(project_kernel, direct, source_blocks),...  2.21 us
    pallas_call x1, Pallas kernels, place(): pl.pallas_call(functools.partial(place_kernel, source_blocks, heads_local...  1.32 us
    pallas_call x2, Pallas kernels, output_half(): pl.pallas_call(kernel, out_shape=jax.ShapeDtypeStruct((rows, w_out.shape[...  1.3 us
    ppermute x3, waiting for transfers between devices, shift(): lax.ppermute(outgoing, axis, [(i, (i + step) % count) for i in range(coun...  1.07 us
  transfers between devices with their start and end apart: 12, of which 6 were waited for; matrix products, arithmetic and copies ran while one was open for 0% of the time, Pallas kernels for 16%

profile of v24, /device:TPU:0, one launch (start us, length us, event | category | flops | bytes accessed | tf_op | source)
XLA Modules:
  0.0 32.9 jit_solution(10487746725879614321)
XLA Ops:
  0.7 1.3 %pick_blocks.2 = (bf16[256,256]{1,0:T(8,128)(2,1)S(1)}, bf16[256,256]{1,0:T(8,128)(2,1)S(1)}, bf16[256,256]{1,0:T(8,128)(2,1)S(1)}) custom-call(s32[2,4,8]{2,1,0:T(4,128)} %bitcast.4, bf16[2,2,512,256]{3,2,1,0:T(8,128)(2,1)} %cache_ref.3), custom_call_target="tpu_custom_call" | custom-call | flops 10000000000 | tf_op jit(solution)/shard_map/pick_blocks/pallas_call | solution.py:135
  2.0 5.1 %collective-permute-start = (bf16[256,256]{1,0:T(8,128)(2,1)S(1)}, bf16[256,256]{1,0:T(8,128)(2,1)S(1)}, u32[]{:S(2)}, u32[]{:S(2)}) collective-permute-start(bf16[256,256]{1,0:T(8,128)(2,1)S(1)} %get-tuple-element.23), channel_id=1, source_target_pairs={{0,12},{4,8},{8,4},{12,0},{1,13},{5,9},{9,5},{13,1},{2,14},{6,10},... | collective-permute-start | bytes 393224 | tf_op jit(solution)/shard_map/ppermute | solution.py:44
  7.2 0.6 %collective-permute-start.2 = (bf16[256,256]{1,0:T(8,128)(2,1)S(1)}, bf16[256,256]{1,0:T(8,128)(2,1)S(1)}, u32[]{:S(2)}, u32[]{:S(2)}) collective-permute-start(bf16[256,256]{1,0:T(8,128)(2,1)S(1)} %get-tuple-element.20.after_ref), channel_id=1, source_target_pairs={{0,4},{4,0},{8,12},{12,8},{1,5},{5,1},{9,13},{13,9},{2,6},{6,2},{1... | collective-permute-start | bytes 393224 | tf_op jit(solution)/shard_map/ppermute | solution.py:44
  7.8 2.2 %project.1 = (f32[48,128]{1,0:T(8,128)S(1)}, f32[48,128]{1,0:T(8,128)S(1)}, f32[48,128]{1,0:T(8,128)S(1)}, f32[48,128]{1,0:T(8,128)S(1)}, f32[4,8,256]{2,1,0:T(8,128)S(1)}) custom-call(bf16[256,256]{1,0:T(8,128)(2,1)S(1)} %get-tuple-element.20.after_ref, bf16[2,4,2048]{2,1,0:T(4,128)(2,1)S(1)} %copy-done.2, bf16[16,128]{1,0:T(8,128)(2,1)S(1)} %bitcast.8, ...), custom_call_target="tpu_custom_call" | custom-call | flops 83886080 | bytes 10485760 | tf_op jit(solution)/shard_map/project/pallas_call | solution.py:245
  10.0 2.4 %collective-permute-start.3 = (f32[48,128]{1,0:T(8,128)S(1)}, f32[48,128]{1,0:T(8,128)S(1)}, u32[]{:S(2)}, u32[]{:S(2)}) collective-permute-start(f32[48,128]{1,0:T(8,128)S(1)} %get-tuple-element.28), channel_id=1, source_target_pairs={{0,8},{4,12},{8,0},{12,4},{1,9},{5,13},{9,1},{13,5},{2,10},{6,14},... | collective-permute-start | bytes 73736 | tf_op jit(solution)/shard_map/ppermute | solution.py:44
  12.4 1.5 %collective-permute-start.4 = (f32[48,128]{1,0:T(8,128)S(1)}, f32[48,128]{1,0:T(8,128)S(1)}, u32[]{:S(2)}, u32[]{:S(2)}) collective-permute-start(f32[48,128]{1,0:T(8,128)S(1)} %get-tuple-element.29), channel_id=1, source_target_pairs={{0,12},{4,8},{8,4},{12,0},{1,13},{5,9},{9,5},{13,1},{2,14},{6,10},... | collective-permute-start | bytes 73736 | tf_op jit(solution)/shard_map/ppermute | solution.py:44
  13.9 3.5 %collective-permute-start.5 = (f32[48,128]{1,0:T(8,128)S(1)}, f32[48,128]{1,0:T(8,128)S(1)}, u32[]{:S(2)}, u32[]{:S(2)}) collective-permute-start(f32[48,128]{1,0:T(8,128)S(1)} %get-tuple-element.30), channel_id=1, source_target_pairs={{0,4},{4,0},{8,12},{12,8},{1,5},{5,1},{9,13},{13,9},{2,6},{6,2},{1... | collective-permute-start | bytes 73736 | tf_op jit(solution)/shard_map/ppermute | solution.py:44
  17.5 1.2 %pick_blocks.3.refs_3_.refs_0_ = bf16[256,256]{1,0:T(8,128)(2,1)S(1)} custom-call(s32[2,4,8]{2,1,0:T(4,128)} %bitcast.5, bf16[2,2,512,256]{3,2,1,0:T(8,128)(2,1)} %cache_ref.3), custom_call_target="tpu_custom_call" | custom-call | flops 1000000 | tf_op jit(solution)/shard_map/pick_blocks/pallas_call | solution.py:135
  18.6 1.5 %collective-permute-done.3.refs_4_ = f32[48,128]{1,0:T(8,128)S(1)} collective-permute-done((f32[48,128]{1,0:T(8,128)S(1)}, f32[48,128]{1,0:T(8,128)S(1)}, u32[]{:S(2)}, u32[]{:S(2)}) %collective-permute-start.3) | collective-permute-done | bytes 24608 | tf_op jit(solution)/shard_map/ppermute | solution.py:44
  20.2 0.5 %attend.1.own_ref.after_ref = bf16[32,128]{1,0:T(8,128)(2,1)S(1)} custom-call(f32[4,8,256]{2,1,0:T(8,128)S(1)} %get-tuple-element.21.which_ref, f32[8,128]{1,0:T(8,128)S(1)} %copy-done.7, f32[8,128]{1,0:T(8,128)S(1)} %copy-done.6, bf16[256,256]{1,0:T(8,128)(2,1)S(1)} %collective-permute-done.refs_0_.refs_3_, ...), custom_call_target="tpu_custom_call" | custom-call | flops 10000000000 | tf_op jit(solution)/shard_map/attend/pallas_call | solution.py:392
  20.7 1.2 %collective-permute-start.8 = (bf16[32,128]{1,0:T(8,128)(2,1)S(1)}, bf16[32,128]{1,0:T(8,128)(2,1)S(1)}, u32[]{:S(2)}, u32[]{:S(2)}) collective-permute-start(bf16[32,128]{1,0:T(8,128)(2,1)S(1)} %attend.1.own_ref.after_ref), channel_id=1, source_target_pairs={{0,4},{4,8},{8,12},{12,0},{1,5},{5,9},{9,13},{13,1},{2,6},{6,10},{... | collective-permute-start | bytes 24584 | tf_op jit(solution)/shard_map/ppermute | solution.py:49
  21.9 2.0 %collective-permute-start.7 = (bf16[32,128]{1,0:T(8,128)(2,1)S(1)}, bf16[32,128]{1,0:T(8,128)(2,1)S(1)}, u32[]{:S(2)}, u32[]{:S(2)}) collective-permute-start(bf16[32,128]{1,0:T(8,128)(2,1)S(1)} %attend.1.own_ref.after_ref), channel_id=1, source_target_pairs={{0,8},{4,12},{8,0},{12,4},{1,9},{5,13},{9,1},{13,5},{2,10},{6,14},... | collective-permute-start | bytes 24584 | tf_op jit(solution)/shard_map/ppermute | solution.py:49
  23.9 1.9 %collective-permute-start.6 = (bf16[32,128]{1,0:T(8,128)(2,1)S(1)}, bf16[32,128]{1,0:T(8,128)(2,1)S(1)}, u32[]{:S(2)}, u32[]{:S(2)}) collective-permute-start(bf16[32,128]{1,0:T(8,128)(2,1)S(1)} %attend.1.own_ref.after_ref), channel_id=1, source_target_pairs={{0,12},{4,0},{8,4},{12,8},{1,13},{5,1},{9,5},{13,9},{2,14},{6,2},{... | collective-permute-start | bytes 24584 | tf_op jit(solution)/shard_map/ppermute | solution.py:49
  25.8 0.4 %collective-permute-done.8.below_ref = bf16[32,128]{1,0:T(8,128)(2,1)S(1)} collective-permute-done((bf16[32,128]{1,0:T(8,128)(2,1)S(1)}, bf16[32,128]{1,0:T(8,128)(2,1)S(1)}, u32[]{:S(2)}, u32[]{:S(2)}) %collective-permute-start.8) | collective-permute-done | bytes 8224 | tf_op jit(solution)/shard_map/ppermute | solution.py:49
  26.2 0.2 collective-permute-done.7.second_ref
  26.5 0.7 %output_half.2.addend_ref = f32[8,2048]{1,0:T(8,128)S(1)} custom-call(bf16[2048,2048]{1,0:T(8,128)(2,1)S(1)} %bitcast.3, bf16[32,128]{1,0:T(8,128)(2,1)S(1)} %attend.1.own_ref.after_ref, bf16[32,128]{1,0:T(8,128)(2,1)S(1)} %collective-permute-done.7.second_ref), custom_call_target="tpu_custom_call" | custom-call | flops 1000000000 | tf_op jit(solution)/shard_map/output_half/pallas_call | solution.py:444
  27.1 0.4 %collective-permute-done.6.above_ref = bf16[32,128]{1,0:T(8,128)(2,1)S(1)} collective-permute-done((bf16[32,128]{1,0:T(8,128)(2,1)S(1)}, bf16[32,128]{1,0:T(8,128)(2,1)S(1)}, u32[]{:S(2)}, u32[]{:S(2)}) %collective-permute-start.6) | collective-permute-done | bytes 8224 | tf_op jit(solution)/shard_map/ppermute | solution.py:49
  27.5 0.7 %output_half.3 = bf16[8,2048]{1,0:T(8,128)(2,1)S(1)} custom-call(bf16[2048,2048]{1,0:T(8,128)(2,1)S(1)} %bitcast.3, bf16[32,128]{1,0:T(8,128)(2,1)S(1)} %collective-permute-done.6.above_ref, bf16[32,128]{1,0:T(8,128)(2,1)S(1)} %collective-permute-done.8.below_ref, f32[8,2048]{1,0:T(8,128)S(1)} %output_half.2.addend_ref), custom_call_target="tpu_custom_call" | custom-call | flops 1000000000 | tf_op jit(solution)/shard_map/output_half/pallas_call | solution.py:444
  28.2 1.5 %collective-permute-start.10 = (bf16[8,2048]{1,0:T(8,128)(2,1)S(1)}, bf16[8,2048]{1,0:T(8,128)(2,1)S(1)}, u32[]{:S(2)}, u32[]{:S(2)}) collective-permute-start(bf16[8,2048]{1,0:T(8,128)(2,1)S(1)} %output_half.3), channel_id=1, source_target_pairs={{0,2},{1,3},{2,0},{3,1},{4,6},{5,7},{6,4},{7,5},{8,10},{9,11},{10,... | collective-permute-start | bytes 98312 | tf_op jit(solution)/shard_map/ppermute | solution.py:44
  29.7 0.3 collective-permute-start.9
  30.1 1.3 %place.1 = bf16[1,1,512,256]{3,2,1,0:T(8,128)(2,1)} custom-call(s32[2,4,8]{2,1,0:T(4,128)S(1)} %bitcast.7, bf16[32,128]{1,0:T(8,128)(2,1)S(1)} %attend.1.own_ref.after_ref, bf16[256,256]{1,0:T(8,128)(2,1)S(1)} %pick_blocks.3.refs_3_.refs_0_, bf16[256,256]{1,0:T(8,128)(2,1)S(1)} %collective-permute-done.2.refs_2_.refs_1_, ...), custom_call_target="tpu_custom_call" | custom-call | flops 1000000000 | tf_op jit(solution)/shard_map/place/pallas_call | solution.py:290
  31.4 0.5 %collective-permute-done.11 = bf16[8,2048]{1,0:T(8,128)(2,1)S(1)} collective-permute-done((bf16[8,2048]{1,0:T(8,128)(2,1)S(1)}, bf16[8,2048]{1,0:T(8,128)(2,1)S(1)}, u32[]{:S(2)}, u32[]{:S(2)}) %collective-permute-start.11) | collective-permute-done | bytes 32800 | tf_op jit(solution)/shard_map/ppermute | solution.py:44
  31.8 0.4 %collective-permute-done.10 = bf16[8,2048]{1,0:T(8,128)(2,1)S(1)} collective-permute-done((bf16[8,2048]{1,0:T(8,128)(2,1)S(1)}, bf16[8,2048]{1,0:T(8,128)(2,1)S(1)}, u32[]{:S(2)}, u32[]{:S(2)}) %collective-permute-start.10) | collective-permute-done | bytes 32800 | tf_op jit(solution)/shard_map/ppermute | solution.py:44
  32.3 0.6 %add_convert_fusion = bf16[2,4,2048]{2,1,0:T(4,128)(2,1)} fusion(f32[2,4,2048]{2,1,0:T(4,128)S(1)} %reshape.11, bf16[2,4,2048]{2,1,0:T(4,128)(2,1)S(1)} %copy-done.2), kind=kLoop, calls=%fused_computation | loop fusion | flops 49152 | bytes 131072 | tf_op jit(solution)/shard_map/convert_element_type | solution.py:532
  (31 shorter events, 0.1 us)
Async XLA Ops:
  0.6 7.2 %copy-start = (bf16[2048,2048]{1,0:T(8,128)(2,1)S(1)}, bf16[2048,2048]{1,0:T(8,128)(2,1)}, u32[]{:S(2)}) copy-start(bf16[2048,2048]{1,0:T(8,128)(2,1)} %wq_ref.1) | copy-start | bytes 25165828
  0.6 7.2 %copy-start.1 = (bf16[2048,2,256]{2,1,0:T(2,128)(2,1)S(1)}, bf16[2048,2,256]{2,1,0:T(2,128)(2,1)}, u32[]{:S(2)}) copy-start(bf16[2048,2,256]{2,1,0:T(2,128)(2,1)} %wkv_ref.1) | copy-start | bytes 6291460
  0.7 7.2 %copy-start.2 = (bf16[2,4,2048]{2,1,0:T(4,128)(2,1)S(1)}, bf16[2,4,2048]{2,1,0:T(4,128)(2,1)}, u32[]{:S(2)}) copy-start(bf16[2,4,2048]{2,1,0:T(4,128)(2,1)} %hidden_ref.1) | copy-start | bytes 98308
  0.7 7.1 %copy-start.3 = (s32[2,8,4]{1,2,0:T(4,128)S(1)}, s32[2,8,4]{1,2,0:T(4,128)}, u32[]{:S(2)}) copy-start(s32[2,8,4]{1,2,0:T(4,128)} %param.10) | copy-start | bytes 772
  0.7 7.1 %copy-start.5 = (bf16[2048]{0:T(1024)(128)(2,1)S(1)}, bf16[2048]{0:T(1024)(128)(2,1)}, u32[]{:S(2)}) copy-start(bf16[2048]{0:T(1024)(128)(2,1)} %param.12) | copy-start | bytes 12292
  2.0 18.1 %copy-start.6 = (f32[8,128]{1,0:T(8,128)S(1)}, f32[8,128]{1,0:T(8,128)}, u32[]{:S(2)}) copy-start(f32[8,128]{1,0:T(8,128)} %constant.5.clone.sin_ref) | copy-start | bytes 12292
  2.0 18.1 %copy-start.7 = (f32[8,128]{1,0:T(8,128)S(1)}, f32[8,128]{1,0:T(8,128)}, u32[]{:S(2)}) copy-start(f32[8,128]{1,0:T(8,128)} %constant.4.clone.cos_ref) | copy-start | bytes 12292
  2.0 11.9 %collective-permute-start = (bf16[256,256]{1,0:T(8,128)(2,1)S(1)}, bf16[256,256]{1,0:T(8,128)(2,1)S(1)}, u32[]{:S(2)}, u32[]{:S(2)}) collective-permute-start(bf16[256,256]{1,0:T(8,128)(2,1)S(1)} %get-tuple-element.23), channel_id=1, source_target_pairs={{0,12},{4,8},{8,4},{12,0},{1,13},{5,9},{9,5},{13,1},{2,14},{6,10},... | collective-permute-start | bytes 393224 | tf_op jit(solution)/shard_map/ppermute | solution.py:44
  7.2 13.0 %collective-permute-start.1 = (bf16[256,256]{1,0:T(8,128)(2,1)S(1)}, bf16[256,256]{1,0:T(8,128)(2,1)S(1)}, u32[]{:S(2)}, u32[]{:S(2)}) collective-permute-start(bf16[256,256]{1,0:T(8,128)(2,1)S(1)} %get-tuple-element.25), channel_id=1, source_target_pairs={{0,8},{4,12},{8,0},{12,4},{1,9},{5,13},{9,1},{13,5},{2,10},{6,14},... | collective-permute-start | bytes 393224 | tf_op jit(solution)/shard_map/ppermute | solution.py:44
  7.2 13.0 %collective-permute-start.2 = (bf16[256,256]{1,0:T(8,128)(2,1)S(1)}, bf16[256,256]{1,0:T(8,128)(2,1)S(1)}, u32[]{:S(2)}, u32[]{:S(2)}) collective-permute-start(bf16[256,256]{1,0:T(8,128)(2,1)S(1)} %get-tuple-element.20.after_ref), channel_id=1, source_target_pairs={{0,4},{4,0},{8,12},{12,8},{1,5},{5,1},{9,13},{13,9},{2,6},{6,2},{1... | collective-permute-start | bytes 393224 | tf_op jit(solution)/shard_map/ppermute | solution.py:44
  10.0 10.1 %collective-permute-start.3 = (f32[48,128]{1,0:T(8,128)S(1)}, f32[48,128]{1,0:T(8,128)S(1)}, u32[]{:S(2)}, u32[]{:S(2)}) collective-permute-start(f32[48,128]{1,0:T(8,128)S(1)} %get-tuple-element.28), channel_id=1, source_target_pairs={{0,8},{4,12},{8,0},{12,4},{1,9},{5,13},{9,1},{13,5},{2,10},{6,14},... | collective-permute-start | bytes 73736 | tf_op jit(solution)/shard_map/ppermute | solution.py:44
  12.4 7.7 %collective-permute-start.4 = (f32[48,128]{1,0:T(8,128)S(1)}, f32[48,128]{1,0:T(8,128)S(1)}, u32[]{:S(2)}, u32[]{:S(2)}) collective-permute-start(f32[48,128]{1,0:T(8,128)S(1)} %get-tuple-element.29), channel_id=1, source_target_pairs={{0,12},{4,8},{8,4},{12,0},{1,13},{5,9},{9,5},{13,1},{2,14},{6,10},... | collective-permute-start | bytes 73736 | tf_op jit(solution)/shard_map/ppermute | solution.py:44
  13.9 6.2 %collective-permute-start.5 = (f32[48,128]{1,0:T(8,128)S(1)}, f32[48,128]{1,0:T(8,128)S(1)}, u32[]{:S(2)}, u32[]{:S(2)}) collective-permute-start(f32[48,128]{1,0:T(8,128)S(1)} %get-tuple-element.30), channel_id=1, source_target_pairs={{0,4},{4,0},{8,12},{12,8},{1,5},{5,1},{9,13},{13,9},{2,6},{6,2},{1... | collective-permute-start | bytes 73736 | tf_op jit(solution)/shard_map/ppermute | solution.py:44
  17.5 9.0 %slice-start = ((s8[8388608]{0:T(1024)(128)(4,1)}), s8[4194304]{0:T(1024)(128)(4,1)S(1)}, s32[]{:S(2)}) async-start(s8[8388608]{0:T(1024)(128)(4,1)} %bitcast.2), calls=%async_computation | async-start | bytes 8388608
  20.2 6.3 %slice-start.1 = ((s8[8388608]{0:T(1024)(128)(4,1)}), s8[4194304]{0:T(1024)(128)(4,1)S(1)}, s32[]{:S(2)}) async-start(s8[8388608]{0:T(1024)(128)(4,1)} %bitcast.2), calls=%async_computation.1 | async-start | bytes 8388608
  20.7 9.3 %copy-start.4 = (s32[2,8,4]{1,2,0:T(4,128)S(1)}, s32[2,8,4]{1,2,0:T(4,128)}, u32[]{:S(2)}) copy-start(s32[2,8,4]{1,2,0:T(4,128)} %param.10) | copy-start | bytes 772
  20.7 5.5 %collective-permute-start.8 = (bf16[32,128]{1,0:T(8,128)(2,1)S(1)}, bf16[32,128]{1,0:T(8,128)(2,1)S(1)}, u32[]{:S(2)}, u32[]{:S(2)}) collective-permute-start(bf16[32,128]{1,0:T(8,128)(2,1)S(1)} %attend.1.own_ref.after_ref), channel_id=1, source_target_pairs={{0,4},{4,8},{8,12},{12,0},{1,5},{5,9},{9,13},{13,1},{2,6},{6,10},{... | collective-permute-start | bytes 24584 | tf_op jit(solution)/shard_map/ppermute | solution.py:49
  21.9 4.5 %collective-permute-start.7 = (bf16[32,128]{1,0:T(8,128)(2,1)S(1)}, bf16[32,128]{1,0:T(8,128)(2,1)S(1)}, u32[]{:S(2)}, u32[]{:S(2)}) collective-permute-start(bf16[32,128]{1,0:T(8,128)(2,1)S(1)} %attend.1.own_ref.after_ref), channel_id=1, source_target_pairs={{0,8},{4,12},{8,0},{12,4},{1,9},{5,13},{9,1},{13,5},{2,10},{6,14},... | collective-permute-start | bytes 24584 | tf_op jit(solution)/shard_map/ppermute | solution.py:49
  23.9 3.7 %collective-permute-start.6 = (bf16[32,128]{1,0:T(8,128)(2,1)S(1)}, bf16[32,128]{1,0:T(8,128)(2,1)S(1)}, u32[]{:S(2)}, u32[]{:S(2)}) collective-permute-start(bf16[32,128]{1,0:T(8,128)(2,1)S(1)} %attend.1.own_ref.after_ref), channel_id=1, source_target_pairs={{0,12},{4,0},{8,4},{12,8},{1,13},{5,1},{9,5},{13,9},{2,14},{6,2},{... | collective-permute-start | bytes 24584 | tf_op jit(solution)/shard_map/ppermute | solution.py:49
  28.2 3.7 %collective-permute-start.11 = (bf16[8,2048]{1,0:T(8,128)(2,1)S(1)}, bf16[8,2048]{1,0:T(8,128)(2,1)S(1)}, u32[]{:S(2)}, u32[]{:S(2)}) collective-permute-start(bf16[8,2048]{1,0:T(8,128)(2,1)S(1)} %output_half.3), channel_id=1, source_target_pairs={{0,3},{1,2},{2,1},{3,0},{4,7},{5,6},{6,5},{7,4},{8,11},{9,10},{10,... | collective-permute-start | bytes 98312 | tf_op jit(solution)/shard_map/ppermute | solution.py:44
  28.2 4.1 %collective-permute-start.10 = (bf16[8,2048]{1,0:T(8,128)(2,1)S(1)}, bf16[8,2048]{1,0:T(8,128)(2,1)S(1)}, u32[]{:S(2)}, u32[]{:S(2)}) collective-permute-start(bf16[8,2048]{1,0:T(8,128)(2,1)S(1)} %output_half.3), channel_id=1, source_target_pairs={{0,2},{1,3},{2,0},{3,1},{4,6},{5,7},{6,4},{7,5},{8,10},{9,11},{10,... | collective-permute-start | bytes 98312 | tf_op jit(solution)/shard_map/ppermute | solution.py:44
  29.7 2.5 %collective-permute-start.9 = (bf16[8,2048]{1,0:T(8,128)(2,1)S(1)}, bf16[8,2048]{1,0:T(8,128)(2,1)S(1)}, u32[]{:S(2)}, u32[]{:S(2)}) collective-permute-start(bf16[8,2048]{1,0:T(8,128)(2,1)S(1)} %output_half.3), channel_id=1, source_target_pairs={{0,1},{1,0},{2,3},{3,2},{4,5},{5,4},{6,7},{7,6},{8,9},{9,8},{10,11... | collective-permute-start | bytes 98312 | tf_op jit(solution)/shard_map/ppermute | solution.py:44
